TPU v7x, 32 devices: a whole 2x2x4 slice. The times are simulated.
32 devices in a mesh: shard: 4 (over y, x), replica: 8 (over z, core).
Axes of the slice: x: 2, y: 2, z: 4, core: 2. Of those that a mesh axis runs over, the one named last changes fastest.
Arguments:
- hidden_in: bfloat16 [1024, 16, 1600], P('shard', 'replica'), may hold values from -6 to 6
- out_grad: bfloat16 [1024, 16, 1600], P('shard', 'replica'), may hold values from -6 to 6
- segments: int32 [1024, 16], P(None, 'replica'), may hold values from 0 to 17, as said below
- ln1_gain: float32 [1600], replicated, may hold values from 0.1 to 1.9
- ln1_bias: float32 [1600], replicated, may hold values from -1.5 to 1.5
- qkv_weight: bfloat16 [4800, 1600], P('shard'), may hold values from -0.15625 to 0.15625
- q_bias: float32 [1600], replicated, may hold values from -2.5 to 2.5
- v_bias: float32 [1600], replicated, may hold values from -2.5 to 2.5
- output_projection_weight: bfloat16 [1600, 1600], P('shard'), may hold values from -0.875 to 0.875
- out_bias: float32 [1600], replicated, may hold values from -1.5 to 1.5
- ln2_gain: float32 [1600], replicated, may hold values from 0.1 to 1.9
- ln2_bias: float32 [1600], replicated, may hold values from -1.5 to 1.5
- up_weight: bfloat16 [6400, 1600], P('shard'), may hold values from -0.15625 to 0.15625
- up_bias: float32 [6400], replicated, may hold values from -2.5 to 2.5
- down_weight: bfloat16 [1600, 6400], P('shard'), may hold values from -0.078125 to 0.078125
- down_bias: float32 [1600], replicated, may hold values from -1.5 to 1.5
Outputs:
- block_out: bfloat16 [1024, 16, 1600], P('shard', 'replica')
- input_grad: float32 [1024, 16, 1600], P('shard', 'replica')
- ln1_gain_grad: float32 [1600], replicated
- ln1_bias_grad: float32 [1600], replicated
- qkv_weight_grad: float32 [4800, 1600], P('shard')
- q_bias_grad: float32 [1600], replicated
- v_bias_grad: float32 [1600], replicated
- out_weight_grad: float32 [1600, 1600], P('shard')
- out_bias_grad: float32 [1600], replicated
- ln2_gain_grad: float32 [1600], replicated
- ln2_bias_grad: float32 [1600], replicated
- up_weight_grad: float32 [6400, 1600], P('shard')
- up_bias_grad: float32 [6400], replicated
- down_weight_grad: float32 [1600, 6400], P('shard')
- down_bias_grad: float32 [1600], replicated
Inputs may be any that keep to these rules, and one draw needn't show every extreme that they name: `segments`: in each sequence the numbers start at 0 and rise by 0 or 1 from one position to the next; every document but a sequence's last has 60 to 800 tokens; of the 2 sequences of one index of replica, one is a single document.
All inputs are finite; a program needn't handle non-finite values.
Results may differ from a plain program's by a relative error of at most 0.019.
Values may be sent and summed in bfloat16 or wider, within the bound.
No kernel may reach another device: no remote copies, remote signals or barrier semaphores. Data moves between devices by JAX's collectives and lax.ppermute only.
A program may use at most 448 MiB of HBM per device.

v0:
```python
import jax
import jax.numpy as jnp
from jax import lax
from jax.sharding import PartitionSpec as P

HEADS = 25
HDIM = 64


def layer_norm(value_rows, gain_vec, shift_vec):
    centre = value_rows - jnp.mean(value_rows, axis=-1, keepdims=True)
    spread = jnp.mean(centre * centre, axis=-1, keepdims=True)
    return centre * lax.rsqrt(spread + 1e-05) * gain_vec + shift_vec


def project(value_rows, weight_matrix):
    return lax.dot_general(
        value_rows, weight_matrix, (((1,), (1,)), ((), ())), preferred_element_type=jnp.float32
    )


def split_heads(array, len_here, seq_count):
    return array.reshape(len_here, seq_count, HEADS, HDIM).transpose(2, 1, 0, 3)


def join_heads(array):
    heads_count, seq_count, len_here, head_dim = array.shape
    return array.transpose(2, 1, 0, 3).reshape(len_here, seq_count, heads_count * head_dim)


def gelu_tanh(value_rows):
    return jax.nn.gelu(value_rows, approximate=True)


def rows_term(left, right):
    return lax.dot_general(
        left, right, (((0,), (0,)), ((), ())), preferred_element_type=jnp.float32
    )


def shards(
    hidden_in,
    out_grad,
    segments,
    ln1_gain,
    ln1_bias,
    qkv_weight,
    q_bias,
    v_bias,
    output_projection_weight,
    out_bias,
    ln2_gain,
    ln2_bias,
    up_weight,
    up_bias,
    down_weight,
    down_bias,
):
    local_len, seq_count, width = hidden_in.shape
    row_count = local_len * seq_count
    full_len = segments.shape[0]
    offset = lax.axis_index("shard") * local_len
    local_seg = lax.dynamic_slice_in_dim(segments, offset, local_len, 0)
    places = jnp.arange(full_len)
    query_places = offset + jnp.arange(local_len)
    allowed = (local_seg.T[:, :, None] == segments.T[:, None, :]) & (
        query_places[None, :, None] >= places[None, None, :]
    )
    gathered = (
        lax.all_gather(qkv_weight, "shard", axis=0, tiled=True),
        lax.all_gather(output_projection_weight, "shard", axis=0, tiled=True),
        lax.all_gather(up_weight, "shard", axis=0, tiled=True),
        lax.all_gather(down_weight, "shard", axis=0, tiled=True),
    )
    w_qkv, w_out, w_up, w_down = gathered
    tokens = hidden_in.reshape(row_count, width).astype(jnp.float32)
    normed = layer_norm(tokens, ln1_gain, ln1_bias).astype(jnp.bfloat16)
    joined = project(normed, w_qkv)
    queries = (joined[:, :width] + q_bias).astype(jnp.bfloat16)
    keys_local = (
        joined[:, width : 2 * width].astype(jnp.bfloat16).reshape(local_len, seq_count, width)
    )
    values_local = (
        (joined[:, 2 * width :] + v_bias).astype(jnp.bfloat16).reshape(local_len, seq_count, width)
    )
    keys_full, values_full = (
        lax.all_gather(keys_local, "shard", axis=0, tiled=True),
        lax.all_gather(values_local, "shard", axis=0, tiled=True),
    )

    def head_forward(operands):
        head_q, head_k, head_v = operands
        scores = jnp.where(
            allowed,
            jnp.einsum("sqd,skd->sqk", head_q, head_k, preferred_element_type=jnp.float32) * 0.125,
            -1e30,
        )
        peak = jnp.max(scores, axis=-1, keepdims=True)
        exp_terms = jnp.exp(scores - peak)
        totals = jnp.sum(exp_terms, axis=-1, keepdims=True)
        soft = (exp_terms / totals).astype(jnp.bfloat16)
        mixed = jnp.einsum("sqk,skd->sqd", soft, head_v, preferred_element_type=jnp.float32)
        return (mixed, (peak + jnp.log(totals))[..., 0])

    heads_q = split_heads(queries, local_len, seq_count)
    mixed_heads, log_totals = lax.map(
        head_forward,
        (
            heads_q,
            split_heads(keys_full, full_len, seq_count),
            split_heads(values_full, full_len, seq_count),
        ),
    )
    attended = join_heads(mixed_heads).reshape(row_count, width).astype(jnp.bfloat16)
    middle = tokens + project(attended, w_out) + out_bias
    normed_two = layer_norm(middle, ln2_gain, ln2_bias).astype(jnp.bfloat16)
    pre_act = project(normed_two, w_up) + up_bias
    activ = gelu_tanh(pre_act).astype(jnp.bfloat16)
    result = (
        (middle + project(activ, w_down) + down_bias)
        .astype(jnp.bfloat16)
        .reshape(local_len, seq_count, width)
    )
    w_qkv, w_out, w_up, w_down = (
        lax.all_gather(qkv_weight, "shard", axis=0, tiled=True),
        lax.all_gather(output_projection_weight, "shard", axis=0, tiled=True),
        lax.all_gather(up_weight, "shard", axis=0, tiled=True),
        lax.all_gather(down_weight, "shard", axis=0, tiled=True),
    )
    grad_out = out_grad.reshape(row_count, width)
    grad_out_f = grad_out.astype(jnp.float32)
    down_bias_grad = jnp.sum(grad_out_f, axis=0)
    grad_act = jnp.dot(grad_out, w_down, preferred_element_type=jnp.float32)
    gelu_out, gelu_pull = jax.vjp(gelu_tanh, pre_act)
    grad_pre = gelu_pull(grad_act)[0].astype(jnp.bfloat16)
    up_bias_grad = jnp.sum(grad_pre.astype(jnp.float32), axis=0)
    grad_norm_two = jnp.dot(grad_pre, w_up, preferred_element_type=jnp.float32)
    norm_out, norm_pull = jax.vjp(layer_norm, middle, ln2_gain, ln2_bias)
    grad_mid_part, ln2_gain_grad, ln2_bias_grad = norm_pull(grad_norm_two)
    grad_middle = grad_out_f + grad_mid_part
    grad_branch = grad_middle.astype(jnp.bfloat16)
    out_bias_grad = jnp.sum(grad_branch.astype(jnp.float32), axis=0)
    grad_attended = jnp.dot(grad_branch, w_out, preferred_element_type=jnp.float32).astype(
        jnp.bfloat16
    )
    keys_full, values_full = (
        lax.all_gather(keys_local, "shard", axis=0, tiled=True),
        lax.all_gather(values_local, "shard", axis=0, tiled=True),
    )
    heads_keys = split_heads(keys_full, full_len, seq_count)
    heads_values = split_heads(values_full, full_len, seq_count)
    heads_grad_att = split_heads(grad_attended, local_len, seq_count)

    def head_backward(operands):
        head_q, head_k, head_v, head_grad, head_lse = operands
        scores = jnp.where(
            allowed,
            jnp.einsum("sqd,skd->sqk", head_q, head_k, preferred_element_type=jnp.float32) * 0.125,
            -1e30,
        )
        soft = jnp.exp(scores - head_lse[..., None])
        soft_low = soft.astype(jnp.bfloat16)
        soft_grad = jnp.einsum(
            "sqd,skd->sqk", head_grad, head_v, preferred_element_type=jnp.float32
        )
        rowdot = jnp.sum(soft * soft_grad, axis=-1, keepdims=True)
        score_grad = (soft * (soft_grad - rowdot)).astype(jnp.bfloat16)
        grad_q = (
            jnp.einsum("sqk,skd->sqd", score_grad, head_k, preferred_element_type=jnp.float32)
            * 0.125
        )
        grad_k = (
            jnp.einsum("sqk,sqd->skd", score_grad, head_q, preferred_element_type=jnp.float32)
            * 0.125
        )
        grad_v = jnp.einsum("sqk,sqd->skd", soft_low, head_grad, preferred_element_type=jnp.float32)
        return (grad_q, grad_k, grad_v)

    heads_grad_q, heads_grad_k, value_grad_per_head = lax.map(
        head_backward, (heads_q, heads_keys, heads_values, heads_grad_att, log_totals)
    )
    key_grad_local, value_grad_local = (
        lax.psum_scatter(
            join_heads(heads_grad_k).astype(jnp.bfloat16), "shard", scatter_dimension=0, tiled=True
        ).astype(jnp.float32),
        lax.psum_scatter(
            join_heads(value_grad_per_head).astype(jnp.bfloat16),
            "shard",
            scatter_dimension=0,
            tiled=True,
        ).astype(jnp.float32),
    )
    grad_queries = join_heads(heads_grad_q).reshape(row_count, width).astype(jnp.bfloat16)
    grad_keys = key_grad_local.reshape(row_count, width).astype(jnp.bfloat16)
    grad_values = value_grad_local.reshape(row_count, width).astype(jnp.bfloat16)
    q_bias_grad = jnp.sum(grad_queries.astype(jnp.float32), axis=0)
    v_bias_grad = jnp.sum(grad_values.astype(jnp.float32), axis=0)
    grad_joined = jnp.concatenate([grad_queries, grad_keys, grad_values], axis=1)
    grad_norm_one = jnp.dot(grad_joined, w_qkv, preferred_element_type=jnp.float32)
    first_out, first_pull = jax.vjp(layer_norm, tokens, ln1_gain, ln1_bias)
    grad_in_part, ln1_gain_grad, ln1_bias_grad = first_pull(grad_norm_one)
    input_grad = (grad_middle + grad_in_part).reshape(local_len, seq_count, width)
    qkv_part = lax.psum_scatter(
        rows_term(grad_joined, normed).astype(jnp.bfloat16),
        "shard",
        scatter_dimension=0,
        tiled=True,
    )
    out_part = lax.psum_scatter(
        rows_term(grad_branch, attended).astype(jnp.bfloat16),
        "shard",
        scatter_dimension=0,
        tiled=True,
    )
    up_projection_part = lax.psum_scatter(
        rows_term(grad_pre, normed_two).astype(jnp.bfloat16),
        "shard",
        scatter_dimension=0,
        tiled=True,
    )
    down_part = lax.psum_scatter(
        rows_term(grad_out, activ).astype(jnp.bfloat16), "shard", scatter_dimension=0, tiled=True
    )
    qkv_total, out_total, up_total, down_total = (
        lax.psum(qkv_part, "replica").astype(jnp.float32),
        lax.psum(out_part, "replica").astype(jnp.float32),
        lax.psum(up_projection_part, "replica").astype(jnp.float32),
        lax.psum(down_part, "replica").astype(jnp.float32),
    )
    summed = lax.psum(
        (
            ln1_gain_grad,
            ln1_bias_grad,
            q_bias_grad,
            v_bias_grad,
            out_bias_grad,
            ln2_gain_grad,
            ln2_bias_grad,
            up_bias_grad,
            down_bias_grad,
        ),
        ("shard", "replica"),
    )
    return (
        result,
        input_grad,
        summed[0],
        summed[1],
        qkv_total,
        summed[2],
        summed[3],
        out_total,
        summed[4],
        summed[5],
        summed[6],
        up_total,
        summed[7],
        down_total,
        summed[8],
    )


def solution(mesh):
    in_specs = (
        P("shard", "replica", None),
        P("shard", "replica", None),
        P(None, "replica"),
        P(),
        P(),
        P("shard", None),
        P(),
        P(),
        P("shard", None),
        P(),
        P(),
        P(),
        P("shard", None),
        P(),
        P("shard", None),
        P(),
    )
    out_specs = (
        P("shard", "replica", None),
        P("shard", "replica", None),
        P(),
        P(),
        P("shard", None),
        P(),
        P(),
        P("shard", None),
        P(),
        P(),
        P(),
        P("shard", None),
        P(),
        P("shard", None),
        P(),
    )
    return jax.shard_map(shards, mesh=mesh, in_specs=in_specs, out_specs=out_specs, check_vma=False)
```

profile of v0, /device:TPU:1, one launch (start us, length us, event | category | flops | bytes accessed | tf_op | source)
XLA Modules:
  0.0 2430.0 jit_solution(16217972032270486567)
XLA Ops:
  28.5 134.2 %all-gather.7.cloned.1.call-done = bf16[4800,1600]{1,0:T(8,128)(2,1)} async-done(((bf16[1200,1600]{1,0:T(8,128)(2,1)}), bf16[4800,1600]{1,0:T(8,128)(2,1)}) %all-gather.7.cloned.1.call-update) | async-done | bytes 15360016 | tf_op jit(solution)/shard_map/all_gather | solution.py:70
  162.7 12.7 fusion.57
  245.4 108.4 %all-gather.17.cloned.1.call-done = bf16[1600,6400]{1,0:T(8,128)(2,1)} async-done(((bf16[400,6400]{1,0:T(8,128)(2,1)}), bf16[1600,6400]{1,0:T(8,128)(2,1)}) %all-gather.17.cloned.1.call-update) | async-done | bytes 20480016 | tf_op jit(solution)/shard_map/all_gather | solution.py:73
  353.8 19.7 fusion.64
  373.5 54.9 %all-gather.9.cloned.1.call-done = bf16[1024,2,1600]{0,2,1:T(8,128)(2,1)} async-done(((bf16[256,2,1600]{0,2,1:T(8,128)(2,1)}), bf16[1024,2,1600]{0,2,1:T(8,128)(2,1)}) %all-gather.9.cloned.1.call-update) | async-done | bytes 6553616 | tf_op jit(solution)/shard_map/all_gather | solution.py:87
  435.4 67.5 %all-gather.11.cloned.1.call-done = bf16[1024,2,1600]{0,2,1:T(8,128)(2,1)} async-done(((bf16[256,2,1600]{0,2,1:T(8,128)(2,1)}), bf16[1024,2,1600]{0,2,1:T(8,128)(2,1)}) %all-gather.11.cloned.1.call-update) | async-done | bytes 6553616 | tf_op jit(solution)/shard_map/all_gather | solution.py:88
  511.2 129.1 %while.28 = (s32[]{:T(128)}, bf16[25,2,256,64]{2,3,1,0:T(8,128)(2,1)}, f32[25,2,256]{2,1,0:T(2,128)}, bf16[25,2,256,64]{2,3,1,0:T(8,128)(2,1)}, bf16[25,2,1024,6...) while((s32[]{:T(128)}, ...), condition=%wide.region_5.6_spmd.clone, body=%wide.region_2.5_spmd.clone.sunk | while | flops 139460096 | bytes 7303281 | solution.py:106
  663.1 101.3 %all-gather.15.cloned.1.call-done = bf16[6400,1600]{1,0:T(8,128)(2,1)} async-done(((bf16[1600,1600]{1,0:T(8,128)(2,1)}), bf16[6400,1600]{1,0:T(8,128)(2,1)}) %all-gather.15.cloned.1.call-update) | async-done | bytes 20480016 | tf_op jit(solution)/shard_map/all_gather | solution.py:72
  764.4 29.4 %convert_reduce_fusion = (f32[6400]{0:T(1024)}, bf16[512,6400]{1,0:T(8,128)(2,1)}, f32[512,6400]{1,0:T(8,128)}) fusion(f32[512,6400]{1,0:T(8,128)} %fusion.64, f32[6400]{0:T(1024)S(1)} %copy-done.30, bf16[6400,1600]{1,0:T(8,128)(2,1)} %all-gather.15.cloned.1.call-done, f32[512,1600]{0,1:T(8,128)} %copy-done.6, f32[1600]{0:T(1024)S(1)} %copy-done.32, ...), kind=kOutput, calls=%fused_computation.65 | convolution fusion | flops 10565216256 | bytes 56592896 | tf_op jit(solution)/shard_map/dot_general | solution.py:17
  793.8 21.6 multiply_reduce_fusion.1
  838.3 218.1 %while.29 = (s32[]{:T(128)}, bf16[25,2,256,64]{2,3,1,0:T(8,128)(2,1)S(1)}, bf16[25,2,1024,64]{2,3,0,1:T(8,128)(2,1)}, bf16[25,2,1024,64]{2,3,0,1:T(8,128)(2,1)},...) while((s32[]{:T(128)}, ...), condition=%wide.region_12.13_spmd.clone, body=%wide.region_10.12_spmd.clone.sunk | while | flops 341474816 | bytes 18244744 | solution.py:179
  1066.3 20.4 convolution_convert_fusion.1
  1088.1 18.8 fusion.42
  1136.1 68.2 %reduce-scatter.16.cloned.1.call-done = bf16[256,2,1600]{0,2,1:T(8,128)(2,1)} async-done(((bf16[1024,2,1600]{0,2,1:T(8,128)(2,1)}), bf16[256,2,1600]{0,2,1:T(8,128)(2,1)}) %reduce-scatter.16.cloned.1.call-update) | async-done | bytes 1638416 | tf_op jit(solution)/shard_map/reduce_scatter | solution.py:186
  1211.6 9.5 concatenate.3
  1221.2 15.5 convolution_convert_fusion.2
  1239.1 32.7 %reduce-scatter.22.cloned.1.call-done = bf16[400,1600]{1,0:T(8,128)(2,1)} async-done(((bf16[1600,1600]{1,0:T(8,128)(2,1)}), bf16[400,1600]{1,0:T(8,128)(2,1)}) %reduce-scatter.22.cloned.1.call-update) | async-done | bytes 1280016
  1271.8 195.2 %reduce-scatter.18.cloned.1.call-done = bf16[1600,1600]{1,0:T(8,128)(2,1)} async-done(((bf16[6400,1600]{1,0:T(8,128)(2,1)}), bf16[1600,1600]{1,0:T(8,128)(2,1)}) %reduce-scatter.18.cloned.1.call-update) | async-done | bytes 5120016 | tf_op jit(solution)/shard_map/reduce_scatter | solution.py:215
  1467.0 220.6 %reduce-scatter.24.cloned.1.call-done = bf16[400,6400]{1,0:T(8,128)(2,1)} async-done(((bf16[1600,6400]{1,0:T(8,128)(2,1)}), bf16[400,6400]{1,0:T(8,128)(2,1)}) %reduce-scatter.24.cloned.1.call-update) | async-done | bytes 5120016
  1687.7 270.4 %reduce-scatter.20.cloned.1.call-done = bf16[1200,1600]{1,0:T(8,128)(2,1)} async-done(((bf16[4800,1600]{1,0:T(8,128)(2,1)}), bf16[1200,1600]{1,0:T(8,128)(2,1)}) %reduce-scatter.20.cloned.1.call-update) | async-done | bytes 3840016
  1958.7 22.6 fusion.53
  1999.6 17.1 fusion.58
  2039.3 239.3 %all-reduce.10.cloned.1.call-done = (bf16[1200,1600]{1,0:T(8,128)(2,1)}, bf16[400,1600]{1,0:T(8,128)(2,1)}, bf16[1600,1600]{1,0:T(8,128)(2,1)}, bf16[400,6400]{1,0:T(8,128)(2,1)}) async-done(((bf16[1200,1600]{1,0:T(8,128)(2,1)}, bf16[400,1600]{1,0:T(8,128)(2,1)}, bf16[1600,1600]{1,0:T(8,128)(2,1)}, bf16[400,6400]{1,0:T(8,128)(2,1)}), (bf16[1200,1600]{1,0:T(8,128)(2,1)}, bf16[400,1600]{1,0:T(8,128)(2,1)}, ...) | async-done | bytes 15360016 | tf_op jit(solution)/shard_map/psum | solution.py:225
  2295.9 115.4 %all-reduce.8.cloned.1.call-done = (f32[1600]{0:T(1024)}, f32[1600]{0:T(1024)}, f32[1600]{0:T(1024)}, f32[1600]{0:T(1024)}, f32[1600]{0:T(1024)}, /*index=5*/f32...) async-done(((f32[1600]{0:T(1024)}, f32[1600]{0:T(1024)}, f32[1600]{0:T(1024)}, f32[1600]{0:T(1024)}, f32[1600]{0:T(1024)}, /*index=5*/f32[1600]{0:T(1024)}, ...) | async-done | bytes 76816 | tf_op jit(solution)/shard_map/psum | solution.py:230
  (471 shorter events, 618.7 us)
Async XLA Ops:
  7.2 155.5 %all-gather.7.cloned.1.call-start = ((), (), s32[]{:S(2)}) async-start(), calls=%async_computation.6 | async-start | bytes 19968000 | tf_op jit(solution)/shard_map/all_gather | solution.py:70
  7.9 345.8 %all-gather.17.cloned.1.call-start = ((), (), s32[]{:S(2)}) async-start(), calls=%async_computation.11 | async-start | bytes 25600000 | tf_op jit(solution)/shard_map/all_gather | solution.py:73
  8.7 419.7 %all-gather.9.cloned.1.call-start = ((), (), s32[]{:S(2)}) async-start(), calls=%async_computation.7 | async-start | bytes 8192000 | tf_op jit(solution)/shard_map/all_gather | solution.py:87
  22.5 632.6 %copy-start = (f32[512,1600]{0,1:T(8,128)}, f32[512,1600]{0,1:T(8,128)S(1)}, u32[]{:S(2)}) copy-start(f32[512,1600]{0,1:T(8,128)S(1)} %copy.79) | copy-start | bytes 9830404
  22.5 140.2 %copy-start.15 = (f32[1600]{0:T(1024)S(1)}, f32[1600]{0:T(1024)}, u32[]{:S(2)}) copy-start(f32[1600]{0:T(1024)} %param.23) | copy-start | bytes 19204
  28.3 147.0 %copy-start.23 = (f32[512]{0:T(512)}, f32[512]{0:T(512)S(1)}, u32[]{:S(2)}) copy-start(f32[512]{0:T(512)S(1)} %add.175) | copy-start | bytes 6148
  28.4 147.0 %copy-start.19 = (f32[512]{0:T(512)}, f32[512]{0:T(512)S(1)}, u32[]{:S(2)}) copy-start(f32[512]{0:T(512)S(1)} %rsqrt.22) | copy-start | bytes 6148
  28.5 146.9 %copy-start.17 = (f32[512]{0:T(512)}, f32[512]{0:T(512)S(1)}, u32[]{:S(2)}) copy-start(f32[512]{0:T(512)S(1)} %div.51) | copy-start | bytes 6148
  195.6 307.3 %all-gather.11.cloned.1.call-start = ((), (), s32[]{:S(2)}) async-start(), calls=%async_computation.8 | async-start | bytes 8192000 | tf_op jit(solution)/shard_map/all_gather | solution.py:88
  213.7 441.4 %all-gather.13.cloned.1.call-start = ((), (), s32[]{:S(2)}) async-start(), calls=%async_computation.9 | async-start | bytes 6656000 | tf_op jit(solution)/shard_map/all_gather | solution.py:71
  214.3 550.1 %all-gather.15.cloned.1.call-start = ((), (), s32[]{:S(2)}) async-start(), calls=%async_computation.10 | async-start | bytes 26624000 | tf_op jit(solution)/shard_map/all_gather | solution.py:72
  214.9 914.0 %reduce-scatter.14.cloned.1.call-start = ((), (), s32[]{:S(2)}) async-start(), calls=%async_computation.12 | async-start | bytes 8192000 | tf_op jit(solution)/shard_map/reduce_scatter | solution.py:183
  661.0 103.4 %copy-start.27 = (f32[1600]{0:T(1024)S(1)}, f32[1600]{0:T(1024)}, u32[]{:S(2)}) copy-start(f32[1600]{0:T(1024)} %param.30) | copy-start | bytes 19204
  661.0 103.4 %copy-start.30 = (f32[6400]{0:T(1024)S(1)}, f32[6400]{0:T(1024)}, u32[]{:S(2)}) copy-start(f32[6400]{0:T(1024)} %param.33) | copy-start | bytes 76804
  661.0 103.4 %copy-start.32 = (f32[1600]{0:T(1024)S(1)}, f32[1600]{0:T(1024)}, u32[]{:S(2)}) copy-start(f32[1600]{0:T(1024)} %param.31) | copy-start | bytes 19204
  663.1 130.7 %copy-start.7 = (f32[512,1600]{0,1:T(8,128)S(1)}, f32[512,1600]{0,1:T(8,128)}, u32[]{:S(2)}) copy-start(f32[512,1600]{0,1:T(8,128)} %copy-done.6) | copy-start | bytes 9830404
  1056.4 50.6 %copy-start.5 = (bf16[25,2,256,64]{2,3,1,0:T(8,128)(2,1)}, bf16[25,2,256,64]{2,3,1,0:T(8,128)(2,1)S(1)}, u32[]{:S(2)}) copy-start(bf16[25,2,256,64]{2,3,1,0:T(8,128)(2,1)S(1)} %get-tuple-element.109) | copy-start | bytes 4915204
  1056.4 148.0 %reduce-scatter.16.cloned.1.call-start = ((), (), s32[]{:S(2)}) async-start(), calls=%async_computation.13 | async-start | bytes 8192000 | tf_op jit(solution)/shard_map/reduce_scatter | solution.py:186
  1057.1 214.7 %reduce-scatter.22.cloned.1.call-start = ((), (), s32[]{:S(2)}) async-start(), calls=%async_computation.16 | async-start | bytes 6656000
  1065.6 401.5 %reduce-scatter.18.cloned.1.call-start = ((), (), s32[]{:S(2)}) async-start(), calls=%async_computation.14 | async-start | bytes 26624000 | tf_op jit(solution)/shard_map/reduce_scatter | solution.py:215
  1086.7 601.0 %reduce-scatter.24.cloned.1.call-start = ((), (), s32[]{:S(2)}) async-start(), calls=%async_computation.17 | async-start | bytes 25600000
  1107.0 851.1 %reduce-scatter.20.cloned.1.call-start = ((), (), s32[]{:S(2)}) async-start(), calls=%async_computation.15 | async-start | bytes 19968000
  1236.7 1041.9 %all-reduce.10.cloned.1.call-start = ((), (), s32[]{:S(2)}) async-start(), calls=%async_computation.19 | async-start | bytes 31539200 | tf_op jit(solution)/shard_map/psum | solution.py:225
  1958.1 453.2 %all-reduce.8.cloned.1.call-start = ((), (), s32[]{:S(2)}) async-start(), calls=%async_computation.18 | async-start | bytes 188416 | tf_op jit(solution)/shard_map/psum | solution.py:230
  (30 other events, 183.7 us)
Sparse Core Ops, SparseCore 0:
  9.9 152.8 all-gather.6
  164.6 189.1 all-gather.16
  356.2 72.1 all-gather.8
  430.7 72.1 all-gather.10
  504.6 62.1 all-gather.12
  568.5 195.8 all-gather.14
  1056.5 72.3 reduce-scatter.13
  1132.0 72.3 reduce-scatter.15
  1208.0 63.8 reduce-scatter.21
  1274.8 192.1 reduce-scatter.17
  1470.4 217.2 reduce-scatter.23
  1689.9 268.0 reduce-scatter.19
  1961.2 317.3 all-reduce.9
  2287.2 124.0 all-reduce.7
where the time goes:
time: 2450 us; the launch traced here: 2430 us
  waiting for transfers between devices  1620 us (66%)
  matrix products  492 us (20%)
  local copies, waits for them, and re-layouts  219 us (9%)
  other arithmetic  81.9 us (3%)
    unnamed x17, waiting for transfers between devices  527 us
    psum x1, waiting for transfers between devices, shards(): lax.psum(qkv_part, 'replica').astype(jnp.float32)  239 us
    reduce_scatter x1, waiting for transfers between devices, shards(): lax.psum_scatter(rows_term(grad_pre, normed_two).astype(jnp.bfloat16), 's...  195 us
    all_gather x1, waiting for transfers between devices, shards(): lax.all_gather(qkv_weight, 'shard', axis=0, tiled=True)  134 us
    psum x1, waiting for transfers between devices, shards(): lax.psum((ln1_gain_grad, ln1_bias_grad, q_bias_grad, v_bias_grad, out_bia...  115 us
    all_gather x1, waiting for transfers between devices, shards(): lax.all_gather(down_weight, 'shard', axis=0, tiled=True)  108 us
    all_gather x1, waiting for transfers between devices, shards(): lax.all_gather(up_weight, 'shard', axis=0, tiled=True)  101 us
    dot_general x4, matrix products, project(): lax.dot_general(value_rows, weight_matrix, (((1,), (1,)), ((), ())), pref...  70.4 us
  transfers between devices with their start and end apart: 14, of which 13 were waited for; matrix products, arithmetic and copies ran while one was open for 20% of the time, Pallas kernels for 0%

commit v1 on v0

v1 whole, which is shorter than its diff:
```python
import functools

import jax
import jax.numpy as jnp
from jax import lax
from jax.experimental import pallas as pl
from jax.experimental.pallas import tpu as pltpu
from jax.sharding import PartitionSpec as P

HEADS = 25
HDIM = 64
OWN_HEADS = HEADS // 2 + 1
FIRST_HEAD = HEADS // 2
OWN = OWN_HEADS * HDIM
BLOCK = 256
AXES = ("shard", "replica")
BF16 = jnp.bfloat16
F32 = jnp.float32


def dot(left, right, left_dim, right_dim):
    return lax.dot_general(
        left, right, (((left_dim,), (right_dim,)), ((), ())), preferred_element_type=F32
    )


def norm_parts(rows):
    centre = rows - jnp.mean(rows, axis=-1, keepdims=True)
    scale = lax.rsqrt(jnp.mean(centre * centre, axis=-1, keepdims=True) + 1e-05)
    return centre * scale, scale


def norm_back(grad, unit, scale, gain):
    inner = grad * gain
    mean_inner = jnp.mean(inner, axis=-1, keepdims=True)
    mean_cross = jnp.mean(inner * unit, axis=-1, keepdims=True)
    return scale * (inner - mean_inner - unit * mean_cross)


def gelu_pair(value):
    root = 0.7978845608028654
    cube = 0.044715
    square = value * value
    tanh = jnp.tanh(root * value * (1.0 + cube * square))
    half = 0.5 * (1.0 + tanh)
    slope = half + 0.5 * value * (1.0 - tanh * tanh) * root * (1.0 + 3.0 * cube * square)
    return value * half, slope


def fill_mask(seg_row, seg_col, mask, blocks):
    for q_at in range(blocks):
        for k_at in range(q_at + 1):
            keys = seg_col[pl.ds(k_at * BLOCK, BLOCK), :]
            queries = seg_row[:, pl.ds(q_at * BLOCK, BLOCK)]
            seen = keys == queries
            if k_at == q_at:
                k_place = lax.broadcasted_iota(jnp.int32, (BLOCK, BLOCK), 0)
                q_place = lax.broadcasted_iota(jnp.int32, (BLOCK, BLOCK), 1)
                seen = seen & (k_place <= q_place)
            mask[pl.ds(k_at * BLOCK, BLOCK), pl.ds(q_at * BLOCK, BLOCK)] = jnp.where(
                seen, 0.0, -1e30
            )


def forward_kernel(seg_row, seg_col, q_ref, k_ref, v_ref, o_ref, lse_ref, mask):
    length = q_ref.shape[1]
    blocks = length // BLOCK

    @pl.when(pl.program_id(0) == 0)
    def _():
        fill_mask(seg_row, seg_col, mask, blocks)

    keys = k_ref[...].T
    for q_at in range(blocks):
        span = (q_at + 1) * BLOCK
        here = pl.ds(q_at * BLOCK, BLOCK)
        scores = dot(keys[:span], q_ref[:, here], 1, 0) + mask[:span, here]
        peak = jnp.max(scores, axis=0, keepdims=True)
        terms = jnp.exp(scores - peak)
        total = jnp.sum(terms, axis=0, keepdims=True)
        mixed = dot(v_ref[:, :span], terms.astype(BF16), 1, 0)
        o_ref[:, here] = (mixed / total).astype(BF16)
        lse_ref[0, :, here] = peak + jnp.log(total)


def backward_kernel(
    seg_row, seg_col, q_ref, k_ref, v_ref, o_ref, g_ref, lse_ref, dq_ref, dk_ref, dv_ref, mask, acc
):
    length = q_ref.shape[1]
    blocks = length // BLOCK

    @pl.when(pl.program_id(0) == 0)
    def _():
        fill_mask(seg_row, seg_col, mask, blocks)

    keys = k_ref[...].T
    values = v_ref[...].T
    delta = jnp.sum(g_ref[...].astype(F32) * o_ref[...].astype(F32), axis=0, keepdims=True)
    lse = lse_ref[0]
    for k_at in range(blocks):
        low = k_at * BLOCK
        here = pl.ds(low, BLOCK)
        rest = pl.ds(low, length - low)
        scores = dot(keys[low : low + BLOCK], q_ref[:, rest], 1, 0) + mask[here, rest]
        soft = jnp.exp(scores - lse[:, low:])
        soft_grad = dot(values[low : low + BLOCK], g_ref[:, rest], 1, 0)
        score_grad = (soft * (soft_grad - delta[:, low:])).astype(BF16)
        dv_ref[:, here] = dot(g_ref[:, rest], soft.astype(BF16), 1, 1).astype(BF16)
        dk_ref[:, here] = dot(q_ref[:, rest], score_grad, 1, 1).astype(BF16)
        grad_q = dot(k_ref[:, here], score_grad, 1, 0)
        if k_at == 0:
            acc[...] = grad_q
        else:
            acc[:, rest] += grad_q
    dq_ref[...] = (acc[...] * 0.125).astype(BF16)


def head_spec(first, length):
    return pl.BlockSpec((HDIM, length), lambda head: (first + head, 0))


def whole_spec(shape):
    return pl.BlockSpec(shape, lambda head: (0,) * len(shape))


def attention(seg, joined):
    length = seg.shape[0]
    lse_spec = pl.BlockSpec((1, 1, length), lambda head: (head, 0, 0))
    pairs = OWN_HEADS * length * length
    return pl.pallas_call(
        forward_kernel,
        grid=(OWN_HEADS,),
        in_specs=[whole_spec((1, length)), whole_spec((length, 1))]
        + [head_spec(part * OWN_HEADS, length) for part in range(3)],
        out_specs=[head_spec(0, length), lse_spec],
        out_shape=[
            jax.ShapeDtypeStruct((OWN, length), BF16),
            jax.ShapeDtypeStruct((OWN_HEADS, 1, length), F32),
        ],
        scratch_shapes=[pltpu.VMEM((length, length), F32)],
        compiler_params=pltpu.CompilerParams(vmem_limit_bytes=40 * 2**20),
        cost_estimate=pl.CostEstimate(
            flops=16 * pairs * HDIM, bytes_accessed=8 * OWN * length, transcendentals=pairs
        ),
        name="attention_forward",
    )(seg.reshape(1, length), seg.reshape(length, 1), joined, joined, joined)


def attention_back(seg, joined, mixed, grad, lse):
    length = seg.shape[0]
    lse_spec = pl.BlockSpec((1, 1, length), lambda head: (head, 0, 0))
    pairs = OWN_HEADS * length * length
    return pl.pallas_call(
        backward_kernel,
        grid=(OWN_HEADS,),
        in_specs=[whole_spec((1, length)), whole_spec((length, 1))]
        + [head_spec(part * OWN_HEADS, length) for part in range(3)]
        + [head_spec(0, length), head_spec(0, length), lse_spec],
        out_specs=[head_spec(0, length)] * 3,
        out_shape=[jax.ShapeDtypeStruct((OWN, length), BF16)] * 3,
        scratch_shapes=[pltpu.VMEM((length, length), F32), pltpu.VMEM((HDIM, length), F32)],
        compiler_params=pltpu.CompilerParams(vmem_limit_bytes=48 * 2**20),
        cost_estimate=pl.CostEstimate(
            flops=40 * pairs * HDIM, bytes_accessed=16 * OWN * length, transcendentals=pairs
        ),
        name="attention_backward",
    )(seg.reshape(1, length), seg.reshape(length, 1), joined, joined, joined, mixed, grad, lse)


class Moves:
    def __init__(self, shard_count, replica_count):
        self.shard_count = shard_count
        self.replica_count = replica_count
        self.shard = lax.axis_index("shard")
        replica = lax.axis_index("replica")
        self.core = replica % 2
        self.column = replica // 2
        self.square = shard_count == 4 and replica_count == 8

    def move(self, array, route):
        pairs = []
        for shard in range(self.shard_count):
            for column in range(self.replica_count // 2):
                for core in range(2):
                    target = route(shard, column, core)
                    if target is not None:
                        to_shard, to_column, to_core = target
                        pairs.append(
                            (
                                shard * self.replica_count + 2 * column + core,
                                to_shard * self.replica_count + 2 * to_column + to_core,
                            )
                        )
        return lax.ppermute(array, AXES, pairs)

    def over_x(self, array):
        return self.move(array, lambda s, z, c: (s ^ 1, z, c))

    def over_y(self, array):
        return self.move(array, lambda s, z, c: (s ^ 2, z, c))

    def over_core(self, array):
        return self.move(array, lambda s, z, c: (s, z, 1 - c))

    def gather(self, piece):
        if not self.square:
            return lax.all_gather(piece, "shard", axis=0, tiled=False)
        rows = piece.shape[0] // 2
        from_x = self.over_x(piece)
        from_y = self.over_y(piece)
        far_low = self.over_x(from_y[:rows])
        far_high = self.over_y(from_x[rows:])
        out = jnp.zeros((4,) + piece.shape, piece.dtype)
        zero = (0,) * (piece.ndim - 1)
        out = lax.dynamic_update_slice(out, piece[None], (self.shard, 0) + zero)
        out = lax.dynamic_update_slice(out, from_x[None], (self.shard ^ 1, 0) + zero)
        out = lax.dynamic_update_slice(out, from_y[None], (self.shard ^ 2, 0) + zero)
        out = lax.dynamic_update_slice(out, far_low[None], (self.shard ^ 3, 0) + zero)
        out = lax.dynamic_update_slice(out, far_high[None], (self.shard ^ 3, rows) + zero)
        return out

    def pick(self, parts, index):
        return lax.dynamic_index_in_dim(parts, index, 0, keepdims=False)

    def scatter(self, parts):
        if not self.square:
            return lax.psum_scatter(parts, "shard", scatter_dimension=0, tiled=False)
        rows = parts.shape[1] // 2
        me = self.shard

        def part(index, high):
            begin = (index, rows if high else 0) + (0,) * (parts.ndim - 2)
            size = (1, parts.shape[1] - rows if high else rows) + parts.shape[2:]
            return lax.dynamic_slice(parts, begin, size)[0]

        low_far, low_y = self.over_x(part(me ^ 3, False)), self.over_x(part(me ^ 1, False))
        high_far, high_x = self.over_y(part(me ^ 3, True)), self.over_y(part(me ^ 2, True))
        low = self.over_y(part(me ^ 2, False) + low_far)
        high = self.over_x(part(me ^ 1, True) + high_far)
        return jnp.concatenate(
            [(part(me, False) + low_y) + low, (part(me, True) + high_x) + high], axis=0
        )

    def total(self, array):
        if not self.square:
            groups = [
                [2 * column + core for column in range(self.replica_count // 2)]
                for core in range(2)
            ]
            return lax.psum(array, "replica", axis_index_groups=groups)
        inward = {0: 1, 3: 2}
        across = {1: 2, 2: 1}
        outward = {1: 0, 2: 3}

        def hop(array, table):
            return self.move(array, lambda s, z, c: (s, table[z], c) if z in table else None)

        pair = array + hop(array, inward)
        full = pair + hop(pair, across)
        middle = (self.column == 1) | (self.column == 2)
        return jnp.where(middle, full, hop(full, outward))

    def owners(self, step, seqs):
        return lambda s, z, c: (seqs * c + (s + step) % seqs, z, s // seqs)

    def to_chips(self, local):
        seqs = local.shape[1]
        came = []
        for step in range(seqs):
            sent = lax.dynamic_index_in_dim(local, (self.shard + step) % seqs, 1, keepdims=False)
            came.append(self.move(sent, self.owners(step, seqs)))
        at = self.shard % seqs
        ring = came[::-1] * 2
        ring = jnp.concatenate(ring[: 2 * seqs - 1], axis=0)
        rows = local.shape[0]
        return lax.dynamic_slice_in_dim(ring, (seqs - 1 - at) * rows, seqs * rows, 0)

    def from_chips(self, half, seqs):
        rows = half.shape[0] // seqs
        at = self.shard % seqs
        outs = []
        for step in range(seqs):
            route = self.owners(step, seqs)
            back = {}
            for s in range(self.shard_count):
                for z in range(self.replica_count // 2):
                    for c in range(2):
                        back[route(s, z, c)] = (s, z, c)
            sent = lax.dynamic_slice_in_dim(half, ((at - step) % seqs) * rows, rows, 0)
            outs.append(self.move(sent, lambda s, z, c: back[(s, z, c)]))
        stacked = jnp.stack(outs, axis=1)
        doubled = jnp.concatenate([stacked, stacked[:, : seqs - 1]], axis=1)
        return lax.dynamic_slice_in_dim(doubled, (seqs - at) % seqs, seqs, 1)

    def both(self, half):
        other = self.over_core(half)
        first = self.core == 0
        return jnp.concatenate(
            [jnp.where(first, half, other), jnp.where(first, other, half)], axis=0
        )


def shards(
    shard_count,
    replica_count,
    hidden_in,
    out_grad,
    segments,
    ln1_gain,
    ln1_bias,
    qkv_weight,
    q_bias,
    v_bias,
    output_projection_weight,
    out_bias,
    ln2_gain,
    ln2_bias,
    up_weight,
    up_bias,
    down_weight,
    down_bias,
):
    moves = Moves(shard_count, replica_count)
    core = moves.core
    seqs = hidden_in.shape[1]
    width = hidden_in.shape[2]
    length = segments.shape[0]
    half_rows = length // 2
    ff = up_bias.shape[0]
    ff_part = ff // shard_count
    ff_half = ff_part // 2
    first_row = core * FIRST_HEAD * HDIM
    own_cols = functools.partial(lax.dynamic_slice_in_dim, slice_size=OWN)

    tokens_half = moves.to_chips(hidden_in)
    qkv_rows = qkv_weight.shape[0] // 2
    qkv_half = moves.gather(lax.dynamic_slice_in_dim(qkv_weight, core * qkv_rows, qkv_rows, 0))
    qkv_other = moves.over_core(qkv_half)
    qkv_full = jnp.where(
        core == 0,
        jnp.concatenate([qkv_half, qkv_other], axis=1),
        jnp.concatenate([qkv_other, qkv_half], axis=1),
    ).reshape(3 * width, width)
    w_out = moves.gather(own_cols(output_projection_weight, first_row, axis=1))
    w_up = moves.gather(lax.dynamic_slice_in_dim(up_weight, core * ff_half, ff_half, 0))
    down_cols = lax.dynamic_index_in_dim(
        down_weight.reshape(-1, shard_count, 2, ff_half), core, 2, keepdims=False
    ).reshape(-1, ff // 2)
    w_down = moves.gather(down_cols)
    w_up = w_up.reshape(ff // 2, width)
    w_down = w_down.reshape(width, ff // 2)
    twice = (core == 1) & (jnp.arange(OWN) < HDIM)
    w_out = jnp.where(twice[None, :], 0, w_out.reshape(width, OWN)).astype(BF16)
    up_bias_own = lax.dynamic_index_in_dim(
        up_bias.reshape(shard_count, 2, ff_half), core, 1, keepdims=False
    ).reshape(-1)
    w_qkv = jnp.concatenate(
        [own_cols(qkv_full, part * width + first_row, axis=0) for part in range(3)], axis=0
    )
    seg_pair = jnp.stack([segments, moves.over_core(segments)])
    home = moves.shard // seqs
    seg = lax.dynamic_index_in_dim(
        lax.dynamic_index_in_dim(seg_pair, (home != core).astype(jnp.int32), 0, keepdims=False),
        moves.shard % seqs,
        1,
        keepdims=False,
    )
    grad_out = moves.both(moves.to_chips(out_grad))

    tokens = moves.both(tokens_half).astype(F32)
    unit_one, scale_one = norm_parts(tokens)
    normed = (unit_one * ln1_gain + ln1_bias).astype(BF16)
    zeros = jnp.zeros((OWN,), F32)
    joined_bias = jnp.concatenate(
        [own_cols(q_bias, first_row, axis=0), zeros, own_cols(v_bias, first_row, axis=0)]
    )
    joined = (dot(w_qkv, normed, 1, 1) + joined_bias[:, None]).astype(BF16)
    row_scale = jnp.where(jnp.arange(3 * OWN) < OWN, 0.125, 1.0).astype(BF16)
    joined = joined * row_scale[:, None]
    mixed, lse = attention(seg, joined)
    branch = dot(mixed, w_out, 0, 1)
    middle = tokens + (branch + moves.over_core(branch.astype(BF16)).astype(F32)) + out_bias
    unit_two, scale_two = norm_parts(middle)
    normed_two = (unit_two * ln2_gain + ln2_bias).astype(BF16)
    activ, slope = gelu_pair(dot(normed_two, w_up, 1, 1) + up_bias_own)
    activ = activ.astype(BF16)
    slope = slope.astype(BF16)
    down = dot(activ, w_down, 1, 1)
    half_of = functools.partial(lax.dynamic_slice_in_dim, slice_size=half_rows, axis=0)
    mine, theirs = core * half_rows, (1 - core) * half_rows
    down_other = moves.over_core(half_of(down.astype(BF16), theirs)).astype(F32)
    result_half = half_of(middle, mine) + (half_of(down, mine) + down_other) + down_bias
    result = moves.from_chips(result_half.astype(BF16), seqs)

    down_grad = dot(grad_out, activ, 0, 0).astype(BF16)
    grad_act = dot(grad_out, w_down, 1, 0)
    grad_pre = (grad_act * slope.astype(F32)).astype(BF16)
    up_grad = dot(grad_pre, normed_two, 0, 0).astype(BF16)
    grad_norm_two = dot(grad_pre, w_up, 1, 0)
    grad_norm_two = grad_norm_two + moves.over_core(grad_norm_two.astype(BF16)).astype(F32)
    grad_out_f = grad_out.astype(F32)
    grad_middle = grad_out_f + norm_back(grad_norm_two, unit_two, scale_two, ln2_gain)
    grad_branch = grad_middle.astype(BF16)
    out_grad_own = dot(grad_branch, mixed, 0, 1).astype(BF16)
    grad_mixed = dot(w_out, grad_branch, 0, 1).astype(BF16)

    down_sum = moves.total(moves.scatter(down_grad.reshape(shard_count, -1, ff // 2)))
    up_sum = moves.total(moves.scatter(up_grad.reshape(shard_count, ff_half, width)))
    out_sum = moves.total(moves.scatter(out_grad_own.reshape(shard_count, -1, OWN)))

    grad_q, grad_k, grad_v = attention_back(seg, joined, mixed, grad_mixed, lse)
    grad_own = jnp.stack([grad_q, grad_k, grad_v])
    grad_other = moves.over_core(grad_own)
    low = jnp.where(core == 0, grad_own, grad_other)
    high = jnp.where(core == 0, grad_other, grad_own)
    grad_joined = jnp.concatenate([low, high[:, HDIM:]], axis=1).reshape(3 * width, length)
    half_width = width // 2
    qkv_grad = dot(
        grad_joined, lax.dynamic_slice_in_dim(normed, core * half_width, half_width, 1), 1, 0
    ).astype(BF16)
    qkv_sum = moves.total(moves.scatter(qkv_grad.reshape(shard_count, -1, half_width)))
    grad_norm_one = dot(
        lax.dynamic_slice_in_dim(grad_joined, mine, half_rows, 1), qkv_full, 0, 0
    )
    unit_half = half_of(unit_one, mine)
    input_half = half_of(grad_middle, mine) + norm_back(
        grad_norm_one, unit_half, half_of(scale_one, mine), ln1_gain
    )
    input_grad = moves.from_chips(input_half.astype(BF16), seqs).astype(F32)

    once = (core == 0).astype(F32)
    up_bias_grad = jnp.sum(grad_pre.astype(F32), axis=0).reshape(shard_count, 1, ff_half)
    up_bias_grad = up_bias_grad * (jnp.arange(2)[None, :, None] == core).astype(F32)
    early = lax.psum(
        jnp.concatenate(
            [
                up_bias_grad.reshape(-1),
                once * jnp.sum(grad_norm_two * unit_two, axis=0),
                once * jnp.sum(grad_norm_two, axis=0),
                once * jnp.sum(grad_out_f, axis=0),
                once * jnp.sum(grad_branch.astype(F32), axis=0),
            ]
        ),
        AXES,
    )
    up_bias_grad, rest = early[:ff], early[ff:]
    ln2_gain_grad, ln2_bias_grad, down_bias_grad, out_bias_grad = rest.reshape(4, width)
    bias_sums = jnp.sum(grad_joined.astype(F32), axis=1).reshape(3, width)
    late = lax.psum(
        jnp.concatenate(
            [
                jnp.sum(grad_norm_one * unit_half, axis=0),
                jnp.sum(grad_norm_one, axis=0),
                once * bias_sums[0],
                once * bias_sums[2],
            ]
        ),
        AXES,
    )
    ln1_gain_grad, ln1_bias_grad, q_bias_grad, v_bias_grad = late.reshape(4, width)

    first = core == 0

    def join(own, axis):
        other = moves.over_core(own)
        low, high = jnp.where(first, own, other), jnp.where(first, other, own)
        return low.astype(F32), high.astype(F32), axis

    def laid(own, axis):
        low, high, axis = join(own, axis)
        return jnp.concatenate([low, high], axis=axis)

    down_low, down_high, _ = join(down_sum.reshape(-1, shard_count, ff_half), 2)
    down_total = jnp.stack([down_low, down_high], axis=2).reshape(-1, ff)
    up_total = laid(up_sum, 0)
    qkv_total = laid(qkv_sum, 1)
    out_low, out_high, _ = join(out_sum, 1)
    out_total = jnp.concatenate([out_low, out_high[:, HDIM:]], axis=1)
    return (
        result,
        input_grad,
        ln1_gain_grad,
        ln1_bias_grad,
        qkv_total,
        q_bias_grad,
        v_bias_grad,
        out_total,
        out_bias_grad,
        ln2_gain_grad,
        ln2_bias_grad,
        up_total,
        up_bias_grad,
        down_total,
        down_bias_grad,
    )


def solution(mesh):
    rows = P("shard", None)
    tokens = P("shard", "replica", None)
    in_specs = (
        tokens,
        tokens,
        P(None, "replica"),
        P(),
        P(),
        rows,
        P(),
        P(),
        rows,
        P(),
        P(),
        P(),
        rows,
        P(),
        rows,
        P(),
    )
    out_specs = (
        tokens,
        tokens,
        P(),
        P(),
        rows,
        P(),
        P(),
        rows,
        P(),
        P(),
        P(),
        rows,
        P(),
        rows,
        P(),
    )
    body = functools.partial(shards, mesh.shape["shard"], mesh.shape["replica"])
    return jax.shard_map(body, mesh=mesh, in_specs=in_specs, out_specs=out_specs, check_vma=False)
```

time: 2450 us -> 1290 us (0.53)
  waiting for transfers between devices: 1620 us -> 460 us
  matrix products: 492 us -> 185 us
  starting transfers between devices: 0.77 us -> 128 us
  other arithmetic: 81.9 us -> 165 us
  Pallas kernels: 0 us -> 54.3 us
  local copies, waits for them, and re-layouts: 219 us -> 264 us
    unnamed x17 -> x1, waiting for transfers between devices: 527 us -> 0.02 us
    all_gather x6 -> x0, waiting for transfers between devices: 466 us -> none  [the longest x1 134 us: shards(): lax.all_gather(qkv_weight, 'shard', axis=0, tiled=True)]
    ppermute x0 -> x72, waiting for transfers between devices: none -> 371 us  [move(): return lax.ppermute(array, AXES, pairs)]
    dot_general x187 -> x12, matrix products: 492 us -> 185 us  [dot(): lax.dot_general(left, right, (((left_dim,), (right_dim,)), ((), ())), pre...]
    reduce_scatter x3 -> x0, waiting for transfers between devices: 272 us -> none  [the longest x1 195 us: shards(): lax.psum_scatter(rows_term(grad_pre, normed_two).astype(jnp.bfloat16), 's...]
    psum x2 -> x1, waiting for transfers between devices: 355 us -> 88.9 us  [shards(): lax.psum(jnp.concatenate([jnp.sum(grad_norm_one * unit_half, axis=0), jnp...]
    ppermute x0 -> x72, starting transfers between devices: none -> 128 us  [move(): return lax.ppermute(array, AXES, pairs)]
    pallas_call x0 -> x2, Pallas kernels: none -> 54.3 us  [the longest x1 27.8 us: attention_back(): pl.pallas_call(backward_kernel, grid=(OWN_HEADS,), in_specs=[whole_spec((...]
  transfers between devices with their start and end apart: 14 -> 73, of which waited for: 13 -> 21; matrix products, arithmetic and copies ran while one was open for 20% -> 39% of each run, Pallas kernels for 0% -> 4%
where the time goes in v1:
time: 1290 us; the launch traced here: 1270 us
  waiting for transfers between devices  460 us (36%)
  local copies, waits for them, and re-layouts  264 us (20%)
  matrix products  185 us (14%)
  other arithmetic  165 us (13%)
  starting transfers between devices  128 us (10%)
  Pallas kernels  54.3 us (4%)
  between operations  15.5 us (1%)
    ppermute x72, waiting for transfers between devices, move(): return lax.ppermute(array, AXES, pairs)  371 us
    dot_general x12, matrix products, dot(): lax.dot_general(left, right, (((left_dim,), (right_dim,)), ((), ())), pre...  185 us
    ppermute x72, starting transfers between devices, move(): return lax.ppermute(array, AXES, pairs)  128 us
    psum x1, waiting for transfers between devices, shards(): lax.psum(jnp.concatenate([jnp.sum(grad_norm_one * unit_half, axis=0), jnp...  88.9 us
    dynamic_slice x1, local copies, waits for them, and re-layouts, part(): return lax.dynamic_slice(parts, begin, size)[0]  29.5 us
    pallas_call x1, Pallas kernels, attention_back(): pl.pallas_call(backward_kernel, grid=(OWN_HEADS,), in_specs=[whole_spec((...  27.8 us
    unnamed x152, local copies, waits for them, and re-layouts  26.5 us
    pallas_call x1, Pallas kernels, attention(): pl.pallas_call(forward_kernel, grid=(OWN_HEADS,), in_specs=[whole_spec((1...  26.5 us
  transfers between devices with their start and end apart: 73, of which 21 were waited for; matrix products, arithmetic and copies ran while one was open for 39% of the time, Pallas kernels for 4%

profile of v1, /device:TPU:1, one launch (start us, length us, event | category | flops | bytes accessed | tf_op | source)
XLA Modules:
  0.0 1271.6 jit_solution(13483142816587812896)
XLA Ops:
  55.7 28.2 %collective-permute-done.10 = bf16[400,832]{1,0:T(8,128)(2,1)S(1)} collective-permute-done((bf16[400,832]{1,0:T(8,128)(2,1)}, bf16[400,832]{1,0:T(8,128)(2,1)S(1)}, u32[]{:S(2)}, u32[]{:S(2)}) %collective-permute-start.10) | collective-permute-done | bytes 665632 | tf_op jit(solution)/shard_map/ppermute | solution.py:194
  130.1 27.9 %collective-permute-done.6 = bf16[300,1600]{1,0:T(8,128)(2,1)} collective-permute-done((bf16[300,1600]{1,0:T(8,128)(2,1)S(1)}, bf16[300,1600]{1,0:T(8,128)(2,1)}, u32[]{:S(2)}, u32[]{:S(2)}) %collective-permute-start.6) | collective-permute-done | bytes 960032 | tf_op jit(solution)/shard_map/ppermute | solution.py:194
  196.0 39.0 %collective-permute-done.19 = bf16[400,3200]{1,0:T(8,128)(2,1)S(1)} collective-permute-done((bf16[400,3200]{1,0:T(8,128)(2,1)S(1)}, bf16[400,3200]{1,0:T(8,128)(2,1)S(1)}, u32[]{:S(2)}, u32[]{:S(2)}) %collective-permute-start.19) | collective-permute-done | bytes 2560032 | tf_op jit(solution)/shard_map/ppermute | solution.py:194
  239.1 53.1 %collective-permute-done.15 = bf16[800,1600]{1,0:T(8,128)(2,1)S(1)} collective-permute-done((bf16[800,1600]{1,0:T(8,128)(2,1)S(1)}, bf16[800,1600]{1,0:T(8,128)(2,1)S(1)}, u32[]{:S(2)}, u32[]{:S(2)}) %collective-permute-start.15) | collective-permute-done | bytes 2560032 | tf_op jit(solution)/shard_map/ppermute | solution.py:194
  301.2 17.6 %maximum_select_fusion = bf16[4,1200,1600]{2,1,0:T(8,128)(2,1)} fusion(bf16[4,600,1600]{2,1,0:T(8,128)(2,1)S(1)} %collective-permute-done.8, bf16[4,600,1600]{2,1,0:T(8,128)(2,1)} %dynamic_update_slice.64, pred[]{:T(512)S(6)} %eq.52), kind=kLoop, calls=%fused_computation.1 | loop fusion | flops 69120000 | bytes 30720000 | tf_op jit(solution)/shard_map/jit(_where)/select_n | solution.py:339
  341.1 26.5 %attention_forward.1 = (bf16[832,1024]{1,0:T(8,128)(2,1)S(1)}, f32[13,1,1024]{2,1,0:T(1,128)S(1)}) custom-call(s32[1,1024]{1,0:T(1,128)S(1)} %bitcast.186, s32[1024,1]{1,0:T(8,128)S(1)} %copy.111.seg_col, bf16[2496,1024]{1,0:T(8,128)(2,1)S(1)} %fusion.12.q_ref.k_ref.v_ref, bf16[2496,1024]{1,0:T(8,128)(2,1)S(1)} %fusion.12.q_ref.k_ref.v_ref, ...), custom_call_target="tpu_custom_call" | custom-call | flops 13958643712 | bytes 6815744 | tf_op jit(solution)/shard_map/attention_forward/pallas_call | solution.py:130
  389.9 21.8 %fusion.54 = f32[1024,3200]{1,0:T(8,128)} fusion(bf16[3200,1600]{1,0:T(8,128)(2,1)} %bitcast.23, f32[1024,1600]{0,1:T(8,128)} %copy-done.3, f32[1600]{0:T(1024)S(1)} %copy-done.64, f32[1600]{0:T(1024)S(1)} %copy-done.49, f32[1024]{0:T(1024)S(1)} %add_rsqrt_fusion, f32[1024]{0:T(1024)S(1)} %broadcast_multiply_fusion.7), kind=kOutput, calls=%fused_computation.222 | convolution fusion | flops 10493952000 | bytes 29921792 | tf_op jit(solution)/shard_map/dot_general | solution.py:22
  411.7 19.7 %fusion.55 = f32[1024,1600]{0,1:T(8,128)} fusion(bf16[1600,3200]{1,0:T(8,128)(2,1)} %bitcast.28, f32[1024,3200]{1,0:T(8,128)} %fusion.54, f32[3200]{0:T(1024)S(1)} %copy-done.54), kind=kOutput, calls=%fused_computation.223 | convolution fusion | flops 10518528000 | bytes 29913600 | tf_op jit(solution)/shard_map/dot_general | solution.py:22
  431.4 27.8 %convert_reduce_fusion.1 = (f32[3200]{0:T(1024)}, bf16[1024,3200]{1,0:T(8,128)(2,1)}) fusion(f32[1024,3200]{1,0:T(8,128)} %fusion.54, f32[3200]{0:T(1024)S(1)} %copy-done.54, bf16[1600,3200]{1,0:T(8,128)(2,1)} %bitcast.28, bf16[512,1600]{0,1:T(8,128)(2,1)S(1)} %copy-done.27, bf16[512,1600]{0,1:T(8,128)(2,1)S(1)} %get-tuple-element.124), kind=kOutput, calls=%fused_computation.4 | convolution fusion | flops 10567676928 | bytes 33203200 | tf_op jit(solution)/shard_map/dot_general | solution.py:22
  459.2 18.5 %convolution_convert_fusion.1 = bf16[1600,3200]{1,0:T(8,128)(2,1)} fusion(bf16[512,1600]{0,1:T(8,128)(2,1)S(1)} %copy-done.27, bf16[512,1600]{0,1:T(8,128)(2,1)S(1)} %get-tuple-element.124, f32[1024,3200]{1,0:T(8,128)} %fusion.54, f32[3200]{0:T(1024)S(1)} %copy-done.54), kind=kOutput, calls=%fused_computation.3 | convolution fusion | flops 10530201600 | bytes 26636800 | tf_op jit(solution)/shard_map/dot_general | solution.py:22
  481.0 18.1 %convolution_convert_fusion = bf16[3200,1600]{0,1:T(8,128)(2,1)} fusion(bf16[1024,3200]{1,0:T(8,128)(2,1)} %get-tuple-element.156, f32[1024,1600]{0,1:T(8,128)} %copy-done.3, f32[1600]{0:T(1024)S(1)} %copy-done.64, f32[1600]{0:T(1024)S(1)} %copy-done.49, f32[1024]{0:T(1024)S(1)} %add_rsqrt_fusion, f32[1024]{0:T(1024)S(1)} %broadcast_multiply_fusion.7), kind=kOutput, calls=%fused_computation.2 | convolution fusion | flops 10499072000 | bytes 23368192 | tf_op jit(solution)/shard_map/dot_general | solution.py:22
  499.1 16.6 %copy.123 = bf16[3200,1600]{1,0:T(8,128)(2,1)} copy(bf16[3200,1600]{0,1:T(8,128)(2,1)} %convolution_convert_fusion) | data formatting | bytes 20480000 | tf_op jit(solution)/shard_map/convert_element_type | solution.py:398
  521.5 19.0 %fusion.61 = (bf16[1024,1600]{0,1:T(8,128)(2,1)}, f32[1024,1600]{0,1:T(8,128)}) fusion(bf16[1024,3200]{1,0:T(8,128)(2,1)} %get-tuple-element.156, bf16[3200,1600]{1,0:T(8,128)(2,1)} %bitcast.23), kind=kOutput, calls=%fused_computation.228 | convolution fusion | flops 10487398400 | bytes 26624000 | tf_op jit(solution)/shard_map/dot_general | solution.py:22
  562.6 43.9 %collective-permute-done.63 = bf16[200,3200]{1,0:T(8,128)(2,1)S(1)} collective-permute-done((bf16[200,3200]{1,0:T(8,128)(2,1)S(1)}, bf16[200,3200]{1,0:T(8,128)(2,1)S(1)}, u32[]{:S(2)}, u32[]{:S(2)}) %collective-permute-start.63) | collective-permute-done | bytes 1280032 | tf_op jit(solution)/shard_map/ppermute | solution.py:194
  611.4 16.6 %collective-permute-done.24 = bf16[256,1600]{0,1:T(8,128)(2,1)S(1)} collective-permute-done((bf16[256,1600]{0,1:T(8,128)(2,1)S(1)}, bf16[256,1600]{0,1:T(8,128)(2,1)S(1)}, u32[]{:S(2)}, u32[]{:S(2)}) %collective-permute-start.24) | collective-permute-done | bytes 819232 | tf_op jit(solution)/shard_map/ppermute | solution.py:194
  659.9 27.8 %attention_backward.1 = (bf16[832,1024]{1,0:T(8,128)(2,1)S(1)}, bf16[832,1024]{1,0:T(8,128)(2,1)S(1)}, bf16[832,1024]{1,0:T(8,128)(2,1)S(1)}) custom-call(s32[1,1024]{1,0:T(1,128)S(1)} %bitcast.187, s32[1024,1]{1,0:T(8,128)S(1)} %copy.111.seg_col, bf16[2496,1024]{1,0:T(8,128)(2,1)} %copy-done.2, bf16[2496,1024]{1,0:T(8,128)(2,1)} %copy-done.2, ...), custom_call_target="tpu_custom_call" | custom-call | flops 34896609280 | bytes 13631488 | tf_op jit(solution)/shard_map/attention_backward/pallas_call | solution.py:153
  700.3 51.1 %collective-permute-done.46 = bf16[200,832]{1,0:T(8,128)(2,1)S(1)} collective-permute-done((bf16[200,832]{1,0:T(8,128)(2,1)S(1)}, bf16[200,832]{1,0:T(8,128)(2,1)S(1)}, u32[]{:S(2)}, u32[]{:S(2)}) %collective-permute-start.46) | collective-permute-done | bytes 332832 | tf_op jit(solution)/shard_map/ppermute | solution.py:194
  766.2 28.3 %collective-permute-done.45 = bf16[200,832]{1,0:T(8,128)(2,1)S(1)} collective-permute-done((bf16[200,832]{1,0:T(8,128)(2,1)S(1)}, bf16[200,832]{1,0:T(8,128)(2,1)S(1)}, u32[]{:S(2)}, u32[]{:S(2)}) %collective-permute-start.45) | collective-permute-done | bytes 332832 | tf_op jit(solution)/shard_map/ppermute | solution.py:194
  861.4 19.0 %reshape.214 = bf16[4,1200,800]{1,0,2:T(4,128)(2,1)} reshape(bf16[4800,800]{0,1:T(8,128)(2,1)} %convolution_convert_fusion.2) | data formatting | bytes 15360000 | tf_op jit(solution)/shard_map/reshape | solution.py:421
  880.4 29.5 %constant_dynamic-slice_fusion.7 = (bf16[1,600,800]{1,0,2:T(2,128)(2,1)}, bf16[1,600,800]{1,0,2:T(2,128)(2,1)}, bf16[1,600,800]{1,0,2:T(2,128)(2,1)}, bf16[1,600...) fusion(bf16[4,1200,800]{1,0,2:T(4,128)(2,1)} %reshape.214, ...), kind=kLoop, calls=%fused_computation.172 | loop fusion | bytes 15360016 | tf_op jit(solution)/shard_map/dynamic_slice | solution.py:234
  967.2 23.2 %collective-permute-done.37 = bf16[600,800]{0,1:T(8,128)(2,1)S(1)} collective-permute-done((bf16[600,800]{0,1:T(8,128)(2,1)S(1)}, bf16[600,800]{0,1:T(8,128)(2,1)S(1)}, u32[]{:S(2)}, u32[]{:S(2)}) %collective-permute-start.37) | collective-permute-done | bytes 960032 | tf_op jit(solution)/shard_map/ppermute | solution.py:194
  999.1 17.6 %multiply_reduce_fusion.4 = (f32[1600]{0:T(1024)}, f32[512]{0:T(512)S(1)}, f32[512]{0:T(512)S(1)}, f32[1600]{0:T(1024)}, f32[512,1600]{0,1:T(8,128)}) fusion(f32[1024,1600]{0,1:T(8,128)} %get-tuple-element.121, s32[]{:T(128)S(6)} %select_n.344, f32[1600]{0:T(1024)S(1)} %copy-done.52, bf16[4800,1600]{1,0:T(8,128)(2,1)} %bitcast.197, ...), kind=kOutput, calls=%fused_computation.50 | convolution fusion | flops 7870050304 | bytes 27467520 | tf_op jit(solution)/shard_map/dot_general | solution.py:22
  1076.3 17.6 %collective-permute-done.60 = bf16[800,1600]{1,0:T(8,128)(2,1)} collective-permute-done((bf16[800,1600]{1,0:T(8,128)(2,1)}, bf16[800,1600]{1,0:T(8,128)(2,1)}, u32[]{:S(2)}, u32[]{:S(2)}) %collective-permute-start.60) | collective-permute-done | bytes 2560032 | tf_op jit(solution)/shard_map/ppermute | solution.py:194
  1114.6 88.9 %all-reduce.3.cloned.1.call-done = (f32[6400]{0:T(1024)}, f32[12800]{0:T(1024)}) async-done(((f32[6400]{0:T(1024)}, f32[12800]{0:T(1024)}), (f32[6400]{0:T(1024)}, f32[12800]{0:T(1024)})) %all-reduce.3.cloned.1.call-update) | async-done | bytes 76816 | tf_op jit(solution)/shard_map/psum | solution.py:449
  (438 shorter events, 558.9 us)
Async XLA Ops:
  7.2 1196.4 %all-reduce.3.cloned.1.call-start = ((), (), s32[]{:S(2)}) async-start(), calls=%async_computation | async-start | bytes 163840 | tf_op jit(solution)/shard_map/psum | solution.py:449
  13.4 105.6 %collective-permute-start.4 = (bf16[600,1600]{1,0:T(8,128)(2,1)}, bf16[600,1600]{1,0:T(8,128)(2,1)}, u32[]{:S(2)}, u32[]{:S(2)}) collective-permute-start(bf16[600,1600]{1,0:T(8,128)(2,1)} %get-tuple-element.87), channel_id=1, source_target_pairs={{0,8},{1,9},{2,10},{3,11},{4,12},{5,13},{6,14},{7,15},{8,0},{9,1},... | collective-permute-start | bytes 5760008 | tf_op jit(solution)/shard_map/ppermute | solution.py:194
  15.5 101.0 %collective-permute-start.5 = (bf16[600,1600]{1,0:T(8,128)(2,1)}, bf16[600,1600]{1,0:T(8,128)(2,1)}, u32[]{:S(2)}, u32[]{:S(2)}) collective-permute-start(bf16[600,1600]{1,0:T(8,128)(2,1)} %get-tuple-element.87), channel_id=1, source_target_pairs={{0,16},{1,17},{2,18},{3,19},{4,20},{5,21},{6,22},{7,23},{8,24},{9,... | collective-permute-start | bytes 5760008 | tf_op jit(solution)/shard_map/ppermute | solution.py:194
  22.9 88.9 %collective-permute-start = (bf16[256,1600]{0,1:T(8,128)(2,1)}, bf16[256,1600]{0,1:T(8,128)(2,1)}, u32[]{:S(2)}, u32[]{:S(2)}) collective-permute-start(bf16[256,1600]{0,1:T(8,128)(2,1)} %get-tuple-element.141), channel_id=1, source_target_pairs={{0,8},{1,24},{2,10},{3,26},{4,12},{5,28},{6,14},{7,30},{8,0},{9,16... | collective-permute-start | bytes 2457608 | tf_op jit(solution)/shard_map/ppermute | solution.py:194
  169.8 131.4 %collective-permute-start.8 = (bf16[4,600,1600]{2,1,0:T(8,128)(2,1)}, bf16[4,600,1600]{2,1,0:T(8,128)(2,1)S(1)}, u32[]{:S(2)}, u32[]{:S(2)}) collective-permute-start(bf16[4,600,1600]{2,1,0:T(8,128)(2,1)} %dynamic_update_slice.64), channel_id=1, source_target_pairs={{0,1},{1,0},{2,3},{3,2},{4,5},{5,4},{6,7},{7,6},{8,9},{9,8},{10,11... | collective-permute-start | bytes 23040008 | tf_op jit(solution)/shard_map/ppermute | solution.py:194
  185.5 108.0 %collective-permute-start.14 = (bf16[800,1600]{1,0:T(8,128)(2,1)S(1)}, bf16[800,1600]{1,0:T(8,128)(2,1)S(1)}, u32[]{:S(2)}, u32[]{:S(2)}) collective-permute-start(bf16[800,1600]{1,0:T(8,128)(2,1)S(1)} %copy-done.33), channel_id=1, source_target_pairs={{0,8},{1,9},{2,10},{3,11},{4,12},{5,13},{6,14},{7,15},{8,0},{9,1},... | collective-permute-start | bytes 7680008 | tf_op jit(solution)/shard_map/ppermute | solution.py:194
  185.8 106.3 %collective-permute-start.15 = (bf16[800,1600]{1,0:T(8,128)(2,1)S(1)}, bf16[800,1600]{1,0:T(8,128)(2,1)S(1)}, u32[]{:S(2)}, u32[]{:S(2)}) collective-permute-start(bf16[800,1600]{1,0:T(8,128)(2,1)S(1)} %copy-done.33), channel_id=1, source_target_pairs={{0,16},{1,17},{2,18},{3,19},{4,20},{5,21},{6,22},{7,23},{8,24},{9,... | collective-permute-start | bytes 7680008 | tf_op jit(solution)/shard_map/ppermute | solution.py:194
  236.1 144.1 %collective-permute-start.20 = (bf16[200,3200]{1,0:T(8,128)(2,1)}, bf16[200,3200]{1,0:T(8,128)(2,1)}, u32[]{:S(2)}, u32[]{:S(2)}) collective-permute-start(bf16[200,3200]{1,0:T(8,128)(2,1)} %slice.76), channel_id=1, source_target_pairs={{0,8},{1,9},{2,10},{3,11},{4,12},{5,13},{6,14},{7,15},{8,0},{9,1},... | collective-permute-start | bytes 3840008 | tf_op jit(solution)/shard_map/ppermute | solution.py:194
  237.6 145.1 %collective-permute-start.21 = (bf16[200,3200]{1,0:T(8,128)(2,1)}, bf16[200,3200]{1,0:T(8,128)(2,1)}, u32[]{:S(2)}, u32[]{:S(2)}) collective-permute-start(bf16[200,3200]{1,0:T(8,128)(2,1)} %slice.77), channel_id=1, source_target_pairs={{0,16},{1,17},{2,18},{3,19},{4,20},{5,21},{6,22},{7,23},{8,24},{9,... | collective-permute-start | bytes 3840008 | tf_op jit(solution)/shard_map/ppermute | solution.py:194
  293.4 83.2 %collective-permute-start.16 = (bf16[400,1600]{1,0:T(8,128)(2,1)}, bf16[400,1600]{1,0:T(8,128)(2,1)S(1)}, u32[]{:S(2)}, u32[]{:S(2)}) collective-permute-start(bf16[400,1600]{1,0:T(8,128)(2,1)} %slice.74), channel_id=1, source_target_pairs={{0,8},{1,9},{2,10},{3,11},{4,12},{5,13},{6,14},{7,15},{8,0},{9,1},... | collective-permute-start | bytes 3840008 | tf_op jit(solution)/shard_map/ppermute | solution.py:194
  294.7 83.0 %collective-permute-start.17 = (bf16[400,1600]{1,0:T(8,128)(2,1)}, bf16[400,1600]{1,0:T(8,128)(2,1)}, u32[]{:S(2)}, u32[]{:S(2)}) collective-permute-start(bf16[400,1600]{1,0:T(8,128)(2,1)} %slice.75), channel_id=1, source_target_pairs={{0,16},{1,17},{2,18},{3,19},{4,20},{5,21},{6,22},{7,23},{8,24},{9,... | collective-permute-start | bytes 3840008 | tf_op jit(solution)/shard_map/ppermute | solution.py:194
  540.5 89.6 %collective-permute-start.28 = (bf16[1024,1600]{0,1:T(8,128)(2,1)}, bf16[1024,1600]{0,1:T(8,128)(2,1)}, u32[]{:S(2)}, u32[]{:S(2)}) collective-permute-start(bf16[1024,1600]{0,1:T(8,128)(2,1)} %get-tuple-element.152), channel_id=1, source_target_pairs={{0,1},{1,0},{2,3},{3,2},{4,5},{5,4},{6,7},{7,6},{8,9},{9,8},{10,11... | collective-permute-start | bytes 9830408 | tf_op jit(solution)/shard_map/ppermute | solution.py:194
  545.5 142.3 %collective-permute-start.52 = (bf16[400,1600]{1,0:T(8,128)(2,1)}, bf16[400,1600]{1,0:T(8,128)(2,1)}, u32[]{:S(2)}, u32[]{:S(2)}) collective-permute-start(bf16[400,1600]{1,0:T(8,128)(2,1)} %get-tuple-element.97), channel_id=1, source_target_pairs={{0,8},{1,9},{2,10},{3,11},{4,12},{5,13},{6,14},{7,15},{8,0},{9,1},... | collective-permute-start | bytes 3840008 | tf_op jit(solution)/shard_map/ppermute | solution.py:194
  545.8 143.6 %collective-permute-start.56 = (bf16[400,1600]{1,0:T(8,128)(2,1)}, bf16[400,1600]{1,0:T(8,128)(2,1)}, u32[]{:S(2)}, u32[]{:S(2)}) collective-permute-start(bf16[400,1600]{1,0:T(8,128)(2,1)} %get-tuple-element.98), channel_id=1, source_target_pairs={{0,16},{1,17},{2,18},{3,19},{4,20},{5,21},{6,22},{7,23},{8,24},{9,... | collective-permute-start | bytes 3840008 | tf_op jit(solution)/shard_map/ppermute | solution.py:194
  611.2 149.0 %collective-permute-start.62 = (bf16[200,3200]{1,0:T(8,128)(2,1)}, bf16[200,3200]{1,0:T(8,128)(2,1)}, u32[]{:S(2)}, u32[]{:S(2)}) collective-permute-start(bf16[200,3200]{1,0:T(8,128)(2,1)} %get-tuple-element.103), channel_id=1, source_target_pairs={{0,8},{1,9},{2,10},{3,11},{4,12},{5,13},{6,14},{7,15},{8,0},{9,1},... | collective-permute-start | bytes 3840008 | tf_op jit(solution)/shard_map/ppermute | solution.py:194
  697.5 134.6 %collective-permute-start.29 = (bf16[3,832,1024]{2,1,0:T(8,128)(2,1)S(1)}, bf16[3,832,1024]{2,1,0:T(8,128)(2,1)}, u32[]{:S(2)}, u32[]{:S(2)}) collective-permute-start(bf16[3,832,1024]{2,1,0:T(8,128)(2,1)S(1)} %pad_maximum_fusion.1), channel_id=1, source_target_pairs={{0,1},{1,0},{2,3},{3,2},{4,5},{5,4},{6,7},{7,6},{8,9},{9,8},{10,11... | collective-permute-start | bytes 15335432 | tf_op jit(solution)/shard_map/ppermute | solution.py:194
  804.0 144.9 %collective-permute-start.58 = (bf16[800,1600]{1,0:T(8,128)(2,1)}, bf16[800,1600]{1,0:T(8,128)(2,1)}, u32[]{:S(2)}, u32[]{:S(2)}) collective-permute-start(bf16[800,1600]{1,0:T(8,128)(2,1)} %pad_maximum_fusion.4), channel_id=1, source_target_pairs={{0,2},{1,3},{6,4},{7,5},{8,10},{9,11},{14,12},{15,13},{16,18},{17,... | collective-permute-start | bytes 7680008 | tf_op jit(solution)/shard_map/ppermute | solution.py:194
  825.0 97.1 %collective-permute-start.68 = (bf16[400,3200]{1,0:T(8,128)(2,1)}, bf16[400,3200]{1,0:T(8,128)(2,1)}, u32[]{:S(2)}, u32[]{:S(2)}) collective-permute-start(bf16[400,3200]{1,0:T(8,128)(2,1)} %pad_maximum_fusion.5), channel_id=1, source_target_pairs={{0,2},{1,3},{6,4},{7,5},{8,10},{9,11},{14,12},{15,13},{16,18},{17,... | collective-permute-start | bytes 7680008 | tf_op jit(solution)/shard_map/ppermute | solution.py:194
  830.8 98.5 %collective-permute-start.50 = (bf16[400,832]{1,0:T(8,128)(2,1)}, bf16[400,832]{1,0:T(8,128)(2,1)}, u32[]{:S(2)}, u32[]{:S(2)}) collective-permute-start(bf16[400,832]{1,0:T(8,128)(2,1)} %add.445), channel_id=1, source_target_pairs={{2,0},{3,1},{4,6},{5,7},{10,8},{11,9},{12,14},{13,15},{18,16},{19,... | collective-permute-start | bytes 1996808 | tf_op jit(solution)/shard_map/ppermute | solution.py:194
  1049.2 162.9 %collective-permute-start.71 = (bf16[400,4,800]{2,0,1:T(8,128)(2,1)}, bf16[400,4,800]{2,0,1:T(8,128)(2,1)}, u32[]{:S(2)}, u32[]{:S(2)}) collective-permute-start(bf16[400,4,800]{2,0,1:T(8,128)(2,1)} %copy.125), channel_id=1, source_target_pairs={{0,1},{1,0},{2,3},{3,2},{4,5},{5,4},{6,7},{7,6},{8,9},{9,8},{10,11... | collective-permute-start | bytes 7680008 | tf_op jit(solution)/shard_map/ppermute | solution.py:194
  1061.4 146.4 %collective-permute-start.30 = (bf16[256,1600]{0,1:T(8,128)(2,1)}, bf16[256,1600]{0,1:T(8,128)(2,1)}, u32[]{:S(2)}, u32[]{:S(2)}) collective-permute-start(bf16[256,1600]{0,1:T(8,128)(2,1)} %get-tuple-element.135), channel_id=1, source_target_pairs={{0,0},{1,16},{2,2},{3,18},{4,4},{5,20},{6,6},{7,22},{8,8},{9,24},{... | collective-permute-start | bytes 2457608 | tf_op jit(solution)/shard_map/ppermute | solution.py:194
  1065.2 142.6 %collective-permute-start.31 = (bf16[256,1600]{0,1:T(8,128)(2,1)}, bf16[256,1600]{0,1:T(8,128)(2,1)}, u32[]{:S(2)}, u32[]{:S(2)}) collective-permute-start(bf16[256,1600]{0,1:T(8,128)(2,1)} %get-tuple-element.134), channel_id=1, source_target_pairs={{0,8},{1,24},{2,10},{3,26},{4,12},{5,28},{6,14},{7,30},{8,0},{9,16... | collective-permute-start | bytes 2457608 | tf_op jit(solution)/shard_map/ppermute | solution.py:194
  1074.6 140.1 %collective-permute-start.40 = (bf16[1200,800]{0,1:T(8,128)(2,1)}, bf16[1200,800]{0,1:T(8,128)(2,1)}, u32[]{:S(2)}, u32[]{:S(2)}) collective-permute-start(bf16[1200,800]{0,1:T(8,128)(2,1)} %add.437), channel_id=1, source_target_pairs={{2,0},{3,1},{4,6},{5,7},{10,8},{11,9},{12,14},{13,15},{18,16},{19,... | collective-permute-start | bytes 5760008 | tf_op jit(solution)/shard_map/ppermute | solution.py:194
  1097.5 143.9 %collective-permute-start.61 = (bf16[800,1600]{1,0:T(8,128)(2,1)}, bf16[800,1600]{1,0:T(8,128)(2,1)}, u32[]{:S(2)}, u32[]{:S(2)}) collective-permute-start(bf16[800,1600]{1,0:T(8,128)(2,1)} %broadcast_select_fusion.1), channel_id=1, source_target_pairs={{0,1},{1,0},{2,3},{3,2},{4,5},{5,4},{6,7},{7,6},{8,9},{9,8},{10,11... | collective-permute-start | bytes 7680008 | tf_op jit(solution)/shard_map/ppermute | solution.py:194
  (122 other events, 3241.4 us)
Sparse Core Ops, SparseCore 0:
  1070.7 132.8 all-reduce.2

commit v2 on v1

v2 whole, which is shorter than its diff:
```python
import functools

import jax
import jax.numpy as jnp
from jax import lax
from jax.experimental import pallas as pl
from jax.experimental.pallas import tpu as pltpu
from jax.sharding import PartitionSpec as P

HEADS = 25
HDIM = 64
OWN_HEADS = HEADS // 2 + 1
FIRST_HEAD = HEADS // 2
OWN = OWN_HEADS * HDIM
BLOCK = 256
AXES = ("shard", "replica")
BF16 = jnp.bfloat16
F32 = jnp.float32


def dot(left, right, left_dim, right_dim):
    return lax.dot_general(
        left, right, (((left_dim,), (right_dim,)), ((), ())), preferred_element_type=F32
    )


COST_SCALE = 8


def cost(flops, bytes_accessed):
    return pl.CostEstimate(
        flops=int(flops * COST_SCALE),
        bytes_accessed=int(bytes_accessed * COST_SCALE),
        transcendentals=0,
    )


def norm_parts(rows):
    centre = rows - jnp.mean(rows, axis=0, keepdims=True)
    scale = lax.rsqrt(jnp.mean(centre * centre, axis=0, keepdims=True) + 1e-05)
    return centre * scale, scale


def norm_back(grad, unit, scale, gain):
    inner = grad * gain
    mean_inner = jnp.mean(inner, axis=0, keepdims=True)
    mean_cross = jnp.mean(inner * unit, axis=0, keepdims=True)
    return scale * (inner - mean_inner - unit * mean_cross)


def gelu_pair(value):
    root = 0.7978845608028654
    cube = 0.044715
    square = value * value
    tanh = jnp.tanh(root * value * (1.0 + cube * square))
    half = 0.5 * (1.0 + tanh)
    slope = half + 0.5 * value * (1.0 - tanh * tanh) * root * (1.0 + 3.0 * cube * square)
    return value * half, slope


def fill_mask(seg_row, seg_col, mask, blocks):
    for q_at in range(blocks):
        for k_at in range(q_at + 1):
            keys = seg_col[pl.ds(k_at * BLOCK, BLOCK), :]
            queries = seg_row[:, pl.ds(q_at * BLOCK, BLOCK)]
            seen = keys == queries
            if k_at == q_at:
                k_place = lax.broadcasted_iota(jnp.int32, (BLOCK, BLOCK), 0)
                q_place = lax.broadcasted_iota(jnp.int32, (BLOCK, BLOCK), 1)
                seen = seen & (k_place <= q_place)
            mask[pl.ds(k_at * BLOCK, BLOCK), pl.ds(q_at * BLOCK, BLOCK)] = jnp.where(
                seen, 0.0, -1e30
            )


def forward_kernel(seg_row, seg_col, q_ref, k_ref, v_ref, *refs):
    o_ref, lse_ref, mask = refs[-3:]
    length = q_ref.shape[1]
    blocks = length // BLOCK

    @pl.when(pl.program_id(0) == 0)
    def _():
        fill_mask(seg_row, seg_col, mask, blocks)

    keys = k_ref[...].T
    for q_at in range(blocks):
        span = (q_at + 1) * BLOCK
        here = pl.ds(q_at * BLOCK, BLOCK)
        scores = dot(keys[:span], q_ref[:, here], 1, 0) + mask[:span, here]
        peak = jnp.max(scores, axis=0, keepdims=True)
        terms = jnp.exp(scores - peak)
        total = jnp.sum(terms, axis=0, keepdims=True)
        mixed = dot(v_ref[:, :span], terms.astype(BF16), 1, 0)
        o_ref[:, here] = (mixed / total).astype(BF16)
        lse_ref[0, :, here] = peak + jnp.log(total)


def backward_kernel(seg_row, seg_col, q_ref, k_ref, v_ref, o_ref, g_ref, lse_ref, *refs):
    grads, mask, acc = refs[-3:]
    length = q_ref.shape[1]
    blocks = length // BLOCK

    @pl.when(pl.program_id(0) == 0)
    def _():
        fill_mask(seg_row, seg_col, mask, blocks)

    keys = k_ref[...].T
    values = v_ref[...].T
    delta = jnp.sum(g_ref[...].astype(F32) * o_ref[...].astype(F32), axis=0, keepdims=True)
    lse = lse_ref[0]
    for k_at in range(blocks):
        low = k_at * BLOCK
        here = pl.ds(low, BLOCK)
        rest = pl.ds(low, length - low)
        scores = dot(keys[low : low + BLOCK], q_ref[:, rest], 1, 0) + mask[here, rest]
        soft = jnp.exp(scores - lse[:, low:])
        soft_grad = dot(values[low : low + BLOCK], g_ref[:, rest], 1, 0)
        score_grad = (soft * (soft_grad - delta[:, low:])).astype(BF16)
        grads[2, :, here] = dot(g_ref[:, rest], soft.astype(BF16), 1, 1).astype(BF16)
        grads[1, :, here] = dot(q_ref[:, rest], score_grad, 1, 1).astype(BF16)
        grad_q = dot(k_ref[:, here], score_grad, 1, 0)
        if k_at == 0:
            acc[...] = grad_q
        else:
            acc[:, rest] += grad_q
    grads[0] = (acc[...] * 0.125).astype(BF16)


def head_spec(first, length):
    return pl.BlockSpec((HDIM, length), lambda head: (first + head, 0))


def whole_spec(shape):
    return pl.BlockSpec(shape, lambda head: (0,) * len(shape))


def attention(seg, joined, wait):
    length = seg.shape[0]
    lse_spec = pl.BlockSpec((1, 1, length), lambda head: (head, 0, 0))
    pairs = OWN_HEADS * length * length
    return pl.pallas_call(
        forward_kernel,
        grid=(OWN_HEADS,),
        in_specs=[whole_spec((1, length)), whole_spec((length, 1))]
        + [head_spec(part * OWN_HEADS, length) for part in range(3)]
        + [pl.BlockSpec(memory_space=pl.ANY)] * len(wait),
        out_specs=[head_spec(0, length), lse_spec],
        out_shape=[
            jax.ShapeDtypeStruct((OWN, length), BF16),
            jax.ShapeDtypeStruct((OWN_HEADS, 1, length), F32),
        ],
        scratch_shapes=[pltpu.VMEM((length, length), F32)],
        compiler_params=pltpu.CompilerParams(vmem_limit_bytes=40 * 2**20),
        cost_estimate=cost(16 * pairs * HDIM, 8 * OWN * length),
        name="attention_forward",
    )(seg.reshape(1, length), seg.reshape(length, 1), joined, joined, joined, *wait)


def attention_back(seg, joined, mixed, grad, lse, wait):
    length = seg.shape[0]
    lse_spec = pl.BlockSpec((1, 1, length), lambda head: (head, 0, 0))
    pairs = OWN_HEADS * length * length
    return pl.pallas_call(
        backward_kernel,
        grid=(OWN_HEADS,),
        in_specs=[whole_spec((1, length)), whole_spec((length, 1))]
        + [head_spec(part * OWN_HEADS, length) for part in range(3)]
        + [head_spec(0, length), head_spec(0, length), lse_spec]
        + [pl.BlockSpec(memory_space=pl.ANY)] * len(wait),
        out_specs=pl.BlockSpec((3, HDIM, length), lambda head: (0, head, 0)),
        out_shape=jax.ShapeDtypeStruct((3, OWN, length), BF16),
        scratch_shapes=[pltpu.VMEM((length, length), F32), pltpu.VMEM((HDIM, length), F32)],
        compiler_params=pltpu.CompilerParams(vmem_limit_bytes=48 * 2**20),
        cost_estimate=cost(40 * pairs * HDIM, 16 * OWN * length),
        name="attention_backward",
    )(
        seg.reshape(1, length),
        seg.reshape(length, 1),
        joined,
        joined,
        joined,
        mixed,
        grad,
        lse,
        *wait,
    )


def product(left, rights, form, block, finish=None, extras=(), outs=((None, BF16),), name="product",
            wait=()):
    rights = rights if isinstance(rights, (list, tuple)) else [rights]
    many = len(rights)
    left_dim, right_dim = (0 if form == "tn" else 1), (1 if form == "nt" else 0)
    m, k = left.shape[1 - left_dim], left.shape[left_dim]
    size = rights[0].shape[1 - right_dim]
    n = size * many
    block = min(block, m)

    def body(left_ref, *refs):
        extra_refs = refs[many : many + len(extras)]
        out_refs = refs[many + len(extras) + len(wait) :]
        for at in range(many):
            value = dot(left_ref[...], refs[at][...], left_dim, right_dim)
            values = (value,)
            if finish is not None:
                values = finish(value, at, *extra_refs)
            for ref, part in zip(out_refs, values):
                if part is not None:
                    width = part.shape[1]
                    begin = at * width % ref.shape[1]
                    ref[:, begin : begin + width] = part.astype(ref.dtype)

    if form == "tn":
        left_spec = pl.BlockSpec((k, block), lambda i: (0, i))
    else:
        left_spec = pl.BlockSpec((block, k), lambda i: (i, 0))
    sizes = [(columns or n, kind) for columns, kind in outs]
    results = pl.pallas_call(
        body,
        grid=(pl.cdiv(m, block),),
        in_specs=[left_spec]
        + [
            pl.BlockSpec(right.shape, lambda i: (0, 0), pipeline_mode=pl.Buffered(1))
            for right in rights
        ]
        + [pl.BlockSpec((block, extra.shape[1]), lambda i: (i, 0)) for extra in extras]
        + [pl.BlockSpec(memory_space=pl.ANY)] * len(wait),
        out_specs=[pl.BlockSpec((block, columns), lambda i: (i, 0)) for columns, _ in sizes],
        out_shape=[jax.ShapeDtypeStruct((m, columns), kind) for columns, kind in sizes],
        compiler_params=pltpu.CompilerParams(vmem_limit_bytes=56 * 2**20),
        cost_estimate=cost(2 * m * n * k, 2 * (m * k + n * k + m * n)),
        name=name,
    )(left, *rights, *extras, *wait)
    return results if len(outs) > 1 else results[0]


def lane_sums(value):
    return sum(value[:, at : at + 128] for at in range(0, value.shape[1], 128))


def lay(places, near, far, parts):
    count, columns = near[0].shape
    size = count // parts
    kind = near[0].dtype

    def body(places_ref, *refs):
        step = pl.program_id(0)
        outs = refs[5:]
        for at in range(3):

            @pl.when(step == at)
            def _(at=at):
                for index, out in enumerate(outs):
                    out[...] = refs[at][index * size : (index + 1) * size]

        @pl.when(step == 3)
        def _():
            start = 0
            for ref in refs[3:5]:
                rows = ref.shape[0]
                for index, out in enumerate(outs):
                    low, high = max(start, index * size), min(start + rows, (index + 1) * size)
                    if low < high:
                        out[low - index * size : high - index * size] = ref[
                            low - start : high - start
                        ]
                start += rows

    pieces = list(near) + list(far)
    return pl.pallas_call(
        body,
        grid_spec=pltpu.PrefetchScalarGridSpec(
            num_scalar_prefetch=1,
            grid=(4,),
            in_specs=[
                pl.BlockSpec(piece.shape, lambda i, p: (0, 0), pipeline_mode=pl.Buffered(1))
                for piece in pieces
            ],
            out_specs=[pl.BlockSpec((size, columns), lambda i, p: (p[i], 0))] * parts,
        ),
        out_shape=[jax.ShapeDtypeStruct((4 * size, columns), kind)] * parts,
        compiler_params=pltpu.CompilerParams(vmem_limit_bytes=56 * 2**20),
        cost_estimate=cost(0, 16 * count * columns),
        name="lay",
    )(places, *pieces)


def lay_heads(core, places, mine, others, count):
    rows, width = mine[0].shape
    over = 2 * rows - count

    def body(core_ref, places_ref, *refs):
        heads_ref, block = refs[10:]
        step = pl.program_id(0)

        def halves(refs, begin, size, at, skip):
            if at < 3:
                block[begin : begin + size - skip] = refs[at][skip:]
            else:
                cut = refs[3].shape[0]
                block[begin : begin + cut - skip] = refs[3][skip:]
                block[begin + cut - skip : begin + size - skip] = refs[4][...]

        for which in range(2):

            @pl.when(core_ref[0] == which)
            def _(which=which):
                low, high = (refs[:5], refs[5:10]) if which == 0 else (refs[5:10], refs[:5])
                for at in range(4):

                    @pl.when(step == at)
                    def _(at=at):
                        halves(low, 0, rows, at, 0)
                        halves(high, rows, rows, at, over)

                for shard in range(4):

                    @pl.when(places_ref[step] == shard)
                    def _(shard=shard):
                        for part in range(3):
                            begin = part * width + which * FIRST_HEAD * HDIM
                            first = max(begin, shard * count)
                            last = min(begin + OWN, (shard + 1) * count)
                            if first < last:
                                heads_ref[
                                    part * OWN + first - begin : part * OWN + last - begin
                                ] = block[first - shard * count : last - shard * count]

    pieces = list(mine) + list(others)
    return pl.pallas_call(
        body,
        grid_spec=pltpu.PrefetchScalarGridSpec(
            num_scalar_prefetch=2,
            grid=(4,),
            in_specs=[
                pl.BlockSpec(piece.shape, lambda i, c, p: (0, 0), pipeline_mode=pl.Buffered(1))
                for piece in pieces
            ],
            out_specs=pl.BlockSpec(
                (3 * OWN, width), lambda i, c, p: (0, 0), pipeline_mode=pl.Buffered(1)
            ),
            scratch_shapes=[pltpu.VMEM((count, width), BF16)],
        ),
        out_shape=jax.ShapeDtypeStruct((3 * OWN, width), BF16),
        compiler_params=pltpu.CompilerParams(vmem_limit_bytes=56 * 2**20),
        cost_estimate=cost(0, 16 * count * width),
        name="lay_heads",
    )(core, places, *pieces)


def join_heads(core, own, other):
    length = own.shape[1]
    rows = 2 * OWN - HDIM

    def body(core_ref, own_ref, other_ref, out):
        for which in range(2):

            @pl.when(core_ref[0] == which)
            def _(which=which):
                low, high = (own_ref, other_ref) if which == 0 else (other_ref, own_ref)
                out[:OWN] = low[...]
                out[OWN:] = high[HDIM:]

    block = pl.BlockSpec((OWN, length), lambda i, c: (i, 0))
    return pl.pallas_call(
        body,
        grid_spec=pltpu.PrefetchScalarGridSpec(
            num_scalar_prefetch=1,
            grid=(3,),
            in_specs=[block, block],
            out_specs=pl.BlockSpec((rows, length), lambda i, c: (i, 0)),
        ),
        out_shape=jax.ShapeDtypeStruct((3 * rows, length), BF16),
        compiler_params=pltpu.CompilerParams(vmem_limit_bytes=56 * 2**20),
        cost_estimate=cost(0, 12 * rows * length),
        name="join_heads",
    )(core, own, other)


def product_parts(order, pairs, cut, wait):
    many = len(pairs)
    lefts = [side_of(left) for left, _ in pairs]
    rights = [side_of(right) for _, right in pairs]
    count = lefts[0][0].shape[0] // 4
    depth = sum(piece.shape[1] for piece in lefts[0])
    columns = rights[0][0].shape[0]
    rest = columns - cut
    filled = to_tiles(rest)
    starts = [0]
    for sides in lefts + rights:
        starts.append(starts[-1] + len(sides))

    def body(order_ref, *refs):
        send_x, send_y, keep_x, keep_y = refs[starts[-1] + len(wait) :]
        step = pl.program_id(0)
        targets = ((send_x, send_y), (send_x, keep_y), (keep_x, send_y), (keep_x, keep_y))
        for pair in range(many):

            @pl.when(step // 4 == pair)
            def _(pair=pair):
                left = refs[starts[pair] : starts[pair + 1]]
                right = refs[starts[many + pair] : starts[many + pair + 1]]
                value = side_product(left, right).astype(BF16)
                for at, (along_x, along_y) in enumerate(targets):

                    @pl.when(step % 4 == at)
                    def _(along_x=along_x, along_y=along_y):
                        along_x[...] = value[:, :cut]
                        along_y[:, :rest] = value[:, cut:]
                        if filled > rest:
                            along_y[:, rest:] = jnp.zeros((count, filled - rest), BF16)

    def left_spec(pair, piece):
        return pl.BlockSpec(
            (count, piece.shape[1]), lambda i, o: (o[jnp.clip(i - 4 * pair, 0, 3)], 0)
        )

    def out_spec(size, second):
        return pl.BlockSpec(
            (count, size), lambda i, o: (jnp.where(i % 4 >= second, many, 0) + i // 4, 0)
        )

    return pl.pallas_call(
        body,
        grid_spec=pltpu.PrefetchScalarGridSpec(
            num_scalar_prefetch=1,
            grid=(4 * many,),
            in_specs=[left_spec(pair, piece) for pair in range(many) for piece in lefts[pair]]
            + [
                pl.BlockSpec(piece.shape, lambda i, o: (0, 0), pipeline_mode=pl.Buffered(1))
                for right in rights
                for piece in right
            ]
            + [pl.BlockSpec(memory_space=pl.ANY)] * len(wait),
            out_specs=[
                out_spec(cut, 1),
                out_spec(filled, 2),
                out_spec(cut, 3),
                out_spec(filled, 3),
            ],
        ),
        out_shape=[
            jax.ShapeDtypeStruct((2 * many * count, size), BF16)
            for size in (cut, filled, cut, filled)
        ],
        compiler_params=pltpu.CompilerParams(vmem_limit_bytes=56 * 2**20),
        cost_estimate=cost(8 * many * count * depth * columns, 8 * many * count * (depth + columns)),
        name="product_parts",
    )(order, *[piece for sides in lefts + rights for piece in sides], *wait)


def side_of(side):
    return list(side) if isinstance(side, (list, tuple)) else [side]


def side_product(left, right):
    if len(left) == len(right) == 1:
        return dot(left[0][...], right[0][...], 1, 1)
    total = None
    size = left[0].shape[1] if len(left) > 1 else right[0].shape[1]
    for at in range(max(len(left), len(right))):
        here = slice(at * size, (at + 1) * size)
        one = left[at][...] if len(left) > 1 else left[0][:, here]
        two = right[at][...] if len(right) > 1 else right[0][:, here]
        value = dot(one, two, 1, 1)
        total = value if total is None else total + value
    return total


def to_tiles(count):
    return -(-count // 128) * 128


def fold(keep_x, came_x, last_x, keep_y, came_y, last_y, columns):
    rows, cut = last_x.shape
    filled = last_y.shape[1]
    rest = columns - cut
    block = 400
    steps = rows // block

    def body(*refs):
        out = refs[6]
        for first, begin, size in ((0, 0, cut), (3, cut, rest)):
            value = refs[first][:, :size].astype(F32) + refs[first + 1][:, :size].astype(F32)
            value = value + refs[first + 2][:, :size].astype(F32)
            out[:, begin : begin + size] = value.astype(BF16)

    def specs(size):
        second = pl.BlockSpec((block, size), lambda i: (steps + i, 0))
        return [second, second, pl.BlockSpec((block, size), lambda i: (i, 0))]

    return pl.pallas_call(
        body,
        grid=(steps,),
        in_specs=specs(cut) + specs(filled),
        out_specs=pl.BlockSpec((block, columns), lambda i: (i, 0)),
        out_shape=jax.ShapeDtypeStruct((rows, columns), BF16),
        compiler_params=pltpu.CompilerParams(vmem_limit_bytes=56 * 2**20),
        cost_estimate=cost(0, 8 * rows * columns),
        name="fold",
    )(keep_x, came_x, last_x, keep_y, came_y, last_y)


def finish_up(quarter, parts):
    rows, width = parts[0].shape

    def body(quarter_ref, *refs):
        for at in range(4):

            @pl.when(pl.program_id(0) == at)
            def _(at=at):
                refs[4][...] = refs[at][...].astype(F32)

    return pl.pallas_call(
        body,
        grid_spec=pltpu.PrefetchScalarGridSpec(
            num_scalar_prefetch=1,
            grid=(4,),
            in_specs=[
                pl.BlockSpec((rows, width), lambda i, q: (0, 0), pipeline_mode=pl.Buffered(1))
            ]
            * 4,
            out_specs=pl.BlockSpec((rows, width), lambda i, q: (q[0] ^ i, 0)),
        ),
        out_shape=jax.ShapeDtypeStruct((4 * rows, width), F32),
        compiler_params=pltpu.CompilerParams(vmem_limit_bytes=56 * 2**20),
        cost_estimate=cost(0, 24 * rows * width),
        name="finish_up",
    )(quarter, *parts)


def finish_down(quarter, parts, shard_count):
    rows, width = parts[0].shape
    strip = width // shard_count
    block = 80 if rows % 80 == 0 else 40
    steps = rows // block

    def body(quarter_ref, *refs):
        for which in range(4):

            @pl.when(quarter_ref[0] == which)
            def _(which=which):
                for shard in range(shard_count):
                    for at in range(4):
                        begin = (4 * shard + at) * strip
                        refs[4][:, begin : begin + strip] = refs[which ^ at][
                            :, shard * strip : (shard + 1) * strip
                        ].astype(F32)

    return pl.pallas_call(
        body,
        grid_spec=pltpu.PrefetchScalarGridSpec(
            num_scalar_prefetch=1,
            grid=(steps,),
            in_specs=[pl.BlockSpec((block, width), lambda i, q: (i, 0))] * 4,
            out_specs=pl.BlockSpec((block, 4 * width), lambda i, q: (i, 0)),
        ),
        out_shape=jax.ShapeDtypeStruct((rows, 4 * width), F32),
        compiler_params=pltpu.CompilerParams(vmem_limit_bytes=56 * 2**20),
        cost_estimate=cost(0, 24 * rows * width),
        name="finish_down",
    )(quarter, *parts)


def finish_sides(core, even, parts):
    rows, width = parts[0].shape
    cut = FIRST_HEAD * HDIM

    def body(core_ref, even_ref, *refs):
        for which in range(2):
            for at in range(2):

                @pl.when((core_ref[0] == which) & (pl.program_id(0) == at))
                def _(which=which, at=at):
                    own, other = refs[at], refs[2 + at]
                    low, high = (own, other) if which == 0 else (other, own)
                    refs[4][:, :cut] = low[:, :cut].astype(F32)
                    refs[4][:, cut:] = high[:, :OWN].astype(F32)

    return pl.pallas_call(
        body,
        grid_spec=pltpu.PrefetchScalarGridSpec(
            num_scalar_prefetch=2,
            grid=(2,),
            in_specs=[
                pl.BlockSpec((rows, width), lambda i, c, e: (0, 0), pipeline_mode=pl.Buffered(1))
            ]
            * 4,
            out_specs=pl.BlockSpec((rows, cut + OWN), lambda i, c, e: (e[0] ^ i, 0)),
        ),
        out_shape=jax.ShapeDtypeStruct((2 * rows, cut + OWN), F32),
        compiler_params=pltpu.CompilerParams(vmem_limit_bytes=56 * 2**20),
        cost_estimate=cost(0, 16 * rows * width),
        name="finish_sides",
    )(core, even, *parts)


def to_sixteen(count):
    return -(-count // 16) * 16


class Moves:
    def __init__(self, shard_count, replica_count):
        self.shard_count = shard_count
        self.replica_count = replica_count
        self.shard = lax.axis_index("shard")
        replica = lax.axis_index("replica")
        self.core = replica % 2
        self.column = replica // 2
        self.square = shard_count == 4 and replica_count == 8
        self.core_ref = self.core.astype(jnp.int32)[None]
        me = self.shard
        self.places = jnp.stack([me, me ^ 1, me ^ 2, me ^ 3]).astype(jnp.int32)
        self.order = jnp.stack([me ^ 3, me ^ 1, me ^ 2, me]).astype(jnp.int32)

    def move(self, array, route):
        pairs, stays = [], []
        for shard in range(self.shard_count):
            for column in range(self.replica_count // 2):
                for core in range(2):
                    target = route(shard, column, core)
                    if target == (shard, column, core):
                        stays.append((shard, core))
                    elif target is not None:
                        to_shard, to_column, to_core = target
                        pairs.append(
                            (
                                shard * self.replica_count + 2 * column + core,
                                to_shard * self.replica_count + 2 * to_column + to_core,
                            )
                        )
        came = lax.ppermute(array, AXES, pairs)
        if not stays:
            return came
        table = [(s, c) in stays for s in range(self.shard_count) for c in range(2)]
        return jnp.where(jnp.asarray(table)[2 * self.shard + self.core], array, came)

    def over_x(self, array):
        return self.move(array, lambda s, z, c: (s ^ 1, z, c))

    def over_y(self, array):
        return self.move(array, lambda s, z, c: (s ^ 2, z, c))

    def over_z(self, array, step):
        return self.move(array, lambda s, z, c: (s, z ^ step, c))

    def over_core(self, array):
        return self.move(array, lambda s, z, c: (s, z, 1 - c))

    def gather_near(self, piece):
        if not self.square:
            return (piece,)
        return piece, self.over_x(piece), self.over_y(piece)

    def gather_far(self, near):
        if not self.square:
            return ()
        count = near[0].shape[0]
        rows = to_sixteen(count // 2)
        return self.over_x(near[2][:rows]), self.over_y(near[1][rows:])

    def lay(self, near, far, parts=1):
        if self.square:
            return lay(self.places, near, far, parts)
        size = near[0].shape[0] // parts
        return [
            lax.all_gather(near[0][at * size : (at + 1) * size], "shard", axis=0, tiled=True)
            for at in range(parts)
        ]

    def scatter(self, pairs, cut, columns, wait=()):
        if not self.square:
            sums = []
            for left, right in pairs:
                left = jnp.concatenate(side_of(left), axis=1)
                right = jnp.concatenate(side_of(right), axis=1)
                value = product(left, right, "nt", 400)
                sums.append(lax.psum_scatter(value, "shard", scatter_dimension=0, tiled=True))
            sums = jnp.concatenate(sums, axis=0)
            return sums, [], [], []
        send_x, send_y, keep_x, keep_y = product_parts(self.order, pairs, cut, wait)
        half = send_x.shape[0] // 2
        came_x, came_y = self.over_x(send_x), self.over_y(send_y)
        last_x = self.over_y(keep_x[:half] + came_x[:half])
        last_y = self.over_x(keep_y[:half] + came_y[:half])
        folded = fold(keep_x, came_x, last_x, keep_y, came_y, last_y, columns)
        return folded, [send_x], [came_x, came_y], [last_x, last_y]

    def total(self, array):
        if not self.square:
            groups = [
                [2 * column + core for column in range(self.replica_count // 2)]
                for core in range(2)
            ]
            return (lax.psum(array, "replica", axis_index_groups=groups),)
        rows = array.shape[0] // 2
        even = self.column % 2
        keep = lax.dynamic_slice_in_dim(array, even * rows, rows, 0)
        send = lax.dynamic_slice_in_dim(array, (1 - even) * rows, rows, 0)
        pair = keep + self.over_z(send, 1)
        full = pair + self.over_z(pair, 2)
        return full, self.over_z(full, 1)

    def sides(self, sums):
        if self.square:
            parts = list(sums) + [self.over_core(half) for half in sums]
            return finish_sides(self.core_ref, (self.column % 2).astype(jnp.int32)[None], parts)
        own = sums[0]
        other = self.over_core(own)
        first = self.core == 0
        low, high = jnp.where(first, own, other), jnp.where(first, other, own)
        return jnp.concatenate([low[:, : FIRST_HEAD * HDIM], high[:, :OWN]], axis=1).astype(F32)

    def total_alike(self, array):
        if not self.square:
            groups = [
                [2 * column + core for column in range(even, self.replica_count // 2, 2)]
                for even in range(2)
                for core in range(2)
            ]
            return lax.psum(array, "replica", axis_index_groups=groups)
        return array + self.over_z(array, 2)

    def total_small(self, array):
        if not self.square:
            return lax.psum(array, AXES)
        array = array + self.over_core(array)
        array = array + self.over_x(array)
        array = array + self.over_y(array)
        array = array + self.over_z(array, 1)
        return array + self.over_z(array, 2)

    def owners(self, step, seqs):
        return lambda s, z, c: (seqs * c + (s + step) % seqs, z, s // seqs)

    def to_chips(self, local, turn):
        seqs, _, count = local.shape
        came = []
        for step in range(seqs):
            at = (self.shard + step) % seqs + turn
            sent = lax.dynamic_index_in_dim(local, at, 0, keepdims=False)
            came.append(self.move(sent, self.owners(step, seqs)))
        at = self.shard % seqs
        if seqs == 2:
            first = at == 0
            return jnp.concatenate(
                [jnp.where(first, came[0], came[1]), jnp.where(first, came[1], came[0])], axis=1
            )
        ring = jnp.concatenate((came[::-1] * 2)[: 2 * seqs - 1], axis=1)
        return lax.dynamic_slice_in_dim(ring, (seqs - 1 - at) * count, seqs * count, 1)

    def from_chips(self, half, seqs):
        count = half.shape[1] // seqs
        at = self.shard % seqs
        outs = []
        for step in range(seqs):
            route = self.owners(step, seqs)
            back = {}
            for s in range(self.shard_count):
                for z in range(self.replica_count // 2):
                    for c in range(2):
                        back[route(s, z, c)] = (s, z, c)
            sent = lax.dynamic_slice_in_dim(half, ((at - step) % seqs) * count, count, 1)
            outs.append(self.move(sent, lambda s, z, c: back[(s, z, c)]))
        if seqs == 2:
            first = at == 0
            return jnp.stack(
                [jnp.where(first, outs[0], outs[1]), jnp.where(first, outs[1], outs[0])]
            )
        stacked = jnp.stack(outs)
        doubled = jnp.concatenate([stacked, stacked[: seqs - 1]], axis=0)
        return lax.dynamic_slice_in_dim(doubled, (seqs - at) % seqs, seqs, 0)

    def both(self, half):
        other = self.over_core(half)
        first = self.core == 0
        return jnp.concatenate(
            [jnp.where(first, half, other), jnp.where(first, other, half)], axis=1
        )

    def spread(self, half):
        across = self.over_z(half, 1)
        return [half, across, self.over_core(half), self.over_core(across)]

    def collect(self, here, there):
        half = here.shape[1] // 2
        came = self.over_core(there)
        across = self.over_z(here[:, half:] + came[:, half:], 1)
        return here[:, :half].astype(F32) + came[:, :half].astype(F32) + across.astype(F32)


def shards(
    shard_count,
    replica_count,
    hidden_in,
    out_grad,
    segments,
    ln1_gain,
    ln1_bias,
    qkv_weight,
    q_bias,
    v_bias,
    output_projection_weight,
    out_bias,
    ln2_gain,
    ln2_bias,
    up_weight,
    up_bias,
    down_weight,
    down_bias,
):
    moves = Moves(shard_count, replica_count)
    core = moves.core
    quarter = 2 * (moves.column % 2) + core
    seqs = hidden_in.shape[1]
    width = hidden_in.shape[2]
    length = segments.shape[0]
    half_len = length // 2
    ff = up_bias.shape[0]
    strip = ff // shard_count // 4
    first_row = core * FIRST_HEAD * HDIM
    rows_of = functools.partial(lax.dynamic_slice_in_dim, slice_size=OWN, axis=0)
    half_of = functools.partial(lax.dynamic_slice_in_dim, slice_size=half_len, axis=1)
    mine, theirs = core * half_len, (1 - core) * half_len

    def column(vector):
        return vector[:, None]

    def after(*arrays):
        return sum(jnp.isnan(array[0, 0]).astype(jnp.int32) for array in arrays)

    qkv_count = qkv_weight.shape[0]
    qkv_rows = to_sixteen(qkv_count // 2)
    qkv_over = 2 * qkv_rows - qkv_count
    qkv_near = moves.gather_near(
        lax.dynamic_slice_in_dim(qkv_weight, core * (qkv_count - qkv_rows), qkv_rows, 0)
    )
    turn = after(*qkv_near[1:]) if moves.square else 0
    tokens_half = moves.to_chips(hidden_in.transpose(1, 2, 0), turn)
    qkv_far = moves.gather_far(qkv_near)
    turn = after(*qkv_far) if moves.square else 0
    twice = (core == 1) & (jnp.arange(OWN) < HDIM)
    out_near = moves.gather_near(
        jnp.where(
            twice[None, :],
            0,
            lax.dynamic_slice_in_dim(output_projection_weight, first_row + turn, OWN, 1),
        ).astype(BF16)
    )
    grad_half = moves.to_chips(out_grad.transpose(1, 2, 0), turn)
    ff_near = moves.gather_near(
        jnp.concatenate(
            [
                lax.dynamic_slice_in_dim(up_weight, quarter * strip + turn, strip, 0),
                jnp.concatenate(
                    [
                        lax.dynamic_slice_in_dim(
                            down_weight, (4 * shard + quarter) * strip, strip, 1
                        )
                        for shard in range(shard_count)
                    ],
                    axis=1,
                ),
            ],
            axis=0,
        )
    )
    out_far = moves.gather_far(out_near)
    (w_out,) = moves.lay(out_near, out_far)
    ff_far = moves.gather_far(ff_near)
    w_up, w_down = moves.lay(ff_near, ff_far, 2)
    if moves.square:
        qkv_own = list(qkv_near) + list(qkv_far)
        qkv_other = [moves.over_core(piece) for piece in qkv_own]
        w_qkv = lay_heads(moves.core_ref, moves.places, qkv_own, qkv_other, qkv_count)
    else:
        (qkv_half,) = moves.lay(qkv_near, qkv_far)
        qkv_other = moves.over_core(qkv_half)
        low = jnp.where(core == 0, qkv_half, qkv_other)
        high = jnp.where(core == 0, qkv_other, qkv_half)
        qkv_full = jnp.concatenate(
            [
                block[shard * qkv_rows + skip : (shard + 1) * qkv_rows]
                for shard in range(shard_count)
                for block, skip in ((low, 0), (high, qkv_over))
            ],
            axis=0,
        )
        w_qkv = jnp.concatenate(
            [rows_of(qkv_full, part * width + first_row) for part in range(3)], axis=0
        )
    up_bias_own = lax.dynamic_index_in_dim(
        up_bias.reshape(shard_count, 4, strip), quarter, 1, keepdims=False
    ).reshape(-1)
    seg_pair = jnp.stack([segments, moves.over_core(segments)])
    home = moves.shard // seqs
    seg = lax.dynamic_index_in_dim(
        lax.dynamic_index_in_dim(seg_pair, (home != core).astype(jnp.int32), 0, keepdims=False),
        moves.shard % seqs,
        1,
        keepdims=False,
    )

    tokens = tokens_half.astype(F32)
    unit_one, scale_one = norm_parts(tokens)
    normed = moves.both((unit_one * column(ln1_gain) + column(ln1_bias)).astype(BF16))
    zeros = jnp.zeros((OWN,), F32)
    joined_bias = jnp.concatenate([rows_of(q_bias, first_row), zeros, rows_of(v_bias, first_row)])
    row_scale = jnp.where(jnp.arange(3 * OWN) < OWN, 0.125, 1.0).astype(F32)
    joined = product(
        w_qkv,
        normed,
        "nn",
        416,
        lambda value, at, bias, scale: (
            (value + bias[...]).astype(BF16).astype(F32) * scale[...],
        ),
        (column(joined_bias), column(row_scale)),
        name="project_qkv",
    )
    mixed, lse = attention(seg, joined, [*out_near[1:], grad_half])
    grad_out = moves.spread(grad_half)
    branch = product(
        w_out, mixed, "nn", 400, name="project_out", wait=[*ff_near[1:], grad_out[1]]
    )
    branch_half = half_of(branch, mine).astype(F32)
    branch_half = branch_half + moves.over_core(half_of(branch, theirs)).astype(F32)
    middle = tokens + branch_half + column(out_bias)
    unit_two, scale_two = norm_parts(middle)
    normed_two = moves.spread((unit_two * column(ln2_gain) + column(ln2_bias)).astype(BF16))
    activ, slope = product(
        w_up,
        normed_two,
        "nn",
        320,
        lambda value, at, bias: gelu_pair(value + bias[...]),
        (column(up_bias_own),),
        ((None, BF16), (None, BF16)),
        name="project_up",
        wait=grad_out,
    )

    ff_cut = 896 if width == 1600 else width // 256 * 128
    down_part, down_made, down_first, down_last = moves.scatter(
        [(grad_out, activ)], ff_cut, width
    )

    def through_gelu(value, at, slope_ref):
        size = value.shape[1]
        slope_here = slope_ref[:, at * size : (at + 1) * size].astype(F32)
        grad = (value * slope_here).astype(BF16)
        return grad, lane_sums(grad.astype(F32))

    def in_halves(value, at):
        half = value.shape[1] // 2
        return value[:, :half], value[:, half:]

    grad_pre, grad_pre_sums = product(
        w_down,
        grad_out,
        "tn",
        256,
        through_gelu,
        (slope,),
        ((None, BF16), (512, F32)),
        name="back_down",
        wait=down_made,
    )
    halves = ((length, BF16), (length, BF16))
    grad_norm_two = moves.collect(
        *product(w_up, grad_pre, "tn", 256, in_halves, (), halves, name="back_up")
    )
    up_part, up_made, up_first, up_last = moves.scatter([(grad_pre, normed_two)], ff_cut, width)
    down_here, down_there = product(
        w_down, activ, "nn", 320, in_halves, (), halves, name="project_down", wait=up_made
    )
    down_half = moves.collect(down_here, down_there)
    grad_out_f = grad_half.astype(F32)
    grad_middle = grad_out_f + norm_back(grad_norm_two, unit_two, scale_two, column(ln2_gain))
    grad_branch_half = grad_middle.astype(BF16)
    grad_branch = moves.both(grad_branch_half)
    grad_mixed = product(
        w_out, grad_branch, "tn", OWN, name="back_out", wait=[down_here, *down_first, *down_last]
    )
    padded = to_tiles(OWN)
    out_part, out_made, out_first, out_last = moves.scatter([(grad_branch, mixed)], 512, padded)
    down_sum = moves.total_alike(down_part)
    up_sum = moves.total_alike(up_part)
    out_sum = moves.total(out_part)
    result = moves.from_chips((middle + down_half + column(down_bias)).astype(BF16), seqs)

    grad_own = attention_back(
        seg, joined, mixed, grad_mixed, lse, [*out_made, *up_first]
    ).reshape(3 * OWN, length)
    grad_other = moves.over_core(grad_own)
    grad_norm_one = product(
        w_qkv, grad_own, "tn", 256, name="back_qkv", wait=[*out_first, *up_last]
    )
    if moves.square:
        grad_joined = join_heads(moves.core_ref, grad_own, grad_other)
    else:
        low = jnp.where(core == 0, grad_own, grad_other)
        high = jnp.where(core == 0, grad_other, grad_own)
        grad_joined = jnp.concatenate(
            [
                piece
                for part in range(3)
                for piece in (
                    low[part * OWN : (part + 1) * OWN],
                    high[part * OWN + HDIM : (part + 1) * OWN],
                )
            ],
            axis=0,
        )
    qkv_part, _, _, _ = moves.scatter(
        [(grad_joined, rows_of(normed, first_row))], 512, padded, [*out_last]
    )
    qkv_sum = moves.total(qkv_part)
    grad_norm_one = half_of(grad_norm_one, mine).astype(F32) + moves.over_core(
        half_of(grad_norm_one, theirs)
    ).astype(F32)
    input_half = grad_middle + norm_back(grad_norm_one, unit_one, scale_one, column(ln1_gain))
    input_grad = moves.from_chips(input_half.astype(BF16), seqs).astype(F32)

    up_bias_grad = jnp.sum(grad_pre_sums, axis=1).reshape(shard_count, 1, strip)
    up_bias_grad = up_bias_grad * (jnp.arange(4)[None, :, None] == quarter).astype(F32)
    head_sums = jnp.sum(grad_own.astype(F32), axis=1).reshape(3, OWN)
    bias_sums = lax.dynamic_update_slice(
        jnp.zeros((3, width), F32), head_sums, (jnp.int32(0), first_row)
    )
    small = moves.total_small(
        jnp.concatenate(
            [
                up_bias_grad.reshape(-1),
                jnp.sum(grad_norm_two * unit_two, axis=1),
                jnp.sum(grad_norm_two, axis=1),
                jnp.sum(grad_out_f, axis=1),
                jnp.sum(grad_branch_half.astype(F32), axis=1),
                jnp.sum(grad_norm_one * unit_one, axis=1),
                jnp.sum(grad_norm_one, axis=1),
                bias_sums[0],
                bias_sums[2],
            ]
        ).reshape(-1, 128)
    ).reshape(-1)
    up_bias_grad, rest = small[:ff], small[ff:]
    (
        ln2_gain_grad,
        ln2_bias_grad,
        down_bias_grad,
        out_bias_grad,
        ln1_gain_grad,
        ln1_bias_grad,
        q_bias_grad,
        v_bias_grad,
    ) = rest.reshape(8, width)

    def quarters(own):
        across = moves.over_z(own, 1)
        return [own, moves.over_core(own), across, moves.over_core(across)]

    quarter_ref = quarter.astype(jnp.int32)[None]
    down_total = finish_down(quarter_ref, quarters(down_sum), shard_count)
    up_total = finish_up(quarter_ref, quarters(up_sum))

    return (
        result.transpose(2, 0, 1),
        input_grad.transpose(2, 0, 1),
        ln1_gain_grad,
        ln1_bias_grad,
        moves.sides(qkv_sum),
        q_bias_grad,
        v_bias_grad,
        moves.sides(out_sum),
        out_bias_grad,
        ln2_gain_grad,
        ln2_bias_grad,
        up_total,
        up_bias_grad,
        down_total,
        down_bias_grad,
    )


def solution(mesh):
    rows = P("shard", None)
    tokens = P("shard", "replica", None)
    in_specs = (
        tokens,
        tokens,
        P(None, "replica"),
        P(),
        P(),
        rows,
        P(),
        P(),
        rows,
        P(),
        P(),
        P(),
        rows,
        P(),
        rows,
        P(),
    )
    out_specs = (
        tokens,
        tokens,
        P(),
        P(),
        rows,
        P(),
        P(),
        rows,
        P(),
        P(),
        P(),
        rows,
        P(),
        rows,
        P(),
    )
    body = functools.partial(shards, mesh.shape["shard"], mesh.shape["replica"])
    return jax.shard_map(body, mesh=mesh, in_specs=in_specs, out_specs=out_specs, check_vma=False)
```

time: 1290 us -> 958 us (0.74)
  Pallas kernels: 54.3 us -> 316 us
  local copies, waits for them, and re-layouts: 264 us -> 55.6 us
  matrix products: 185 us -> 0 us
  other arithmetic: 165 us -> 77.3 us
  starting transfers between devices: 128 us -> 78.8 us
  waiting for transfers between devices: 460 us -> 416 us
    pallas_call x0 -> x24, Pallas kernels: none -> 260 us  [the longest x8 123 us: product(): pl.pallas_call(body, grid=(pl.cdiv(m, block),), in_specs=[left_spec] + [p...]
    dot_general x12 -> x0, matrix products: 185 us -> none  [dot(): lax.dot_general(left, right, (((left_dim,), (right_dim,)), ((), ())), pre...]
    psum x1 -> x0, waiting for transfers between devices: 88.9 us -> none  [shards(): lax.psum(jnp.concatenate([jnp.sum(grad_norm_one * unit_half, axis=0), jnp...]
    reshape x8 -> x2, local copies, waits for them, and re-layouts: 65.9 us -> 1.54 us  [the longest x1 1.46 us: shards(): up_bias.reshape(shard_count, 4, strip)]
    ppermute x72 -> x80, starting transfers between devices: 128 us -> 78.8 us  [move(): came = lax.ppermute(array, AXES, pairs)]
    dynamic_update_slice x20 -> x1, local copies, waits for them, and re-layouts: 47.3 us -> 0.26 us  [shards(): lax.dynamic_update_slice(jnp.zeros((3, width), F32), head_sums, (jnp.int3...]
    ppermute x72 -> x80, waiting for transfers between devices: 371 us -> 416 us  [move(): came = lax.ppermute(array, AXES, pairs)]
    select_n x12 -> x4, other arithmetic: 44.7 us -> 7.67 us  [the longest x2 4.16 us: to_chips(): jnp.where(first, came[0], came[1])]
  transfers between devices with their start and end apart: 73 -> 80, of which waited for: 21 -> 23; matrix products, arithmetic and copies ran while one was open for 39% -> 11% of each run, Pallas kernels for 4% -> 20%
where the time goes in v2:
time: 958 us; the launch traced here: 951 us
  waiting for transfers between devices  416 us (43%)
  Pallas kernels  316 us (33%)
  starting transfers between devices  78.8 us (8%)
  other arithmetic  77.3 us (8%)
  local copies, waits for them, and re-layouts  55.6 us (6%)
    ppermute x80, waiting for transfers between devices, move(): came = lax.ppermute(array, AXES, pairs)  416 us
    pallas_call x8, Pallas kernels, product(): pl.pallas_call(body, grid=(pl.cdiv(m, block),), in_specs=[left_spec] + [p...  123 us
    ppermute x80, starting transfers between devices, move(): came = lax.ppermute(array, AXES, pairs)  78.8 us
    pallas_call x4, Pallas kernels, product_parts(): pl.pallas_call(body, grid_spec=pltpu.PrefetchScalarGridSpec(num_scalar_pr...  64.8 us
    pallas_call x1, Pallas kernels, attention_back(): pl.pallas_call(backward_kernel, grid=(OWN_HEADS,), in_specs=[whole_spec((...  29.4 us
    pallas_call x1, Pallas kernels, attention(): pl.pallas_call(forward_kernel, grid=(OWN_HEADS,), in_specs=[whole_spec((1...  26.5 us
  transfers between devices with their start and end apart: 80, of which 23 were waited for; matrix products, arithmetic and copies ran while one was open for 11% of the time, Pallas kernels for 20%

profile of v2, /device:TPU:1, one launch (start us, length us, event | category | flops | bytes accessed | tf_op | source)
XLA Modules:
  0.0 951.3 jit_solution(16335232656293661467)
XLA Ops:
  7.1 42.9 %collective-permute-done.1.refs_2_ = bf16[608,1600]{1,0:T(8,128)(2,1)} collective-permute-done((bf16[608,1600]{1,0:T(8,128)(2,1)}, bf16[608,1600]{1,0:T(8,128)(2,1)}, u32[]{:S(2)}, u32[]{:S(2)}) %collective-permute-start.1) | collective-permute-done | bytes 1945632 | tf_op jit(solution)/shard_map/ppermute | solution.py:632
  129.3 14.0 %collective-permute-done.18 = bf16[1600,256]{1,0:T(8,128)(2,1)S(1)} collective-permute-done((bf16[1600,256]{1,0:T(8,128)(2,1)S(1)}, bf16[1600,256]{1,0:T(8,128)(2,1)S(1)}, u32[]{:S(2)}, u32[]{:S(2)}) %collective-permute-start.18) | collective-permute-done | bytes 819232 | tf_op jit(solution)/shard_map/ppermute | solution.py:632
  181.5 14.1 %project_qkv.1.q_ref.k_ref.v_ref = bf16[2496,1024]{1,0:T(8,128)(2,1)} custom-call(bf16[2496,1600]{1,0:T(8,128)(2,1)} %lay_heads.1.left_ref, bf16[1600,1024]{1,0:T(8,128)(2,1)} %pad_maximum_fusion.refs_0_, f32[2496,1]{1,0:T(8,128)} %broadcast_in_dim.68.refs_1_, f32[2496,1]{1,0:T(8,128)} %fusion.20.refs_2_), custom_call_target="tpu_custom_call" | custom-call | flops 65431142400 | bytes 131006464 | tf_op jit(solution)/shard_map/project_qkv/pallas_call | solution.py:218
  198.1 26.5 %attention_forward.1 = (bf16[832,1024]{1,0:T(8,128)(2,1)S(1)}, f32[13,1,1024]{2,1,0:T(1,128)S(1)}) custom-call(s32[1,1024]{1,0:T(1,128)S(1)} %bitcast.50, s32[1024,1]{1,0:T(8,128)S(1)} %copy.36.seg_col, bf16[2496,1024]{1,0:T(8,128)(2,1)S(1)} %copy-done.9, bf16[2496,1024]{1,0:T(8,128)(2,1)S(1)} %copy-done.9, bf16[2496,1024]{1,0:T(8,128)(2,1)S(1)} %copy-done.9, ...), custom_call_target="tpu_custom_call" | custom-call | flops 111669149696 | bytes 54525952 | tf_op jit(solution)/shard_map/attention_forward/pallas_call | solution.py:141
  250.5 32.7 %collective-permute-done.25.refs_1_.refs_2_ = bf16[1600,512]{1,0:T(8,128)(2,1)} collective-permute-done((bf16[1600,512]{1,0:T(8,128)(2,1)S(1)}, bf16[1600,512]{1,0:T(8,128)(2,1)}, u32[]{:S(2)}, u32[]{:S(2)}) %collective-permute-start.25) | collective-permute-done | bytes 1638432 | tf_op jit(solution)/shard_map/ppermute | solution.py:632
  292.4 25.4 %collective-permute-done.24.refs_4_ = bf16[400,1600]{1,0:T(8,128)(2,1)} collective-permute-done((bf16[400,1600]{1,0:T(8,128)(2,1)S(1)}, bf16[400,1600]{1,0:T(8,128)(2,1)}, u32[]{:S(2)}, u32[]{:S(2)}) %collective-permute-start.24) | collective-permute-done | bytes 1280032 | tf_op jit(solution)/shard_map/ppermute | solution.py:632
  327.1 24.0 %project_up.1 = (bf16[1600,2048]{1,0:T(8,128)(2,1)}, bf16[1600,2048]{1,0:T(8,128)(2,1)}) custom-call(bf16[1600,1600]{1,0:T(8,128)(2,1)} %get-tuple-element.45.left_ref, bf16[1600,512]{1,0:T(8,128)(2,1)} %copy-done.48, bf16[1600,512]{1,0:T(8,128)(2,1)} %collective-permute-done.25.refs_1_.refs_2_, bf16[1600,512]{1,0:T(8,128)(2,1)} %collective-permute-done.26.refs_2_.refs_3_, ...), custom_call_target="tpu_custom_call" | custom-call | flops 83886080000 | bytes 145817600 | tf_op jit(solution)/shard_map/project_up/pallas_call | solution.py:218
  351.1 19.5 %product_parts.4 = (bf16[800,896]{1,0:T(8,128)(2,1)}, bf16[800,768]{1,0:T(8,128)(2,1)}, bf16[800,896]{1,0:T(8,128)(2,1)}, bf16[800,768]{1,0:T(8,128)(2,1)}) custom-call(s32[4]{0:T(128)} %pad_add_fusion.1.order_ref, bf16[1600,512]{1,0:T(8,128)(2,1)} %pad_maximum_fusion.4.refs_2_.refs_5_.refs_0_, ...), custom_call_target="tpu_custom_call" | custom-call | flops 83886080000 | bytes 93388800 | tf_op jit(solution)/shard_map/product_parts/pallas_call | solution.py:423
  370.6 19.6 %back_down.1 = (bf16[1600,2048]{1,0:T(8,128)(2,1)}, f32[1600,512]{1,0:T(8,128)}) custom-call(bf16[1600,1600]{1,0:T(8,128)(2,1)} %get-tuple-element.44.left_ref, bf16[1600,512]{1,0:T(8,128)(2,1)} %pad_maximum_fusion.4.refs_2_.refs_5_.refs_0_, bf16[1600,512]{1,0:T(8,128)(2,1)} %collective-permute-done.21.refs_3_.refs_6_.refs_1_, ...), custom_call_target="tpu_custom_call" | custom-call | flops 83886080000 | bytes 145817600 | tf_op jit(solution)/shard_map/back_down/pallas_call | solution.py:218
  390.2 18.7 %back_up.1 = (bf16[1600,1024]{1,0:T(8,128)(2,1)}, bf16[1600,1024]{1,0:T(8,128)(2,1)}) custom-call(bf16[1600,1600]{1,0:T(8,128)(2,1)} %get-tuple-element.45.left_ref, bf16[1600,2048]{1,0:T(8,128)(2,1)} %get-tuple-element.49.refs_0_), custom_call_target="tpu_custom_call" | custom-call | flops 83886080000 | bytes 145817600 | tf_op jit(solution)/shard_map/back_up/pallas_call | solution.py:218
  409.6 19.4 %product_parts.5 = (bf16[800,896]{1,0:T(8,128)(2,1)}, bf16[800,768]{1,0:T(8,128)(2,1)}, bf16[800,896]{1,0:T(8,128)(2,1)}, bf16[800,768]{1,0:T(8,128)(2,1)}) custom-call(s32[4]{0:T(128)} %pad_add_fusion.1.order_ref, bf16[1600,2048]{1,0:T(8,128)(2,1)} %get-tuple-element.49.refs_0_, bf16[1600,512]{1,0:T(8,128)(2,1)} %copy-done.48, ...), custom_call_target="tpu_custom_call" | custom-call | flops 83886080000 | bytes 93388800 | tf_op jit(solution)/shard_map/product_parts/pallas_call | solution.py:423
  429.0 17.0 %project_down.1 = (bf16[1600,1024]{1,0:T(8,128)(2,1)}, bf16[1600,1024]{1,0:T(8,128)(2,1)}) custom-call(bf16[1600,1600]{1,0:T(8,128)(2,1)} %get-tuple-element.44.left_ref, bf16[1600,2048]{1,0:T(8,128)(2,1)} %get-tuple-element.46.refs_4_.refs_0_, bf16[800,896]{1,0:T(8,128)(2,1)} %get-tuple-element.50.refs_1_), custom_call_target="tpu_custom_call" | custom-call | flops 83886080000 | bytes 145817600 | tf_op jit(solution)/shard_map/project_down/pallas_call | solution.py:218
  453.9 30.8 %collective-permute-done.35 = bf16[1600,512]{1,0:T(8,128)(2,1)S(1)} collective-permute-done((bf16[1600,512]{1,0:T(8,128)(2,1)S(1)}, bf16[1600,512]{1,0:T(8,128)(2,1)S(1)}, u32[]{:S(2)}, u32[]{:S(2)}) %collective-permute-start.35) | collective-permute-done | bytes 1638432 | tf_op jit(solution)/shard_map/ppermute | solution.py:632
  488.9 31.0 %collective-permute-done.31 = bf16[1600,512]{1,0:T(8,128)(2,1)S(1)} collective-permute-done((bf16[1600,512]{1,0:T(8,128)(2,1)S(1)}, bf16[1600,512]{1,0:T(8,128)(2,1)S(1)}, u32[]{:S(2)}, u32[]{:S(2)}) %collective-permute-start.31) | collective-permute-done | bytes 1638432 | tf_op jit(solution)/shard_map/ppermute | solution.py:632
  541.7 30.4 %collective-permute-done.40.refs_5_ = bf16[400,768]{1,0:T(8,128)(2,1)} collective-permute-done((bf16[400,768]{1,0:T(8,128)(2,1)}, bf16[400,768]{1,0:T(8,128)(2,1)}, u32[]{:S(2)}, u32[]{:S(2)}) %collective-permute-start.40) | collective-permute-done | bytes 614432 | tf_op jit(solution)/shard_map/ppermute | solution.py:632
  579.4 29.4 %attention_backward.1 = bf16[3,832,1024]{2,1,0:T(8,128)(2,1)} custom-call(s32[1,1024]{1,0:T(1,128)S(1)} %bitcast.51, s32[1024,1]{1,0:T(8,128)S(1)} %copy.36.seg_col, bf16[2496,1024]{1,0:T(8,128)(2,1)} %project_qkv.1.q_ref.k_ref.v_ref, bf16[2496,1024]{1,0:T(8,128)(2,1)} %project_qkv.1.q_ref.k_ref.v_ref, bf16[2496,1024]{1,0:T(8,128)(2,1)} %project_qkv.1.q_ref.k_ref.v_ref, ...), custom_call_target="tpu_custom_call" | custom-call | flops 279172874240 | bytes 109051904 | tf_op jit(solution)/shard_map/attention_backward/pallas_call | solution.py:163
  613.0 16.6 %collective-permute-done.43.refs_1_ = bf16[800,512]{1,0:T(8,128)(2,1)S(1)} collective-permute-done((bf16[800,512]{1,0:T(8,128)(2,1)S(1)}, bf16[800,512]{1,0:T(8,128)(2,1)S(1)}, u32[]{:S(2)}, u32[]{:S(2)}) %collective-permute-start.43) | collective-permute-done | bytes 819232 | tf_op jit(solution)/shard_map/ppermute | solution.py:632
  664.3 17.3 %product_parts.7 = (bf16[2400,512]{1,0:T(8,128)(2,1)}, bf16[2400,384]{1,0:T(8,128)(2,1)}, bf16[2400,512]{1,0:T(8,128)(2,1)}, bf16[2400,384]{1,0:T(8,128)(2,1)}) custom-call(s32[4]{0:T(128)} %pad_add_fusion.1.order_ref, bf16[4800,1024]{1,0:T(8,128)(2,1)} %join_heads.1.refs_0_, bf16[832,1024]{1,0:T(8,128)(2,1)} %fusion.19.refs_1_, ...), custom_call_target="tpu_custom_call" | custom-call | flops 65431142400 | bytes 142540800 | tf_op jit(solution)/shard_map/product_parts/pallas_call | solution.py:423
  682.8 15.0 %back_qkv.1 = bf16[1600,1024]{1,0:T(8,128)(2,1)} custom-call(bf16[2496,1600]{1,0:T(8,128)(2,1)} %lay_heads.1.left_ref, bf16[2496,1024]{1,0:T(8,128)(2,1)} %bitcast.54, bf16[800,512]{1,0:T(8,128)(2,1)} %copy-done.46, bf16[800,384]{1,0:T(8,128)(2,1)} %copy-done.51, bf16[400,896]{1,0:T(8,128)(2,1)} %copy-done.61, bf16[400,768]{1,0:T(8,128)(2,1)} %copy-done.62), custom_call_target="tpu_custom_call" | custom-call | flops 65431142400 | bytes 131006464 | tf_op jit(solution)/shard_map/back_qkv/pallas_call | solution.py:218
  697.8 37.0 %collective-permute-done.58.refs_1_ = bf16[2400,512]{1,0:T(8,128)(2,1)S(1)} collective-permute-done((bf16[2400,512]{1,0:T(8,128)(2,1)}, bf16[2400,512]{1,0:T(8,128)(2,1)S(1)}, u32[]{:S(2)}, u32[]{:S(2)}) %collective-permute-start.58) | collective-permute-done | bytes 2457632 | tf_op jit(solution)/shard_map/ppermute | solution.py:632
  751.8 14.2 %collective-permute-done.76 = bf16[400,1600]{1,0:T(8,128)(2,1)} collective-permute-done((bf16[400,1600]{1,0:T(8,128)(2,1)}, bf16[400,1600]{1,0:T(8,128)(2,1)}, u32[]{:S(2)}, u32[]{:S(2)}) %collective-permute-start.76) | collective-permute-done | bytes 1280032 | tf_op jit(solution)/shard_map/ppermute | solution.py:632
  786.3 16.0 %collective-permute-done.67 = bf16[200,896]{1,0:T(8,128)(2,1)} collective-permute-done((bf16[200,896]{1,0:T(8,128)(2,1)}, bf16[200,896]{1,0:T(8,128)(2,1)}, u32[]{:S(2)}, u32[]{:S(2)}) %collective-permute-start.67) | collective-permute-done | bytes 358432 | tf_op jit(solution)/shard_map/ppermute | solution.py:632
  810.4 37.3 %collective-permute-done.68 = bf16[200,896]{1,0:T(8,128)(2,1)} collective-permute-done((bf16[200,896]{1,0:T(8,128)(2,1)}, bf16[200,896]{1,0:T(8,128)(2,1)}, u32[]{:S(2)}, u32[]{:S(2)}) %collective-permute-start.68) | collective-permute-done | bytes 358432 | tf_op jit(solution)/shard_map/ppermute | solution.py:632
  872.0 29.3 %collective-permute-done.63 = bf16[600,896]{1,0:T(8,128)(2,1)S(1)} collective-permute-done((bf16[600,896]{1,0:T(8,128)(2,1)S(1)}, bf16[600,896]{1,0:T(8,128)(2,1)S(1)}, u32[]{:S(2)}, u32[]{:S(2)}) %collective-permute-start.63) | collective-permute-done | bytes 1075232 | tf_op jit(solution)/shard_map/ppermute | solution.py:632
  (473 shorter events, 365.6 us)
Async XLA Ops:
  60.6 52.3 %collective-permute-start.11 = (bf16[608,1600]{1,0:T(8,128)(2,1)}, bf16[608,1600]{1,0:T(8,128)(2,1)}, u32[]{:S(2)}, u32[]{:S(2)}) collective-permute-start(bf16[608,1600]{1,0:T(8,128)(2,1)} %constant_dynamic-slice_fusion.13.refs_0_), channel_id=1, source_target_pairs={{0,1},{1,0},{2,3},{3,2},{4,5},{5,4},{6,7},{7,6},{8,9},{9,8},{10,11... | collective-permute-start | bytes 5836808 | tf_op jit(solution)/shard_map/ppermute | solution.py:632
  83.0 68.2 %collective-permute-start.13 = (bf16[608,1600]{1,0:T(8,128)(2,1)}, bf16[608,1600]{1,0:T(8,128)(2,1)}, u32[]{:S(2)}, u32[]{:S(2)}) collective-permute-start(bf16[608,1600]{1,0:T(8,128)(2,1)} %collective-permute-done.1.refs_2_), channel_id=1, source_target_pairs={{0,1},{1,0},{2,3},{3,2},{4,5},{5,4},{6,7},{7,6},{8,9},{9,8},{10,11... | collective-permute-start | bytes 5836808 | tf_op jit(solution)/shard_map/ppermute | solution.py:632
  155.4 70.4 %collective-permute-start.20 = (bf16[800,1600]{1,0:T(8,128)(2,1)}, bf16[800,1600]{1,0:T(8,128)(2,1)}, u32[]{:S(2)}, u32[]{:S(2)}) collective-permute-start(bf16[800,1600]{1,0:T(8,128)(2,1)} %pad_maximum_fusion.2.refs_0_), channel_id=1, source_target_pairs={{0,16},{1,17},{2,18},{3,19},{4,20},{5,21},{6,22},{7,23},{8,24},{9,... | collective-permute-start | bytes 7680008 | tf_op jit(solution)/shard_map/ppermute | solution.py:632
  156.9 68.9 %collective-permute-start.19 = (bf16[800,1600]{1,0:T(8,128)(2,1)}, bf16[800,1600]{1,0:T(8,128)(2,1)}, u32[]{:S(2)}, u32[]{:S(2)}) collective-permute-start(bf16[800,1600]{1,0:T(8,128)(2,1)} %pad_maximum_fusion.2.refs_0_), channel_id=1, source_target_pairs={{0,8},{1,9},{2,10},{3,11},{4,12},{5,13},{6,14},{7,15},{8,0},{9,1},... | collective-permute-start | bytes 7680008 | tf_op jit(solution)/shard_map/ppermute | solution.py:632
  168.6 57.1 %collective-permute-start.21 = (bf16[1600,512]{1,0:T(8,128)(2,1)}, bf16[1600,512]{1,0:T(8,128)(2,1)}, u32[]{:S(2)}, u32[]{:S(2)}) collective-permute-start(bf16[1600,512]{1,0:T(8,128)(2,1)} %pad_maximum_fusion.4.refs_2_.refs_5_.refs_0_), channel_id=1, source_target_pairs={{0,2},{1,3},{2,0},{3,1},{4,6},{5,7},{6,4},{7,5},{8,10},{9,11},{10,... | collective-permute-start | bytes 4915208 | tf_op jit(solution)/shard_map/ppermute | solution.py:632
  249.3 77.8 %collective-permute-start.28 = (bf16[1600,512]{1,0:T(8,128)(2,1)}, bf16[1600,512]{1,0:T(8,128)(2,1)}, u32[]{:S(2)}, u32[]{:S(2)}) collective-permute-start(bf16[1600,512]{1,0:T(8,128)(2,1)} %pad_maximum_fusion.4.refs_2_.refs_5_.refs_0_), channel_id=1, source_target_pairs={{0,1},{1,0},{2,3},{3,2},{4,5},{5,4},{6,7},{7,6},{8,9},{9,8},{10,11... | collective-permute-start | bytes 4915208 | tf_op jit(solution)/shard_map/ppermute | solution.py:632
  250.0 77.1 %collective-permute-start.29 = (bf16[1600,512]{1,0:T(8,128)(2,1)}, bf16[1600,512]{1,0:T(8,128)(2,1)}, u32[]{:S(2)}, u32[]{:S(2)}) collective-permute-start(bf16[1600,512]{1,0:T(8,128)(2,1)} %collective-permute-done.21.refs_3_.refs_6_.refs_1_), channel_id=1, source_target_pairs={{0,1},{1,0},{2,3},{3,2},{4,5},{5,4},{6,7},{7,6},{8,9},{9,8},{10,11... | collective-permute-start | bytes 4915208 | tf_op jit(solution)/shard_map/ppermute | solution.py:632
  250.0 77.1 %collective-permute-start.26 = (bf16[1600,512]{1,0:T(8,128)(2,1)S(1)}, bf16[1600,512]{1,0:T(8,128)(2,1)}, u32[]{:S(2)}, u32[]{:S(2)}) collective-permute-start(bf16[1600,512]{1,0:T(8,128)(2,1)S(1)} %add_convert_fusion.1.refs_0_.refs_1_), channel_id=1, source_target_pairs={{0,1},{1,0},{2,3},{3,2},{4,5},{5,4},{6,7},{7,6},{8,9},{9,8},{10,11... | collective-permute-start | bytes 4915208 | tf_op jit(solution)/shard_map/ppermute | solution.py:632
  452.3 67.5 %collective-permute-start.31 = (bf16[1600,512]{1,0:T(8,128)(2,1)S(1)}, bf16[1600,512]{1,0:T(8,128)(2,1)S(1)}, u32[]{:S(2)}, u32[]{:S(2)}) collective-permute-start(bf16[1600,512]{1,0:T(8,128)(2,1)S(1)} %slice_add_fusion.1), channel_id=1, source_target_pairs={{0,2},{1,3},{2,0},{3,1},{4,6},{5,7},{6,4},{7,5},{8,10},{9,11},{10,... | collective-permute-start | bytes 4915208 | tf_op jit(solution)/shard_map/ppermute | solution.py:632
  452.8 75.4 %collective-permute-start.37 = (bf16[800,896]{1,0:T(8,128)(2,1)S(1)}, bf16[800,896]{1,0:T(8,128)(2,1)S(1)}, u32[]{:S(2)}, u32[]{:S(2)}) collective-permute-start(bf16[800,896]{1,0:T(8,128)(2,1)S(1)} %copy-done.100), channel_id=1, source_target_pairs={{0,8},{1,9},{2,10},{3,11},{4,12},{5,13},{6,14},{7,15},{8,0},{9,1},... | collective-permute-start | bytes 4300808 | tf_op jit(solution)/shard_map/ppermute | solution.py:632
  453.8 72.9 %collective-permute-start.38 = (bf16[800,768]{1,0:T(8,128)(2,1)S(1)}, bf16[800,768]{1,0:T(8,128)(2,1)S(1)}, u32[]{:S(2)}, u32[]{:S(2)}) collective-permute-start(bf16[800,768]{1,0:T(8,128)(2,1)S(1)} %copy-done.101), channel_id=1, source_target_pairs={{0,16},{1,17},{2,18},{3,19},{4,20},{5,21},{6,22},{7,23},{8,24},{9,... | collective-permute-start | bytes 3686408 | tf_op jit(solution)/shard_map/ppermute | solution.py:632
  525.6 53.7 %collective-permute-start.41 = (bf16[800,896]{1,0:T(8,128)(2,1)}, bf16[800,896]{1,0:T(8,128)(2,1)S(1)}, u32[]{:S(2)}, u32[]{:S(2)}) collective-permute-start(bf16[800,896]{1,0:T(8,128)(2,1)} %get-tuple-element.50.refs_1_), channel_id=1, source_target_pairs={{0,8},{1,9},{2,10},{3,11},{4,12},{5,13},{6,14},{7,15},{8,0},{9,1},... | collective-permute-start | bytes 4300808 | tf_op jit(solution)/shard_map/ppermute | solution.py:632
  526.7 52.6 %collective-permute-start.42 = (bf16[800,768]{1,0:T(8,128)(2,1)}, bf16[800,768]{1,0:T(8,128)(2,1)S(1)}, u32[]{:S(2)}, u32[]{:S(2)}) collective-permute-start(bf16[800,768]{1,0:T(8,128)(2,1)} %get-tuple-element.60), channel_id=1, source_target_pairs={{0,16},{1,17},{2,18},{3,19},{4,20},{5,21},{6,22},{7,23},{8,24},{9,... | collective-permute-start | bytes 3686408 | tf_op jit(solution)/shard_map/ppermute | solution.py:632
  648.2 100.1 %collective-permute-start.72 = (bf16[400,1600]{1,0:T(8,128)(2,1)}, bf16[400,1600]{1,0:T(8,128)(2,1)}, u32[]{:S(2)}, u32[]{:S(2)}) collective-permute-start(bf16[400,1600]{1,0:T(8,128)(2,1)} %fold.6), channel_id=1, source_target_pairs={{0,4},{1,5},{2,6},{3,7},{4,0},{5,1},{6,2},{7,3},{8,12},{9,13},{10,... | collective-permute-start | bytes 3840008 | tf_op jit(solution)/shard_map/ppermute | solution.py:632
  654.1 112.0 %collective-permute-start.76 = (bf16[400,1600]{1,0:T(8,128)(2,1)}, bf16[400,1600]{1,0:T(8,128)(2,1)}, u32[]{:S(2)}, u32[]{:S(2)}) collective-permute-start(bf16[400,1600]{1,0:T(8,128)(2,1)} %fold.7), channel_id=1, source_target_pairs={{0,4},{1,5},{2,6},{3,7},{4,0},{5,1},{6,2},{7,3},{8,12},{9,13},{10,... | collective-permute-start | bytes 3840008 | tf_op jit(solution)/shard_map/ppermute | solution.py:632
  681.6 55.8 %collective-permute-start.60 = (bf16[2400,384]{1,0:T(8,128)(2,1)}, bf16[2400,384]{1,0:T(8,128)(2,1)}, u32[]{:S(2)}, u32[]{:S(2)}) collective-permute-start(bf16[2400,384]{1,0:T(8,128)(2,1)} %get-tuple-element.70), channel_id=1, source_target_pairs={{0,16},{1,17},{2,18},{3,19},{4,20},{5,21},{6,22},{7,23},{8,24},{9,... | collective-permute-start | bytes 5529608 | tf_op jit(solution)/shard_map/ppermute | solution.py:632
  681.6 53.2 %collective-permute-start.58 = (bf16[2400,512]{1,0:T(8,128)(2,1)}, bf16[2400,512]{1,0:T(8,128)(2,1)S(1)}, u32[]{:S(2)}, u32[]{:S(2)}) collective-permute-start(bf16[2400,512]{1,0:T(8,128)(2,1)} %get-tuple-element.68), channel_id=1, source_target_pairs={{0,8},{1,9},{2,10},{3,11},{4,12},{5,13},{6,14},{7,15},{8,0},{9,1},... | collective-permute-start | bytes 7372808 | tf_op jit(solution)/shard_map/ppermute | solution.py:632
  742.1 62.1 %collective-permute-start.47 = (bf16[1600,512]{1,0:T(8,128)(2,1)}, bf16[1600,512]{1,0:T(8,128)(2,1)S(1)}, u32[]{:S(2)}, u32[]{:S(2)}) collective-permute-start(bf16[1600,512]{1,0:T(8,128)(2,1)} %constant_dynamic-slice_fusion.4), channel_id=1, source_target_pairs={{0,1},{1,0},{2,3},{3,2},{4,5},{5,4},{6,7},{7,6},{8,9},{9,8},{10,11... | collective-permute-start | bytes 4915208 | tf_op jit(solution)/shard_map/ppermute | solution.py:632
  751.4 105.5 %collective-permute-start.74 = (bf16[400,1600]{1,0:T(8,128)(2,1)}, bf16[400,1600]{1,0:T(8,128)(2,1)}, u32[]{:S(2)}, u32[]{:S(2)}) collective-permute-start(bf16[400,1600]{1,0:T(8,128)(2,1)} %add.395.refs_0_), channel_id=1, source_target_pairs={{0,2},{1,3},{2,0},{3,1},{4,6},{5,7},{6,4},{7,5},{8,10},{9,11},{10,... | collective-permute-start | bytes 3840008 | tf_op jit(solution)/shard_map/ppermute | solution.py:632
  766.0 99.3 %collective-permute-start.73 = (bf16[400,1600]{1,0:T(8,128)(2,1)}, bf16[400,1600]{1,0:T(8,128)(2,1)}, u32[]{:S(2)}, u32[]{:S(2)}) collective-permute-start(bf16[400,1600]{1,0:T(8,128)(2,1)} %add.395.refs_0_), channel_id=1, source_target_pairs={{0,1},{1,0},{2,3},{3,2},{4,5},{5,4},{6,7},{7,6},{8,9},{9,8},{10,11... | collective-permute-start | bytes 3840008 | tf_op jit(solution)/shard_map/ppermute | solution.py:632
  781.2 67.3 %collective-permute-start.62 = (bf16[600,896]{1,0:T(8,128)(2,1)}, bf16[600,896]{1,0:T(8,128)(2,1)}, u32[]{:S(2)}, u32[]{:S(2)}) collective-permute-start(bf16[600,896]{1,0:T(8,128)(2,1)} %constant_dynamic-slice_fusion.1), channel_id=1, source_target_pairs={{0,2},{1,3},{2,0},{3,1},{4,6},{5,7},{6,4},{7,5},{8,10},{9,11},{10,... | collective-permute-start | bytes 3225608 | tf_op jit(solution)/shard_map/ppermute | solution.py:632
  802.4 62.4 %collective-permute-start.78 = (bf16[400,1600]{1,0:T(8,128)(2,1)}, bf16[400,1600]{1,0:T(8,128)(2,1)}, u32[]{:S(2)}, u32[]{:S(2)}) collective-permute-start(bf16[400,1600]{1,0:T(8,128)(2,1)} %add.396.refs_0_), channel_id=1, source_target_pairs={{0,2},{1,3},{2,0},{3,1},{4,6},{5,7},{6,4},{7,5},{8,10},{9,11},{10,... | collective-permute-start | bytes 3840008 | tf_op jit(solution)/shard_map/ppermute | solution.py:632
  851.1 50.1 %collective-permute-start.63 = (bf16[600,896]{1,0:T(8,128)(2,1)S(1)}, bf16[600,896]{1,0:T(8,128)(2,1)S(1)}, u32[]{:S(2)}, u32[]{:S(2)}) collective-permute-start(bf16[600,896]{1,0:T(8,128)(2,1)S(1)} %dynamic-slice_add_fusion), channel_id=1, source_target_pairs={{0,4},{1,5},{2,6},{3,7},{4,0},{5,1},{6,2},{7,3},{8,12},{9,13},{10,... | collective-permute-start | bytes 3225608 | tf_op jit(solution)/shard_map/ppermute | solution.py:632
  865.2 48.1 %collective-permute-start.79 = (bf16[400,1600]{1,0:T(8,128)(2,1)}, bf16[400,1600]{1,0:T(8,128)(2,1)S(1)}, u32[]{:S(2)}, u32[]{:S(2)}) collective-permute-start(bf16[400,1600]{1,0:T(8,128)(2,1)} %collective-permute-done.78.refs_2_), channel_id=1, source_target_pairs={{0,1},{1,0},{2,3},{3,2},{4,5},{5,4},{6,7},{7,6},{8,9},{9,8},{10,11... | collective-permute-start | bytes 3840008 | tf_op jit(solution)/shard_map/ppermute | solution.py:632
  (160 other events, 4114.3 us)

commit v3 on v2

--- a/solution.py
+++ b/solution.py
@@ -285,21 +285,27 @@
     )(places, *pieces)
 
 
-def lay_heads(core, places, mine, others, count):
-    rows, width = mine[0].shape
-    over = 2 * rows - count
+def lay_heads(core, places, mine, others, counts, taken, wait):
+    width = mine[0].shape[1]
+    split = mine[3].shape[0]
+    cut = FIRST_HEAD * HDIM
 
     def body(core_ref, places_ref, *refs):
-        heads_ref, block = refs[10:]
+        heads_ref, out_ref, block, out_block = refs[-4:]
         step = pl.program_id(0)
 
-        def halves(refs, begin, size, at, skip):
+        def copy(halves, at, begin, end, target, row):
             if at < 3:
-                block[begin : begin + size - skip] = refs[at][skip:]
-            else:
-                cut = refs[3].shape[0]
-                block[begin : begin + cut - skip] = refs[3][skip:]
-                block[begin + cut - skip : begin + size - skip] = refs[4][...]
+                target[row : row + end - begin] = halves[at][begin:end]
+                return
+            if begin < split:
+                middle = min(end, split)
+                target[row : row + middle - begin] = halves[3][begin:middle]
+            if end > split:
+                middle = max(begin, split)
+                target[row + middle - begin : row + end - begin] = halves[4][
+                    middle - split : end - split
+                ]
 
         for which in range(2):
 
@@ -310,21 +316,28 @@
 
                     @pl.when(step == at)
                     def _(at=at):
-                        halves(low, 0, rows, at, 0)
-                        halves(high, rows, rows, at, over)
-
+                        begin = 0
+                        for target, rows, count in zip((block, out_block), taken, counts):
+                            copy(low, at, begin, begin + rows, target, 0)
+                            over = 2 * rows - count
+                            copy(high, at, begin + over, begin + rows, target, rows)
+                            begin += rows
+
+                out_ref[...] = out_block[:, which * cut : which * cut + OWN]
+                if which == 1:
+                    out_ref[:, :HDIM] = jnp.zeros((counts[1], HDIM), BF16)
                 for shard in range(4):
 
                     @pl.when(places_ref[step] == shard)
                     def _(shard=shard):
                         for part in range(3):
-                            begin = part * width + which * FIRST_HEAD * HDIM
-                            first = max(begin, shard * count)
-                            last = min(begin + OWN, (shard + 1) * count)
+                            begin = part * width + which * cut
+                            first = max(begin, shard * counts[0])
+                            last = min(begin + OWN, (shard + 1) * counts[0])
                             if first < last:
                                 heads_ref[
                                     part * OWN + first - begin : part * OWN + last - begin
-                                ] = block[first - shard * count : last - shard * count]
+                                ] = block[first - shard * counts[0] : last - shard * counts[0]]
 
     pieces = list(mine) + list(others)
     return pl.pallas_call(
@@ -335,17 +348,24 @@
             in_specs=[
                 pl.BlockSpec(piece.shape, lambda i, c, p: (0, 0), pipeline_mode=pl.Buffered(1))
                 for piece in pieces
+            ]
+            + [pl.BlockSpec(memory_space=pl.ANY)] * len(wait),
+            out_specs=[
+                pl.BlockSpec(
+                    (3 * OWN, width), lambda i, c, p: (0, 0), pipeline_mode=pl.Buffered(1)
+                ),
+                pl.BlockSpec((counts[1], OWN), lambda i, c, p: (p[i], 0)),
             ],
-            out_specs=pl.BlockSpec(
-                (3 * OWN, width), lambda i, c, p: (0, 0), pipeline_mode=pl.Buffered(1)
-            ),
-            scratch_shapes=[pltpu.VMEM((count, width), BF16)],
+            scratch_shapes=[pltpu.VMEM((count, width), BF16) for count in counts],
         ),
-        out_shape=jax.ShapeDtypeStruct((3 * OWN, width), BF16),
+        out_shape=[
+            jax.ShapeDtypeStruct((3 * OWN, width), BF16),
+            jax.ShapeDtypeStruct((4 * counts[1], OWN), BF16),
+        ],
         compiler_params=pltpu.CompilerParams(vmem_limit_bytes=56 * 2**20),
-        cost_estimate=cost(0, 16 * count * width),
+        cost_estimate=cost(0, 16 * counts[0] * width),
         name="lay_heads",
-    )(core, places, *pieces)
+    )(core, places, *pieces, *wait)
 
 
 def join_heads(core, own, other):
@@ -599,6 +619,14 @@
     return -(-count // 16) * 16
 
 
+def late(arrays, events):
+    arrays = list(arrays)
+    events = [event for event in events if event is not None]
+    if not events:
+        return arrays
+    return lax.optimization_barrier((*arrays, *events))[: len(arrays)]
+
+
 class Moves:
     def __init__(self, shard_count, replica_count):
         self.shard_count = shard_count
@@ -647,18 +675,6 @@
     def over_core(self, array):
         return self.move(array, lambda s, z, c: (s, z, 1 - c))
 
-    def gather_near(self, piece):
-        if not self.square:
-            return (piece,)
-        return piece, self.over_x(piece), self.over_y(piece)
-
-    def gather_far(self, near):
-        if not self.square:
-            return ()
-        count = near[0].shape[0]
-        rows = to_sixteen(count // 2)
-        return self.over_x(near[2][:rows]), self.over_y(near[1][rows:])
-
     def lay(self, near, far, parts=1):
         if self.square:
             return lay(self.places, near, far, parts)
@@ -668,38 +684,65 @@
             for at in range(parts)
         ]
 
-    def scatter(self, pairs, cut, columns, wait=()):
+    def scatter_first(self, pairs, cut, wait=()):
         if not self.square:
-            sums = []
-            for left, right in pairs:
-                left = jnp.concatenate(side_of(left), axis=1)
-                right = jnp.concatenate(side_of(right), axis=1)
-                value = product(left, right, "nt", 400)
-                sums.append(lax.psum_scatter(value, "shard", scatter_dimension=0, tiled=True))
-            sums = jnp.concatenate(sums, axis=0)
-            return sums, [], [], []
-        send_x, send_y, keep_x, keep_y = product_parts(self.order, pairs, cut, wait)
-        half = send_x.shape[0] // 2
-        came_x, came_y = self.over_x(send_x), self.over_y(send_y)
+            return [
+                product(
+                    jnp.concatenate(side_of(left), axis=1),
+                    jnp.concatenate(side_of(right), axis=1),
+                    "nt",
+                    400,
+                )
+                for left, right in pairs
+            ]
+        return product_parts(self.order, pairs, cut, wait)
+
+    def scatter_near(self, parts, wait=()):
+        if not self.square:
+            return parts, []
+        send_x, send_y = late(parts[:2], wait)
+        return parts, [self.over_x(send_x), self.over_y(send_y)]
+
+    def scatter_far(self, near, wait=()):
+        parts, came = near
+        if not self.square:
+            return near, []
+        keep_x, keep_y = parts[2:]
+        half = keep_x.shape[0] // 2
+        came_x, came_y = late(came, wait)
         last_x = self.over_y(keep_x[:half] + came_x[:half])
         last_y = self.over_x(keep_y[:half] + came_y[:half])
-        folded = fold(keep_x, came_x, last_x, keep_y, came_y, last_y, columns)
-        return folded, [send_x], [came_x, came_y], [last_x, last_y]
-
-    def total(self, array):
+        return near, [last_x, last_y]
+
+    def scatter_last(self, far, columns):
+        (parts, came), last = far
+        if not self.square:
+            sums = [
+                lax.psum_scatter(part, "shard", scatter_dimension=0, tiled=True) for part in parts
+            ]
+            return jnp.concatenate(sums, axis=0)
+        return fold(parts[2], came[0], last[0], parts[3], came[1], last[1], columns)
+
+    def total_pair(self, array):
+        if not self.square:
+            return array
+        rows = array.shape[0] // 2
+        even = self.column % 2
+        keep = lax.dynamic_slice_in_dim(array, even * rows, rows, 0)
+        send = lax.dynamic_slice_in_dim(array, (1 - even) * rows, rows, 0)
+        return keep + self.over_z(send, 1)
+
+    def total_all(self, pair):
         if not self.square:
             groups = [
                 [2 * column + core for column in range(self.replica_count // 2)]
                 for core in range(2)
             ]
-            return (lax.psum(array, "replica", axis_index_groups=groups),)
-        rows = array.shape[0] // 2
-        even = self.column % 2
-        keep = lax.dynamic_slice_in_dim(array, even * rows, rows, 0)
-        send = lax.dynamic_slice_in_dim(array, (1 - even) * rows, rows, 0)
-        pair = keep + self.over_z(send, 1)
-        full = pair + self.over_z(pair, 2)
-        return full, self.over_z(full, 1)
+            return lax.psum(pair, "replica", axis_index_groups=groups)
+        return pair + self.over_z(pair, 2)
+
+    def total_halves(self, full):
+        return (full, self.over_z(full, 1)) if self.square else (full,)
 
     def sides(self, sums):
         if self.square:
@@ -711,7 +754,7 @@
         low, high = jnp.where(first, own, other), jnp.where(first, other, own)
         return jnp.concatenate([low[:, : FIRST_HEAD * HDIM], high[:, :OWN]], axis=1).astype(F32)
 
-    def total_alike(self, array):
+    def alike(self, array):
         if not self.square:
             groups = [
                 [2 * column + core for column in range(even, self.replica_count // 2, 2)]
@@ -719,7 +762,10 @@
                 for core in range(2)
             ]
             return lax.psum(array, "replica", axis_index_groups=groups)
-        return array + self.over_z(array, 2)
+        return self.over_z(array, 2)
+
+    def alike_sum(self, array, came):
+        return array + came if self.square else came
 
     def total_small(self, array):
         if not self.square:
@@ -733,13 +779,18 @@
     def owners(self, step, seqs):
         return lambda s, z, c: (seqs * c + (s + step) % seqs, z, s // seqs)
 
-    def to_chips(self, local, turn):
+    def to_chips(self, local):
         seqs, _, count = local.shape
         came = []
         for step in range(seqs):
-            at = (self.shard + step) % seqs + turn
+            at = (self.shard + step) % seqs
             sent = lax.dynamic_index_in_dim(local, at, 0, keepdims=False)
             came.append(self.move(sent, self.owners(step, seqs)))
+        return came
+
+    def in_half(self, came):
+        seqs = len(came)
+        count = came[0].shape[1]
         at = self.shard % seqs
         if seqs == 2:
             first = at == 0
@@ -771,22 +822,11 @@
         doubled = jnp.concatenate([stacked, stacked[: seqs - 1]], axis=0)
         return lax.dynamic_slice_in_dim(doubled, (seqs - at) % seqs, seqs, 0)
 
-    def both(self, half):
-        other = self.over_core(half)
+    def ordered(self, half, other):
         first = self.core == 0
         return jnp.concatenate(
             [jnp.where(first, half, other), jnp.where(first, other, half)], axis=1
         )
-
-    def spread(self, half):
-        across = self.over_z(half, 1)
-        return [half, across, self.over_core(half), self.over_core(across)]
-
-    def collect(self, here, there):
-        half = here.shape[1] // 2
-        came = self.over_core(there)
-        across = self.over_z(here[:, half:] + came[:, half:], 1)
-        return here[:, :half].astype(F32) + came[:, :half].astype(F32) + across.astype(F32)
 
 
 def shards(
@@ -826,84 +866,105 @@
     def column(vector):
         return vector[:, None]
 
-    def after(*arrays):
-        return sum(jnp.isnan(array[0, 0]).astype(jnp.int32) for array in arrays)
-
-    qkv_count = qkv_weight.shape[0]
-    qkv_rows = to_sixteen(qkv_count // 2)
-    qkv_over = 2 * qkv_rows - qkv_count
-    qkv_near = moves.gather_near(
-        lax.dynamic_slice_in_dim(qkv_weight, core * (qkv_count - qkv_rows), qkv_rows, 0)
-    )
-    turn = after(*qkv_near[1:]) if moves.square else 0
-    tokens_half = moves.to_chips(hidden_in.transpose(1, 2, 0), turn)
-    qkv_far = moves.gather_far(qkv_near)
-    turn = after(*qkv_far) if moves.square else 0
-    twice = (core == 1) & (jnp.arange(OWN) < HDIM)
-    out_near = moves.gather_near(
-        jnp.where(
-            twice[None, :],
-            0,
-            lax.dynamic_slice_in_dim(output_projection_weight, first_row + turn, OWN, 1),
-        ).astype(BF16)
-    )
-    grad_half = moves.to_chips(out_grad.transpose(1, 2, 0), turn)
-    ff_near = moves.gather_near(
-        jnp.concatenate(
-            [
-                lax.dynamic_slice_in_dim(up_weight, quarter * strip + turn, strip, 0),
-                jnp.concatenate(
-                    [
-                        lax.dynamic_slice_in_dim(
-                            down_weight, (4 * shard + quarter) * strip, strip, 1
-                        )
-                        for shard in range(shard_count)
-                    ],
-                    axis=1,
-                ),
-            ],
-            axis=0,
+
+    counts = (qkv_weight.shape[0], output_projection_weight.shape[0])
+    taken = tuple(to_sixteen(count // 2) for count in counts)
+    mine_of = [
+        lax.dynamic_slice_in_dim(weight, core * (count - rows), rows, 0)
+        for weight, count, rows in zip((qkv_weight, output_projection_weight), counts, taken)
+    ]
+    ff_piece = jnp.concatenate(
+        [
+            lax.dynamic_slice_in_dim(up_weight, quarter * strip, strip, 0),
+            jnp.concatenate(
+                [
+                    lax.dynamic_slice_in_dim(down_weight, (4 * shard + quarter) * strip, strip, 1)
+                    for shard in range(shard_count)
+                ],
+                axis=1,
+            ),
+        ],
+        axis=0,
+    )
+    up_bias_own = lax.dynamic_index_in_dim(
+        up_bias.reshape(shard_count, 4, strip), quarter, 1, keepdims=False
+    ).reshape(-1)
+    tokens_came = moves.to_chips(hidden_in.transpose(1, 2, 0))
+    if moves.square:
+        heads_piece = jnp.concatenate(mine_of, axis=0)
+        heads_x, heads_y = moves.over_x(heads_piece), moves.over_y(heads_piece)
+        other_own = moves.over_core(heads_piece)
+        events = [heads_x, heads_y, other_own, *tokens_came, ff_piece]
+
+        heads_x, heads_y, segments_sent, *tokens_came = late(
+            [heads_x, heads_y, segments, *tokens_came], events
         )
-    )
-    out_far = moves.gather_far(out_near)
-    (w_out,) = moves.lay(out_near, out_far)
-    ff_far = moves.gather_far(ff_near)
-    w_up, w_down = moves.lay(ff_near, ff_far, 2)
+        split = to_sixteen(heads_piece.shape[0] // 2)
+        heads_low = moves.over_x(heads_y[:split])
+        heads_high = moves.over_y(heads_x[split:])
+        other_x, other_y = moves.over_core(heads_x), moves.over_core(heads_y)
+        segments_other = moves.over_core(segments_sent)
+        events = [heads_low, heads_high, other_x, other_y, segments_other]
+    else:
+        segments_other = moves.over_core(segments)
+        events = []
+    tokens = moves.in_half(tokens_came).astype(F32)
+    unit_one, scale_one = norm_parts(tokens)
+    normed_half = (unit_one * column(ln1_gain) + column(ln1_bias)).astype(BF16)
+    events = [*events, normed_half]
+    home = moves.shard // seqs
+    seg = jnp.where(home == core, segments, segments_other)
+    seg = lax.dynamic_index_in_dim(seg, moves.shard % seqs, 1, keepdims=False)
+
+    out_grad, normed_half = late([out_grad, normed_half], events)
     if moves.square:
-        qkv_own = list(qkv_near) + list(qkv_far)
-        qkv_other = [moves.over_core(piece) for piece in qkv_own]
-        w_qkv = lay_heads(moves.core_ref, moves.places, qkv_own, qkv_other, qkv_count)
+        heads_low, heads_high = late([heads_low, heads_high], events)
+        other_low, other_high = moves.over_core(heads_low), moves.over_core(heads_high)
+        events = [other_low, other_high]
     else:
-        (qkv_half,) = moves.lay(qkv_near, qkv_far)
+        events = []
+    normed_other = moves.over_core(normed_half)
+    grad_came = moves.to_chips(out_grad.transpose(1, 2, 0))
+    events = [*events, normed_other, *grad_came]
+
+    ff_piece, normed_other, *grad_came = late([ff_piece, normed_other, *grad_came], events)
+    if moves.square:
+        ff_x, ff_y = moves.over_x(ff_piece), moves.over_y(ff_piece)
+        w_qkv, w_out = lay_heads(
+            moves.core_ref,
+            moves.places,
+            [heads_piece, heads_x, heads_y, heads_low, heads_high],
+            [other_own, other_x, other_y, other_low, other_high],
+            counts,
+            taken,
+            events,
+        )
+        events = [ff_x, ff_y]
+    else:
+        (qkv_half,) = moves.lay([mine_of[0]], ())
         qkv_other = moves.over_core(qkv_half)
         low = jnp.where(core == 0, qkv_half, qkv_other)
         high = jnp.where(core == 0, qkv_other, qkv_half)
+        rows = taken[0]
         qkv_full = jnp.concatenate(
             [
-                block[shard * qkv_rows + skip : (shard + 1) * qkv_rows]
+                block[shard * rows + skip : (shard + 1) * rows]
                 for shard in range(shard_count)
-                for block, skip in ((low, 0), (high, qkv_over))
+                for block, skip in ((low, 0), (high, 2 * rows - counts[0]))
             ],
             axis=0,
         )
         w_qkv = jnp.concatenate(
             [rows_of(qkv_full, part * width + first_row) for part in range(3)], axis=0
         )
-    up_bias_own = lax.dynamic_index_in_dim(
-        up_bias.reshape(shard_count, 4, strip), quarter, 1, keepdims=False
-    ).reshape(-1)
-    seg_pair = jnp.stack([segments, moves.over_core(segments)])
-    home = moves.shard // seqs
-    seg = lax.dynamic_index_in_dim(
-        lax.dynamic_index_in_dim(seg_pair, (home != core).astype(jnp.int32), 0, keepdims=False),
-        moves.shard % seqs,
-        1,
-        keepdims=False,
-    )
-
-    tokens = tokens_half.astype(F32)
-    unit_one, scale_one = norm_parts(tokens)
-    normed = moves.both((unit_one * column(ln1_gain) + column(ln1_bias)).astype(BF16))
+        twice = (core == 1) & (jnp.arange(OWN) < HDIM)
+        own = lax.dynamic_slice_in_dim(output_projection_weight, first_row, OWN, 1)
+        (w_out,) = moves.lay([jnp.where(twice[None, :], 0, own).astype(BF16)], ())
+        w_up, w_down = moves.lay([ff_piece], (), 2)
+        events = []
+    grad_half = moves.in_half(grad_came)
+    grad_across = moves.over_z(grad_half, 1)
+    normed = moves.ordered(normed_half, normed_other)
     zeros = jnp.zeros((OWN,), F32)
     joined_bias = jnp.concatenate([rows_of(q_bias, first_row), zeros, rows_of(v_bias, first_row)])
     row_scale = jnp.where(jnp.arange(3 * OWN) < OWN, 0.125, 1.0).astype(F32)
@@ -918,16 +979,32 @@
         (column(joined_bias), column(row_scale)),
         name="project_qkv",
     )
-    mixed, lse = attention(seg, joined, [*out_near[1:], grad_half])
-    grad_out = moves.spread(grad_half)
-    branch = product(
-        w_out, mixed, "nn", 400, name="project_out", wait=[*ff_near[1:], grad_out[1]]
-    )
+    mixed, lse = attention(seg, joined, [])
+    branch = product(w_out, mixed, "nn", 400, name="project_out")
+    events = [*events, branch, grad_across]
+
+    branch, grad_half, grad_across = late([branch, grad_half, grad_across], events)
+    grad_other, grad_far = moves.over_core(grad_half), moves.over_core(grad_across)
     branch_half = half_of(branch, mine).astype(F32)
     branch_half = branch_half + moves.over_core(half_of(branch, theirs)).astype(F32)
     middle = tokens + branch_half + column(out_bias)
     unit_two, scale_two = norm_parts(middle)
-    normed_two = moves.spread((unit_two * column(ln2_gain) + column(ln2_bias)).astype(BF16))
+    norm_half = (unit_two * column(ln2_gain) + column(ln2_bias)).astype(BF16)
+    events = [norm_half, grad_other, grad_far]
+    grad_out = [grad_half, grad_across, grad_other, grad_far]
+
+    (norm_half,) = late([norm_half], events)
+    norm_across = moves.over_z(norm_half, 1)
+    norm_other = moves.over_core(norm_half)
+    if moves.square:
+        ff_x, ff_y = late([ff_x, ff_y], events)
+        split = ff_piece.shape[0] // 2
+        ff_low, ff_high = moves.over_x(ff_y[:split]), moves.over_y(ff_x[split:])
+        (norm_across,) = late([norm_across], [ff_low, ff_high])
+        w_up, w_down = moves.lay((ff_piece, ff_x, ff_y), (ff_low, ff_high), 2)
+    norm_far = moves.over_core(norm_across)
+    normed_two = [norm_half, norm_across, norm_other, norm_far]
+
     activ, slope = product(
         w_up,
         normed_two,
@@ -940,20 +1017,17 @@
         wait=grad_out,
     )
 
-    ff_cut = 896 if width == 1600 else width // 256 * 128
-    down_part, down_made, down_first, down_last = moves.scatter(
-        [(grad_out, activ)], ff_cut, width
-    )
+    def in_halves(value, at):
+        half = value.shape[1] // 2
+        return value[:, :half], value[:, half:]
+
+    halves = ((length, BF16), (length, BF16))
 
     def through_gelu(value, at, slope_ref):
         size = value.shape[1]
         slope_here = slope_ref[:, at * size : (at + 1) * size].astype(F32)
         grad = (value * slope_here).astype(BF16)
         return grad, lane_sums(grad.astype(F32))
-
-    def in_halves(value, at):
-        half = value.shape[1] // 2
-        return value[:, :half], value[:, half:]
 
     grad_pre, grad_pre_sums = product(
         w_down,
@@ -964,43 +1038,61 @@
         (slope,),
         ((None, BF16), (512, F32)),
         name="back_down",
-        wait=down_made,
-    )
-    halves = ((length, BF16), (length, BF16))
-    grad_norm_two = moves.collect(
-        *product(w_up, grad_pre, "tn", 256, in_halves, (), halves, name="back_up")
-    )
-    up_part, up_made, up_first, up_last = moves.scatter([(grad_pre, normed_two)], ff_cut, width)
+    )
+    ff_cut = 896 if width == 1600 else width // 256 * 128
+    norm_here, norm_there = product(
+        w_up, grad_pre, "tn", 256, in_halves, (), halves, name="back_up"
+    )
+
+    norm_came = moves.over_core(norm_there)
+    down_parts = moves.scatter_first([(grad_out, activ)], ff_cut, [norm_there])
+    events = [norm_came, down_parts[0]]
+
+    norm_came, norm_here = late([norm_came, norm_here], events)
+    norm_last = moves.over_z(norm_here[:, half_len:] + norm_came[:, half_len:], 1)
+    down_near = moves.scatter_near(down_parts, events)
+    up_parts = moves.scatter_first([(grad_pre, normed_two)], ff_cut, events)
     down_here, down_there = product(
-        w_down, activ, "nn", 320, in_halves, (), halves, name="project_down", wait=up_made
-    )
-    down_half = moves.collect(down_here, down_there)
+        w_down, activ, "nn", 320, in_halves, (), halves, name="project_down", wait=up_parts[:1]
+    )
+    events = [norm_last, *down_near[1], down_there]
+
+    norm_last, down_there = late([norm_last, down_there], events)
+    up_near = moves.scatter_near(up_parts, events)
+    down_came = moves.over_core(down_there)
+    grad_norm_two = norm_here[:, :half_len].astype(F32) + norm_came[:, :half_len].astype(F32)
+    grad_norm_two = grad_norm_two + norm_last.astype(F32)
     grad_out_f = grad_half.astype(F32)
     grad_middle = grad_out_f + norm_back(grad_norm_two, unit_two, scale_two, column(ln2_gain))
     grad_branch_half = grad_middle.astype(BF16)
-    grad_branch = moves.both(grad_branch_half)
-    grad_mixed = product(
-        w_out, grad_branch, "tn", OWN, name="back_out", wait=[down_here, *down_first, *down_last]
-    )
+    grad_branch = moves.ordered(grad_branch_half, moves.over_core(grad_branch_half))
+    grad_mixed = product(w_out, grad_branch, "tn", OWN, name="back_out")
     padded = to_tiles(OWN)
-    out_part, out_made, out_first, out_last = moves.scatter([(grad_branch, mixed)], 512, padded)
-    down_sum = moves.total_alike(down_part)
-    up_sum = moves.total_alike(up_part)
-    out_sum = moves.total(out_part)
-    result = moves.from_chips((middle + down_half + column(down_bias)).astype(BF16), seqs)
-
-    grad_own = attention_back(
-        seg, joined, mixed, grad_mixed, lse, [*out_made, *up_first]
-    ).reshape(3 * OWN, length)
-    grad_other = moves.over_core(grad_own)
-    grad_norm_one = product(
-        w_qkv, grad_own, "tn", 256, name="back_qkv", wait=[*out_first, *up_last]
-    )
+    out_parts = moves.scatter_first([(grad_branch, mixed)], 512, [grad_mixed])
+    events = [*up_near[1], down_came, grad_mixed, out_parts[0]]
+
+    down_here, down_came = late([down_here, down_came], events)
+    down_last = moves.over_z(down_here[:, half_len:] + down_came[:, half_len:], 1)
+    down_far = moves.scatter_far(down_near, events)
+    out_near = moves.scatter_near(out_parts, events)
+    grad_own = attention_back(seg, joined, mixed, grad_mixed, lse, events).reshape(3 * OWN, length)
+    events = [down_last, *down_far[1], *out_near[1], grad_own]
+
+    (grad_own,) = late([grad_own], events)
+    grad_heads = moves.over_core(grad_own)
+    down_part = moves.scatter_last(down_far, width)
+    down_come = moves.alike(down_part)
+    up_far = moves.scatter_far(up_near, events)
+    norm_one = product(w_qkv, grad_own, "tn", 256, name="back_qkv", wait=[down_part])
+    events = [grad_heads, *up_far[1], norm_one]
+
+    (grad_heads,) = late([grad_heads], events)
+    out_far = moves.scatter_far(out_near, events)
     if moves.square:
-        grad_joined = join_heads(moves.core_ref, grad_own, grad_other)
+        grad_joined = join_heads(moves.core_ref, grad_own, grad_heads)
     else:
-        low = jnp.where(core == 0, grad_own, grad_other)
-        high = jnp.where(core == 0, grad_other, grad_own)
+        low = jnp.where(core == 0, grad_own, grad_heads)
+        high = jnp.where(core == 0, grad_heads, grad_own)
         grad_joined = jnp.concatenate(
             [
                 piece
@@ -1012,15 +1104,50 @@
             ],
             axis=0,
         )
-    qkv_part, _, _, _ = moves.scatter(
-        [(grad_joined, rows_of(normed, first_row))], 512, padded, [*out_last]
-    )
-    qkv_sum = moves.total(qkv_part)
-    grad_norm_one = half_of(grad_norm_one, mine).astype(F32) + moves.over_core(
-        half_of(grad_norm_one, theirs)
-    ).astype(F32)
+    qkv_parts = moves.scatter_first([(grad_joined, rows_of(normed, first_row))], 512, events)
+    qkv_near = moves.scatter_near(qkv_parts)
+    up_part = moves.scatter_last(up_far, width)
+    down_come, up_part = late([down_come, up_part], [qkv_parts[0]])
+    down_sum = moves.alike_sum(down_part, down_come)
+    down_across = moves.over_z(down_sum, 1)
+    up_come = moves.alike(late([up_part], [down_come])[0])
+    out_part = moves.scatter_last(out_far, padded)
+    events = qkv_near[1]
+
+    qkv_far = moves.scatter_far(qkv_near, events)
+    norm_one, out_part = late([norm_one, out_part], events)
+    norm_one_came = moves.over_core(half_of(norm_one, theirs))
+    out_pair = moves.total_pair(out_part)
+    events = [*qkv_far[1], norm_one_came, down_across, out_pair]
+
+    norm_one, norm_one_came, down_sum = late([norm_one, norm_one_came, down_sum], events)
+    qkv_pair = moves.total_pair(moves.scatter_last(qkv_far, padded))
+    grad_norm_one = half_of(norm_one, mine).astype(F32) + norm_one_came.astype(F32)
     input_half = grad_middle + norm_back(grad_norm_one, unit_one, scale_one, column(ln1_gain))
-    input_grad = moves.from_chips(input_half.astype(BF16), seqs).astype(F32)
+    input_came = moves.from_chips(input_half.astype(BF16), seqs)
+    down_other = moves.over_core(down_sum)
+    events = [qkv_pair, input_came, down_other, up_come]
+
+    result_half = middle + down_here[:, :half_len].astype(F32)
+    result_half = result_half + down_came[:, :half_len].astype(F32) + down_last.astype(F32)
+    result_half = (result_half + column(down_bias)).astype(BF16)
+    up_sum = moves.alike_sum(up_part, up_come)
+    qkv_pair, up_sum, result_half, out_pair, down_across = late(
+        [qkv_pair, up_sum, result_half, out_pair, down_across], events
+    )
+    qkv_full = moves.total_all(qkv_pair)
+    up_across = moves.over_z(up_sum, 1)
+    result = moves.from_chips(result_half, seqs)
+    out_full = moves.total_all(out_pair)
+    down_far_other = moves.over_core(down_across)
+    events = [qkv_full, up_across, out_full, down_far_other]
+
+    qkv_full, out_full, up_across, up_sum, down_far_other = late(
+        [qkv_full, out_full, up_across, up_sum, down_far_other], [*events, result]
+    )
+    qkv_sum = moves.total_halves(qkv_full)
+    out_sum = moves.total_halves(out_full)
+    input_grad = input_came.astype(F32)
 
     up_bias_grad = jnp.sum(grad_pre_sums, axis=1).reshape(shard_count, 1, strip)
     up_bias_grad = up_bias_grad * (jnp.arange(4)[None, :, None] == quarter).astype(F32)
@@ -1055,13 +1182,13 @@
         v_bias_grad,
     ) = rest.reshape(8, width)
 
-    def quarters(own):
-        across = moves.over_z(own, 1)
-        return [own, moves.over_core(own), across, moves.over_core(across)]
-
     quarter_ref = quarter.astype(jnp.int32)[None]
-    down_total = finish_down(quarter_ref, quarters(down_sum), shard_count)
-    up_total = finish_up(quarter_ref, quarters(up_sum))
+    down_total = finish_down(
+        quarter_ref, [down_sum, down_other, down_across, down_far_other], shard_count
+    )
+    up_total = finish_up(
+        quarter_ref, [up_sum, moves.over_core(up_sum), up_across, moves.over_core(up_across)]
+    )
 
     return (
         result.transpose(2, 0, 1),

time: 958 us -> 866 us (0.904)
  waiting for transfers between devices: 416 us -> 324 us
    ppermute x80 -> x76, waiting for transfers between devices: 416 us -> 324 us  [move(): came = lax.ppermute(array, AXES, pairs)]
    ppermute x80 -> x76, starting transfers between devices: 78.8 us -> 78.8 us  [move(): came = lax.ppermute(array, AXES, pairs)]
  transfers between devices with their start and end apart: 80 -> 76, of which waited for: 23 -> 26; matrix products, arithmetic and copies ran while one was open for 11% -> 13% of each run, Pallas kernels for 20% -> 26%
where the time goes in v3:
time: 866 us; the launch traced here: 859 us
  waiting for transfers between devices  324 us (37%)
  Pallas kernels  314 us (36%)
  other arithmetic  86.7 us (10%)
  starting transfers between devices  78.8 us (9%)
  local copies, waits for them, and re-layouts  53.1 us (6%)
    ppermute x76, waiting for transfers between devices, move(): came = lax.ppermute(array, AXES, pairs)  324 us
    pallas_call x8, Pallas kernels, product(): pl.pallas_call(body, grid=(pl.cdiv(m, block),), in_specs=[left_spec] + [p...  122 us
    ppermute x76, starting transfers between devices, move(): came = lax.ppermute(array, AXES, pairs)  78.8 us
    pallas_call x4, Pallas kernels, product_parts(): pl.pallas_call(body, grid_spec=pltpu.PrefetchScalarGridSpec(num_scalar_pr...  65.6 us
    pallas_call x1, Pallas kernels, attention_back(): pl.pallas_call(backward_kernel, grid=(OWN_HEADS,), in_specs=[whole_spec((...  28.6 us
    pallas_call x1, Pallas kernels, attention(): pl.pallas_call(forward_kernel, grid=(OWN_HEADS,), in_specs=[whole_spec((1...  26.5 us
  transfers between devices with their start and end apart: 76, of which 26 were waited for; matrix products, arithmetic and copies ran while one was open for 13% of the time, Pallas kernels for 26%

profile of v3, /device:TPU:1, one launch (start us, length us, event | category | flops | bytes accessed | tf_op | source)
XLA Modules:
  0.0 858.7 jit_solution(11959769478726731314)
XLA Ops:
  25.5 57.0 %collective-permute-done.2 = bf16[1600,256]{1,0:T(8,128)(2,1)} collective-permute-done((bf16[1600,256]{1,0:T(8,128)(2,1)S(1)}, bf16[1600,256]{1,0:T(8,128)(2,1)}, u32[]{:S(2)}, u32[]{:S(2)}) %collective-permute-start.2) | collective-permute-done | bytes 819232 | tf_op jit(solution)/shard_map/ppermute | solution.py:660
  98.3 25.3 %collective-permute-done.7.refs_4_ = bf16[400,1600]{1,0:T(8,128)(2,1)} collective-permute-done((bf16[400,1600]{1,0:T(8,128)(2,1)}, bf16[400,1600]{1,0:T(8,128)(2,1)}, u32[]{:S(2)}, u32[]{:S(2)}) %collective-permute-start.7) | collective-permute-done | bytes 1280032 | tf_op jit(solution)/shard_map/ppermute | solution.py:660
  139.0 10.2 %collective-permute-done.13 = bf16[1600,256]{1,0:T(8,128)(2,1)} collective-permute-done((bf16[1600,256]{1,0:T(8,128)(2,1)}, bf16[1600,256]{1,0:T(8,128)(2,1)}, u32[]{:S(2)}, u32[]{:S(2)}) %collective-permute-start.13) | collective-permute-done | bytes 819232 | tf_op jit(solution)/shard_map/ppermute | solution.py:660
  159.4 14.6 %lay_heads.1 = (bf16[2496,1600]{1,0:T(8,128)(2,1)}, bf16[1600,832]{1,0:T(8,128)(2,1)}) custom-call(s32[1]{0:T(128)} %bitcast.5.core_ref, s32[4]{0:T(128)} %pad_add_fusion.1.places_ref, bf16[816,1600]{1,0:T(8,128)(2,1)} %copy-done.26, bf16[816,1600]{1,0:T(8,128)(2,1)} %collective-permute-done.refs_1_, bf16[816,1600]{1,0:T(8,128)(2,1)} %collective-permute-done.1.refs_2_, ...), custom_call_target="tpu_custom_call" | custom-call | bytes 245760000 | tf_op jit(solution)/shard_map/lay_heads/pallas_call | solution.py:343
  174.0 14.0 %project_qkv.1.q_ref.k_ref.v_ref = bf16[2496,1024]{1,0:T(8,128)(2,1)} custom-call(bf16[2496,1600]{1,0:T(8,128)(2,1)} %get-tuple-element.114.left_ref, bf16[1600,1024]{1,0:T(8,128)(2,1)} %pad_maximum_fusion.refs_0_, f32[2496,1]{1,0:T(8,128)} %broadcast_in_dim.28.refs_1_, f32[2496,1]{1,0:T(8,128)} %fusion.20.refs_2_), custom_call_target="tpu_custom_call" | custom-call | flops 65431142400 | bytes 131006464 | tf_op jit(solution)/shard_map/project_qkv/pallas_call | solution.py:218
  190.4 26.5 %attention_forward.1 = (bf16[832,1024]{1,0:T(8,128)(2,1)S(1)}, f32[13,1,1024]{2,1,0:T(1,128)S(1)}) custom-call(s32[1,1024]{1,0:T(1,128)S(1)} %bitcast.44, s32[1024,1]{1,0:T(8,128)S(1)} %get-tuple-element.219.seg_col, bf16[2496,1024]{1,0:T(8,128)(2,1)S(1)} %copy-done.10, bf16[2496,1024]{1,0:T(8,128)(2,1)S(1)} %copy-done.10, bf16[2496,1024]{1,0:T(8,128)(2,1)S(1)} %copy-done.10), custom_call_target="tpu_custom_call" | custom-call | flops 111669149696 | bytes 54525952 | tf_op jit(solution)/shard_map/attention_forward/pallas_call | solution.py:141
  247.3 28.9 %collective-permute-done.21.refs_3_ = bf16[400,1600]{1,0:T(8,128)(2,1)S(1)} collective-permute-done((bf16[400,1600]{1,0:T(8,128)(2,1)S(1)}, bf16[400,1600]{1,0:T(8,128)(2,1)S(1)}, u32[]{:S(2)}, u32[]{:S(2)}) %collective-permute-start.21) | collective-permute-done | bytes 1280032 | tf_op jit(solution)/shard_map/ppermute | solution.py:660
  282.3 9.8 %lay.1 = (bf16[1600,1600]{1,0:T(8,128)(2,1)}, bf16[1600,1600]{1,0:T(8,128)(2,1)}) custom-call(s32[4]{0:T(128)} %pad_add_fusion.1.places_ref, bf16[800,1600]{1,0:T(8,128)(2,1)} %pad_maximum_fusion.3.refs_0_, bf16[800,1600]{1,0:T(8,128)(2,1)} %collective-permute-done.16.refs_1_, bf16[800,1600]{1,0:T(8,128)(2,1)} %collective-permute-done.17.refs_2_, ...), custom_call_target="tpu_custom_call" | custom-call | bytes 163840000 | tf_op jit(solution)/shard_map/lay/pallas_call | solution.py:270
  292.1 23.9 %project_up.1 = (bf16[1600,2048]{1,0:T(8,128)(2,1)}, bf16[1600,2048]{1,0:T(8,128)(2,1)}) custom-call(bf16[1600,1600]{1,0:T(8,128)(2,1)} %get-tuple-element.126.left_ref, bf16[1600,512]{1,0:T(8,128)(2,1)} %copy-done.53, bf16[1600,512]{1,0:T(8,128)(2,1)} %collective-permute-done.23.refs_1_.refs_2_, bf16[1600,512]{1,0:T(8,128)(2,1)} %collective-permute-done.24.refs_2_.refs_3_, ...), custom_call_target="tpu_custom_call" | custom-call | flops 83886080000 | bytes 145817600 | tf_op jit(solution)/shard_map/project_up/pallas_call | solution.py:218
  316.0 19.6 %back_down.1 = (bf16[1600,2048]{1,0:T(8,128)(2,1)}, f32[1600,512]{1,0:T(8,128)}) custom-call(bf16[1600,1600]{1,0:T(8,128)(2,1)} %get-tuple-element.127.left_ref, bf16[1600,512]{1,0:T(8,128)(2,1)} %pad_maximum_fusion.5.refs_5_.refs_0_, bf16[1600,512]{1,0:T(8,128)(2,1)} %collective-permute-done.15.refs_6_.refs_1_, bf16[1600,512]{1,0:T(8,128)(2,1)} %copy-done.99, ...), custom_call_target="tpu_custom_call" | custom-call | flops 83886080000 | bytes 145817600 | tf_op jit(solution)/shard_map/back_down/pallas_call | solution.py:218
  335.6 18.7 %back_up.1 = (bf16[1600,1024]{1,0:T(8,128)(2,1)}, bf16[1600,1024]{1,0:T(8,128)(2,1)}) custom-call(bf16[1600,1600]{1,0:T(8,128)(2,1)} %get-tuple-element.126.left_ref, bf16[1600,2048]{1,0:T(8,128)(2,1)} %get-tuple-element.131.refs_0_), custom_call_target="tpu_custom_call" | custom-call | flops 83886080000 | bytes 145817600 | tf_op jit(solution)/shard_map/back_up/pallas_call | solution.py:218
  354.3 19.7 %product_parts.4 = (bf16[800,896]{1,0:T(8,128)(2,1)}, bf16[800,768]{1,0:T(8,128)(2,1)}, bf16[800,896]{1,0:T(8,128)(2,1)}, bf16[800,768]{1,0:T(8,128)(2,1)}) custom-call(s32[4]{0:T(128)} %pad_add_fusion.order_ref, bf16[1600,512]{1,0:T(8,128)(2,1)} %pad_maximum_fusion.5.refs_5_.refs_0_, bf16[1600,512]{1,0:T(8,128)(2,1)} %collective-permute-done.15.refs_6_.refs_1_, ...), custom_call_target="tpu_custom_call" | custom-call | flops 83886080000 | bytes 93388800 | tf_op jit(solution)/shard_map/product_parts/pallas_call | solution.py:443
  376.5 19.4 %product_parts.5 = (bf16[800,896]{1,0:T(8,128)(2,1)}, bf16[800,768]{1,0:T(8,128)(2,1)}, bf16[800,896]{1,0:T(8,128)(2,1)}, bf16[800,768]{1,0:T(8,128)(2,1)}) custom-call(s32[4]{0:T(128)} %pad_add_fusion.order_ref, bf16[1600,2048]{1,0:T(8,128)(2,1)} %get-tuple-element.131.refs_0_, bf16[1600,512]{1,0:T(8,128)(2,1)} %copy-done.53, ...), custom_call_target="tpu_custom_call" | custom-call | flops 83886080000 | bytes 93388800 | tf_op jit(solution)/shard_map/product_parts/pallas_call | solution.py:443
  395.9 16.9 %project_down.1 = (bf16[1600,1024]{1,0:T(8,128)(2,1)}, bf16[1600,1024]{1,0:T(8,128)(2,1)}) custom-call(bf16[1600,1600]{1,0:T(8,128)(2,1)} %get-tuple-element.127.left_ref, bf16[1600,2048]{1,0:T(8,128)(2,1)} %get-tuple-element.134.refs_4_.refs_0_, bf16[800,896]{1,0:T(8,128)(2,1)} %get-tuple-element.146.refs_1_), custom_call_target="tpu_custom_call" | custom-call | flops 83886080000 | bytes 145817600 | tf_op jit(solution)/shard_map/project_down/pallas_call | solution.py:218
  469.4 28.6 %attention_backward.1 = bf16[3,832,1024]{2,1,0:T(8,128)(2,1)} custom-call(s32[1,1024]{1,0:T(1,128)S(1)} %bitcast.45, s32[1024,1]{1,0:T(8,128)S(1)} %copy-done.5, bf16[2496,1024]{1,0:T(8,128)(2,1)} %project_qkv.1.q_ref.k_ref.v_ref, bf16[2496,1024]{1,0:T(8,128)(2,1)} %project_qkv.1.q_ref.k_ref.v_ref, bf16[2496,1024]{1,0:T(8,128)(2,1)} %project_qkv.1.q_ref.k_ref.v_ref, ...), custom_call_target="tpu_custom_call" | custom-call | flops 279172874240 | bytes 109051904 | tf_op jit(solution)/shard_map/attention_backward/pallas_call | solution.py:163
  510.4 14.5 %back_qkv.1.refs_5_ = bf16[1600,1024]{1,0:T(8,128)(2,1)} custom-call(bf16[2496,1600]{1,0:T(8,128)(2,1)} %get-tuple-element.114.left_ref, bf16[2496,1024]{1,0:T(8,128)(2,1)} %bitcast.47, bf16[400,1600]{1,0:T(8,128)(2,1)} %fold.4.refs_1_), custom_call_target="tpu_custom_call" | custom-call | flops 65431142400 | bytes 131006464 | tf_op jit(solution)/shard_map/back_qkv/pallas_call | solution.py:218
  536.7 17.8 %product_parts.7 = (bf16[2400,512]{1,0:T(8,128)(2,1)}, bf16[2400,384]{1,0:T(8,128)(2,1)}, bf16[2400,512]{1,0:T(8,128)(2,1)}, bf16[2400,384]{1,0:T(8,128)(2,1)}) custom-call(s32[4]{0:T(128)} %pad_add_fusion.order_ref, bf16[4800,1024]{1,0:T(8,128)(2,1)} %join_heads.1.refs_0_, bf16[832,1024]{1,0:T(8,128)(2,1)} %fusion.19.refs_1_, ...), custom_call_target="tpu_custom_call" | custom-call | flops 65431142400 | bytes 142540800 | tf_op jit(solution)/shard_map/product_parts/pallas_call | solution.py:443
  568.9 47.7 %collective-permute-done.47 = bf16[400,1600]{1,0:T(8,128)(2,1)} collective-permute-done((bf16[400,1600]{1,0:T(8,128)(2,1)S(1)}, bf16[400,1600]{1,0:T(8,128)(2,1)}, u32[]{:S(2)}, u32[]{:S(2)}) %collective-permute-start.47) | collective-permute-done | bytes 1280032 | tf_op jit(solution)/shard_map/ppermute | solution.py:660
  647.8 14.6 %collective-permute-done.44.refs_2_ = bf16[1200,512]{1,0:T(8,128)(2,1)} collective-permute-done((bf16[1200,512]{1,0:T(8,128)(2,1)}, bf16[1200,512]{1,0:T(8,128)(2,1)}, u32[]{:S(2)}, u32[]{:S(2)}) %collective-permute-start.44) | collective-permute-done | bytes 1228832 | tf_op jit(solution)/shard_map/ppermute | solution.py:660
  669.0 17.5 %collective-permute-done.51 = bf16[200,896]{1,0:T(8,128)(2,1)} collective-permute-done((bf16[200,896]{1,0:T(8,128)(2,1)}, bf16[200,896]{1,0:T(8,128)(2,1)}, u32[]{:S(2)}, u32[]{:S(2)}) %collective-permute-start.51) | collective-permute-done | bytes 358432 | tf_op jit(solution)/shard_map/ppermute | solution.py:660
  698.7 10.7 %collective-permute-done.46 = bf16[600,896]{1,0:T(8,128)(2,1)S(1)} collective-permute-done((bf16[600,896]{1,0:T(8,128)(2,1)S(1)}, bf16[600,896]{1,0:T(8,128)(2,1)S(1)}, u32[]{:S(2)}, u32[]{:S(2)}) %collective-permute-start.46) | collective-permute-done | bytes 1075232 | tf_op jit(solution)/shard_map/ppermute | solution.py:660
  730.9 39.4 %collective-permute-done.62 = f32[150,128]{1,0:T(8,128)S(1)} collective-permute-done((f32[150,128]{1,0:T(8,128)S(1)}, f32[150,128]{1,0:T(8,128)S(1)}, u32[]{:S(2)}, u32[]{:S(2)}) %collective-permute-start.62) | collective-permute-done | bytes 76832 | tf_op jit(solution)/shard_map/ppermute | solution.py:660
  773.8 9.5 %collective-permute-done.65 = bf16[200,896]{1,0:T(8,128)(2,1)S(1)} collective-permute-done((bf16[200,896]{1,0:T(8,128)(2,1)}, bf16[200,896]{1,0:T(8,128)(2,1)S(1)}, u32[]{:S(2)}, u32[]{:S(2)}) %collective-permute-start.65) | collective-permute-done | bytes 358432 | tf_op jit(solution)/shard_map/ppermute | solution.py:660
  797.1 9.2 %collective-permute-done.54 = bf16[1600,256]{1,0:T(8,128)(2,1)} collective-permute-done((bf16[1600,256]{1,0:T(8,128)(2,1)}, bf16[1600,256]{1,0:T(8,128)(2,1)}, u32[]{:S(2)}, u32[]{:S(2)}) %collective-permute-start.54) | collective-permute-done | bytes 819232 | tf_op jit(solution)/shard_map/ppermute | solution.py:660
  (463 shorter events, 342.5 us)
Async XLA Ops:
  4.0 81.4 %collective-permute-start.4 = (bf16[816,1600]{1,0:T(8,128)(2,1)S(1)}, bf16[816,1600]{1,0:T(8,128)(2,1)}, u32[]{:S(2)}, u32[]{:S(2)}) collective-permute-start(bf16[816,1600]{1,0:T(8,128)(2,1)S(1)} %pad_maximum_fusion.2.refs_0_), channel_id=1, source_target_pairs={{0,1},{1,0},{2,3},{3,2},{4,5},{5,4},{6,7},{7,6},{8,9},{9,8},{10,11... | collective-permute-start | bytes 7833608 | tf_op jit(solution)/shard_map/ppermute | solution.py:660
  4.1 81.3 %collective-permute-start.1 = (bf16[816,1600]{1,0:T(8,128)(2,1)S(1)}, bf16[816,1600]{1,0:T(8,128)(2,1)}, u32[]{:S(2)}, u32[]{:S(2)}) collective-permute-start(bf16[816,1600]{1,0:T(8,128)(2,1)S(1)} %pad_maximum_fusion.2.refs_0_), channel_id=1, source_target_pairs={{0,16},{1,17},{2,18},{3,19},{4,20},{5,21},{6,22},{7,23},{8,24},{9,... | collective-permute-start | bytes 7833608 | tf_op jit(solution)/shard_map/ppermute | solution.py:660
  6.8 78.6 %collective-permute-start = (bf16[816,1600]{1,0:T(8,128)(2,1)S(1)}, bf16[816,1600]{1,0:T(8,128)(2,1)}, u32[]{:S(2)}, u32[]{:S(2)}) collective-permute-start(bf16[816,1600]{1,0:T(8,128)(2,1)S(1)} %pad_maximum_fusion.2.refs_0_), channel_id=1, source_target_pairs={{0,8},{1,9},{2,10},{3,11},{4,12},{5,13},{6,14},{7,15},{8,0},{9,1},... | collective-permute-start | bytes 7833608 | tf_op jit(solution)/shard_map/ppermute | solution.py:660
  10.4 72.1 %collective-permute-start.2 = (bf16[1600,256]{1,0:T(8,128)(2,1)S(1)}, bf16[1600,256]{1,0:T(8,128)(2,1)}, u32[]{:S(2)}, u32[]{:S(2)}) collective-permute-start(bf16[1600,256]{1,0:T(8,128)(2,1)S(1)} %get-tuple-element.245), channel_id=1, source_target_pairs={{1,16},{3,18},{5,20},{7,22},{9,24},{11,26},{13,28},{15,30},{16,1},... | collective-permute-start | bytes 2457608 | tf_op jit(solution)/shard_map/ppermute | solution.py:660
  13.1 72.3 %collective-permute-start.3 = (bf16[1600,256]{1,0:T(8,128)(2,1)}, bf16[1600,256]{1,0:T(8,128)(2,1)}, u32[]{:S(2)}, u32[]{:S(2)}) collective-permute-start(bf16[1600,256]{1,0:T(8,128)(2,1)} %get-tuple-element.244), channel_id=1, source_target_pairs={{0,8},{1,24},{2,10},{3,26},{4,12},{5,28},{6,14},{7,30},{8,0},{9,16... | collective-permute-start | bytes 2457608 | tf_op jit(solution)/shard_map/ppermute | solution.py:660
  151.4 73.8 %collective-permute-start.17 = (bf16[800,1600]{1,0:T(8,128)(2,1)}, bf16[800,1600]{1,0:T(8,128)(2,1)}, u32[]{:S(2)}, u32[]{:S(2)}) collective-permute-start(bf16[800,1600]{1,0:T(8,128)(2,1)} %pad_maximum_fusion.3.refs_0_), channel_id=1, source_target_pairs={{0,16},{1,17},{2,18},{3,19},{4,20},{5,21},{6,22},{7,23},{8,24},{9,... | collective-permute-start | bytes 7680008 | tf_op jit(solution)/shard_map/ppermute | solution.py:660
  151.5 73.8 %collective-permute-start.16 = (bf16[800,1600]{1,0:T(8,128)(2,1)}, bf16[800,1600]{1,0:T(8,128)(2,1)}, u32[]{:S(2)}, u32[]{:S(2)}) collective-permute-start(bf16[800,1600]{1,0:T(8,128)(2,1)} %pad_maximum_fusion.3.refs_0_), channel_id=1, source_target_pairs={{0,8},{1,9},{2,10},{3,11},{4,12},{5,13},{6,14},{7,15},{8,0},{9,1},... | collective-permute-start | bytes 7680008 | tf_op jit(solution)/shard_map/ppermute | solution.py:660
  155.2 70.1 %collective-permute-start.15 = (bf16[1600,512]{1,0:T(8,128)(2,1)}, bf16[1600,512]{1,0:T(8,128)(2,1)}, u32[]{:S(2)}, u32[]{:S(2)}) collective-permute-start(bf16[1600,512]{1,0:T(8,128)(2,1)} %pad_maximum_fusion.5.refs_5_.refs_0_), channel_id=1, source_target_pairs={{0,2},{1,3},{2,0},{3,1},{4,6},{5,7},{6,4},{7,5},{8,10},{9,11},{10,... | collective-permute-start | bytes 4915208 | tf_op jit(solution)/shard_map/ppermute | solution.py:660
  246.3 45.8 %collective-permute-start.24 = (bf16[1600,512]{1,0:T(8,128)(2,1)S(1)}, bf16[1600,512]{1,0:T(8,128)(2,1)}, u32[]{:S(2)}, u32[]{:S(2)}) collective-permute-start(bf16[1600,512]{1,0:T(8,128)(2,1)S(1)} %add_convert_fusion.1.refs_0_.refs_1_), channel_id=1, source_target_pairs={{0,1},{1,0},{2,3},{3,2},{4,5},{5,4},{6,7},{7,6},{8,9},{9,8},{10,11... | collective-permute-start | bytes 4915208 | tf_op jit(solution)/shard_map/ppermute | solution.py:660
  554.5 69.9 %collective-permute-start.42 = (bf16[2400,512]{1,0:T(8,128)(2,1)}, bf16[2400,512]{1,0:T(8,128)(2,1)}, u32[]{:S(2)}, u32[]{:S(2)}) collective-permute-start(bf16[2400,512]{1,0:T(8,128)(2,1)} %get-tuple-element.167), channel_id=1, source_target_pairs={{0,8},{1,9},{2,10},{3,11},{4,12},{5,13},{6,14},{7,15},{8,0},{9,1},... | collective-permute-start | bytes 7372808 | tf_op jit(solution)/shard_map/ppermute | solution.py:660
  555.4 69.0 %collective-permute-start.43 = (bf16[2400,384]{1,0:T(8,128)(2,1)}, bf16[2400,384]{1,0:T(8,128)(2,1)}, u32[]{:S(2)}, u32[]{:S(2)}) collective-permute-start(bf16[2400,384]{1,0:T(8,128)(2,1)} %get-tuple-element.168), channel_id=1, source_target_pairs={{0,16},{1,17},{2,18},{3,19},{4,20},{5,21},{6,22},{7,23},{8,24},{9,... | collective-permute-start | bytes 5529608 | tf_op jit(solution)/shard_map/ppermute | solution.py:660
  556.2 60.4 %collective-permute-start.47 = (bf16[400,1600]{1,0:T(8,128)(2,1)S(1)}, bf16[400,1600]{1,0:T(8,128)(2,1)}, u32[]{:S(2)}, u32[]{:S(2)}) collective-permute-start(bf16[400,1600]{1,0:T(8,128)(2,1)S(1)} %copy-done.34), channel_id=1, source_target_pairs={{0,4},{1,5},{2,6},{3,7},{4,0},{5,1},{6,2},{7,3},{8,12},{9,13},{10,... | collective-permute-start | bytes 3840008 | tf_op jit(solution)/shard_map/ppermute | solution.py:660
  560.3 61.5 %collective-permute-start.49 = (bf16[400,512]{1,0:T(8,128)(2,1)}, bf16[400,512]{1,0:T(8,128)(2,1)}, u32[]{:S(2)}, u32[]{:S(2)}) collective-permute-start(bf16[400,512]{1,0:T(8,128)(2,1)} %slice_add_fusion.8), channel_id=1, source_target_pairs={{0,16},{1,17},{2,18},{3,19},{4,20},{5,21},{6,22},{7,23},{8,24},{9,... | collective-permute-start | bytes 1228808 | tf_op jit(solution)/shard_map/ppermute | solution.py:660
  562.0 57.3 %collective-permute-start.50 = (bf16[400,384]{1,0:T(8,128)(2,1)S(1)}, bf16[400,384]{1,0:T(8,128)(2,1)}, u32[]{:S(2)}, u32[]{:S(2)}) collective-permute-start(bf16[400,384]{1,0:T(8,128)(2,1)S(1)} %slice_add_fusion.9), channel_id=1, source_target_pairs={{0,8},{1,9},{2,10},{3,11},{4,12},{5,13},{6,14},{7,15},{8,0},{9,1},... | collective-permute-start | bytes 921608 | tf_op jit(solution)/shard_map/ppermute | solution.py:660
  619.3 72.6 %collective-permute-start.48 = (bf16[400,1600]{1,0:T(8,128)(2,1)}, bf16[400,1600]{1,0:T(8,128)(2,1)}, u32[]{:S(2)}, u32[]{:S(2)}) collective-permute-start(bf16[400,1600]{1,0:T(8,128)(2,1)} %fold.6), channel_id=1, source_target_pairs={{0,4},{1,5},{2,6},{3,7},{4,0},{5,1},{6,2},{7,3},{8,12},{9,13},{10,... | collective-permute-start | bytes 3840008 | tf_op jit(solution)/shard_map/ppermute | solution.py:660
  619.3 69.0 %collective-permute-start.52 = (bf16[400,1600]{1,0:T(8,128)(2,1)}, bf16[400,1600]{1,0:T(8,128)(2,1)}, u32[]{:S(2)}, u32[]{:S(2)}) collective-permute-start(bf16[400,1600]{1,0:T(8,128)(2,1)} %add.326.refs_0_), channel_id=1, source_target_pairs={{0,2},{1,3},{2,0},{3,1},{4,6},{5,7},{6,4},{7,5},{8,10},{9,11},{10,... | collective-permute-start | bytes 3840008 | tf_op jit(solution)/shard_map/ppermute | solution.py:660
  628.8 59.5 %collective-permute-start.53 = (bf16[1600,512]{1,0:T(8,128)(2,1)}, bf16[1600,512]{1,0:T(8,128)(2,1)}, u32[]{:S(2)}, u32[]{:S(2)}) collective-permute-start(bf16[1600,512]{1,0:T(8,128)(2,1)} %constant_dynamic-slice_fusion.5), channel_id=1, source_target_pairs={{0,1},{1,0},{2,3},{3,2},{4,5},{5,4},{6,7},{7,6},{8,9},{9,8},{10,11... | collective-permute-start | bytes 4915208 | tf_op jit(solution)/shard_map/ppermute | solution.py:660
  646.4 40.1 %collective-permute-start.51 = (bf16[200,896]{1,0:T(8,128)(2,1)}, bf16[200,896]{1,0:T(8,128)(2,1)}, u32[]{:S(2)}, u32[]{:S(2)}) collective-permute-start(bf16[200,896]{1,0:T(8,128)(2,1)} %constant_dynamic-slice_fusion.6), channel_id=1, source_target_pairs={{0,2},{1,3},{2,0},{3,1},{4,6},{5,7},{6,4},{7,5},{8,10},{9,11},{10,... | collective-permute-start | bytes 1075208 | tf_op jit(solution)/shard_map/ppermute | solution.py:660
  668.9 40.5 %collective-permute-start.46 = (bf16[600,896]{1,0:T(8,128)(2,1)S(1)}, bf16[600,896]{1,0:T(8,128)(2,1)S(1)}, u32[]{:S(2)}, u32[]{:S(2)}) collective-permute-start(bf16[600,896]{1,0:T(8,128)(2,1)S(1)} %constant_dynamic-slice_fusion.7), channel_id=1, source_target_pairs={{0,2},{1,3},{2,0},{3,1},{4,6},{5,7},{6,4},{7,5},{8,10},{9,11},{10,... | collective-permute-start | bytes 3225608 | tf_op jit(solution)/shard_map/ppermute | solution.py:660
  710.7 77.3 %collective-permute-start.66 = (bf16[400,1600]{1,0:T(8,128)(2,1)}, bf16[400,1600]{1,0:T(8,128)(2,1)}, u32[]{:S(2)}, u32[]{:S(2)}) collective-permute-start(bf16[400,1600]{1,0:T(8,128)(2,1)} %add.315.refs_0_), channel_id=1, source_target_pairs={{0,2},{1,3},{2,0},{3,1},{4,6},{5,7},{6,4},{7,5},{8,10},{9,11},{10,... | collective-permute-start | bytes 3840008 | tf_op jit(solution)/shard_map/ppermute | solution.py:660
  718.4 67.7 %collective-permute-start.64 = (bf16[600,896]{1,0:T(8,128)(2,1)}, bf16[600,896]{1,0:T(8,128)(2,1)}, u32[]{:S(2)}, u32[]{:S(2)}) collective-permute-start(bf16[600,896]{1,0:T(8,128)(2,1)} %dynamic-slice_add_fusion), channel_id=1, source_target_pairs={{0,4},{1,5},{2,6},{3,7},{4,0},{5,1},{6,2},{7,3},{8,12},{9,13},{10,... | collective-permute-start | bytes 3225608 | tf_op jit(solution)/shard_map/ppermute | solution.py:660
  720.3 70.6 %collective-permute-start.67 = (bf16[400,1600]{1,0:T(8,128)(2,1)}, bf16[400,1600]{1,0:T(8,128)(2,1)}, u32[]{:S(2)}, u32[]{:S(2)}) collective-permute-start(bf16[400,1600]{1,0:T(8,128)(2,1)} %collective-permute-done.52.refs_2_), channel_id=1, source_target_pairs={{0,1},{1,0},{2,3},{3,2},{4,5},{5,4},{6,7},{7,6},{8,9},{9,8},{10,11... | collective-permute-start | bytes 3840008 | tf_op jit(solution)/shard_map/ppermute | solution.py:660
  725.4 57.9 %collective-permute-start.65 = (bf16[200,896]{1,0:T(8,128)(2,1)}, bf16[200,896]{1,0:T(8,128)(2,1)S(1)}, u32[]{:S(2)}, u32[]{:S(2)}) collective-permute-start(bf16[200,896]{1,0:T(8,128)(2,1)} %dynamic-slice_add_fusion.1), channel_id=1, source_target_pairs={{0,4},{1,5},{2,6},{3,7},{4,0},{5,1},{6,2},{7,3},{8,12},{9,13},{10,... | collective-permute-start | bytes 1075208 | tf_op jit(solution)/shard_map/ppermute | solution.py:660
  728.5 41.8 %collective-permute-start.62 = (f32[150,128]{1,0:T(8,128)S(1)}, f32[150,128]{1,0:T(8,128)S(1)}, u32[]{:S(2)}, u32[]{:S(2)}) collective-permute-start(f32[150,128]{1,0:T(8,128)S(1)} %add.335), channel_id=1, source_target_pairs={{0,2},{1,3},{2,0},{3,1},{4,6},{5,7},{6,4},{7,5},{8,10},{9,11},{10,... | collective-permute-start | bytes 230408 | tf_op jit(solution)/shard_map/ppermute | solution.py:660
  (155 other events, 2929.2 us)

commit v4 on v3

--- a/solution.py
+++ b/solution.py
@@ -27,25 +27,12 @@
 COST_SCALE = 8
 
 
-def cost(flops, bytes_accessed):
+def cost(flops, bytes_accessed, share=1.0):
     return pl.CostEstimate(
-        flops=int(flops * COST_SCALE),
-        bytes_accessed=int(bytes_accessed * COST_SCALE),
+        flops=int(flops * COST_SCALE * share),
+        bytes_accessed=int(bytes_accessed * COST_SCALE * share),
         transcendentals=0,
     )
-
-
-def norm_parts(rows):
-    centre = rows - jnp.mean(rows, axis=0, keepdims=True)
-    scale = lax.rsqrt(jnp.mean(centre * centre, axis=0, keepdims=True) + 1e-05)
-    return centre * scale, scale
-
-
-def norm_back(grad, unit, scale, gain):
-    inner = grad * gain
-    mean_inner = jnp.mean(inner, axis=0, keepdims=True)
-    mean_cross = jnp.mean(inner * unit, axis=0, keepdims=True)
-    return scale * (inner - mean_inner - unit * mean_cross)
 
 
 def gelu_pair(value):
@@ -187,7 +174,7 @@
 
 
 def product(left, rights, form, block, finish=None, extras=(), outs=((None, BF16),), name="product",
-            wait=()):
+            wait=(), share=1.0):
     rights = rights if isinstance(rights, (list, tuple)) else [rights]
     many = len(rights)
     left_dim, right_dim = (0 if form == "tn" else 1), (1 if form == "nt" else 0)
@@ -228,7 +215,7 @@
         out_specs=[pl.BlockSpec((block, columns), lambda i: (i, 0)) for columns, _ in sizes],
         out_shape=[jax.ShapeDtypeStruct((m, columns), kind) for columns, kind in sizes],
         compiler_params=pltpu.CompilerParams(vmem_limit_bytes=56 * 2**20),
-        cost_estimate=cost(2 * m * n * k, 2 * (m * k + n * k + m * n)),
+        cost_estimate=cost(2 * m * n * k, 2 * (m * k + n * k + m * n), share),
         name=name,
     )(left, *rights, *extras, *wait)
     return results if len(outs) > 1 else results[0]
@@ -236,6 +223,204 @@
 
 def lane_sums(value):
     return sum(value[:, at : at + 128] for at in range(0, value.shape[1], 128))
+
+
+PARAMS = pltpu.CompilerParams(vmem_limit_bytes=56 * 2**20)
+
+
+def norm_parts(rows):
+    centre = rows - jnp.mean(rows, axis=0, keepdims=True)
+    scale = lax.rsqrt(jnp.mean(centre * centre, axis=0, keepdims=True) + 1e-05)
+    return centre * scale, scale
+
+
+def norm_back(grad, unit, scale, gain):
+    inner = grad * gain
+    mean_inner = jnp.mean(inner, axis=0, keepdims=True)
+    mean_cross = jnp.mean(inner * unit, axis=0, keepdims=True)
+    return scale * (inner - mean_inner - unit * mean_cross)
+
+
+def column_specs(shape, size, many):
+    return [pl.BlockSpec((shape[0], size), lambda i, *_: (0, i))] * many
+
+
+def fixed_specs(shape, many):
+    return [pl.BlockSpec(shape, lambda i, *_: (0,) * len(shape))] * many
+
+
+def norm_in(at, came, gain, bias):
+    pieces = len(came)
+    rows, count = came[0].shape
+
+    def body(at_ref, *refs):
+        gain_ref, bias_ref, tokens_ref, norm_ref = refs[pieces:]
+        which = lax.rem(at_ref[0] - pl.program_id(0) + pieces, pieces)
+        for piece in range(pieces):
+
+            @pl.when(which == piece)
+            def _(piece=piece):
+                tokens_ref[...] = refs[piece][...]
+
+        unit, _ = norm_parts(tokens_ref[...].astype(F32))
+        norm_ref[...] = (unit * gain_ref[...] + bias_ref[...]).astype(BF16)
+
+    return pl.pallas_call(
+        body,
+        grid_spec=pltpu.PrefetchScalarGridSpec(
+            num_scalar_prefetch=1,
+            grid=(pieces,),
+            in_specs=fixed_specs((rows, count), pieces) + fixed_specs((rows, 1), 2),
+            out_specs=column_specs((rows, pieces * count), count, 2),
+        ),
+        out_shape=[jax.ShapeDtypeStruct((rows, pieces * count), BF16)] * 2,
+        compiler_params=PARAMS,
+        cost_estimate=cost(0, 40 * rows * pieces * count),
+        name="norm_in",
+    )(at, *came, gain, bias)
+
+
+def norm_mid(tokens, mine, came, shift, gain, bias):
+    rows, columns = tokens.shape
+    size = columns // 2
+
+    def body(tokens_ref, mine_ref, came_ref, shift_ref, gain_ref, bias_ref, middle_ref, norm_ref):
+        middle = mine_ref[...].astype(F32) + came_ref[...].astype(F32)
+        middle = tokens_ref[...].astype(F32) + middle + shift_ref[...]
+        middle_ref[...] = middle
+        unit, _ = norm_parts(middle)
+        norm_ref[...] = (unit * gain_ref[...] + bias_ref[...]).astype(BF16)
+
+    return pl.pallas_call(
+        body,
+        grid=(2,),
+        in_specs=column_specs((rows, columns), size, 3) + fixed_specs((rows, 1), 3),
+        out_specs=column_specs((rows, columns), size, 2),
+        out_shape=[
+            jax.ShapeDtypeStruct((rows, columns), F32),
+            jax.ShapeDtypeStruct((rows, columns), BF16),
+        ],
+        compiler_params=PARAMS,
+        cost_estimate=cost(0, 40 * rows * columns),
+        name="norm_mid",
+    )(tokens, mine, came, shift, gain, bias)
+
+
+def norm_mid_back(parts, middle, grad, gain, wait):
+    rows, columns = middle.shape
+    size = columns // 2
+    many = len(parts)
+
+    def body(*refs):
+        middle_ref, grad_ref, gain_ref = refs[many : many + 3]
+        out_ref, low_ref, sums_ref = refs[-3:]
+        norm_grad = sum(ref[...].astype(F32) for ref in refs[:many])
+        unit, scale = norm_parts(middle_ref[...])
+        through = grad_ref[...].astype(F32)
+        value = through + norm_back(norm_grad, unit, scale, gain_ref[...])
+        out_ref[...] = value
+        low_ref[...] = value.astype(BF16)
+        sums = (norm_grad * unit, norm_grad, through, value.astype(BF16).astype(F32))
+        for at, rows_of_sum in enumerate(sums):
+            here = lane_sums(rows_of_sum)
+
+            @pl.when(pl.program_id(0) == 0)
+            def _(at=at, here=here):
+                sums_ref[at] = here
+
+            @pl.when(pl.program_id(0) > 0)
+            def _(at=at, here=here):
+                sums_ref[at] += here
+
+    return pl.pallas_call(
+        body,
+        grid=(2,),
+        in_specs=column_specs((rows, columns), size, many + 2)
+        + fixed_specs((rows, 1), 1)
+        + [pl.BlockSpec(memory_space=pl.ANY)] * len(wait),
+        out_specs=column_specs((rows, columns), size, 2) + fixed_specs((4, rows, 128), 1),
+        out_shape=[
+            jax.ShapeDtypeStruct((rows, columns), F32),
+            jax.ShapeDtypeStruct((rows, columns), BF16),
+            jax.ShapeDtypeStruct((4, rows, 128), F32),
+        ],
+        compiler_params=PARAMS,
+        cost_estimate=cost(0, 60 * rows * columns),
+        name="norm_mid_back",
+    )(*parts, middle, grad, gain, *wait)
+
+
+def norm_in_back(parts, tokens, grad, gain):
+    rows, columns = tokens.shape
+    size = columns // 2
+    many = len(parts)
+
+    def body(*refs):
+        tokens_ref, grad_ref, gain_ref, out_ref, sums_ref = refs[many:]
+        norm_grad = sum(ref[...].astype(F32) for ref in refs[:many])
+        unit, scale = norm_parts(tokens_ref[...].astype(F32))
+        value = grad_ref[...] + norm_back(norm_grad, unit, scale, gain_ref[...])
+        out_ref[...] = value.astype(BF16)
+        for at, rows_of_sum in enumerate((norm_grad * unit, norm_grad)):
+            here = lane_sums(rows_of_sum)
+
+            @pl.when(pl.program_id(0) == 0)
+            def _(at=at, here=here):
+                sums_ref[at] = here
+
+            @pl.when(pl.program_id(0) > 0)
+            def _(at=at, here=here):
+                sums_ref[at] += here
+
+    return pl.pallas_call(
+        body,
+        grid=(2,),
+        in_specs=column_specs((rows, columns), size, many + 2) + fixed_specs((rows, 1), 1),
+        out_specs=column_specs((rows, columns), size, 1) + fixed_specs((2, rows, 128), 1),
+        out_shape=[
+            jax.ShapeDtypeStruct((rows, columns), BF16),
+            jax.ShapeDtypeStruct((2, rows, 128), F32),
+        ],
+        compiler_params=PARAMS,
+        cost_estimate=cost(0, 60 * rows * columns),
+        name="norm_in_back",
+    )(*parts, tokens, grad, gain)
+
+
+def results(at, pieces, middle, parts, shift, input_half):
+    rows, columns = middle.shape
+    size = columns // pieces
+    many = len(parts)
+
+    def body(at_ref, middle_ref, *refs):
+        shift_ref, input_ref = refs[many : many + 2]
+        outs = refs[many + 2 :]
+        value = middle_ref[...] + shift_ref[...]
+        for ref in refs[:many]:
+            value = value + ref[...].astype(F32)
+        value = value.astype(BF16)
+        which = lax.rem(at_ref[0] - pl.program_id(0) + pieces, pieces)
+        for piece, out in enumerate(outs):
+
+            @pl.when(which == piece)
+            def _(out=out):
+                out[:rows] = value
+                out[rows:] = input_ref[...]
+
+    block = column_specs((rows, columns), size, 1)
+    return pl.pallas_call(
+        body,
+        grid_spec=pltpu.PrefetchScalarGridSpec(
+            num_scalar_prefetch=1,
+            grid=(pieces,),
+            in_specs=block * (1 + many) + fixed_specs((rows, 1), 1) + block,
+            out_specs=fixed_specs((2 * rows, size), pieces),
+        ),
+        out_shape=[jax.ShapeDtypeStruct((2 * rows, size), BF16)] * pieces,
+        compiler_params=PARAMS,
+        cost_estimate=cost(0, 40 * rows * columns),
+        name="results",
+    )(at, middle, *parts, shift, input_half)
 
 
 def lay(places, near, far, parts):
@@ -368,33 +553,45 @@
     )(core, places, *pieces, *wait)
 
 
-def join_heads(core, own, other):
+def join_heads(core, own, other, count, taken, wait):
     length = own.shape[1]
     rows = 2 * OWN - HDIM
 
-    def body(core_ref, own_ref, other_ref, out):
+    def body(core_ref, own_ref, other_ref, *refs):
+        out = refs[-1]
+        step = pl.program_id(0)
         for which in range(2):
-
-            @pl.when(core_ref[0] == which)
-            def _(which=which):
-                low, high = (own_ref, other_ref) if which == 0 else (other_ref, own_ref)
-                out[:OWN] = low[...]
-                out[OWN:] = high[HDIM:]
-
-    block = pl.BlockSpec((OWN, length), lambda i, c: (i, 0))
+            for shard in range(4):
+
+                @pl.when((core_ref[0] == which) & (step == shard))
+                def _(which=which, shard=shard):
+                    low, high = (own_ref, other_ref) if which == 0 else (other_ref, own_ref)
+                    begin = shard * count + which * (count - taken)
+                    at = begin
+                    while at < begin + taken:
+                        part, row = at // rows, at % rows
+                        source, skip, last = (
+                            (low, 0, OWN) if row < OWN else (high, OWN - HDIM, rows)
+                        )
+                        end = min(begin + taken, part * rows + last)
+                        first = part * OWN + row - skip
+                        out[at - begin : end - begin] = source[first : first + end - at]
+                        at = end
+
+    whole = pl.BlockSpec(own.shape, lambda i, c: (0, 0), pipeline_mode=pl.Buffered(1))
     return pl.pallas_call(
         body,
         grid_spec=pltpu.PrefetchScalarGridSpec(
             num_scalar_prefetch=1,
-            grid=(3,),
-            in_specs=[block, block],
-            out_specs=pl.BlockSpec((rows, length), lambda i, c: (i, 0)),
+            grid=(4,),
+            in_specs=[whole, whole] + [pl.BlockSpec(memory_space=pl.ANY)] * len(wait),
+            out_specs=pl.BlockSpec((taken, length), lambda i, c: (i, 0)),
         ),
-        out_shape=jax.ShapeDtypeStruct((3 * rows, length), BF16),
+        out_shape=jax.ShapeDtypeStruct((4 * taken, length), BF16),
         compiler_params=pltpu.CompilerParams(vmem_limit_bytes=56 * 2**20),
         cost_estimate=cost(0, 12 * rows * length),
         name="join_heads",
-    )(core, own, other)
+    )(core, own, other, *wait)
 
 
 def product_parts(order, pairs, cut, wait):
@@ -474,15 +671,16 @@
 
 
 def side_product(left, right):
-    if len(left) == len(right) == 1:
-        return dot(left[0][...], right[0][...], 1, 1)
     total = None
-    size = left[0].shape[1] if len(left) > 1 else right[0].shape[1]
-    for at in range(max(len(left), len(right))):
-        here = slice(at * size, (at + 1) * size)
-        one = left[at][...] if len(left) > 1 else left[0][:, here]
-        two = right[at][...] if len(right) > 1 else right[0][:, here]
-        value = dot(one, two, 1, 1)
+    size = min(piece.shape[1] for piece in (*left, *right))
+    depth = sum(piece.shape[1] for piece in left)
+
+    def chunk(pieces, begin):
+        width = pieces[0].shape[1]
+        return pieces[begin // width][:, begin % width : begin % width + size]
+
+    for begin in range(0, depth, size):
+        value = dot(chunk(left, begin), chunk(right, begin), 1, 1)
         total = value if total is None else total + value
     return total
 
@@ -495,7 +693,7 @@
     rows, cut = last_x.shape
     filled = last_y.shape[1]
     rest = columns - cut
-    block = 400
+    block = 400 if rows % 400 == 0 else rows // 2
     steps = rows // block
 
     def body(*refs):
@@ -516,7 +714,7 @@
         out_specs=pl.BlockSpec((block, columns), lambda i: (i, 0)),
         out_shape=jax.ShapeDtypeStruct((rows, columns), BF16),
         compiler_params=pltpu.CompilerParams(vmem_limit_bytes=56 * 2**20),
-        cost_estimate=cost(0, 8 * rows * columns),
+        cost_estimate=cost(0, 8 * rows * columns, 0.01),
         name="fold",
     )(keep_x, came_x, last_x, keep_y, came_y, last_y)
 
@@ -612,6 +810,53 @@
         compiler_params=pltpu.CompilerParams(vmem_limit_bytes=56 * 2**20),
         cost_estimate=cost(0, 16 * rows * width),
         name="finish_sides",
+    )(core, even, *parts)
+
+
+def finish_rows(core, even, parts, count):
+    rows, width = parts[0].shape
+    over = 4 * rows - count
+
+    def body(core_ref, even_ref, *refs):
+        out = refs[4]
+        for which in range(2):
+            for parity in range(2):
+
+                @pl.when((core_ref[0] == which) & (even_ref[0] == parity))
+                def _(which=which, parity=parity):
+                    mine = [refs[parity], refs[1 - parity]]
+                    others = [refs[2 + parity], refs[3 - parity]]
+                    low, high = (mine, others) if which == 0 else (others, mine)
+                    for at in range(2):
+
+                        @pl.when(pl.program_id(0) == at)
+                        def _(at=at):
+                            out[...] = low[at][...].astype(F32)
+
+                    @pl.when(pl.program_id(0) == 2)
+                    def _():
+                        out[: rows - over] = high[0][over:].astype(F32)
+                        out[rows - over :] = high[1][:over].astype(F32)
+
+                    @pl.when(pl.program_id(0) == 3)
+                    def _():
+                        out[: rows - over] = high[1][over:].astype(F32)
+
+    return pl.pallas_call(
+        body,
+        grid_spec=pltpu.PrefetchScalarGridSpec(
+            num_scalar_prefetch=2,
+            grid=(4,),
+            in_specs=[
+                pl.BlockSpec((rows, width), lambda i, c, e: (0, 0), pipeline_mode=pl.Buffered(1))
+            ]
+            * 4,
+            out_specs=pl.BlockSpec((rows, width), lambda i, c, e: (i, 0)),
+        ),
+        out_shape=jax.ShapeDtypeStruct((count, width), F32),
+        compiler_params=pltpu.CompilerParams(vmem_limit_bytes=56 * 2**20),
+        cost_estimate=cost(0, 24 * rows * width),
+        name="finish_rows",
     )(core, even, *parts)
 
 
@@ -744,37 +989,51 @@
     def total_halves(self, full):
         return (full, self.over_z(full, 1)) if self.square else (full,)
 
-    def sides(self, sums):
+    def four(self, sums):
+        return list(sums) + [self.over_core(half) for half in sums]
+
+    def sides(self, parts):
+        even = (self.column % 2).astype(jnp.int32)[None]
         if self.square:
-            parts = list(sums) + [self.over_core(half) for half in sums]
-            return finish_sides(self.core_ref, (self.column % 2).astype(jnp.int32)[None], parts)
-        own = sums[0]
-        other = self.over_core(own)
+            return finish_sides(self.core_ref, even, parts)
         first = self.core == 0
-        low, high = jnp.where(first, own, other), jnp.where(first, other, own)
+        low, high = jnp.where(first, *parts), jnp.where(first, *parts[::-1])
         return jnp.concatenate([low[:, : FIRST_HEAD * HDIM], high[:, :OWN]], axis=1).astype(F32)
 
+    def rows(self, parts, count):
+        if self.square:
+            even = (self.column % 2).astype(jnp.int32)[None]
+            return finish_rows(self.core_ref, even, parts, count)
+        first = self.core == 0
+        low, high = jnp.where(first, *parts), jnp.where(first, *parts[::-1])
+        return jnp.concatenate([low, high[2 * low.shape[0] - count :]], axis=0).astype(F32)
+
     def alike(self, array):
+        return self.over_z(array, 2) if self.square else self.total_alike(array)
+
+    def alike_sum(self, array, came):
+        came = jnp.concatenate(came, axis=0)
+        return array + came if self.square else came
+
+    def total_alike(self, array):
+        groups = [
+            [2 * column + core for column in range(even, self.replica_count // 2, 2)]
+            for even in range(2)
+            for core in range(2)
+        ]
+        return lax.psum(array, "replica", axis_index_groups=groups)
+
+    def small_cores(self, array):
+        return array + self.over_core(array) if self.square else lax.psum(array, AXES)
+
+    def small_square(self, array):
         if not self.square:
-            groups = [
-                [2 * column + core for column in range(even, self.replica_count // 2, 2)]
-                for even in range(2)
-                for core in range(2)
-            ]
-            return lax.psum(array, "replica", axis_index_groups=groups)
-        return self.over_z(array, 2)
-
-    def alike_sum(self, array, came):
-        return array + came if self.square else came
-
-    def total_small(self, array):
-        if not self.square:
-            return lax.psum(array, AXES)
-        array = array + self.over_core(array)
+            return array
         array = array + self.over_x(array)
-        array = array + self.over_y(array)
-        array = array + self.over_z(array, 1)
-        return array + self.over_z(array, 2)
+        return array + self.over_y(array)
+
+    def small_columns(self, array, step):
+        return array + self.over_z(array, step) if self.square else array
 
     def owners(self, step, seqs):
         return lambda s, z, c: (seqs * c + (s + step) % seqs, z, s // seqs)
@@ -800,8 +1059,8 @@
         ring = jnp.concatenate((came[::-1] * 2)[: 2 * seqs - 1], axis=1)
         return lax.dynamic_slice_in_dim(ring, (seqs - 1 - at) * count, seqs * count, 1)
 
-    def from_chips(self, half, seqs):
-        count = half.shape[1] // seqs
+    def from_chips(self, pieces):
+        seqs = len(pieces)
         at = self.shard % seqs
         outs = []
         for step in range(seqs):
@@ -811,8 +1070,7 @@
                 for z in range(self.replica_count // 2):
                     for c in range(2):
                         back[route(s, z, c)] = (s, z, c)
-            sent = lax.dynamic_slice_in_dim(half, ((at - step) % seqs) * count, count, 1)
-            outs.append(self.move(sent, lambda s, z, c: back[(s, z, c)]))
+            outs.append(self.move(pieces[step], lambda s, z, c: back[(s, z, c)]))
         if seqs == 2:
             first = at == 0
             return jnp.stack(
@@ -860,8 +1118,6 @@
     strip = ff // shard_count // 4
     first_row = core * FIRST_HEAD * HDIM
     rows_of = functools.partial(lax.dynamic_slice_in_dim, slice_size=OWN, axis=0)
-    half_of = functools.partial(lax.dynamic_slice_in_dim, slice_size=half_len, axis=1)
-    mine, theirs = core * half_len, (1 - core) * half_len
 
     def column(vector):
         return vector[:, None]
@@ -908,9 +1164,8 @@
     else:
         segments_other = moves.over_core(segments)
         events = []
-    tokens = moves.in_half(tokens_came).astype(F32)
-    unit_one, scale_one = norm_parts(tokens)
-    normed_half = (unit_one * column(ln1_gain) + column(ln1_bias)).astype(BF16)
+    at = (moves.shard % seqs).astype(jnp.int32)[None]
+    tokens, normed_half = norm_in(at, tokens_came, column(ln1_gain), column(ln1_bias))
     events = [*events, normed_half]
     home = moves.shard // seqs
     seg = jnp.where(home == core, segments, segments_other)
@@ -925,9 +1180,10 @@
         events = []
     normed_other = moves.over_core(normed_half)
     grad_came = moves.to_chips(out_grad.transpose(1, 2, 0))
-    events = [*events, normed_other, *grad_came]
-
-    ff_piece, normed_other, *grad_came = late([ff_piece, normed_other, *grad_came], events)
+    normed = moves.ordered(normed_half, normed_other)
+    events = [*events, normed, *grad_came]
+
+    ff_piece, normed, *grad_came = late([ff_piece, normed, *grad_came], events)
     if moves.square:
         ff_x, ff_y = moves.over_x(ff_piece), moves.over_y(ff_piece)
         w_qkv, w_out = lay_heads(
@@ -962,9 +1218,8 @@
         (w_out,) = moves.lay([jnp.where(twice[None, :], 0, own).astype(BF16)], ())
         w_up, w_down = moves.lay([ff_piece], (), 2)
         events = []
-    grad_half = moves.in_half(grad_came)
+    grad_half = moves.in_half(late(grad_came, [w_qkv]))
     grad_across = moves.over_z(grad_half, 1)
-    normed = moves.ordered(normed_half, normed_other)
     zeros = jnp.zeros((OWN,), F32)
     joined_bias = jnp.concatenate([rows_of(q_bias, first_row), zeros, rows_of(v_bias, first_row)])
     row_scale = jnp.where(jnp.arange(3 * OWN) < OWN, 0.125, 1.0).astype(F32)
@@ -980,26 +1235,39 @@
         name="project_qkv",
     )
     mixed, lse = attention(seg, joined, [])
-    branch = product(w_out, mixed, "nn", 400, name="project_out")
-    events = [*events, branch, grad_across]
-
-    branch, grad_half, grad_across = late([branch, grad_half, grad_across], events)
+    side = jnp.broadcast_to(core.astype(F32), (width, 1))
+    halves = ((half_len, BF16), (half_len, BF16))
+
+    def by_side(value, at, side_ref):
+        first, second = value[:, :half_len], value[:, half_len:]
+        mine = side_ref[...] == 0
+        return jnp.where(mine, first, second), jnp.where(mine, second, first)
+
+    branch, branch_sent = product(
+        w_out, mixed, "nn", 400, by_side, (side,), halves, name="project_out"
+    )
+    events = [*events, branch_sent, grad_across]
+
+    branch_sent, grad_half, grad_across = late([branch_sent, grad_half, grad_across], events)
+    branch_came = moves.over_core(branch_sent)
     grad_other, grad_far = moves.over_core(grad_half), moves.over_core(grad_across)
-    branch_half = half_of(branch, mine).astype(F32)
-    branch_half = branch_half + moves.over_core(half_of(branch, theirs)).astype(F32)
-    middle = tokens + branch_half + column(out_bias)
-    unit_two, scale_two = norm_parts(middle)
-    norm_half = (unit_two * column(ln2_gain) + column(ln2_bias)).astype(BF16)
+    middle, norm_half = norm_mid(
+        tokens, branch, branch_came, column(out_bias), column(ln2_gain), column(ln2_bias)
+    )
     events = [norm_half, grad_other, grad_far]
+    if moves.square:
+        split = ff_piece.shape[0] // 2
+        ff_x, ff_y = late([ff_x, ff_y], [branch_sent])
+        low_sent, high_sent = ff_y[:split], ff_x[split:]
+        events = [*events, low_sent, high_sent]
     grad_out = [grad_half, grad_across, grad_other, grad_far]
 
     (norm_half,) = late([norm_half], events)
     norm_across = moves.over_z(norm_half, 1)
     norm_other = moves.over_core(norm_half)
     if moves.square:
-        ff_x, ff_y = late([ff_x, ff_y], events)
-        split = ff_piece.shape[0] // 2
-        ff_low, ff_high = moves.over_x(ff_y[:split]), moves.over_y(ff_x[split:])
+        low_sent, high_sent = late([low_sent, high_sent], events)
+        ff_low, ff_high = moves.over_x(low_sent), moves.over_y(high_sent)
         (norm_across,) = late([norm_across], [ff_low, ff_high])
         w_up, w_down = moves.lay((ff_piece, ff_x, ff_y), (ff_low, ff_high), 2)
     norm_far = moves.over_core(norm_across)
@@ -1021,75 +1289,87 @@
         half = value.shape[1] // 2
         return value[:, :half], value[:, half:]
 
-    halves = ((length, BF16), (length, BF16))
+    pairs = ((length, BF16), (length, BF16))
 
     def through_gelu(value, at, slope_ref):
         size = value.shape[1]
         slope_here = slope_ref[:, at * size : (at + 1) * size].astype(F32)
         grad = (value * slope_here).astype(BF16)
-        return grad, lane_sums(grad.astype(F32))
-
-    grad_pre, grad_pre_sums = product(
+        sums = lane_sums(grad.astype(F32))
+        return (grad, None, sums) if at < 2 else (None, grad, sums)
+
+    ff_cut = 896 if width == 1600 else width // 256 * 128
+    down_parts = moves.scatter_first([(grad_out, activ)], ff_cut)
+    down_near = moves.scatter_near(down_parts)
+    pre_here, pre_there, grad_pre_sums = product(
         w_down,
         grad_out,
         "tn",
         256,
         through_gelu,
         (slope,),
-        ((None, BF16), (512, F32)),
+        (*pairs, (512, F32)),
         name="back_down",
-    )
-    ff_cut = 896 if width == 1600 else width // 256 * 128
-    norm_here, norm_there = product(
-        w_up, grad_pre, "tn", 256, in_halves, (), halves, name="back_up"
-    )
+        wait=down_parts[:1],
+    )
+    norm_there = product(w_up, pre_there, "tn", 256, name="back_up")
 
     norm_came = moves.over_core(norm_there)
-    down_parts = moves.scatter_first([(grad_out, activ)], ff_cut, [norm_there])
-    events = [norm_came, down_parts[0]]
+    norm_here = product(
+        w_up, pre_here, "tn", 256, name="back_up", wait=[norm_there, *down_near[1]]
+    )
+    events = [norm_came, norm_here]
 
     norm_came, norm_here = late([norm_came, norm_here], events)
     norm_last = moves.over_z(norm_here[:, half_len:] + norm_came[:, half_len:], 1)
-    down_near = moves.scatter_near(down_parts, events)
-    up_parts = moves.scatter_first([(grad_pre, normed_two)], ff_cut, events)
+    down_far = moves.scatter_far(down_near, events)
     down_here, down_there = product(
-        w_down, activ, "nn", 320, in_halves, (), halves, name="project_down", wait=up_parts[:1]
-    )
-    events = [norm_last, *down_near[1], down_there]
-
-    norm_last, down_there = late([norm_last, down_there], events)
+        w_down, activ, "nn", 320, in_halves, (), pairs, name="project_down", wait=events
+    )
+    up_parts = moves.scatter_first([([pre_here, pre_there], normed_two)], ff_cut, [down_there])
+    events = [norm_last, *down_far[1], up_parts[0]]
+
+    (norm_last,) = late([norm_last], events)
+    grad_middle, grad_branch_half, mid_sums = norm_mid_back(
+        (norm_here, norm_came, norm_last), middle, grad_half, column(ln2_gain), events
+    )
+    (down_part,) = late([moves.scatter_last(down_far, width)], [grad_branch_half])
+    grad_branch = moves.ordered(grad_branch_half, moves.over_core(grad_branch_half))
+    grad_mixed = product(w_out, grad_branch, "tn", OWN, name="back_out", wait=[down_part], share=0.01)
+    upper = to_sixteen(down_part.shape[0] // 2)
+    down_low, down_high = down_part[:upper], down_part[upper:]
+    events = [grad_mixed, down_low, down_high]
+
     up_near = moves.scatter_near(up_parts, events)
+    down_there, down_low, down_high = late([down_there, down_low, down_high], events)
     down_came = moves.over_core(down_there)
-    grad_norm_two = norm_here[:, :half_len].astype(F32) + norm_came[:, :half_len].astype(F32)
-    grad_norm_two = grad_norm_two + norm_last.astype(F32)
-    grad_out_f = grad_half.astype(F32)
-    grad_middle = grad_out_f + norm_back(grad_norm_two, unit_two, scale_two, column(ln2_gain))
-    grad_branch_half = grad_middle.astype(BF16)
-    grad_branch = moves.ordered(grad_branch_half, moves.over_core(grad_branch_half))
-    grad_mixed = product(w_out, grad_branch, "tn", OWN, name="back_out")
-    padded = to_tiles(OWN)
-    out_parts = moves.scatter_first([(grad_branch, mixed)], 512, [grad_mixed])
-    events = [*up_near[1], down_came, grad_mixed, out_parts[0]]
-
-    down_here, down_came = late([down_here, down_came], events)
-    down_last = moves.over_z(down_here[:, half_len:] + down_came[:, half_len:], 1)
-    down_far = moves.scatter_far(down_near, events)
-    out_near = moves.scatter_near(out_parts, events)
+    down_come = [moves.alike(down_low)]
     grad_own = attention_back(seg, joined, mixed, grad_mixed, lse, events).reshape(3 * OWN, length)
-    events = [down_last, *down_far[1], *out_near[1], grad_own]
+    events = [*up_near[1], down_came, down_come[0], grad_own]
 
     (grad_own,) = late([grad_own], events)
     grad_heads = moves.over_core(grad_own)
-    down_part = moves.scatter_last(down_far, width)
-    down_come = moves.alike(down_part)
     up_far = moves.scatter_far(up_near, events)
-    norm_one = product(w_qkv, grad_own, "tn", 256, name="back_qkv", wait=[down_part])
-    events = [grad_heads, *up_far[1], norm_one]
-
-    (grad_heads,) = late([grad_heads], events)
-    out_far = moves.scatter_far(out_near, events)
+    (down_high,) = late([down_high], events)
+    down_come.append(moves.alike(down_high))
+    down_sent = down_here[:, half_len:] + down_came[:, half_len:]
+    padded = to_tiles(OWN)
+    out_parts = moves.scatter_first([(grad_branch, mixed)], 512, events)
+    norm_one, norm_one_sent = product(
+        w_qkv, grad_own, "tn", 256, by_side, (side,), halves, name="back_qkv", wait=out_parts[:1]
+    )
+    events = [grad_heads, *up_far[1], down_come[1], norm_one_sent]
+
+    grad_heads, norm_one_sent = late([grad_heads, norm_one_sent], events)
+    down_sum = moves.alike_sum(down_part, late(down_come, events))
+    down_across = moves.over_z(down_sum, 1)
+    (up_part,) = late([moves.scatter_last(up_far, width)], events)
+    norm_one_came = moves.over_core(norm_one_sent)
+    out_near = moves.scatter_near(out_parts, events)
     if moves.square:
-        grad_joined = join_heads(moves.core_ref, grad_own, grad_heads)
+        grad_rows = join_heads(
+            moves.core_ref, grad_own, grad_heads, counts[0], taken[0], [up_part]
+        )
     else:
         low = jnp.where(core == 0, grad_own, grad_heads)
         high = jnp.where(core == 0, grad_heads, grad_own)
@@ -1104,72 +1384,95 @@
             ],
             axis=0,
         )
-    qkv_parts = moves.scatter_first([(grad_joined, rows_of(normed, first_row))], 512, events)
-    qkv_near = moves.scatter_near(qkv_parts)
-    up_part = moves.scatter_last(up_far, width)
-    down_come, up_part = late([down_come, up_part], [qkv_parts[0]])
-    down_sum = moves.alike_sum(down_part, down_come)
-    down_across = moves.over_z(down_sum, 1)
-    up_come = moves.alike(late([up_part], [down_come])[0])
-    out_part = moves.scatter_last(out_far, padded)
-    events = qkv_near[1]
-
-    qkv_far = moves.scatter_far(qkv_near, events)
-    norm_one, out_part = late([norm_one, out_part], events)
-    norm_one_came = moves.over_core(half_of(norm_one, theirs))
-    out_pair = moves.total_pair(out_part)
-    events = [*qkv_far[1], norm_one_came, down_across, out_pair]
-
-    norm_one, norm_one_came, down_sum = late([norm_one, norm_one_came, down_sum], events)
-    qkv_pair = moves.total_pair(moves.scatter_last(qkv_far, padded))
-    grad_norm_one = half_of(norm_one, mine).astype(F32) + norm_one_came.astype(F32)
-    input_half = grad_middle + norm_back(grad_norm_one, unit_one, scale_one, column(ln1_gain))
-    input_came = moves.from_chips(input_half.astype(BF16), seqs)
-    down_other = moves.over_core(down_sum)
-    events = [qkv_pair, input_came, down_other, up_come]
-
-    result_half = middle + down_here[:, :half_len].astype(F32)
-    result_half = result_half + down_came[:, :half_len].astype(F32) + down_last.astype(F32)
-    result_half = (result_half + column(down_bias)).astype(BF16)
-    up_sum = moves.alike_sum(up_part, up_come)
-    qkv_pair, up_sum, result_half, out_pair, down_across = late(
-        [qkv_pair, up_sum, result_half, out_pair, down_across], events
-    )
-    qkv_full = moves.total_all(qkv_pair)
-    up_across = moves.over_z(up_sum, 1)
-    result = moves.from_chips(result_half, seqs)
-    out_full = moves.total_all(out_pair)
-    down_far_other = moves.over_core(down_across)
-    events = [qkv_full, up_across, out_full, down_far_other]
-
-    qkv_full, out_full, up_across, up_sum, down_far_other = late(
-        [qkv_full, out_full, up_across, up_sum, down_far_other], [*events, result]
-    )
-    qkv_sum = moves.total_halves(qkv_full)
-    out_sum = moves.total_halves(out_full)
-    input_grad = input_came.astype(F32)
-
+        grad_rows = jnp.concatenate(
+            [
+                lax.dynamic_slice_in_dim(
+                    grad_joined, shard * counts[0] + core * (counts[0] - taken[0]), taken[0], 0
+                )
+                for shard in range(shard_count)
+            ],
+            axis=0,
+        )
+    qkv_parts = moves.scatter_first([(grad_rows, normed)], ff_cut, events)
+    up_low, up_high = up_part[:upper], up_part[upper:]
+    events = [qkv_parts[0], norm_one_came, down_across, *out_near[1], up_low, up_high, down_sent]
+
+    qkv_near = moves.scatter_near(qkv_parts, events)
+    down_sent, norm_one_came, up_low, up_high = late(
+        [down_sent, norm_one_came, up_low, up_high], events
+    )
+    up_come = [moves.alike(up_low)]
+    down_last = moves.over_z(down_sent, 1)
+    input_half, in_sums = norm_in_back(
+        (norm_one, norm_one_came), tokens, grad_middle, column(ln1_gain)
+    )
     up_bias_grad = jnp.sum(grad_pre_sums, axis=1).reshape(shard_count, 1, strip)
     up_bias_grad = up_bias_grad * (jnp.arange(4)[None, :, None] == quarter).astype(F32)
     head_sums = jnp.sum(grad_own.astype(F32), axis=1).reshape(3, OWN)
     bias_sums = lax.dynamic_update_slice(
         jnp.zeros((3, width), F32), head_sums, (jnp.int32(0), first_row)
     )
-    small = moves.total_small(
-        jnp.concatenate(
-            [
-                up_bias_grad.reshape(-1),
-                jnp.sum(grad_norm_two * unit_two, axis=1),
-                jnp.sum(grad_norm_two, axis=1),
-                jnp.sum(grad_out_f, axis=1),
-                jnp.sum(grad_branch_half.astype(F32), axis=1),
-                jnp.sum(grad_norm_one * unit_one, axis=1),
-                jnp.sum(grad_norm_one, axis=1),
-                bias_sums[0],
-                bias_sums[2],
-            ]
-        ).reshape(-1, 128)
-    ).reshape(-1)
+    small = jnp.concatenate(
+        [
+            up_bias_grad.reshape(-1),
+            jnp.sum(mid_sums, axis=2).reshape(-1),
+            jnp.sum(in_sums, axis=2).reshape(-1),
+            bias_sums[0],
+            bias_sums[2],
+        ]
+    ).reshape(-1, 128)
+    events = [*qkv_near[1], down_last, up_come[0], input_half, small]
+
+    qkv_far = moves.scatter_far(qkv_near, events)
+    out_far = moves.scatter_far(out_near, events)
+    up_high, down_last, small = late([up_high, down_last, small], events)
+    up_come.append(moves.alike(up_high))
+    small = moves.small_cores(small)
+    tokens_back = results(
+        at, seqs, middle, (down_here, down_came, down_last), column(down_bias), input_half
+    )
+    events = [*qkv_far[1], *out_far[1], up_come[1], small, *tokens_back]
+
+    down_sum, down_across, *tokens_back = late([down_sum, down_across, *tokens_back], events)
+    tokens_came = moves.from_chips(tokens_back)
+    qkv_pair = moves.total_pair(moves.scatter_last(qkv_far, width))
+    out_pair = moves.total_pair(moves.scatter_last(out_far, padded))
+    down_other = moves.over_core(down_sum)
+    down_far_other = moves.over_core(down_across)
+    events = [qkv_pair, out_pair, down_other, down_far_other, tokens_came]
+
+    up_sum = moves.alike_sum(up_part, late(up_come, events))
+    qkv_pair, up_sum, small, down_far_other = late(
+        [qkv_pair, up_sum, small, down_far_other], events
+    )
+    qkv_full = moves.total_all(qkv_pair)
+    up_across = moves.over_z(up_sum, 1)
+    small = moves.small_columns(moves.small_square(small), 1)
+    quarter_ref = quarter.astype(jnp.int32)[None]
+    down_total = finish_down(
+        quarter_ref, [down_sum, down_other, down_across, down_far_other], shard_count
+    )
+    events = [qkv_full, up_across, small, down_total]
+
+    qkv_full, out_pair, up_across, up_sum, small = late(
+        [qkv_full, out_pair, up_across, up_sum, small], events
+    )
+    qkv_sum = moves.total_halves(qkv_full)
+    out_full = moves.total_all(out_pair)
+    small = moves.small_columns(small, 2).reshape(-1)
+    up_parts = [up_sum, moves.over_core(up_sum), up_across, moves.over_core(up_across)]
+    events = [*qkv_sum, out_full, *up_parts]
+
+    (out_full,) = late([out_full], events)
+    out_sum = moves.total_halves(out_full)
+    qkv_sum = moves.four(late(qkv_sum, events))
+    up_total = finish_up(quarter_ref, late(up_parts, events))
+    qkv_total = moves.rows(late(qkv_sum, [up_total]), counts[0])
+    out_sum = moves.four(late(out_sum, [up_total]))
+    out_total = moves.sides(late(out_sum, [qkv_total]))
+    (tokens_came,) = late([tokens_came], [up_total])
+    result, input_grad = tokens_came[:, :width], tokens_came[:, width:].astype(F32)
+
     up_bias_grad, rest = small[:ff], small[ff:]
     (
         ln2_gain_grad,
@@ -1182,23 +1485,15 @@
         v_bias_grad,
     ) = rest.reshape(8, width)
 
-    quarter_ref = quarter.astype(jnp.int32)[None]
-    down_total = finish_down(
-        quarter_ref, [down_sum, down_other, down_across, down_far_other], shard_count
-    )
-    up_total = finish_up(
-        quarter_ref, [up_sum, moves.over_core(up_sum), up_across, moves.over_core(up_across)]
-    )
-
     return (
         result.transpose(2, 0, 1),
         input_grad.transpose(2, 0, 1),
         ln1_gain_grad,
         ln1_bias_grad,
-        moves.sides(qkv_sum),
+        qkv_total,
         q_bias_grad,
         v_bias_grad,
-        moves.sides(out_sum),
+        out_total,
         out_bias_grad,
         ln2_gain_grad,
         ln2_bias_grad,

time: 866 us -> 831 us (0.960)
  waiting for transfers between devices: 324 us -> 268 us
  Pallas kernels: 314 us -> 351 us
  other arithmetic: 86.7 us -> 66.4 us
  local copies, waits for them, and re-layouts: 53.1 us -> 63.6 us
    ppermute x76, waiting for transfers between devices: 324 us -> 268 us  [move(): came = lax.ppermute(array, AXES, pairs)]
    pallas_call x0 -> x6, Pallas kernels: none -> 42 us  [the longest x1 10.9 us: norm_mid_back(): pl.pallas_call(body, grid=(2,), in_specs=column_specs((rows, columns), si...]
    reduce_sum x8 -> x2, other arithmetic: 22 us -> 5.43 us  [the longest x1 2.88 us: shards(): jnp.sum(mid_sums, axis=2).reshape(-1)]
    pallas_call x8 -> x9, Pallas kernels: 122 us -> 127 us  [product(): pl.pallas_call(body, grid=(pl.cdiv(m, block),), in_specs=[left_spec] + [p...]
    unnamed x207 -> x159, local copies, waits for them, and re-layouts: 14 us -> 17.7 us
  transfers between devices with their start and end apart: 76 -> 76, of which waited for: 26 -> 20; matrix products, arithmetic and copies ran while one was open for 13% -> 12% of each run, Pallas kernels for 26% -> 35%
where the time goes in v4:
time: 831 us; the launch traced here: 823 us
  Pallas kernels  351 us (42%)
  waiting for transfers between devices  268 us (32%)
  starting transfers between devices  71.7 us (9%)
  other arithmetic  66.4 us (8%)
  local copies, waits for them, and re-layouts  63.6 us (8%)
    ppermute x76, waiting for transfers between devices, move(): came = lax.ppermute(array, AXES, pairs)  268 us
    pallas_call x9, Pallas kernels, product(): pl.pallas_call(body, grid=(pl.cdiv(m, block),), in_specs=[left_spec] + [p...  127 us
    ppermute x76, starting transfers between devices, move(): came = lax.ppermute(array, AXES, pairs)  71.7 us
    pallas_call x4, Pallas kernels, product_parts(): pl.pallas_call(body, grid_spec=pltpu.PrefetchScalarGridSpec(num_scalar_pr...  63.6 us
    pallas_call x1, Pallas kernels, attention_back(): pl.pallas_call(backward_kernel, grid=(OWN_HEADS,), in_specs=[whole_spec((...  28.8 us
    pallas_call x1, Pallas kernels, attention(): pl.pallas_call(forward_kernel, grid=(OWN_HEADS,), in_specs=[whole_spec((1...  26.6 us
    unnamed x159, local copies, waits for them, and re-layouts  17.7 us
  transfers between devices with their start and end apart: 76, of which 20 were waited for; matrix products, arithmetic and copies ran while one was open for 12% of the time, Pallas kernels for 35%

profile of v4, /device:TPU:1, one launch (start us, length us, event | category | flops | bytes accessed | tf_op | source)
XLA Modules:
  0.0 822.7 jit_solution(12609946617364668855)
XLA Ops:
  24.6 60.3 %collective-permute-done.2 = bf16[1600,256]{1,0:T(8,128)(2,1)} collective-permute-done((bf16[1600,256]{1,0:T(8,128)(2,1)S(1)}, bf16[1600,256]{1,0:T(8,128)(2,1)}, u32[]{:S(2)}, u32[]{:S(2)}) %collective-permute-start.2) | collective-permute-done | bytes 819232 | tf_op jit(solution)/shard_map/ppermute | solution.py:905
  104.2 18.9 %collective-permute-done.6.refs_4_ = bf16[400,1600]{1,0:T(8,128)(2,1)} collective-permute-done((bf16[400,1600]{1,0:T(8,128)(2,1)S(1)}, bf16[400,1600]{1,0:T(8,128)(2,1)}, u32[]{:S(2)}, u32[]{:S(2)}) %collective-permute-start.6) | collective-permute-done | bytes 1280032 | tf_op jit(solution)/shard_map/ppermute | solution.py:905
  153.7 14.6 %lay_heads.1 = (bf16[2496,1600]{1,0:T(8,128)(2,1)}, bf16[1600,832]{1,0:T(8,128)(2,1)}) custom-call(s32[1]{0:T(128)} %bitcast.5.core_ref, s32[4]{0:T(128)} %pad_add_fusion.1.places_ref, bf16[816,1600]{1,0:T(8,128)(2,1)} %pad_maximum_fusion.3.refs_0_, bf16[816,1600]{1,0:T(8,128)(2,1)} %collective-permute-done.refs_1_, ...), custom_call_target="tpu_custom_call" | custom-call | bytes 245760000 | tf_op jit(solution)/shard_map/lay_heads/pallas_call | solution.py:528
  172.3 14.0 %project_qkv.1.q_ref.k_ref.v_ref = bf16[2496,1024]{1,0:T(8,128)(2,1)} custom-call(bf16[2496,1600]{1,0:T(8,128)(2,1)} %get-tuple-element.162.left_ref, bf16[1600,1024]{1,0:T(8,128)(2,1)} %pad_maximum_fusion.refs_12_.refs_0_.refs_1_, f32[2496,1]{1,0:T(8,128)} %broadcast_in_dim.73.refs_1_, f32[2496,1]{1,0:T(8,128)} %fusion.refs_2_), custom_call_target="tpu_custom_call" | custom-call | flops 65431142400 | bytes 131006464 | tf_op jit(solution)/shard_map/project_qkv/pallas_call | solution.py:205
  188.7 26.6 %attention_forward.1 = (bf16[832,1024]{1,0:T(8,128)(2,1)S(1)}, f32[13,1,1024]{2,1,0:T(1,128)S(1)}) custom-call(s32[1,1024]{1,0:T(1,128)S(1)} %bitcast.38, s32[1024,1]{1,0:T(8,128)S(1)} %get-tuple-element.298.seg_col, bf16[2496,1024]{1,0:T(8,128)(2,1)S(1)} %copy-done.9, bf16[2496,1024]{1,0:T(8,128)(2,1)S(1)} %copy-done.9, bf16[2496,1024]{1,0:T(8,128)(2,1)S(1)} %copy-done.9), custom_call_target="tpu_custom_call" | custom-call | flops 111669149696 | bytes 54525952 | tf_op jit(solution)/shard_map/attention_forward/pallas_call | solution.py:128
  243.8 28.6 %collective-permute-done.21.refs_3_ = bf16[400,1600]{1,0:T(8,128)(2,1)S(1)} collective-permute-done((bf16[400,1600]{1,0:T(8,128)(2,1)S(1)}, bf16[400,1600]{1,0:T(8,128)(2,1)S(1)}, u32[]{:S(2)}, u32[]{:S(2)}) %collective-permute-start.21) | collective-permute-done | bytes 1280032 | tf_op jit(solution)/shard_map/ppermute | solution.py:905
  282.1 9.4 %lay.1 = (bf16[1600,1600]{1,0:T(8,128)(2,1)}, bf16[1600,1600]{1,0:T(8,128)(2,1)}) custom-call(s32[4]{0:T(128)} %pad_add_fusion.1.places_ref, bf16[800,1600]{1,0:T(8,128)(2,1)} %pad_maximum_fusion.4.refs_0_, bf16[800,1600]{1,0:T(8,128)(2,1)} %collective-permute-done.16.refs_1_, bf16[800,1600]{1,0:T(8,128)(2,1)} %collective-permute-done.17.refs_2_, ...), custom_call_target="tpu_custom_call" | custom-call | bytes 163840000 | tf_op jit(solution)/shard_map/lay/pallas_call | solution.py:455
  291.5 23.9 %project_up.1 = (bf16[1600,2048]{1,0:T(8,128)(2,1)}, bf16[1600,2048]{1,0:T(8,128)(2,1)}) custom-call(bf16[1600,1600]{1,0:T(8,128)(2,1)} %get-tuple-element.181.left_ref, bf16[1600,512]{1,0:T(8,128)(2,1)} %get-tuple-element.182.refs_0_.refs_2_, bf16[1600,512]{1,0:T(8,128)(2,1)} %collective-permute-done.23.refs_1_.refs_3_, ...), custom_call_target="tpu_custom_call" | custom-call | flops 83886080000 | bytes 145817600 | tf_op jit(solution)/shard_map/project_up/pallas_call | solution.py:205
  315.4 19.5 %product_parts.4 = (bf16[800,896]{1,0:T(8,128)(2,1)}, bf16[800,768]{1,0:T(8,128)(2,1)}, bf16[800,896]{1,0:T(8,128)(2,1)}, bf16[800,768]{1,0:T(8,128)(2,1)}) custom-call(s32[4]{0:T(128)} %pad_add_fusion.order_ref, bf16[1600,512]{1,0:T(8,128)(2,1)} %pad_maximum_fusion.5.refs_5_.refs_0_.refs_4_, bf16[1600,512]{1,0:T(8,128)(2,1)} %collective-permute-done.15.refs_6_.refs_1_, ...), custom_call_target="tpu_custom_call" | custom-call | flops 83886080000 | bytes 93388800 | tf_op jit(solution)/shard_map/product_parts/pallas_call | solution.py:640
  335.9 19.6 %back_down.1 = (bf16[1600,1024]{1,0:T(8,128)(2,1)}, bf16[1600,1024]{1,0:T(8,128)(2,1)}, f32[1600,512]{1,0:T(8,128)}) custom-call(bf16[1600,1600]{1,0:T(8,128)(2,1)} %get-tuple-element.188.left_ref, bf16[1600,512]{1,0:T(8,128)(2,1)} %pad_maximum_fusion.5.refs_5_.refs_0_.refs_4_, bf16[1600,512]{1,0:T(8,128)(2,1)} %collective-permute-done.15.refs_6_.refs_1_, ...), custom_call_target="tpu_custom_call" | custom-call | flops 83886080000 | bytes 145817600 | tf_op jit(solution)/shard_map/back_down/pallas_call | solution.py:205
  355.6 11.4 %back_up.2.refs_1_ = bf16[1600,1024]{1,0:T(8,128)(2,1)} custom-call(bf16[1600,1600]{1,0:T(8,128)(2,1)} %get-tuple-element.181.left_ref, bf16[1600,1024]{1,0:T(8,128)(2,1)} %get-tuple-element.190.refs_0_.refs_1_), custom_call_target="tpu_custom_call" | custom-call | flops 41943040000 | bytes 93388800 | tf_op jit(solution)/shard_map/back_up/pallas_call | solution.py:205
  369.3 11.4 %back_up.3.refs_2_.refs_0_ = bf16[1600,1024]{1,0:T(8,128)(2,1)} custom-call(bf16[1600,1600]{1,0:T(8,128)(2,1)} %get-tuple-element.181.left_ref, bf16[1600,1024]{1,0:T(8,128)(2,1)} %get-tuple-element.191.refs_0_, bf16[1600,1024]{1,0:T(8,128)(2,1)} %back_up.2.refs_1_, bf16[800,896]{1,0:T(8,128)(2,1)} %copy-done.27, bf16[800,768]{1,0:T(8,128)(2,1)} %copy-done.31), custom_call_target="tpu_custom_call" | custom-call | flops 41943040000 | bytes 93388800 | tf_op jit(solution)/shard_map/back_up/pallas_call | solution.py:205
  388.5 17.2 %project_down.1 = (bf16[1600,1024]{1,0:T(8,128)(2,1)}, bf16[1600,1024]{1,0:T(8,128)(2,1)}) custom-call(bf16[1600,1600]{1,0:T(8,128)(2,1)} %get-tuple-element.188.left_ref, bf16[1600,2048]{1,0:T(8,128)(2,1)} %get-tuple-element.184.refs_4_.refs_0_, bf16[1600,1024]{1,0:T(8,128)(2,1)} %copy-done.14, bf16[1600,1024]{1,0:T(8,128)(2,1)} %back_up.3.refs_2_.refs_0_), custom_call_target="tpu_custom_call" | custom-call | flops 83886080000 | bytes 145817600 | tf_op jit(solution)/shard_map/project_down/pallas_call | solution.py:205
  405.7 19.2 %product_parts.5 = (bf16[800,896]{1,0:T(8,128)(2,1)}, bf16[800,768]{1,0:T(8,128)(2,1)}, bf16[800,896]{1,0:T(8,128)(2,1)}, bf16[800,768]{1,0:T(8,128)(2,1)}) custom-call(s32[4]{0:T(128)} %pad_add_fusion.order_ref, bf16[1600,1024]{1,0:T(8,128)(2,1)} %get-tuple-element.191.refs_0_, bf16[1600,1024]{1,0:T(8,128)(2,1)} %get-tuple-element.190.refs_0_.refs_1_, ...), custom_call_target="tpu_custom_call" | custom-call | flops 83886080000 | bytes 93388800 | tf_op jit(solution)/shard_map/product_parts/pallas_call | solution.py:640
  425.0 10.9 %norm_mid_back.1 = (f32[1600,512]{1,0:T(8,128)}, bf16[1600,512]{1,0:T(8,128)(2,1)}, f32[4,1600,128]{2,1,0:T(8,128)}) custom-call(bf16[1600,1024]{1,0:T(8,128)(2,1)} %back_up.3.refs_2_.refs_0_, bf16[1600,1024]{1,0:T(8,128)(2,1)} %copy-done.14, bf16[1600,512]{1,0:T(8,128)(2,1)} %collective-permute-done.31.refs_2_.refs_6_, ...), custom_call_target="tpu_custom_call" | custom-call | bytes 393216000 | tf_op jit(solution)/shard_map/norm_mid_back/pallas_call | solution.py:335
  459.4 28.8 %attention_backward.1 = bf16[3,832,1024]{2,1,0:T(8,128)(2,1)} custom-call(s32[1,1024]{1,0:T(1,128)S(1)} %bitcast.39, s32[1024,1]{1,0:T(8,128)S(1)} %copy-done.4, bf16[2496,1024]{1,0:T(8,128)(2,1)} %project_qkv.1.q_ref.k_ref.v_ref, bf16[2496,1024]{1,0:T(8,128)(2,1)} %project_qkv.1.q_ref.k_ref.v_ref, bf16[2496,1024]{1,0:T(8,128)(2,1)} %project_qkv.1.q_ref.k_ref.v_ref, ...), custom_call_target="tpu_custom_call" | custom-call | flops 279172874240 | bytes 109051904 | tf_op jit(solution)/shard_map/attention_backward/pallas_call | solution.py:150
  504.3 14.8 %back_qkv.1 = (bf16[1600,512]{1,0:T(8,128)(2,1)}, bf16[1600,512]{1,0:T(8,128)(2,1)}) custom-call(bf16[2496,1600]{1,0:T(8,128)(2,1)} %get-tuple-element.162.left_ref, bf16[2496,1024]{1,0:T(8,128)(2,1)} %bitcast.42, f32[1600,1]{1,0:T(8,128)} %broadcast_in_dim.63.refs_1_, bf16[800,512]{1,0:T(8,128)(2,1)} %get-tuple-element.226.refs_2_), custom_call_target="tpu_custom_call" | custom-call | flops 65431142400 | bytes 131006464 | tf_op jit(solution)/shard_map/back_qkv/pallas_call | solution.py:205
  539.6 16.4 %product_parts.7 = (bf16[1216,896]{1,0:T(8,128)(2,1)}, bf16[1216,768]{1,0:T(8,128)(2,1)}, bf16[1216,896]{1,0:T(8,128)(2,1)}, bf16[1216,768]{1,0:T(8,128)(2,1)}) custom-call(s32[4]{0:T(128)} %pad_add_fusion.order_ref, bf16[2432,1024]{1,0:T(8,128)(2,1)} %join_heads.1.refs_0_, bf16[1600,1024]{1,0:T(8,128)(2,1)} %pad_maximum_fusion.refs_12_.refs_0_.refs_1_, ...), custom_call_target="tpu_custom_call" | custom-call | flops 63753420800 | bytes 102105088 | tf_op jit(solution)/shard_map/product_parts/pallas_call | solution.py:640
  577.1 8.8 %norm_in_back.1 = (bf16[1600,512]{1,0:T(8,128)(2,1)}, f32[2,1600,128]{2,1,0:T(8,128)}) custom-call(bf16[1600,512]{1,0:T(8,128)(2,1)} %get-tuple-element.232.refs_0_, bf16[1600,512]{1,0:T(8,128)(2,1)} %copy-done.40, bf16[1600,512]{1,0:T(8,128)(2,1)} %get-tuple-element.176.tokens_ref.refs_2_, f32[1600,512]{1,0:T(8,128)} %get-tuple-element.234.refs_3_, ...), custom_call_target="tpu_custom_call" | custom-call | bytes 393216000 | tf_op jit(solution)/shard_map/norm_in_back/pallas_call | solution.py:375
  590.7 24.7 %collective-permute-done.48 = bf16[208,1600]{1,0:T(8,128)(2,1)} collective-permute-done((bf16[208,1600]{1,0:T(8,128)(2,1)}, bf16[208,1600]{1,0:T(8,128)(2,1)}, u32[]{:S(2)}, u32[]{:S(2)}) %collective-permute-start.48) | collective-permute-done | bytes 665632 | tf_op jit(solution)/shard_map/ppermute | solution.py:905
  639.7 8.8 %collective-permute-done.52.refs_5_ = bf16[400,384]{1,0:T(8,128)(2,1)} collective-permute-done((bf16[400,384]{1,0:T(8,128)(2,1)}, bf16[400,384]{1,0:T(8,128)(2,1)}, u32[]{:S(2)}, u32[]{:S(2)}) %collective-permute-start.52) | collective-permute-done | bytes 307232 | tf_op jit(solution)/shard_map/ppermute | solution.py:905
  670.5 25.7 %collective-permute-done.58 = bf16[200,896]{1,0:T(8,128)(2,1)} collective-permute-done((bf16[200,896]{1,0:T(8,128)(2,1)}, bf16[200,896]{1,0:T(8,128)(2,1)}, u32[]{:S(2)}, u32[]{:S(2)}) %collective-permute-start.58) | collective-permute-done | bytes 358432 | tf_op jit(solution)/shard_map/ppermute | solution.py:905
  725.4 35.9 %collective-permute-done.65 = f32[150,128]{1,0:T(8,128)S(1)} collective-permute-done((f32[150,128]{1,0:T(8,128)S(1)}, f32[150,128]{1,0:T(8,128)S(1)}, u32[]{:S(2)}, u32[]{:S(2)}) %collective-permute-start.65) | collective-permute-done | bytes 76832 | tf_op jit(solution)/shard_map/ppermute | solution.py:905
  765.4 26.6 %collective-permute-done.69 = bf16[200,896]{1,0:T(8,128)(2,1)S(1)} collective-permute-done((bf16[200,896]{1,0:T(8,128)(2,1)S(1)}, bf16[200,896]{1,0:T(8,128)(2,1)S(1)}, u32[]{:S(2)}, u32[]{:S(2)}) %collective-permute-start.69) | collective-permute-done | bytes 358432 | tf_op jit(solution)/shard_map/ppermute | solution.py:905
  (410 shorter events, 324.6 us)
Async XLA Ops:
  4.4 83.3 %collective-permute-start = (bf16[816,1600]{1,0:T(8,128)(2,1)}, bf16[816,1600]{1,0:T(8,128)(2,1)}, u32[]{:S(2)}, u32[]{:S(2)}) collective-permute-start(bf16[816,1600]{1,0:T(8,128)(2,1)} %pad_maximum_fusion.3.refs_0_), channel_id=1, source_target_pairs={{0,8},{1,9},{2,10},{3,11},{4,12},{5,13},{6,14},{7,15},{8,0},{9,1},... | collective-permute-start | bytes 7833608 | tf_op jit(solution)/shard_map/ppermute | solution.py:905
  6.4 81.3 %collective-permute-start.1 = (bf16[816,1600]{1,0:T(8,128)(2,1)}, bf16[816,1600]{1,0:T(8,128)(2,1)}, u32[]{:S(2)}, u32[]{:S(2)}) collective-permute-start(bf16[816,1600]{1,0:T(8,128)(2,1)} %pad_maximum_fusion.3.refs_0_), channel_id=1, source_target_pairs={{0,16},{1,17},{2,18},{3,19},{4,20},{5,21},{6,22},{7,23},{8,24},{9,... | collective-permute-start | bytes 7833608 | tf_op jit(solution)/shard_map/ppermute | solution.py:905
  7.7 80.0 %collective-permute-start.4 = (bf16[816,1600]{1,0:T(8,128)(2,1)}, bf16[816,1600]{1,0:T(8,128)(2,1)}, u32[]{:S(2)}, u32[]{:S(2)}) collective-permute-start(bf16[816,1600]{1,0:T(8,128)(2,1)} %pad_maximum_fusion.3.refs_0_), channel_id=1, source_target_pairs={{0,1},{1,0},{2,3},{3,2},{4,5},{5,4},{6,7},{7,6},{8,9},{9,8},{10,11... | collective-permute-start | bytes 7833608 | tf_op jit(solution)/shard_map/ppermute | solution.py:905
  11.3 73.6 %collective-permute-start.2 = (bf16[1600,256]{1,0:T(8,128)(2,1)S(1)}, bf16[1600,256]{1,0:T(8,128)(2,1)}, u32[]{:S(2)}, u32[]{:S(2)}) collective-permute-start(bf16[1600,256]{1,0:T(8,128)(2,1)S(1)} %get-tuple-element.316), channel_id=1, source_target_pairs={{1,16},{3,18},{5,20},{7,22},{9,24},{11,26},{13,28},{15,30},{16,1},... | collective-permute-start | bytes 2457608 | tf_op jit(solution)/shard_map/ppermute | solution.py:905
  13.3 74.4 %collective-permute-start.3 = (bf16[1600,256]{1,0:T(8,128)(2,1)}, bf16[1600,256]{1,0:T(8,128)(2,1)}, u32[]{:S(2)}, u32[]{:S(2)}) collective-permute-start(bf16[1600,256]{1,0:T(8,128)(2,1)} %get-tuple-element.315), channel_id=1, source_target_pairs={{0,8},{1,24},{2,10},{3,26},{4,12},{5,28},{6,14},{7,30},{8,0},{9,16... | collective-permute-start | bytes 2457608 | tf_op jit(solution)/shard_map/ppermute | solution.py:905
  87.7 35.4 %collective-permute-start.7 = (bf16[816,1600]{1,0:T(8,128)(2,1)}, bf16[816,1600]{1,0:T(8,128)(2,1)}, u32[]{:S(2)}, u32[]{:S(2)}) collective-permute-start(bf16[816,1600]{1,0:T(8,128)(2,1)} %collective-permute-done.refs_1_), channel_id=1, source_target_pairs={{0,1},{1,0},{2,3},{3,2},{4,5},{5,4},{6,7},{7,6},{8,9},{9,8},{10,11... | collective-permute-start | bytes 7833608 | tf_op jit(solution)/shard_map/ppermute | solution.py:905
  87.8 35.3 %collective-permute-start.8 = (bf16[816,1600]{1,0:T(8,128)(2,1)}, bf16[816,1600]{1,0:T(8,128)(2,1)}, u32[]{:S(2)}, u32[]{:S(2)}) collective-permute-start(bf16[816,1600]{1,0:T(8,128)(2,1)} %collective-permute-done.1.refs_2_), channel_id=1, source_target_pairs={{0,1},{1,0},{2,3},{3,2},{4,5},{5,4},{6,7},{7,6},{8,9},{9,8},{10,11... | collective-permute-start | bytes 7833608 | tf_op jit(solution)/shard_map/ppermute | solution.py:905
  152.0 73.0 %collective-permute-start.16 = (bf16[800,1600]{1,0:T(8,128)(2,1)}, bf16[800,1600]{1,0:T(8,128)(2,1)}, u32[]{:S(2)}, u32[]{:S(2)}) collective-permute-start(bf16[800,1600]{1,0:T(8,128)(2,1)} %pad_maximum_fusion.4.refs_0_), channel_id=1, source_target_pairs={{0,8},{1,9},{2,10},{3,11},{4,12},{5,13},{6,14},{7,15},{8,0},{9,1},... | collective-permute-start | bytes 7680008 | tf_op jit(solution)/shard_map/ppermute | solution.py:905
  153.3 71.7 %collective-permute-start.17 = (bf16[800,1600]{1,0:T(8,128)(2,1)}, bf16[800,1600]{1,0:T(8,128)(2,1)}, u32[]{:S(2)}, u32[]{:S(2)}) collective-permute-start(bf16[800,1600]{1,0:T(8,128)(2,1)} %pad_maximum_fusion.4.refs_0_), channel_id=1, source_target_pairs={{0,16},{1,17},{2,18},{3,19},{4,20},{5,21},{6,22},{7,23},{8,24},{9,... | collective-permute-start | bytes 7680008 | tf_op jit(solution)/shard_map/ppermute | solution.py:905
  171.0 54.0 %collective-permute-start.15 = (bf16[1600,512]{1,0:T(8,128)(2,1)}, bf16[1600,512]{1,0:T(8,128)(2,1)}, u32[]{:S(2)}, u32[]{:S(2)}) collective-permute-start(bf16[1600,512]{1,0:T(8,128)(2,1)} %pad_maximum_fusion.5.refs_5_.refs_0_.refs_4_), channel_id=1, source_target_pairs={{0,2},{1,3},{2,0},{3,1},{4,6},{5,7},{6,4},{7,5},{8,10},{9,11},{10,... | collective-permute-start | bytes 4915208 | tf_op jit(solution)/shard_map/ppermute | solution.py:905
  241.6 37.7 %collective-permute-start.23 = (bf16[1600,512]{1,0:T(8,128)(2,1)}, bf16[1600,512]{1,0:T(8,128)(2,1)}, u32[]{:S(2)}, u32[]{:S(2)}) collective-permute-start(bf16[1600,512]{1,0:T(8,128)(2,1)} %get-tuple-element.182.refs_0_.refs_2_), channel_id=1, source_target_pairs={{0,2},{1,3},{2,0},{3,1},{4,6},{5,7},{6,4},{7,5},{8,10},{9,11},{10,... | collective-permute-start | bytes 4915208 | tf_op jit(solution)/shard_map/ppermute | solution.py:905
  242.9 48.6 %collective-permute-start.24 = (bf16[1600,512]{1,0:T(8,128)(2,1)}, bf16[1600,512]{1,0:T(8,128)(2,1)}, u32[]{:S(2)}, u32[]{:S(2)}) collective-permute-start(bf16[1600,512]{1,0:T(8,128)(2,1)} %get-tuple-element.182.refs_0_.refs_2_), channel_id=1, source_target_pairs={{0,1},{1,0},{2,3},{3,2},{4,5},{5,4},{6,7},{7,6},{8,9},{9,8},{10,11... | collective-permute-start | bytes 4915208 | tf_op jit(solution)/shard_map/ppermute | solution.py:905
  384.7 40.2 %collective-permute-start.31 = (bf16[1600,512]{1,0:T(8,128)(2,1)}, bf16[1600,512]{1,0:T(8,128)(2,1)}, u32[]{:S(2)}, u32[]{:S(2)}) collective-permute-start(bf16[1600,512]{1,0:T(8,128)(2,1)} %slice_add_fusion.1), channel_id=1, source_target_pairs={{0,2},{1,3},{2,0},{3,1},{4,6},{5,7},{6,4},{7,5},{8,10},{9,11},{10,... | collective-permute-start | bytes 4915208 | tf_op jit(solution)/shard_map/ppermute | solution.py:905
  385.8 39.1 %collective-permute-start.30 = (bf16[400,768]{1,0:T(8,128)(2,1)}, bf16[400,768]{1,0:T(8,128)(2,1)}, u32[]{:S(2)}, u32[]{:S(2)}) collective-permute-start(bf16[400,768]{1,0:T(8,128)(2,1)} %slice_add_fusion.7), channel_id=1, source_target_pairs={{0,8},{1,9},{2,10},{3,11},{4,12},{5,13},{6,14},{7,15},{8,0},{9,1},... | collective-permute-start | bytes 1843208 | tf_op jit(solution)/shard_map/ppermute | solution.py:905
  387.3 37.7 %collective-permute-start.29 = (bf16[400,896]{1,0:T(8,128)(2,1)}, bf16[400,896]{1,0:T(8,128)(2,1)}, u32[]{:S(2)}, u32[]{:S(2)}) collective-permute-start(bf16[400,896]{1,0:T(8,128)(2,1)} %slice_add_fusion.5), channel_id=1, source_target_pairs={{0,16},{1,17},{2,18},{3,19},{4,20},{5,21},{6,22},{7,23},{8,24},{9,... | collective-permute-start | bytes 2150408 | tf_op jit(solution)/shard_map/ppermute | solution.py:905
  564.2 52.4 %collective-permute-start.46 = (bf16[1216,896]{1,0:T(8,128)(2,1)}, bf16[1216,896]{1,0:T(8,128)(2,1)}, u32[]{:S(2)}, u32[]{:S(2)}) collective-permute-start(bf16[1216,896]{1,0:T(8,128)(2,1)} %get-tuple-element.237), channel_id=1, source_target_pairs={{0,8},{1,9},{2,10},{3,11},{4,12},{5,13},{6,14},{7,15},{8,0},{9,1},... | collective-permute-start | bytes 6537224 | tf_op jit(solution)/shard_map/ppermute | solution.py:905
  564.3 52.2 %collective-permute-start.47 = (bf16[1216,768]{1,0:T(8,128)(2,1)}, bf16[1216,768]{1,0:T(8,128)(2,1)}, u32[]{:S(2)}, u32[]{:S(2)}) collective-permute-start(bf16[1216,768]{1,0:T(8,128)(2,1)} %get-tuple-element.238), channel_id=1, source_target_pairs={{0,16},{1,17},{2,18},{3,19},{4,20},{5,21},{6,22},{7,23},{8,24},{9,... | collective-permute-start | bytes 5603336 | tf_op jit(solution)/shard_map/ppermute | solution.py:905
  565.2 51.3 %collective-permute-start.45 = (bf16[1600,512]{1,0:T(8,128)(2,1)}, bf16[1600,512]{1,0:T(8,128)(2,1)}, u32[]{:S(2)}, u32[]{:S(2)}) collective-permute-start(bf16[1600,512]{1,0:T(8,128)(2,1)} %slice_add_fusion), channel_id=1, source_target_pairs={{0,2},{1,3},{2,0},{3,1},{4,6},{5,7},{6,4},{7,5},{8,10},{9,11},{10,... | collective-permute-start | bytes 4915208 | tf_op jit(solution)/shard_map/ppermute | solution.py:905
  568.8 46.6 %collective-permute-start.48 = (bf16[208,1600]{1,0:T(8,128)(2,1)}, bf16[208,1600]{1,0:T(8,128)(2,1)}, u32[]{:S(2)}, u32[]{:S(2)}) collective-permute-start(bf16[208,1600]{1,0:T(8,128)(2,1)} %slice.124), channel_id=1, source_target_pairs={{0,4},{1,5},{2,6},{3,7},{4,0},{5,1},{6,2},{7,3},{8,12},{9,13},{10,... | collective-permute-start | bytes 1996808 | tf_op jit(solution)/shard_map/ppermute | solution.py:905
  654.1 45.4 %collective-permute-start.55 = (bf16[3200,256]{1,0:T(8,128)(2,1)}, bf16[3200,256]{1,0:T(8,128)(2,1)}, u32[]{:S(2)}, u32[]{:S(2)}) collective-permute-start(bf16[3200,256]{1,0:T(8,128)(2,1)} %get-tuple-element.254), channel_id=1, source_target_pairs={{1,16},{3,18},{5,20},{7,22},{9,24},{11,26},{13,28},{15,30},{16,1},... | collective-permute-start | bytes 4915208 | tf_op jit(solution)/shard_map/ppermute | solution.py:905
  656.8 42.6 %collective-permute-start.56 = (bf16[3200,256]{1,0:T(8,128)(2,1)}, bf16[3200,256]{1,0:T(8,128)(2,1)}, u32[]{:S(2)}, u32[]{:S(2)}) collective-permute-start(bf16[3200,256]{1,0:T(8,128)(2,1)} %get-tuple-element.255), channel_id=1, source_target_pairs={{0,8},{1,24},{2,10},{3,26},{4,12},{5,28},{6,14},{7,30},{8,0},{9,16... | collective-permute-start | bytes 4915208 | tf_op jit(solution)/shard_map/ppermute | solution.py:905
  707.0 54.7 %collective-permute-start.62 = (bf16[400,1600]{1,0:T(8,128)(2,1)S(1)}, bf16[400,1600]{1,0:T(8,128)(2,1)S(1)}, u32[]{:S(2)}, u32[]{:S(2)}) collective-permute-start(bf16[400,1600]{1,0:T(8,128)(2,1)S(1)} %maximum_add_fusion.1.refs_0_), channel_id=1, source_target_pairs={{0,2},{1,3},{2,0},{3,1},{4,6},{5,7},{6,4},{7,5},{8,10},{9,11},{10,... | collective-permute-start | bytes 3840008 | tf_op jit(solution)/shard_map/ppermute | solution.py:905
  707.0 54.3 %collective-permute-start.61 = (bf16[304,1600]{1,0:T(8,128)(2,1)S(1)}, bf16[304,1600]{1,0:T(8,128)(2,1)S(1)}, u32[]{:S(2)}, u32[]{:S(2)}) collective-permute-start(bf16[304,1600]{1,0:T(8,128)(2,1)S(1)} %dynamic-slice_add_fusion), channel_id=1, source_target_pairs={{0,4},{1,5},{2,6},{3,7},{4,0},{5,1},{6,2},{7,3},{8,12},{9,13},{10,... | collective-permute-start | bytes 2918408 | tf_op jit(solution)/shard_map/ppermute | solution.py:905
  716.5 44.8 %collective-permute-start.65 = (f32[150,128]{1,0:T(8,128)S(1)}, f32[150,128]{1,0:T(8,128)S(1)}, u32[]{:S(2)}, u32[]{:S(2)}) collective-permute-start(f32[150,128]{1,0:T(8,128)S(1)} %add.203), channel_id=1, source_target_pairs={{0,2},{1,3},{2,0},{3,1},{4,6},{5,7},{6,4},{7,5},{8,10},{9,11},{10,... | collective-permute-start | bytes 230408 | tf_op jit(solution)/shard_map/ppermute | solution.py:905
  (131 other events, 2014.9 us)

commit v5 on v4

--- a/solution.py
+++ b/solution.py
@@ -468,6 +468,61 @@
         cost_estimate=cost(0, 16 * count * columns),
         name="lay",
     )(places, *pieces)
+
+
+def lay_near(places, near, parts):
+    count, columns = near[0].shape
+    size = count // parts
+
+    def body(places_ref, *refs):
+        for at in range(3):
+
+            @pl.when(pl.program_id(0) == at)
+            def _(at=at):
+                for index, out in enumerate(refs[3:]):
+                    out[...] = refs[at][index * size : (index + 1) * size]
+
+    return pl.pallas_call(
+        body,
+        grid_spec=pltpu.PrefetchScalarGridSpec(
+            num_scalar_prefetch=1,
+            grid=(3,),
+            in_specs=[
+                pl.BlockSpec(piece.shape, lambda i, p: (0, 0), pipeline_mode=pl.Buffered(1))
+                for piece in near
+            ],
+            out_specs=[pl.BlockSpec((size, columns), lambda i, p: (p[i], 0))] * parts,
+        ),
+        out_shape=[jax.ShapeDtypeStruct((4 * size, columns), near[0].dtype)] * parts,
+        compiler_params=PARAMS,
+        cost_estimate=cost(0, 12 * count * columns),
+        name="lay_near",
+    )(places, *near)
+
+
+def lay_far(places, far, laid):
+    parts = len(far)
+    size, columns = far[0].shape
+
+    def body(places_ref, *refs):
+        for ref, out in zip(refs[:parts], refs[2 * parts :]):
+            out[...] = ref[...]
+
+    return pl.pallas_call(
+        body,
+        grid_spec=pltpu.PrefetchScalarGridSpec(
+            num_scalar_prefetch=1,
+            grid=(1,),
+            in_specs=[pl.BlockSpec(piece.shape, lambda i, p: (0, 0)) for piece in far]
+            + [pl.BlockSpec(memory_space=pl.ANY)] * parts,
+            out_specs=[pl.BlockSpec((size, columns), lambda i, p: (p[3], 0))] * parts,
+        ),
+        out_shape=[jax.ShapeDtypeStruct(array.shape, array.dtype) for array in laid],
+        input_output_aliases={1 + parts + index: index for index in range(parts)},
+        compiler_params=PARAMS,
+        cost_estimate=cost(0, 4 * size * columns),
+        name="lay_far",
+    )(places, *far, *laid)
 
 
 def lay_heads(core, places, mine, others, counts, taken, wait):
@@ -689,24 +744,51 @@
     return -(-count // 128) * 128
 
 
-def fold(keep_x, came_x, last_x, keep_y, came_y, last_y, columns):
+def fold(keep_x, came_x, last_x, keep_y, came_y, last_y, columns, even=None):
     rows, cut = last_x.shape
     filled = last_y.shape[1]
     rest = columns - cut
-    block = 400 if rows % 400 == 0 else rows // 2
+    block = 400 if even is None else rows // 2
     steps = rows // block
 
-    def body(*refs):
-        out = refs[6]
+    def fill(refs, out):
         for first, begin, size in ((0, 0, cut), (3, cut, rest)):
             value = refs[first][:, :size].astype(F32) + refs[first + 1][:, :size].astype(F32)
             value = value + refs[first + 2][:, :size].astype(F32)
             out[:, begin : begin + size] = value.astype(BF16)
 
+    def body(*refs):
+        if even is None:
+            fill(refs[:6], refs[6])
+            return
+        mine = pl.program_id(0) == refs[0][0]
+
+        @pl.when(mine)
+        def _():
+            fill(refs[1:7], refs[7])
+
+        @pl.when(jnp.logical_not(mine))
+        def _():
+            fill(refs[1:7], refs[8])
+
     def specs(size):
-        second = pl.BlockSpec((block, size), lambda i: (steps + i, 0))
-        return [second, second, pl.BlockSpec((block, size), lambda i: (i, 0))]
-
+        second = pl.BlockSpec((block, size), lambda i, *_: (steps + i, 0))
+        return [second, second, pl.BlockSpec((block, size), lambda i, *_: (i, 0))]
+
+    if even is not None:
+        return pl.pallas_call(
+            body,
+            grid_spec=pltpu.PrefetchScalarGridSpec(
+                num_scalar_prefetch=1,
+                grid=(2,),
+                in_specs=specs(cut) + specs(filled),
+                out_specs=fixed_specs((block, columns), 2),
+            ),
+            out_shape=[jax.ShapeDtypeStruct((block, columns), BF16)] * 2,
+            compiler_params=PARAMS,
+            cost_estimate=cost(0, 8 * rows * columns, 0.01),
+            name="fold_halves",
+        )(even, keep_x, came_x, last_x, keep_y, came_y, last_y)
     return pl.pallas_call(
         body,
         grid=(steps,),
@@ -951,16 +1033,15 @@
     def scatter_far(self, near, wait=()):
         parts, came = near
         if not self.square:
-            return near, []
+            return near, [], []
         keep_x, keep_y = parts[2:]
         half = keep_x.shape[0] // 2
         came_x, came_y = late(came, wait)
-        last_x = self.over_y(keep_x[:half] + came_x[:half])
-        last_y = self.over_x(keep_y[:half] + came_y[:half])
-        return near, [last_x, last_y]
+        sent_x, sent_y = keep_x[:half] + came_x[:half], keep_y[:half] + came_y[:half]
+        return near, [self.over_y(sent_x), self.over_x(sent_y)], [sent_x, sent_y]
 
     def scatter_last(self, far, columns):
-        (parts, came), last = far
+        (parts, came), last, _ = far
         if not self.square:
             sums = [
                 lax.psum_scatter(part, "shard", scatter_dimension=0, tiled=True) for part in parts
@@ -968,14 +1049,19 @@
             return jnp.concatenate(sums, axis=0)
         return fold(parts[2], came[0], last[0], parts[3], came[1], last[1], columns)
 
-    def total_pair(self, array):
+    def scatter_pair(self, far, columns):
+        (parts, came), last, _ = far
         if not self.square:
-            return array
+            return self.scatter_last(far, columns)
+        even = (self.column % 2).astype(jnp.int32)[None]
+        keep, send = fold(parts[2], came[0], last[0], parts[3], came[1], last[1], columns, even)
+        return keep + self.over_z(send, 1)
+
+    def halves(self, array):
         rows = array.shape[0] // 2
         even = self.column % 2
         keep = lax.dynamic_slice_in_dim(array, even * rows, rows, 0)
-        send = lax.dynamic_slice_in_dim(array, (1 - even) * rows, rows, 0)
-        return keep + self.over_z(send, 1)
+        return keep, lax.dynamic_slice_in_dim(array, (1 - even) * rows, rows, 0)
 
     def total_all(self, pair):
         if not self.square:
@@ -1268,8 +1354,9 @@
     if moves.square:
         low_sent, high_sent = late([low_sent, high_sent], events)
         ff_low, ff_high = moves.over_x(low_sent), moves.over_y(high_sent)
-        (norm_across,) = late([norm_across], [ff_low, ff_high])
-        w_up, w_down = moves.lay((ff_piece, ff_x, ff_y), (ff_low, ff_high), 2)
+        laid = lay_near(moves.places, late([ff_piece, ff_x, ff_y], events), 2)
+        w_up, w_down = lay_far(moves.places, (ff_low, ff_high), laid)
+        (norm_across,) = late([norm_across], [w_up])
     norm_far = moves.over_core(norm_across)
     normed_two = [norm_half, norm_across, norm_other, norm_far]
 
@@ -1353,22 +1440,23 @@
     (down_high,) = late([down_high], events)
     down_come.append(moves.alike(down_high))
     down_sent = down_here[:, half_len:] + down_came[:, half_len:]
+    down_last = [moves.over_z(down_sent[:, : half_len // 2], 1)]
     padded = to_tiles(OWN)
     out_parts = moves.scatter_first([(grad_branch, mixed)], 512, events)
     norm_one, norm_one_sent = product(
         w_qkv, grad_own, "tn", 256, by_side, (side,), halves, name="back_qkv", wait=out_parts[:1]
     )
-    events = [grad_heads, *up_far[1], down_come[1], norm_one_sent]
+    events = [grad_heads, *up_far[1], down_come[1], norm_one_sent, down_last[0]]
 
     grad_heads, norm_one_sent = late([grad_heads, norm_one_sent], events)
     down_sum = moves.alike_sum(down_part, late(down_come, events))
     down_across = moves.over_z(down_sum, 1)
-    (up_part,) = late([moves.scatter_last(up_far, width)], events)
+    down_sent = down_sent[:, half_len // 2 :]
     norm_one_came = moves.over_core(norm_one_sent)
     out_near = moves.scatter_near(out_parts, events)
     if moves.square:
         grad_rows = join_heads(
-            moves.core_ref, grad_own, grad_heads, counts[0], taken[0], [up_part]
+            moves.core_ref, grad_own, grad_heads, counts[0], taken[0], []
         )
     else:
         low = jnp.where(core == 0, grad_own, grad_heads)
@@ -1394,15 +1482,15 @@
             axis=0,
         )
     qkv_parts = moves.scatter_first([(grad_rows, normed)], ff_cut, events)
+    events = [qkv_parts[0], norm_one_came, down_across, *out_near[1], down_sent]
+
+    qkv_near = moves.scatter_near(qkv_parts, events)
+    down_sent, norm_one_came = late([down_sent, norm_one_came], events)
+    up_part = moves.scatter_last(up_far, width)
+    (up_part,) = late([up_part], events)
     up_low, up_high = up_part[:upper], up_part[upper:]
-    events = [qkv_parts[0], norm_one_came, down_across, *out_near[1], up_low, up_high, down_sent]
-
-    qkv_near = moves.scatter_near(qkv_parts, events)
-    down_sent, norm_one_came, up_low, up_high = late(
-        [down_sent, norm_one_came, up_low, up_high], events
-    )
     up_come = [moves.alike(up_low)]
-    down_last = moves.over_z(down_sent, 1)
+    down_last.append(moves.over_z(down_sent, 1))
     input_half, in_sums = norm_in_back(
         (norm_one, norm_one_came), tokens, grad_middle, column(ln1_gain)
     )
@@ -1421,50 +1509,63 @@
             bias_sums[2],
         ]
     ).reshape(-1, 128)
-    events = [*qkv_near[1], down_last, up_come[0], input_half, small]
+    up_low_sum = moves.alike_sum(up_low, up_come)
+    events = [*qkv_near[1], down_last[1], up_low_sum, input_half, small, up_high]
 
     qkv_far = moves.scatter_far(qkv_near, events)
-    out_far = moves.scatter_far(out_near, events)
-    up_high, down_last, small = late([up_high, down_last, small], events)
+    up_high, up_low_sum, small, *down_last = late(
+        [up_high, up_low_sum, small, *down_last], events
+    )
+    down_last = jnp.concatenate(down_last, axis=1)
     up_come.append(moves.alike(up_high))
+    up_across = [moves.over_z(up_low_sum, 1)]
     small = moves.small_cores(small)
     tokens_back = results(
         at, seqs, middle, (down_here, down_came, down_last), column(down_bias), input_half
     )
-    events = [*qkv_far[1], *out_far[1], up_come[1], small, *tokens_back]
-
-    down_sum, down_across, *tokens_back = late([down_sum, down_across, *tokens_back], events)
-    tokens_came = moves.from_chips(tokens_back)
-    qkv_pair = moves.total_pair(moves.scatter_last(qkv_far, width))
-    out_pair = moves.total_pair(moves.scatter_last(out_far, padded))
+    events = [*qkv_far[1], up_come[1], up_across[0], small, *tokens_back]
+
+    down_sum, down_across, small = late([down_sum, down_across, small], events)
+    out_far = moves.scatter_far(out_near, events)
+    small = moves.small_square(small)
+    qkv_pair = moves.scatter_pair(qkv_far, width)
+    out_part = moves.scatter_last(out_far, padded)
     down_other = moves.over_core(down_sum)
     down_far_other = moves.over_core(down_across)
-    events = [qkv_pair, out_pair, down_other, down_far_other, tokens_came]
-
-    up_sum = moves.alike_sum(up_part, late(up_come, events))
-    qkv_pair, up_sum, small, down_far_other = late(
-        [qkv_pair, up_sum, small, down_far_other], events
-    )
+    up_high_sum = moves.alike_sum(up_high, late(up_come[1:], events))
+    out_halves = moves.halves(out_part) if moves.square else [out_part, out_part]
+    events = [qkv_pair, *out_halves, down_other, down_far_other, up_high_sum, small]
+
+    qkv_pair, up_high_sum, down_far_other, *out_halves = late(
+        [qkv_pair, up_high_sum, down_far_other, *out_halves], events
+    )
+    tokens_back = late(tokens_back, events)
     qkv_full = moves.total_all(qkv_pair)
-    up_across = moves.over_z(up_sum, 1)
-    small = moves.small_columns(moves.small_square(small), 1)
+    up_across.append(moves.over_z(up_high_sum, 1))
+    up_sum = jnp.concatenate([up_low_sum, up_high_sum], axis=0)
+    out_pair = out_halves[0]
+    if moves.square:
+        out_pair = out_pair + moves.over_z(out_halves[1], 1)
+    tokens_came = moves.from_chips(tokens_back)
     quarter_ref = quarter.astype(jnp.int32)[None]
     down_total = finish_down(
         quarter_ref, [down_sum, down_other, down_across, down_far_other], shard_count
     )
-    events = [qkv_full, up_across, small, down_total]
-
-    qkv_full, out_pair, up_across, up_sum, small = late(
-        [qkv_full, out_pair, up_across, up_sum, small], events
+    events = [qkv_full, up_across[1], tokens_came, down_total, up_sum, out_pair]
+
+    qkv_full, out_pair, up_sum, small, tokens_came, *up_across = late(
+        [qkv_full, out_pair, up_sum, small, tokens_came, *up_across], events
     )
     qkv_sum = moves.total_halves(qkv_full)
     out_full = moves.total_all(out_pair)
-    small = moves.small_columns(small, 2).reshape(-1)
+    small = moves.small_columns(small, 1)
+    up_across = jnp.concatenate(up_across, axis=0)
     up_parts = [up_sum, moves.over_core(up_sum), up_across, moves.over_core(up_across)]
-    events = [*qkv_sum, out_full, *up_parts]
+    events = [*qkv_sum, out_full, *up_parts, small]
 
     (out_full,) = late([out_full], events)
     out_sum = moves.total_halves(out_full)
+    small = moves.small_columns(late([small], events)[0], 2).reshape(-1)
     qkv_sum = moves.four(late(qkv_sum, events))
     up_total = finish_up(quarter_ref, late(up_parts, events))
     qkv_total = moves.rows(late(qkv_sum, [up_total]), counts[0])

time: 831 us -> 794 us (0.955)
  waiting for transfers between devices: 268 us -> 215 us
  starting transfers between devices: 71.7 us -> 86.8 us
    ppermute x76 -> x78, waiting for transfers between devices: 268 us -> 215 us  [move(): came = lax.ppermute(array, AXES, pairs)]
    ppermute x76 -> x78, starting transfers between devices: 71.7 us -> 86.8 us  [move(): came = lax.ppermute(array, AXES, pairs)]
    unnamed x159 -> x166, local copies, waits for them, and re-layouts: 17.7 us -> 16.2 us
  transfers between devices with their start and end apart: 76 -> 78, of which waited for: 20 -> 21; matrix products, arithmetic and copies ran while one was open for 12% -> 13% of each run, Pallas kernels for 35% -> 37%
where the time goes in v5:
time: 794 us; the launch traced here: 786 us
  Pallas kernels  354 us (45%)
  waiting for transfers between devices  215 us (27%)
  starting transfers between devices  86.8 us (11%)
  other arithmetic  64.6 us (8%)
  local copies, waits for them, and re-layouts  62.9 us (8%)
    ppermute x78, waiting for transfers between devices, move(): came = lax.ppermute(array, AXES, pairs)  215 us
    pallas_call x9, Pallas kernels, product(): pl.pallas_call(body, grid=(pl.cdiv(m, block),), in_specs=[left_spec] + [p...  127 us
    ppermute x78, starting transfers between devices, move(): came = lax.ppermute(array, AXES, pairs)  86.8 us
    pallas_call x4, Pallas kernels, product_parts(): pl.pallas_call(body, grid_spec=pltpu.PrefetchScalarGridSpec(num_scalar_pr...  63.4 us
    pallas_call x1, Pallas kernels, attention_back(): pl.pallas_call(backward_kernel, grid=(OWN_HEADS,), in_specs=[whole_spec((...  28.9 us
    pallas_call x1, Pallas kernels, attention(): pl.pallas_call(forward_kernel, grid=(OWN_HEADS,), in_specs=[whole_spec((1...  26.6 us
    unnamed x166, local copies, waits for them, and re-layouts  16.2 us
  transfers between devices with their start and end apart: 78, of which 21 were waited for; matrix products, arithmetic and copies ran while one was open for 13% of the time, Pallas kernels for 37%

profile of v5, /device:TPU:1, one launch (start us, length us, event | category | flops | bytes accessed | tf_op | source)
XLA Modules:
  0.0 785.7 jit_solution(1351683080858387920)
XLA Ops:
  24.6 60.3 %collective-permute-done.2 = bf16[1600,256]{1,0:T(8,128)(2,1)} collective-permute-done((bf16[1600,256]{1,0:T(8,128)(2,1)S(1)}, bf16[1600,256]{1,0:T(8,128)(2,1)}, u32[]{:S(2)}, u32[]{:S(2)}) %collective-permute-start.2) | collective-permute-done | bytes 819232 | tf_op jit(solution)/shard_map/ppermute | solution.py:987
  104.2 18.9 %collective-permute-done.7.refs_4_ = bf16[400,1600]{1,0:T(8,128)(2,1)} collective-permute-done((bf16[400,1600]{1,0:T(8,128)(2,1)S(1)}, bf16[400,1600]{1,0:T(8,128)(2,1)}, u32[]{:S(2)}, u32[]{:S(2)}) %collective-permute-start.7) | collective-permute-done | bytes 1280032 | tf_op jit(solution)/shard_map/ppermute | solution.py:987
  153.8 14.8 %lay_heads.1 = (bf16[2496,1600]{1,0:T(8,128)(2,1)}, bf16[1600,832]{1,0:T(8,128)(2,1)}) custom-call(s32[1]{0:T(128)} %bitcast.5.core_ref, s32[4]{0:T(128)} %pad_add_fusion.1.places_ref, bf16[816,1600]{1,0:T(8,128)(2,1)} %pad_maximum_fusion.3.refs_0_, bf16[816,1600]{1,0:T(8,128)(2,1)} %collective-permute-done.refs_1_, ...), custom_call_target="tpu_custom_call" | custom-call | bytes 245760000 | tf_op jit(solution)/shard_map/lay_heads/pallas_call | solution.py:583
  172.5 14.0 %project_qkv.1.q_ref.k_ref.v_ref = bf16[2496,1024]{1,0:T(8,128)(2,1)} custom-call(bf16[2496,1600]{1,0:T(8,128)(2,1)} %get-tuple-element.172.left_ref, bf16[1600,1024]{1,0:T(8,128)(2,1)} %pad_maximum_fusion.refs_12_.refs_0_.refs_1_, f32[2496,1]{1,0:T(8,128)} %broadcast_in_dim.74.refs_1_, f32[2496,1]{1,0:T(8,128)} %fusion.refs_2_), custom_call_target="tpu_custom_call" | custom-call | flops 65431142400 | bytes 131006464 | tf_op jit(solution)/shard_map/project_qkv/pallas_call | solution.py:205
  188.9 26.6 %attention_forward.1 = (bf16[832,1024]{1,0:T(8,128)(2,1)S(1)}, f32[13,1,1024]{2,1,0:T(1,128)S(1)}) custom-call(s32[1,1024]{1,0:T(1,128)S(1)} %bitcast.38, s32[1024,1]{1,0:T(8,128)S(1)} %get-tuple-element.320.seg_col, bf16[2496,1024]{1,0:T(8,128)(2,1)S(1)} %copy-done.9, bf16[2496,1024]{1,0:T(8,128)(2,1)S(1)} %copy-done.9, bf16[2496,1024]{1,0:T(8,128)(2,1)S(1)} %copy-done.9), custom_call_target="tpu_custom_call" | custom-call | flops 111669149696 | bytes 54525952 | tf_op jit(solution)/shard_map/attention_forward/pallas_call | solution.py:128
  251.8 20.7 %collective-permute-done.21.refs_0_ = bf16[400,1600]{1,0:T(8,128)(2,1)S(1)} collective-permute-done((bf16[400,1600]{1,0:T(8,128)(2,1)S(1)}, bf16[400,1600]{1,0:T(8,128)(2,1)S(1)}, u32[]{:S(2)}, u32[]{:S(2)}) %collective-permute-start.21) | collective-permute-done | bytes 1280032 | tf_op jit(solution)/shard_map/ppermute | solution.py:987
  283.5 23.9 %project_up.1 = (bf16[1600,2048]{1,0:T(8,128)(2,1)}, bf16[1600,2048]{1,0:T(8,128)(2,1)}) custom-call(bf16[1600,1600]{1,0:T(8,128)(2,1)} %get-tuple-element.197.left_ref, bf16[1600,512]{1,0:T(8,128)(2,1)} %get-tuple-element.199.refs_0_.refs_2_, bf16[1600,512]{1,0:T(8,128)(2,1)} %copy-done.78, bf16[1600,512]{1,0:T(8,128)(2,1)} %collective-permute-done.24.refs_2_.refs_4_, ...), custom_call_target="tpu_custom_call" | custom-call | flops 83886080000 | bytes 145817600 | tf_op jit(solution)/shard_map/project_up/pallas_call | solution.py:205
  307.4 19.5 %product_parts.4 = (bf16[800,896]{1,0:T(8,128)(2,1)}, bf16[800,768]{1,0:T(8,128)(2,1)}, bf16[800,896]{1,0:T(8,128)(2,1)}, bf16[800,768]{1,0:T(8,128)(2,1)}) custom-call(s32[4]{0:T(128)} %pad_add_fusion.order_ref, bf16[1600,512]{1,0:T(8,128)(2,1)} %pad_maximum_fusion.5.refs_5_.refs_0_.refs_4_, bf16[1600,512]{1,0:T(8,128)(2,1)} %collective-permute-done.17.refs_6_.refs_1_, ...), custom_call_target="tpu_custom_call" | custom-call | flops 83886080000 | bytes 93388800 | tf_op jit(solution)/shard_map/product_parts/pallas_call | solution.py:695
  328.1 19.7 %back_down.1 = (bf16[1600,1024]{1,0:T(8,128)(2,1)}, bf16[1600,1024]{1,0:T(8,128)(2,1)}, f32[1600,512]{1,0:T(8,128)}) custom-call(bf16[1600,1600]{1,0:T(8,128)(2,1)} %get-tuple-element.198.left_ref, bf16[1600,512]{1,0:T(8,128)(2,1)} %pad_maximum_fusion.5.refs_5_.refs_0_.refs_4_, bf16[1600,512]{1,0:T(8,128)(2,1)} %collective-permute-done.17.refs_6_.refs_1_, ...), custom_call_target="tpu_custom_call" | custom-call | flops 83886080000 | bytes 145817600 | tf_op jit(solution)/shard_map/back_down/pallas_call | solution.py:205
  347.8 11.4 %back_up.2.refs_1_ = bf16[1600,1024]{1,0:T(8,128)(2,1)} custom-call(bf16[1600,1600]{1,0:T(8,128)(2,1)} %get-tuple-element.197.left_ref, bf16[1600,1024]{1,0:T(8,128)(2,1)} %get-tuple-element.204.refs_0_.refs_1_), custom_call_target="tpu_custom_call" | custom-call | flops 41943040000 | bytes 93388800 | tf_op jit(solution)/shard_map/back_up/pallas_call | solution.py:205
  362.4 11.5 %back_up.3.refs_2_.refs_0_ = bf16[1600,1024]{1,0:T(8,128)(2,1)} custom-call(bf16[1600,1600]{1,0:T(8,128)(2,1)} %get-tuple-element.197.left_ref, bf16[1600,1024]{1,0:T(8,128)(2,1)} %get-tuple-element.205.refs_0_, bf16[1600,1024]{1,0:T(8,128)(2,1)} %back_up.2.refs_1_, bf16[800,896]{1,0:T(8,128)(2,1)} %copy-done.28, bf16[800,768]{1,0:T(8,128)(2,1)} %copy-done.34), custom_call_target="tpu_custom_call" | custom-call | flops 41943040000 | bytes 93388800 | tf_op jit(solution)/shard_map/back_up/pallas_call | solution.py:205
  382.1 17.2 %project_down.1 = (bf16[1600,1024]{1,0:T(8,128)(2,1)}, bf16[1600,1024]{1,0:T(8,128)(2,1)}) custom-call(bf16[1600,1600]{1,0:T(8,128)(2,1)} %get-tuple-element.198.left_ref, bf16[1600,2048]{1,0:T(8,128)(2,1)} %get-tuple-element.202.refs_4_.refs_0_, bf16[1600,1024]{1,0:T(8,128)(2,1)} %copy-done.13, bf16[1600,1024]{1,0:T(8,128)(2,1)} %back_up.3.refs_2_.refs_0_), custom_call_target="tpu_custom_call" | custom-call | flops 83886080000 | bytes 145817600 | tf_op jit(solution)/shard_map/project_down/pallas_call | solution.py:205
  399.3 19.2 %product_parts.5 = (bf16[800,896]{1,0:T(8,128)(2,1)}, bf16[800,768]{1,0:T(8,128)(2,1)}, bf16[800,896]{1,0:T(8,128)(2,1)}, bf16[800,768]{1,0:T(8,128)(2,1)}) custom-call(s32[4]{0:T(128)} %pad_add_fusion.order_ref, bf16[1600,1024]{1,0:T(8,128)(2,1)} %get-tuple-element.205.refs_0_, bf16[1600,1024]{1,0:T(8,128)(2,1)} %get-tuple-element.204.refs_0_.refs_1_, ...), custom_call_target="tpu_custom_call" | custom-call | flops 83886080000 | bytes 93388800 | tf_op jit(solution)/shard_map/product_parts/pallas_call | solution.py:695
  418.9 10.9 %norm_mid_back.1 = (f32[1600,512]{1,0:T(8,128)}, bf16[1600,512]{1,0:T(8,128)(2,1)}, f32[4,1600,128]{2,1,0:T(8,128)}) custom-call(bf16[1600,1024]{1,0:T(8,128)(2,1)} %back_up.3.refs_2_.refs_0_, bf16[1600,1024]{1,0:T(8,128)(2,1)} %copy-done.13, bf16[1600,512]{1,0:T(8,128)(2,1)} %collective-permute-done.29.refs_2_.refs_6_, ...), custom_call_target="tpu_custom_call" | custom-call | bytes 393216000 | tf_op jit(solution)/shard_map/norm_mid_back/pallas_call | solution.py:335
  453.1 28.9 %attention_backward.1 = bf16[3,832,1024]{2,1,0:T(8,128)(2,1)} custom-call(s32[1,1024]{1,0:T(1,128)S(1)} %bitcast.39, s32[1024,1]{1,0:T(8,128)S(1)} %copy-done.4, bf16[2496,1024]{1,0:T(8,128)(2,1)} %project_qkv.1.q_ref.k_ref.v_ref, bf16[2496,1024]{1,0:T(8,128)(2,1)} %project_qkv.1.q_ref.k_ref.v_ref, bf16[2496,1024]{1,0:T(8,128)(2,1)} %project_qkv.1.q_ref.k_ref.v_ref, ...), custom_call_target="tpu_custom_call" | custom-call | flops 279172874240 | bytes 109051904 | tf_op jit(solution)/shard_map/attention_backward/pallas_call | solution.py:150
  493.8 8.4 %product_parts.6 = (bf16[800,512]{1,0:T(8,128)(2,1)}, bf16[800,384]{1,0:T(8,128)(2,1)}, bf16[800,512]{1,0:T(8,128)(2,1)}, bf16[800,384]{1,0:T(8,128)(2,1)}) custom-call(s32[4]{0:T(128)} %pad_add_fusion.order_ref, bf16[1600,1024]{1,0:T(8,128)(2,1)} %pad_maximum_fusion.1.refs_0_, bf16[832,1024]{1,0:T(8,128)(2,1)} %copy-done.7, ...), custom_call_target="tpu_custom_call" | custom-call | flops 21810380800 | bytes 47513600 | tf_op jit(solution)/shard_map/product_parts/pallas_call | solution.py:695
  502.2 14.8 %back_qkv.1 = (bf16[1600,512]{1,0:T(8,128)(2,1)}, bf16[1600,512]{1,0:T(8,128)(2,1)}) custom-call(bf16[2496,1600]{1,0:T(8,128)(2,1)} %get-tuple-element.172.left_ref, bf16[2496,1024]{1,0:T(8,128)(2,1)} %bitcast.41, f32[1600,1]{1,0:T(8,128)} %broadcast_in_dim.65.refs_1_, bf16[800,512]{1,0:T(8,128)(2,1)} %get-tuple-element.243.refs_2_), custom_call_target="tpu_custom_call" | custom-call | flops 65431142400 | bytes 131006464 | tf_op jit(solution)/shard_map/back_qkv/pallas_call | solution.py:205
  531.4 16.3 %product_parts.7 = (bf16[1216,896]{1,0:T(8,128)(2,1)}, bf16[1216,768]{1,0:T(8,128)(2,1)}, bf16[1216,896]{1,0:T(8,128)(2,1)}, bf16[1216,768]{1,0:T(8,128)(2,1)}) custom-call(s32[4]{0:T(128)} %pad_add_fusion.order_ref, bf16[2432,1024]{1,0:T(8,128)(2,1)} %join_heads.1.refs_0_, bf16[1600,1024]{1,0:T(8,128)(2,1)} %pad_maximum_fusion.refs_12_.refs_0_.refs_1_, ...), custom_call_target="tpu_custom_call" | custom-call | flops 63753420800 | bytes 102105088 | tf_op jit(solution)/shard_map/product_parts/pallas_call | solution.py:695
  572.4 8.7 %norm_in_back.1 = (bf16[1600,512]{1,0:T(8,128)(2,1)}, f32[2,1600,128]{2,1,0:T(8,128)}) custom-call(bf16[1600,512]{1,0:T(8,128)(2,1)} %get-tuple-element.249.refs_0_, bf16[1600,512]{1,0:T(8,128)(2,1)} %copy-done.43, bf16[1600,512]{1,0:T(8,128)(2,1)} %get-tuple-element.185.tokens_ref.refs_2_, f32[1600,512]{1,0:T(8,128)} %get-tuple-element.251.refs_3_, ...), custom_call_target="tpu_custom_call" | custom-call | bytes 393216000 | tf_op jit(solution)/shard_map/norm_in_back/pallas_call | solution.py:375
  645.0 8.1 %collective-permute-done.61 = f32[150,128]{1,0:T(8,128)S(1)} collective-permute-done((f32[150,128]{1,0:T(8,128)S(1)}, f32[150,128]{1,0:T(8,128)S(1)}, u32[]{:S(2)}, u32[]{:S(2)}) %collective-permute-start.61) | collective-permute-done | bytes 76832 | tf_op jit(solution)/shard_map/ppermute | solution.py:987
  675.7 8.0 %finish_down.1 = f32[400,6400]{1,0:T(8,128)} custom-call(s32[1]{0:T(128)} %bitcast.22.quarter_ref, bf16[400,1600]{1,0:T(8,128)(2,1)} %copy-done.18, bf16[400,1600]{1,0:T(8,128)(2,1)} %collective-permute-done.59.refs_1_, bf16[400,1600]{1,0:T(8,128)(2,1)} %collective-permute-done.43.refs_2_, bf16[400,1600]{1,0:T(8,128)(2,1)} %collective-permute-done.56.refs_3_), custom_call_target="tpu_custom_call" | custom-call | bytes 122880000 | tf_op jit(solution)/shard_map/finish_down/pallas_call | solution.py:850
  683.8 20.4 %collective-permute-done.63 = bf16[200,896]{1,0:T(8,128)(2,1)S(1)} collective-permute-done((bf16[200,896]{1,0:T(8,128)(2,1)S(1)}, bf16[200,896]{1,0:T(8,128)(2,1)S(1)}, u32[]{:S(2)}, u32[]{:S(2)}) %collective-permute-start.63) | collective-permute-done | bytes 358432 | tf_op jit(solution)/shard_map/ppermute | solution.py:987
  704.3 15.4 %collective-permute-done.62 = bf16[304,1600]{1,0:T(8,128)(2,1)S(1)} collective-permute-done((bf16[304,1600]{1,0:T(8,128)(2,1)S(1)}, bf16[304,1600]{1,0:T(8,128)(2,1)S(1)}, u32[]{:S(2)}, u32[]{:S(2)}) %collective-permute-start.62) | collective-permute-done | bytes 972832 | tf_op jit(solution)/shard_map/ppermute | solution.py:987
  727.1 31.3 %collective-permute-done.71 = f32[150,128]{1,0:T(8,128)S(1)} collective-permute-done((f32[150,128]{1,0:T(8,128)S(1)}, f32[150,128]{1,0:T(8,128)S(1)}, u32[]{:S(2)}, u32[]{:S(2)}) %collective-permute-start.71) | collective-permute-done | bytes 76832 | tf_op jit(solution)/shard_map/ppermute | solution.py:987
  (426 shorter events, 335.0 us)
Async XLA Ops:
  4.4 83.3 %collective-permute-start = (bf16[816,1600]{1,0:T(8,128)(2,1)}, bf16[816,1600]{1,0:T(8,128)(2,1)}, u32[]{:S(2)}, u32[]{:S(2)}) collective-permute-start(bf16[816,1600]{1,0:T(8,128)(2,1)} %pad_maximum_fusion.3.refs_0_), channel_id=1, source_target_pairs={{0,8},{1,9},{2,10},{3,11},{4,12},{5,13},{6,14},{7,15},{8,0},{9,1},... | collective-permute-start | bytes 7833608 | tf_op jit(solution)/shard_map/ppermute | solution.py:987
  6.4 81.3 %collective-permute-start.1 = (bf16[816,1600]{1,0:T(8,128)(2,1)}, bf16[816,1600]{1,0:T(8,128)(2,1)}, u32[]{:S(2)}, u32[]{:S(2)}) collective-permute-start(bf16[816,1600]{1,0:T(8,128)(2,1)} %pad_maximum_fusion.3.refs_0_), channel_id=1, source_target_pairs={{0,16},{1,17},{2,18},{3,19},{4,20},{5,21},{6,22},{7,23},{8,24},{9,... | collective-permute-start | bytes 7833608 | tf_op jit(solution)/shard_map/ppermute | solution.py:987
  7.7 80.0 %collective-permute-start.4 = (bf16[816,1600]{1,0:T(8,128)(2,1)}, bf16[816,1600]{1,0:T(8,128)(2,1)}, u32[]{:S(2)}, u32[]{:S(2)}) collective-permute-start(bf16[816,1600]{1,0:T(8,128)(2,1)} %pad_maximum_fusion.3.refs_0_), channel_id=1, source_target_pairs={{0,1},{1,0},{2,3},{3,2},{4,5},{5,4},{6,7},{7,6},{8,9},{9,8},{10,11... | collective-permute-start | bytes 7833608 | tf_op jit(solution)/shard_map/ppermute | solution.py:987
  11.3 73.6 %collective-permute-start.2 = (bf16[1600,256]{1,0:T(8,128)(2,1)S(1)}, bf16[1600,256]{1,0:T(8,128)(2,1)}, u32[]{:S(2)}, u32[]{:S(2)}) collective-permute-start(bf16[1600,256]{1,0:T(8,128)(2,1)S(1)} %get-tuple-element.340), channel_id=1, source_target_pairs={{1,16},{3,18},{5,20},{7,22},{9,24},{11,26},{13,28},{15,30},{16,1},... | collective-permute-start | bytes 2457608 | tf_op jit(solution)/shard_map/ppermute | solution.py:987
  13.3 74.4 %collective-permute-start.3 = (bf16[1600,256]{1,0:T(8,128)(2,1)}, bf16[1600,256]{1,0:T(8,128)(2,1)}, u32[]{:S(2)}, u32[]{:S(2)}) collective-permute-start(bf16[1600,256]{1,0:T(8,128)(2,1)} %get-tuple-element.339), channel_id=1, source_target_pairs={{0,8},{1,24},{2,10},{3,26},{4,12},{5,28},{6,14},{7,30},{8,0},{9,16... | collective-permute-start | bytes 2457608 | tf_op jit(solution)/shard_map/ppermute | solution.py:987
  87.7 35.4 %collective-permute-start.8 = (bf16[816,1600]{1,0:T(8,128)(2,1)}, bf16[816,1600]{1,0:T(8,128)(2,1)}, u32[]{:S(2)}, u32[]{:S(2)}) collective-permute-start(bf16[816,1600]{1,0:T(8,128)(2,1)} %collective-permute-done.refs_1_), channel_id=1, source_target_pairs={{0,1},{1,0},{2,3},{3,2},{4,5},{5,4},{6,7},{7,6},{8,9},{9,8},{10,11... | collective-permute-start | bytes 7833608 | tf_op jit(solution)/shard_map/ppermute | solution.py:987
  87.8 35.3 %collective-permute-start.9 = (bf16[816,1600]{1,0:T(8,128)(2,1)}, bf16[816,1600]{1,0:T(8,128)(2,1)}, u32[]{:S(2)}, u32[]{:S(2)}) collective-permute-start(bf16[816,1600]{1,0:T(8,128)(2,1)} %collective-permute-done.1.refs_2_), channel_id=1, source_target_pairs={{0,1},{1,0},{2,3},{3,2},{4,5},{5,4},{6,7},{7,6},{8,9},{9,8},{10,11... | collective-permute-start | bytes 7833608 | tf_op jit(solution)/shard_map/ppermute | solution.py:987
  152.0 73.2 %collective-permute-start.15 = (bf16[800,1600]{1,0:T(8,128)(2,1)}, bf16[800,1600]{1,0:T(8,128)(2,1)}, u32[]{:S(2)}, u32[]{:S(2)}) collective-permute-start(bf16[800,1600]{1,0:T(8,128)(2,1)} %pad_maximum_fusion.4.refs_0_), channel_id=1, source_target_pairs={{0,8},{1,9},{2,10},{3,11},{4,12},{5,13},{6,14},{7,15},{8,0},{9,1},... | collective-permute-start | bytes 7680008 | tf_op jit(solution)/shard_map/ppermute | solution.py:987
  153.3 71.9 %collective-permute-start.16 = (bf16[800,1600]{1,0:T(8,128)(2,1)}, bf16[800,1600]{1,0:T(8,128)(2,1)}, u32[]{:S(2)}, u32[]{:S(2)}) collective-permute-start(bf16[800,1600]{1,0:T(8,128)(2,1)} %pad_maximum_fusion.4.refs_0_), channel_id=1, source_target_pairs={{0,16},{1,17},{2,18},{3,19},{4,20},{5,21},{6,22},{7,23},{8,24},{9,... | collective-permute-start | bytes 7680008 | tf_op jit(solution)/shard_map/ppermute | solution.py:987
  171.2 54.0 %collective-permute-start.17 = (bf16[1600,512]{1,0:T(8,128)(2,1)}, bf16[1600,512]{1,0:T(8,128)(2,1)}, u32[]{:S(2)}, u32[]{:S(2)}) collective-permute-start(bf16[1600,512]{1,0:T(8,128)(2,1)} %pad_maximum_fusion.5.refs_5_.refs_0_.refs_4_), channel_id=1, source_target_pairs={{0,2},{1,3},{2,0},{3,1},{4,6},{5,7},{6,4},{7,5},{8,10},{9,11},{10,... | collective-permute-start | bytes 4915208 | tf_op jit(solution)/shard_map/ppermute | solution.py:987
  241.8 37.6 %collective-permute-start.23 = (bf16[1600,512]{1,0:T(8,128)(2,1)}, bf16[1600,512]{1,0:T(8,128)(2,1)S(1)}, u32[]{:S(2)}, u32[]{:S(2)}) collective-permute-start(bf16[1600,512]{1,0:T(8,128)(2,1)} %get-tuple-element.199.refs_0_.refs_2_), channel_id=1, source_target_pairs={{0,2},{1,3},{2,0},{3,1},{4,6},{5,7},{6,4},{7,5},{8,10},{9,11},{10,... | collective-permute-start | bytes 4915208 | tf_op jit(solution)/shard_map/ppermute | solution.py:987
  243.2 39.0 %collective-permute-start.24 = (bf16[1600,512]{1,0:T(8,128)(2,1)}, bf16[1600,512]{1,0:T(8,128)(2,1)}, u32[]{:S(2)}, u32[]{:S(2)}) collective-permute-start(bf16[1600,512]{1,0:T(8,128)(2,1)} %get-tuple-element.199.refs_0_.refs_2_), channel_id=1, source_target_pairs={{0,1},{1,0},{2,3},{3,2},{4,5},{5,4},{6,7},{7,6},{8,9},{9,8},{10,11... | collective-permute-start | bytes 4915208 | tf_op jit(solution)/shard_map/ppermute | solution.py:987
  376.5 42.0 %collective-permute-start.31 = (bf16[400,768]{1,0:T(8,128)(2,1)}, bf16[400,768]{1,0:T(8,128)(2,1)}, u32[]{:S(2)}, u32[]{:S(2)}) collective-permute-start(bf16[400,768]{1,0:T(8,128)(2,1)} %slice_add_fusion.7), channel_id=1, source_target_pairs={{0,8},{1,9},{2,10},{3,11},{4,12},{5,13},{6,14},{7,15},{8,0},{9,1},... | collective-permute-start | bytes 1843208 | tf_op jit(solution)/shard_map/ppermute | solution.py:987
  378.8 39.7 %collective-permute-start.30 = (bf16[400,896]{1,0:T(8,128)(2,1)}, bf16[400,896]{1,0:T(8,128)(2,1)}, u32[]{:S(2)}, u32[]{:S(2)}) collective-permute-start(bf16[400,896]{1,0:T(8,128)(2,1)} %slice_add_fusion.5), channel_id=1, source_target_pairs={{0,16},{1,17},{2,18},{3,19},{4,20},{5,21},{6,22},{7,23},{8,24},{9,... | collective-permute-start | bytes 2150408 | tf_op jit(solution)/shard_map/ppermute | solution.py:987
  381.8 37.1 %collective-permute-start.29 = (bf16[1600,512]{1,0:T(8,128)(2,1)}, bf16[1600,512]{1,0:T(8,128)(2,1)}, u32[]{:S(2)}, u32[]{:S(2)}) collective-permute-start(bf16[1600,512]{1,0:T(8,128)(2,1)} %slice_add_fusion.1), channel_id=1, source_target_pairs={{0,2},{1,3},{2,0},{3,1},{4,6},{5,7},{6,4},{7,5},{8,10},{9,11},{10,... | collective-permute-start | bytes 4915208 | tf_op jit(solution)/shard_map/ppermute | solution.py:987
  448.1 37.2 %collective-permute-start.36 = (bf16[208,1600]{1,0:T(8,128)(2,1)}, bf16[208,1600]{1,0:T(8,128)(2,1)}, u32[]{:S(2)}, u32[]{:S(2)}) collective-permute-start(bf16[208,1600]{1,0:T(8,128)(2,1)} %slice.122.refs_1_), channel_id=1, source_target_pairs={{0,4},{1,5},{2,6},{3,7},{4,0},{5,1},{6,2},{7,3},{8,12},{9,13},{10,... | collective-permute-start | bytes 1996808 | tf_op jit(solution)/shard_map/ppermute | solution.py:987
  450.5 34.8 %collective-permute-start.33 = (bf16[800,896]{1,0:T(8,128)(2,1)}, bf16[800,896]{1,0:T(8,128)(2,1)}, u32[]{:S(2)}, u32[]{:S(2)}) collective-permute-start(bf16[800,896]{1,0:T(8,128)(2,1)} %get-tuple-element.221.refs_9_), channel_id=1, source_target_pairs={{0,8},{1,9},{2,10},{3,11},{4,12},{5,13},{6,14},{7,15},{8,0},{9,1},... | collective-permute-start | bytes 4300808 | tf_op jit(solution)/shard_map/ppermute | solution.py:987
  550.3 46.2 %collective-permute-start.46 = (bf16[1216,896]{1,0:T(8,128)(2,1)}, bf16[1216,896]{1,0:T(8,128)(2,1)}, u32[]{:S(2)}, u32[]{:S(2)}) collective-permute-start(bf16[1216,896]{1,0:T(8,128)(2,1)} %get-tuple-element.245), channel_id=1, source_target_pairs={{0,8},{1,9},{2,10},{3,11},{4,12},{5,13},{6,14},{7,15},{8,0},{9,1},... | collective-permute-start | bytes 6537224 | tf_op jit(solution)/shard_map/ppermute | solution.py:987
  550.4 46.1 %collective-permute-start.47 = (bf16[1216,768]{1,0:T(8,128)(2,1)}, bf16[1216,768]{1,0:T(8,128)(2,1)}, u32[]{:S(2)}, u32[]{:S(2)}) collective-permute-start(bf16[1216,768]{1,0:T(8,128)(2,1)} %get-tuple-element.246), channel_id=1, source_target_pairs={{0,16},{1,17},{2,18},{3,19},{4,20},{5,21},{6,22},{7,23},{8,24},{9,... | collective-permute-start | bytes 5603336 | tf_op jit(solution)/shard_map/ppermute | solution.py:987
  627.9 38.4 %collective-permute-start.56 = (bf16[400,1600]{1,0:T(8,128)(2,1)}, bf16[400,1600]{1,0:T(8,128)(2,1)}, u32[]{:S(2)}, u32[]{:S(2)}) collective-permute-start(bf16[400,1600]{1,0:T(8,128)(2,1)} %collective-permute-done.43.refs_2_), channel_id=1, source_target_pairs={{0,1},{1,0},{2,3},{3,2},{4,5},{5,4},{6,7},{7,6},{8,9},{9,8},{10,11... | collective-permute-start | bytes 3840008 | tf_op jit(solution)/shard_map/ppermute | solution.py:987
  666.3 53.6 %collective-permute-start.64 = (bf16[3200,256]{1,0:T(8,128)(2,1)S(1)}, bf16[3200,256]{1,0:T(8,128)(2,1)S(1)}, u32[]{:S(2)}, u32[]{:S(2)}) collective-permute-start(bf16[3200,256]{1,0:T(8,128)(2,1)S(1)} %copy-done.41), channel_id=1, source_target_pairs={{1,16},{3,18},{5,20},{7,22},{9,24},{11,26},{13,28},{15,30},{16,1},... | collective-permute-start | bytes 4915208 | tf_op jit(solution)/shard_map/ppermute | solution.py:987
  671.8 48.2 %collective-permute-start.65 = (bf16[3200,256]{1,0:T(8,128)(2,1)}, bf16[3200,256]{1,0:T(8,128)(2,1)}, u32[]{:S(2)}, u32[]{:S(2)}) collective-permute-start(bf16[3200,256]{1,0:T(8,128)(2,1)} %get-tuple-element.281), channel_id=1, source_target_pairs={{0,8},{1,24},{2,10},{3,26},{4,12},{5,28},{6,14},{7,30},{8,0},{9,16... | collective-permute-start | bytes 4915208 | tf_op jit(solution)/shard_map/ppermute | solution.py:987
  672.8 46.9 %collective-permute-start.62 = (bf16[304,1600]{1,0:T(8,128)(2,1)S(1)}, bf16[304,1600]{1,0:T(8,128)(2,1)S(1)}, u32[]{:S(2)}, u32[]{:S(2)}) collective-permute-start(bf16[304,1600]{1,0:T(8,128)(2,1)S(1)} %add.189), channel_id=1, source_target_pairs={{0,4},{1,5},{2,6},{3,7},{4,0},{5,1},{6,2},{7,3},{8,12},{9,13},{10,... | collective-permute-start | bytes 2918408 | tf_op jit(solution)/shard_map/ppermute | solution.py:987
  674.6 48.3 %collective-permute-start.66 = (bf16[192,1600]{1,0:T(8,128)(2,1)S(1)}, bf16[192,1600]{1,0:T(8,128)(2,1)}, u32[]{:S(2)}, u32[]{:S(2)}) collective-permute-start(bf16[192,1600]{1,0:T(8,128)(2,1)S(1)} %add.191), channel_id=1, source_target_pairs={{0,2},{1,3},{2,0},{3,1},{4,6},{5,7},{6,4},{7,5},{8,10},{9,11},{10,... | collective-permute-start | bytes 1843208 | tf_op jit(solution)/shard_map/ppermute | solution.py:987
  (136 other events, 1951.4 us)

commit v6 on v5

--- a/solution.py
+++ b/solution.py
@@ -1124,14 +1124,18 @@
     def owners(self, step, seqs):
         return lambda s, z, c: (seqs * c + (s + step) % seqs, z, s // seqs)
 
-    def to_chips(self, local):
-        seqs, _, count = local.shape
-        came = []
-        for step in range(seqs):
-            at = (self.shard + step) % seqs
-            sent = lax.dynamic_index_in_dim(local, at, 0, keepdims=False)
-            came.append(self.move(sent, self.owners(step, seqs)))
-        return came
+    def pieces(self, local):
+        seqs = local.shape[0]
+        return [
+            lax.dynamic_index_in_dim(local, (self.shard + step) % seqs, 0, keepdims=False)
+            for step in range(seqs)
+        ]
+
+    def to_chips(self, pieces):
+        seqs = len(pieces)
+        return [
+            self.move(piece, self.owners(step, seqs)) for step, piece in enumerate(pieces)
+        ]
 
     def in_half(self, came):
         seqs = len(came)
@@ -1215,28 +1219,26 @@
         lax.dynamic_slice_in_dim(weight, core * (count - rows), rows, 0)
         for weight, count, rows in zip((qkv_weight, output_projection_weight), counts, taken)
     ]
-    ff_piece = jnp.concatenate(
-        [
-            lax.dynamic_slice_in_dim(up_weight, quarter * strip, strip, 0),
-            jnp.concatenate(
-                [
-                    lax.dynamic_slice_in_dim(down_weight, (4 * shard + quarter) * strip, strip, 1)
-                    for shard in range(shard_count)
-                ],
-                axis=1,
-            ),
-        ],
-        axis=0,
-    )
+    ff_piece = [
+        lax.dynamic_slice_in_dim(up_weight, quarter * strip, strip, 0),
+        jnp.concatenate(
+            [
+                lax.dynamic_slice_in_dim(down_weight, (4 * shard + quarter) * strip, strip, 1)
+                for shard in range(shard_count)
+            ],
+            axis=1,
+        ),
+    ]
     up_bias_own = lax.dynamic_index_in_dim(
         up_bias.reshape(shard_count, 4, strip), quarter, 1, keepdims=False
     ).reshape(-1)
-    tokens_came = moves.to_chips(hidden_in.transpose(1, 2, 0))
+    tokens_came = moves.to_chips(moves.pieces(hidden_in.transpose(1, 2, 0)))
+    grad_pieces = moves.pieces(out_grad.transpose(1, 2, 0))
     if moves.square:
         heads_piece = jnp.concatenate(mine_of, axis=0)
         heads_x, heads_y = moves.over_x(heads_piece), moves.over_y(heads_piece)
         other_own = moves.over_core(heads_piece)
-        events = [heads_x, heads_y, other_own, *tokens_came, ff_piece]
+        events = [heads_x, heads_y, other_own, *tokens_came, *ff_piece, *grad_pieces]
 
         heads_x, heads_y, segments_sent, *tokens_came = late(
             [heads_x, heads_y, segments, *tokens_came], events
@@ -1257,7 +1259,7 @@
     seg = jnp.where(home == core, segments, segments_other)
     seg = lax.dynamic_index_in_dim(seg, moves.shard % seqs, 1, keepdims=False)
 
-    out_grad, normed_half = late([out_grad, normed_half], events)
+    normed_half, *grad_pieces = late([normed_half, *grad_pieces], events)
     if moves.square:
         heads_low, heads_high = late([heads_low, heads_high], events)
         other_low, other_high = moves.over_core(heads_low), moves.over_core(heads_high)
@@ -1265,13 +1267,15 @@
     else:
         events = []
     normed_other = moves.over_core(normed_half)
-    grad_came = moves.to_chips(out_grad.transpose(1, 2, 0))
+    grad_came = moves.to_chips(grad_pieces)
     normed = moves.ordered(normed_half, normed_other)
     events = [*events, normed, *grad_came]
 
-    ff_piece, normed, *grad_came = late([ff_piece, normed, *grad_came], events)
+    normed, *grad_came = late([normed, *grad_came], events)
+    ff_piece = late(ff_piece, events)
     if moves.square:
-        ff_x, ff_y = moves.over_x(ff_piece), moves.over_y(ff_piece)
+        ff_x = [moves.over_x(piece) for piece in ff_piece]
+        ff_y = [moves.over_y(piece) for piece in ff_piece]
         w_qkv, w_out = lay_heads(
             moves.core_ref,
             moves.places,
@@ -1281,7 +1285,7 @@
             taken,
             events,
         )
-        events = [ff_x, ff_y]
+        events = [*ff_x, *ff_y]
     else:
         (qkv_half,) = moves.lay([mine_of[0]], ())
         qkv_other = moves.over_core(qkv_half)
@@ -1302,7 +1306,7 @@
         twice = (core == 1) & (jnp.arange(OWN) < HDIM)
         own = lax.dynamic_slice_in_dim(output_projection_weight, first_row, OWN, 1)
         (w_out,) = moves.lay([jnp.where(twice[None, :], 0, own).astype(BF16)], ())
-        w_up, w_down = moves.lay([ff_piece], (), 2)
+        (w_up,), (w_down,) = moves.lay(ff_piece[:1], ()), moves.lay(ff_piece[1:], ())
         events = []
     grad_half = moves.in_half(late(grad_came, [w_qkv]))
     grad_across = moves.over_z(grad_half, 1)
@@ -1341,22 +1345,20 @@
         tokens, branch, branch_came, column(out_bias), column(ln2_gain), column(ln2_bias)
     )
     events = [norm_half, grad_other, grad_far]
-    if moves.square:
-        split = ff_piece.shape[0] // 2
-        ff_x, ff_y = late([ff_x, ff_y], [branch_sent])
-        low_sent, high_sent = ff_y[:split], ff_x[split:]
-        events = [*events, low_sent, high_sent]
     grad_out = [grad_half, grad_across, grad_other, grad_far]
 
     (norm_half,) = late([norm_half], events)
     norm_across = moves.over_z(norm_half, 1)
     norm_other = moves.over_core(norm_half)
     if moves.square:
-        low_sent, high_sent = late([low_sent, high_sent], events)
-        ff_low, ff_high = moves.over_x(low_sent), moves.over_y(high_sent)
-        laid = lay_near(moves.places, late([ff_piece, ff_x, ff_y], events), 2)
-        w_up, w_down = lay_far(moves.places, (ff_low, ff_high), laid)
-        (norm_across,) = late([norm_across], [w_up])
+        ff_x, ff_y = late(ff_x, events), late(ff_y, events)
+        ff_low, ff_high = moves.over_x(ff_y[0]), moves.over_y(ff_x[1])
+        laid = [
+            lay_near(moves.places, near, 1) for near in zip(late(ff_piece, events), ff_x, ff_y)
+        ]
+        (w_up,) = lay_far(moves.places, (ff_low,), laid[0])
+        (w_down,) = lay_far(moves.places, (ff_high,), laid[1])
+        (norm_across,) = late([norm_across], [w_up, w_down])
     norm_far = moves.over_core(norm_across)
     normed_two = [norm_half, norm_across, norm_other, norm_far]
 
@@ -1558,21 +1560,21 @@
     )
     qkv_sum = moves.total_halves(qkv_full)
     out_full = moves.total_all(out_pair)
-    small = moves.small_columns(small, 1)
     up_across = jnp.concatenate(up_across, axis=0)
-    up_parts = [up_sum, moves.over_core(up_sum), up_across, moves.over_core(up_across)]
-    events = [*qkv_sum, out_full, *up_parts, small]
+    up_total = finish_up(
+        quarter_ref, [up_sum, moves.over_core(up_sum), up_across, moves.over_core(up_across)]
+    )
+    result, input_grad = tokens_came[:, :width], tokens_came[:, width:].astype(F32)
+    small = moves.small_columns(late([small], [up_total, input_grad])[0], 1)
+    events = [*qkv_sum, out_full, small]
 
     (out_full,) = late([out_full], events)
     out_sum = moves.total_halves(out_full)
     small = moves.small_columns(late([small], events)[0], 2).reshape(-1)
     qkv_sum = moves.four(late(qkv_sum, events))
-    up_total = finish_up(quarter_ref, late(up_parts, events))
-    qkv_total = moves.rows(late(qkv_sum, [up_total]), counts[0])
-    out_sum = moves.four(late(out_sum, [up_total]))
-    out_total = moves.sides(late(out_sum, [qkv_total]))
-    (tokens_came,) = late([tokens_came], [up_total])
-    result, input_grad = tokens_came[:, :width], tokens_came[:, width:].astype(F32)
+    qkv_total = moves.rows(qkv_sum, counts[0])
+    out_sum = [*out_sum[:1], *late(out_sum[1:], [qkv_total])]
+    out_total = moves.sides(moves.four(out_sum))
 
     up_bias_grad, rest = small[:ff], small[ff:]
     (

time: 794 us -> 789 us (level)
    ppermute x78 -> x80, waiting for transfers between devices: 215 us -> 208 us  [move(): came = lax.ppermute(array, AXES, pairs)]
    unnamed x166 -> x170, local copies, waits for them, and re-layouts: 16.2 us -> 18.1 us
    ppermute x78 -> x80, starting transfers between devices: 86.8 us -> 85.9 us  [move(): came = lax.ppermute(array, AXES, pairs)]
  transfers between devices with their start and end apart: 78 -> 80, of which waited for: 21 -> 26; matrix products, arithmetic and copies ran while one was open for 13% -> 12% of each run, Pallas kernels for 37% -> 38%
where the time goes in v6:
time: 789 us; the launch traced here: 781 us
  Pallas kernels  359 us (46%)
  waiting for transfers between devices  208 us (26%)
  starting transfers between devices  85.9 us (11%)
  local copies, waits for them, and re-layouts  65.5 us (8%)
  other arithmetic  61.1 us (8%)
    ppermute x80, waiting for transfers between devices, move(): came = lax.ppermute(array, AXES, pairs)  208 us
    pallas_call x9, Pallas kernels, product(): pl.pallas_call(body, grid=(pl.cdiv(m, block),), in_specs=[left_spec] + [p...  127 us
    ppermute x80, starting transfers between devices, move(): came = lax.ppermute(array, AXES, pairs)  85.9 us
    pallas_call x4, Pallas kernels, product_parts(): pl.pallas_call(body, grid_spec=pltpu.PrefetchScalarGridSpec(num_scalar_pr...  63.3 us
    pallas_call x1, Pallas kernels, attention_back(): pl.pallas_call(backward_kernel, grid=(OWN_HEADS,), in_specs=[whole_spec((...  28.9 us
    pallas_call x1, Pallas kernels, attention(): pl.pallas_call(forward_kernel, grid=(OWN_HEADS,), in_specs=[whole_spec((1...  26.6 us
    unnamed x170, local copies, waits for them, and re-layouts  18.1 us
  transfers between devices with their start and end apart: 80, of which 26 were waited for; matrix products, arithmetic and copies ran while one was open for 12% of the time, Pallas kernels for 38%

profile of v6, /device:TPU:1, one launch (start us, length us, event | category | flops | bytes accessed | tf_op | source)
XLA Modules:
  0.0 780.9 jit_solution(13947525458090382559)
XLA Ops:
  25.2 59.7 %collective-permute-done.2 = bf16[1600,256]{1,0:T(8,128)(2,1)} collective-permute-done((bf16[1600,256]{1,0:T(8,128)(2,1)S(1)}, bf16[1600,256]{1,0:T(8,128)(2,1)}, u32[]{:S(2)}, u32[]{:S(2)}) %collective-permute-start.2) | collective-permute-done | bytes 819232 | tf_op jit(solution)/shard_map/ppermute | solution.py:987
  104.1 18.7 %collective-permute-done.7.refs_4_ = bf16[400,1600]{1,0:T(8,128)(2,1)} collective-permute-done((bf16[400,1600]{1,0:T(8,128)(2,1)S(1)}, bf16[400,1600]{1,0:T(8,128)(2,1)}, u32[]{:S(2)}, u32[]{:S(2)}) %collective-permute-start.7) | collective-permute-done | bytes 1280032 | tf_op jit(solution)/shard_map/ppermute | solution.py:987
  134.6 9.8 %collective-permute-done.13 = bf16[1600,256]{1,0:T(8,128)(2,1)} collective-permute-done((bf16[1600,256]{1,0:T(8,128)(2,1)S(1)}, bf16[1600,256]{1,0:T(8,128)(2,1)}, u32[]{:S(2)}, u32[]{:S(2)}) %collective-permute-start.13) | collective-permute-done | bytes 819232 | tf_op jit(solution)/shard_map/ppermute | solution.py:987
  155.2 14.7 %lay_heads.1 = (bf16[2496,1600]{1,0:T(8,128)(2,1)}, bf16[1600,832]{1,0:T(8,128)(2,1)}) custom-call(s32[1]{0:T(128)} %bitcast.5.core_ref, s32[4]{0:T(128)} %pad_add_fusion.1.places_ref, bf16[816,1600]{1,0:T(8,128)(2,1)} %pad_maximum_fusion.3.refs_0_, bf16[816,1600]{1,0:T(8,128)(2,1)} %collective-permute-done.refs_1_, ...), custom_call_target="tpu_custom_call" | custom-call | bytes 245760000 | tf_op jit(solution)/shard_map/lay_heads/pallas_call | solution.py:583
  173.7 14.0 %project_qkv.1.q_ref.k_ref.v_ref = bf16[2496,1024]{1,0:T(8,128)(2,1)} custom-call(bf16[2496,1600]{1,0:T(8,128)(2,1)} %get-tuple-element.157.left_ref, bf16[1600,1024]{1,0:T(8,128)(2,1)} %pad_maximum_fusion.refs_12_.refs_0_.refs_1_, f32[2496,1]{1,0:T(8,128)} %broadcast_in_dim.74.refs_1_, f32[2496,1]{1,0:T(8,128)} %fusion.refs_2_), custom_call_target="tpu_custom_call" | custom-call | flops 65431142400 | bytes 131006464 | tf_op jit(solution)/shard_map/project_qkv/pallas_call | solution.py:205
  190.2 26.6 %attention_forward.1 = (bf16[832,1024]{1,0:T(8,128)(2,1)S(1)}, f32[13,1,1024]{2,1,0:T(1,128)S(1)}) custom-call(s32[1,1024]{1,0:T(1,128)S(1)} %bitcast.38, s32[1024,1]{1,0:T(8,128)S(1)} %get-tuple-element.288.seg_col, bf16[2496,1024]{1,0:T(8,128)(2,1)S(1)} %copy-done.9, bf16[2496,1024]{1,0:T(8,128)(2,1)S(1)} %copy-done.9, bf16[2496,1024]{1,0:T(8,128)(2,1)S(1)} %copy-done.9), custom_call_target="tpu_custom_call" | custom-call | flops 111669149696 | bytes 54525952 | tf_op jit(solution)/shard_map/attention_forward/pallas_call | solution.py:128
  254.7 16.5 %collective-permute-done.24.refs_0_ = bf16[400,1600]{1,0:T(8,128)(2,1)S(1)} collective-permute-done((bf16[400,1600]{1,0:T(8,128)(2,1)}, bf16[400,1600]{1,0:T(8,128)(2,1)S(1)}, u32[]{:S(2)}, u32[]{:S(2)}) %collective-permute-start.24) | collective-permute-done | bytes 1280032 | tf_op jit(solution)/shard_map/ppermute | solution.py:987
  284.0 23.9 %project_up.1 = (bf16[1600,2048]{1,0:T(8,128)(2,1)}, bf16[1600,2048]{1,0:T(8,128)(2,1)}) custom-call(bf16[1600,1600]{1,0:T(8,128)(2,1)} %lay_far.2.left_ref, bf16[1600,512]{1,0:T(8,128)(2,1)} %get-tuple-element.180.refs_0_.refs_2_, bf16[1600,512]{1,0:T(8,128)(2,1)} %copy-done.79, bf16[1600,512]{1,0:T(8,128)(2,1)} %collective-permute-done.26.refs_2_.refs_4_, ...), custom_call_target="tpu_custom_call" | custom-call | flops 83886080000 | bytes 145817600 | tf_op jit(solution)/shard_map/project_up/pallas_call | solution.py:205
  307.8 19.4 %product_parts.4 = (bf16[800,896]{1,0:T(8,128)(2,1)}, bf16[800,768]{1,0:T(8,128)(2,1)}, bf16[800,896]{1,0:T(8,128)(2,1)}, bf16[800,768]{1,0:T(8,128)(2,1)}) custom-call(s32[4]{0:T(128)} %pad_add_fusion.order_ref, bf16[1600,512]{1,0:T(8,128)(2,1)} %pad_maximum_fusion.4.refs_5_.refs_0_.refs_4_, bf16[1600,512]{1,0:T(8,128)(2,1)} %collective-permute-done.17.refs_6_.refs_1_, ...), custom_call_target="tpu_custom_call" | custom-call | flops 83886080000 | bytes 93388800 | tf_op jit(solution)/shard_map/product_parts/pallas_call | solution.py:695
  330.2 19.6 %back_down.1 = (bf16[1600,1024]{1,0:T(8,128)(2,1)}, bf16[1600,1024]{1,0:T(8,128)(2,1)}, f32[1600,512]{1,0:T(8,128)}) custom-call(bf16[1600,1600]{1,0:T(8,128)(2,1)} %lay_far.3.left_ref, bf16[1600,512]{1,0:T(8,128)(2,1)} %pad_maximum_fusion.4.refs_5_.refs_0_.refs_4_, bf16[1600,512]{1,0:T(8,128)(2,1)} %collective-permute-done.17.refs_6_.refs_1_, ...), custom_call_target="tpu_custom_call" | custom-call | flops 83886080000 | bytes 145817600 | tf_op jit(solution)/shard_map/back_down/pallas_call | solution.py:205
  349.8 11.4 %back_up.2.refs_1_ = bf16[1600,1024]{1,0:T(8,128)(2,1)} custom-call(bf16[1600,1600]{1,0:T(8,128)(2,1)} %lay_far.2.left_ref, bf16[1600,1024]{1,0:T(8,128)(2,1)} %get-tuple-element.185.refs_0_.refs_1_), custom_call_target="tpu_custom_call" | custom-call | flops 41943040000 | bytes 93388800 | tf_op jit(solution)/shard_map/back_up/pallas_call | solution.py:205
  364.4 11.5 %back_up.3.refs_2_.refs_0_ = bf16[1600,1024]{1,0:T(8,128)(2,1)} custom-call(bf16[1600,1600]{1,0:T(8,128)(2,1)} %lay_far.2.left_ref, bf16[1600,1024]{1,0:T(8,128)(2,1)} %get-tuple-element.186.refs_0_, bf16[1600,1024]{1,0:T(8,128)(2,1)} %back_up.2.refs_1_, bf16[800,896]{1,0:T(8,128)(2,1)} %copy-done.28, bf16[800,768]{1,0:T(8,128)(2,1)} %copy-done.34), custom_call_target="tpu_custom_call" | custom-call | flops 41943040000 | bytes 93388800 | tf_op jit(solution)/shard_map/back_up/pallas_call | solution.py:205
  383.3 17.2 %project_down.1 = (bf16[1600,1024]{1,0:T(8,128)(2,1)}, bf16[1600,1024]{1,0:T(8,128)(2,1)}) custom-call(bf16[1600,1600]{1,0:T(8,128)(2,1)} %lay_far.3.left_ref, bf16[1600,2048]{1,0:T(8,128)(2,1)} %get-tuple-element.183.refs_4_.refs_0_, bf16[1600,1024]{1,0:T(8,128)(2,1)} %copy-done.13, bf16[1600,1024]{1,0:T(8,128)(2,1)} %back_up.3.refs_2_.refs_0_), custom_call_target="tpu_custom_call" | custom-call | flops 83886080000 | bytes 145817600 | tf_op jit(solution)/shard_map/project_down/pallas_call | solution.py:205
  400.5 19.2 %product_parts.5 = (bf16[800,896]{1,0:T(8,128)(2,1)}, bf16[800,768]{1,0:T(8,128)(2,1)}, bf16[800,896]{1,0:T(8,128)(2,1)}, bf16[800,768]{1,0:T(8,128)(2,1)}) custom-call(s32[4]{0:T(128)} %pad_add_fusion.order_ref, bf16[1600,1024]{1,0:T(8,128)(2,1)} %get-tuple-element.186.refs_0_, bf16[1600,1024]{1,0:T(8,128)(2,1)} %get-tuple-element.185.refs_0_.refs_1_, ...), custom_call_target="tpu_custom_call" | custom-call | flops 83886080000 | bytes 93388800 | tf_op jit(solution)/shard_map/product_parts/pallas_call | solution.py:695
  419.7 10.9 %norm_mid_back.1 = (f32[1600,512]{1,0:T(8,128)}, bf16[1600,512]{1,0:T(8,128)(2,1)}, f32[4,1600,128]{2,1,0:T(8,128)}) custom-call(bf16[1600,1024]{1,0:T(8,128)(2,1)} %back_up.3.refs_2_.refs_0_, bf16[1600,1024]{1,0:T(8,128)(2,1)} %copy-done.13, bf16[1600,512]{1,0:T(8,128)(2,1)} %collective-permute-done.31.refs_2_.refs_6_, ...), custom_call_target="tpu_custom_call" | custom-call | bytes 393216000 | tf_op jit(solution)/shard_map/norm_mid_back/pallas_call | solution.py:335
  455.1 28.9 %attention_backward.1 = bf16[3,832,1024]{2,1,0:T(8,128)(2,1)} custom-call(s32[1,1024]{1,0:T(1,128)S(1)} %bitcast.39, s32[1024,1]{1,0:T(8,128)S(1)} %copy-done.4, bf16[2496,1024]{1,0:T(8,128)(2,1)} %project_qkv.1.q_ref.k_ref.v_ref, bf16[2496,1024]{1,0:T(8,128)(2,1)} %project_qkv.1.q_ref.k_ref.v_ref, bf16[2496,1024]{1,0:T(8,128)(2,1)} %project_qkv.1.q_ref.k_ref.v_ref, ...), custom_call_target="tpu_custom_call" | custom-call | flops 279172874240 | bytes 109051904 | tf_op jit(solution)/shard_map/attention_backward/pallas_call | solution.py:150
  495.0 8.4 %product_parts.6 = (bf16[800,512]{1,0:T(8,128)(2,1)}, bf16[800,384]{1,0:T(8,128)(2,1)}, bf16[800,512]{1,0:T(8,128)(2,1)}, bf16[800,384]{1,0:T(8,128)(2,1)}) custom-call(s32[4]{0:T(128)} %pad_add_fusion.order_ref, bf16[1600,1024]{1,0:T(8,128)(2,1)} %pad_maximum_fusion.1.refs_0_, bf16[832,1024]{1,0:T(8,128)(2,1)} %copy-done.7, ...), custom_call_target="tpu_custom_call" | custom-call | flops 21810380800 | bytes 47513600 | tf_op jit(solution)/shard_map/product_parts/pallas_call | solution.py:695
  503.4 14.8 %back_qkv.1 = (bf16[1600,512]{1,0:T(8,128)(2,1)}, bf16[1600,512]{1,0:T(8,128)(2,1)}) custom-call(bf16[2496,1600]{1,0:T(8,128)(2,1)} %get-tuple-element.157.left_ref, bf16[2496,1024]{1,0:T(8,128)(2,1)} %bitcast.41, f32[1600,1]{1,0:T(8,128)} %broadcast_in_dim.65.refs_1_, bf16[800,512]{1,0:T(8,128)(2,1)} %get-tuple-element.224.refs_2_), custom_call_target="tpu_custom_call" | custom-call | flops 65431142400 | bytes 131006464 | tf_op jit(solution)/shard_map/back_qkv/pallas_call | solution.py:205
  532.7 16.2 %product_parts.7 = (bf16[1216,896]{1,0:T(8,128)(2,1)}, bf16[1216,768]{1,0:T(8,128)(2,1)}, bf16[1216,896]{1,0:T(8,128)(2,1)}, bf16[1216,768]{1,0:T(8,128)(2,1)}) custom-call(s32[4]{0:T(128)} %pad_add_fusion.order_ref, bf16[2432,1024]{1,0:T(8,128)(2,1)} %join_heads.1.refs_0_, bf16[1600,1024]{1,0:T(8,128)(2,1)} %pad_maximum_fusion.refs_12_.refs_0_.refs_1_, ...), custom_call_target="tpu_custom_call" | custom-call | flops 63753420800 | bytes 102105088 | tf_op jit(solution)/shard_map/product_parts/pallas_call | solution.py:695
  572.8 8.7 %norm_in_back.1 = (bf16[1600,512]{1,0:T(8,128)(2,1)}, f32[2,1600,128]{2,1,0:T(8,128)}) custom-call(bf16[1600,512]{1,0:T(8,128)(2,1)} %get-tuple-element.230.refs_0_, bf16[1600,512]{1,0:T(8,128)(2,1)} %copy-done.42, bf16[1600,512]{1,0:T(8,128)(2,1)} %get-tuple-element.163.tokens_ref.refs_2_, f32[1600,512]{1,0:T(8,128)} %get-tuple-element.232.refs_3_, ...), custom_call_target="tpu_custom_call" | custom-call | bytes 393216000 | tf_op jit(solution)/shard_map/norm_in_back/pallas_call | solution.py:375
  677.1 8.0 %finish_down.1 = f32[400,6400]{1,0:T(8,128)} custom-call(s32[1]{0:T(128)} %bitcast.23.quarter_ref, bf16[400,1600]{1,0:T(8,128)(2,1)} %copy-done.18, bf16[400,1600]{1,0:T(8,128)(2,1)} %collective-permute-done.61.refs_1_, bf16[400,1600]{1,0:T(8,128)(2,1)} %collective-permute-done.45.refs_2_, bf16[400,1600]{1,0:T(8,128)(2,1)} %collective-permute-done.58.refs_3_), custom_call_target="tpu_custom_call" | custom-call | bytes 122880000 | tf_op jit(solution)/shard_map/finish_down/pallas_call | solution.py:850
  685.2 20.4 %collective-permute-done.65 = bf16[200,896]{1,0:T(8,128)(2,1)S(1)} collective-permute-done((bf16[200,896]{1,0:T(8,128)(2,1)S(1)}, bf16[200,896]{1,0:T(8,128)(2,1)S(1)}, u32[]{:S(2)}, u32[]{:S(2)}) %collective-permute-start.65) | collective-permute-done | bytes 358432 | tf_op jit(solution)/shard_map/ppermute | solution.py:987
  705.6 13.9 %collective-permute-done.64 = bf16[304,1600]{1,0:T(8,128)(2,1)S(1)} collective-permute-done((bf16[304,1600]{1,0:T(8,128)(2,1)S(1)}, bf16[304,1600]{1,0:T(8,128)(2,1)S(1)}, u32[]{:S(2)}, u32[]{:S(2)}) %collective-permute-start.64) | collective-permute-done | bytes 972832 | tf_op jit(solution)/shard_map/ppermute | solution.py:987
  736.8 17.8 %collective-permute-done.73 = bf16[200,896]{1,0:T(8,128)(2,1)S(1)} collective-permute-done((bf16[200,896]{1,0:T(8,128)(2,1)S(1)}, bf16[200,896]{1,0:T(8,128)(2,1)S(1)}, u32[]{:S(2)}, u32[]{:S(2)}) %collective-permute-start.73) | collective-permute-done | bytes 358432 | tf_op jit(solution)/shard_map/ppermute | solution.py:987
  (433 shorter events, 348.6 us)
Async XLA Ops:
  4.4 83.3 %collective-permute-start = (bf16[816,1600]{1,0:T(8,128)(2,1)}, bf16[816,1600]{1,0:T(8,128)(2,1)}, u32[]{:S(2)}, u32[]{:S(2)}) collective-permute-start(bf16[816,1600]{1,0:T(8,128)(2,1)} %pad_maximum_fusion.3.refs_0_), channel_id=1, source_target_pairs={{0,8},{1,9},{2,10},{3,11},{4,12},{5,13},{6,14},{7,15},{8,0},{9,1},... | collective-permute-start | bytes 7833608 | tf_op jit(solution)/shard_map/ppermute | solution.py:987
  6.4 81.3 %collective-permute-start.1 = (bf16[816,1600]{1,0:T(8,128)(2,1)}, bf16[816,1600]{1,0:T(8,128)(2,1)}, u32[]{:S(2)}, u32[]{:S(2)}) collective-permute-start(bf16[816,1600]{1,0:T(8,128)(2,1)} %pad_maximum_fusion.3.refs_0_), channel_id=1, source_target_pairs={{0,16},{1,17},{2,18},{3,19},{4,20},{5,21},{6,22},{7,23},{8,24},{9,... | collective-permute-start | bytes 7833608 | tf_op jit(solution)/shard_map/ppermute | solution.py:987
  7.7 80.0 %collective-permute-start.4 = (bf16[816,1600]{1,0:T(8,128)(2,1)}, bf16[816,1600]{1,0:T(8,128)(2,1)}, u32[]{:S(2)}, u32[]{:S(2)}) collective-permute-start(bf16[816,1600]{1,0:T(8,128)(2,1)} %pad_maximum_fusion.3.refs_0_), channel_id=1, source_target_pairs={{0,1},{1,0},{2,3},{3,2},{4,5},{5,4},{6,7},{7,6},{8,9},{9,8},{10,11... | collective-permute-start | bytes 7833608 | tf_op jit(solution)/shard_map/ppermute | solution.py:987
  11.3 73.6 %collective-permute-start.2 = (bf16[1600,256]{1,0:T(8,128)(2,1)S(1)}, bf16[1600,256]{1,0:T(8,128)(2,1)}, u32[]{:S(2)}, u32[]{:S(2)}) collective-permute-start(bf16[1600,256]{1,0:T(8,128)(2,1)S(1)} %get-tuple-element.308), channel_id=1, source_target_pairs={{1,16},{3,18},{5,20},{7,22},{9,24},{11,26},{13,28},{15,30},{16,1},... | collective-permute-start | bytes 2457608 | tf_op jit(solution)/shard_map/ppermute | solution.py:987
  13.3 74.4 %collective-permute-start.3 = (bf16[1600,256]{1,0:T(8,128)(2,1)}, bf16[1600,256]{1,0:T(8,128)(2,1)S(1)}, u32[]{:S(2)}, u32[]{:S(2)}) collective-permute-start(bf16[1600,256]{1,0:T(8,128)(2,1)} %get-tuple-element.307), channel_id=1, source_target_pairs={{0,8},{1,24},{2,10},{3,26},{4,12},{5,28},{6,14},{7,30},{8,0},{9,16... | collective-permute-start | bytes 2457608 | tf_op jit(solution)/shard_map/ppermute | solution.py:987
  152.2 74.2 %collective-permute-start.15 = (bf16[400,1600]{1,0:T(8,128)(2,1)}, bf16[400,1600]{1,0:T(8,128)(2,1)}, u32[]{:S(2)}, u32[]{:S(2)}) collective-permute-start(bf16[400,1600]{1,0:T(8,128)(2,1)} %constant_dynamic-slice_fusion.7.refs_0_), channel_id=1, source_target_pairs={{0,16},{1,17},{2,18},{3,19},{4,20},{5,21},{6,22},{7,23},{8,24},{9,... | collective-permute-start | bytes 3840008 | tf_op jit(solution)/shard_map/ppermute | solution.py:987
  152.3 74.2 %collective-permute-start.18 = (bf16[400,1600]{1,0:T(8,128)(2,1)}, bf16[400,1600]{1,0:T(8,128)(2,1)}, u32[]{:S(2)}, u32[]{:S(2)}) collective-permute-start(bf16[400,1600]{1,0:T(8,128)(2,1)} %constant_dynamic-slice_fusion.7.refs_0_), channel_id=1, source_target_pairs={{0,8},{1,9},{2,10},{3,11},{4,12},{5,13},{6,14},{7,15},{8,0},{9,1},... | collective-permute-start | bytes 3840008 | tf_op jit(solution)/shard_map/ppermute | solution.py:987
  153.6 72.9 %collective-permute-start.16 = (bf16[400,1600]{1,0:T(8,128)(2,1)}, bf16[400,1600]{1,0:T(8,128)(2,1)}, u32[]{:S(2)}, u32[]{:S(2)}) collective-permute-start(bf16[400,1600]{1,0:T(8,128)(2,1)} %concatenate.34.refs_0_), channel_id=1, source_target_pairs={{0,16},{1,17},{2,18},{3,19},{4,20},{5,21},{6,22},{7,23},{8,24},{9,... | collective-permute-start | bytes 3840008 | tf_op jit(solution)/shard_map/ppermute | solution.py:987
  155.0 71.5 %collective-permute-start.19 = (bf16[400,1600]{1,0:T(8,128)(2,1)}, bf16[400,1600]{1,0:T(8,128)(2,1)}, u32[]{:S(2)}, u32[]{:S(2)}) collective-permute-start(bf16[400,1600]{1,0:T(8,128)(2,1)} %concatenate.34.refs_0_), channel_id=1, source_target_pairs={{0,8},{1,9},{2,10},{3,11},{4,12},{5,13},{6,14},{7,15},{8,0},{9,1},... | collective-permute-start | bytes 3840008 | tf_op jit(solution)/shard_map/ppermute | solution.py:987
  172.4 54.1 %collective-permute-start.17 = (bf16[1600,512]{1,0:T(8,128)(2,1)}, bf16[1600,512]{1,0:T(8,128)(2,1)}, u32[]{:S(2)}, u32[]{:S(2)}) collective-permute-start(bf16[1600,512]{1,0:T(8,128)(2,1)} %pad_maximum_fusion.4.refs_5_.refs_0_.refs_4_), channel_id=1, source_target_pairs={{0,2},{1,3},{2,0},{3,1},{4,6},{5,7},{6,4},{7,5},{8,10},{9,11},{10,... | collective-permute-start | bytes 4915208 | tf_op jit(solution)/shard_map/ppermute | solution.py:987
  240.0 39.7 %collective-permute-start.25 = (bf16[1600,512]{1,0:T(8,128)(2,1)}, bf16[1600,512]{1,0:T(8,128)(2,1)S(1)}, u32[]{:S(2)}, u32[]{:S(2)}) collective-permute-start(bf16[1600,512]{1,0:T(8,128)(2,1)} %get-tuple-element.180.refs_0_.refs_2_), channel_id=1, source_target_pairs={{0,2},{1,3},{2,0},{3,1},{4,6},{5,7},{6,4},{7,5},{8,10},{9,11},{10,... | collective-permute-start | bytes 4915208 | tf_op jit(solution)/shard_map/ppermute | solution.py:987
  243.2 39.5 %collective-permute-start.26 = (bf16[1600,512]{1,0:T(8,128)(2,1)}, bf16[1600,512]{1,0:T(8,128)(2,1)}, u32[]{:S(2)}, u32[]{:S(2)}) collective-permute-start(bf16[1600,512]{1,0:T(8,128)(2,1)} %get-tuple-element.180.refs_0_.refs_2_), channel_id=1, source_target_pairs={{0,1},{1,0},{2,3},{3,2},{4,5},{5,4},{6,7},{7,6},{8,9},{9,8},{10,11... | collective-permute-start | bytes 4915208 | tf_op jit(solution)/shard_map/ppermute | solution.py:987
  378.6 41.1 %collective-permute-start.33 = (bf16[400,768]{1,0:T(8,128)(2,1)}, bf16[400,768]{1,0:T(8,128)(2,1)}, u32[]{:S(2)}, u32[]{:S(2)}) collective-permute-start(bf16[400,768]{1,0:T(8,128)(2,1)} %slice_add_fusion.7), channel_id=1, source_target_pairs={{0,8},{1,9},{2,10},{3,11},{4,12},{5,13},{6,14},{7,15},{8,0},{9,1},... | collective-permute-start | bytes 1843208 | tf_op jit(solution)/shard_map/ppermute | solution.py:987
  380.6 39.1 %collective-permute-start.32 = (bf16[400,896]{1,0:T(8,128)(2,1)}, bf16[400,896]{1,0:T(8,128)(2,1)}, u32[]{:S(2)}, u32[]{:S(2)}) collective-permute-start(bf16[400,896]{1,0:T(8,128)(2,1)} %slice_add_fusion.5), channel_id=1, source_target_pairs={{0,16},{1,17},{2,18},{3,19},{4,20},{5,21},{6,22},{7,23},{8,24},{9,... | collective-permute-start | bytes 2150408 | tf_op jit(solution)/shard_map/ppermute | solution.py:987
  382.0 37.7 %collective-permute-start.31 = (bf16[1600,512]{1,0:T(8,128)(2,1)}, bf16[1600,512]{1,0:T(8,128)(2,1)}, u32[]{:S(2)}, u32[]{:S(2)}) collective-permute-start(bf16[1600,512]{1,0:T(8,128)(2,1)} %slice_add_fusion.1), channel_id=1, source_target_pairs={{0,2},{1,3},{2,0},{3,1},{4,6},{5,7},{6,4},{7,5},{8,10},{9,11},{10,... | collective-permute-start | bytes 4915208 | tf_op jit(solution)/shard_map/ppermute | solution.py:987
  449.4 38.9 %collective-permute-start.38 = (bf16[208,1600]{1,0:T(8,128)(2,1)}, bf16[208,1600]{1,0:T(8,128)(2,1)}, u32[]{:S(2)}, u32[]{:S(2)}) collective-permute-start(bf16[208,1600]{1,0:T(8,128)(2,1)} %slice.114.refs_1_), channel_id=1, source_target_pairs={{0,4},{1,5},{2,6},{3,7},{4,0},{5,1},{6,2},{7,3},{8,12},{9,13},{10,... | collective-permute-start | bytes 1996808 | tf_op jit(solution)/shard_map/ppermute | solution.py:987
  451.7 36.6 %collective-permute-start.35 = (bf16[800,896]{1,0:T(8,128)(2,1)}, bf16[800,896]{1,0:T(8,128)(2,1)}, u32[]{:S(2)}, u32[]{:S(2)}) collective-permute-start(bf16[800,896]{1,0:T(8,128)(2,1)} %get-tuple-element.202.refs_9_), channel_id=1, source_target_pairs={{0,8},{1,9},{2,10},{3,11},{4,12},{5,13},{6,14},{7,15},{8,0},{9,1},... | collective-permute-start | bytes 4300808 | tf_op jit(solution)/shard_map/ppermute | solution.py:987
  452.1 36.2 %collective-permute-start.36 = (bf16[800,768]{1,0:T(8,128)(2,1)}, bf16[800,768]{1,0:T(8,128)(2,1)}, u32[]{:S(2)}, u32[]{:S(2)}) collective-permute-start(bf16[800,768]{1,0:T(8,128)(2,1)} %get-tuple-element.203), channel_id=1, source_target_pairs={{0,16},{1,17},{2,18},{3,19},{4,20},{5,21},{6,22},{7,23},{8,24},{9,... | collective-permute-start | bytes 3686408 | tf_op jit(solution)/shard_map/ppermute | solution.py:987
  551.8 46.3 %collective-permute-start.48 = (bf16[1216,896]{1,0:T(8,128)(2,1)}, bf16[1216,896]{1,0:T(8,128)(2,1)}, u32[]{:S(2)}, u32[]{:S(2)}) collective-permute-start(bf16[1216,896]{1,0:T(8,128)(2,1)} %get-tuple-element.226), channel_id=1, source_target_pairs={{0,8},{1,9},{2,10},{3,11},{4,12},{5,13},{6,14},{7,15},{8,0},{9,1},... | collective-permute-start | bytes 6537224 | tf_op jit(solution)/shard_map/ppermute | solution.py:987
  552.8 44.7 %collective-permute-start.49 = (bf16[1216,768]{1,0:T(8,128)(2,1)}, bf16[1216,768]{1,0:T(8,128)(2,1)}, u32[]{:S(2)}, u32[]{:S(2)}) collective-permute-start(bf16[1216,768]{1,0:T(8,128)(2,1)} %get-tuple-element.227), channel_id=1, source_target_pairs={{0,16},{1,17},{2,18},{3,19},{4,20},{5,21},{6,22},{7,23},{8,24},{9,... | collective-permute-start | bytes 5603336 | tf_op jit(solution)/shard_map/ppermute | solution.py:987
  667.3 52.5 %collective-permute-start.66 = (bf16[3200,256]{1,0:T(8,128)(2,1)S(1)}, bf16[3200,256]{1,0:T(8,128)(2,1)S(1)}, u32[]{:S(2)}, u32[]{:S(2)}) collective-permute-start(bf16[3200,256]{1,0:T(8,128)(2,1)S(1)} %copy-done.40), channel_id=1, source_target_pairs={{1,16},{3,18},{5,20},{7,22},{9,24},{11,26},{13,28},{15,30},{16,1},... | collective-permute-start | bytes 4915208 | tf_op jit(solution)/shard_map/ppermute | solution.py:987
  674.1 45.7 %collective-permute-start.67 = (bf16[3200,256]{1,0:T(8,128)(2,1)}, bf16[3200,256]{1,0:T(8,128)(2,1)}, u32[]{:S(2)}, u32[]{:S(2)}) collective-permute-start(bf16[3200,256]{1,0:T(8,128)(2,1)} %get-tuple-element.262), channel_id=1, source_target_pairs={{0,8},{1,24},{2,10},{3,26},{4,12},{5,28},{6,14},{7,30},{8,0},{9,16... | collective-permute-start | bytes 4915208 | tf_op jit(solution)/shard_map/ppermute | solution.py:987
  674.2 45.4 %collective-permute-start.64 = (bf16[304,1600]{1,0:T(8,128)(2,1)S(1)}, bf16[304,1600]{1,0:T(8,128)(2,1)S(1)}, u32[]{:S(2)}, u32[]{:S(2)}) collective-permute-start(bf16[304,1600]{1,0:T(8,128)(2,1)S(1)} %add.189), channel_id=1, source_target_pairs={{0,4},{1,5},{2,6},{3,7},{4,0},{5,1},{6,2},{7,3},{8,12},{9,13},{10,... | collective-permute-start | bytes 2918408 | tf_op jit(solution)/shard_map/ppermute | solution.py:987
  675.9 46.8 %collective-permute-start.68 = (bf16[192,1600]{1,0:T(8,128)(2,1)S(1)}, bf16[192,1600]{1,0:T(8,128)(2,1)}, u32[]{:S(2)}, u32[]{:S(2)}) collective-permute-start(bf16[192,1600]{1,0:T(8,128)(2,1)S(1)} %add.191), channel_id=1, source_target_pairs={{0,2},{1,3},{2,0},{3,1},{4,6},{5,7},{6,4},{7,5},{8,10},{9,11},{10,... | collective-permute-start | bytes 1843208 | tf_op jit(solution)/shard_map/ppermute | solution.py:987
  (140 other events, 1904.1 us)

commit v7 on v6

--- a/solution.py
+++ b/solution.py
@@ -24,7 +24,7 @@
     )
 
 
-COST_SCALE = 8
+COST_SCALE = 12
 
 
 def cost(flops, bytes_accessed, share=1.0):

time: 789 us -> 788 us (level)
    unnamed x170 -> x166, local copies, waits for them, and re-layouts: 18.1 us -> 16 us
  transfers between devices with their start and end apart: 80 -> 80, of which waited for: 26 -> 25; matrix products, arithmetic and copies ran while one was open for 12% -> 13% of each run, Pallas kernels for 38% -> 38%
where the time goes in v7:
time: 788 us; the launch traced here: 780 us
  Pallas kernels  359 us (46%)
  waiting for transfers between devices  206 us (26%)
  starting transfers between devices  87.8 us (11%)
  local copies, waits for them, and re-layouts  63.4 us (8%)
  other arithmetic  61.7 us (8%)
    ppermute x80, waiting for transfers between devices, move(): came = lax.ppermute(array, AXES, pairs)  206 us
    pallas_call x9, Pallas kernels, product(): pl.pallas_call(body, grid=(pl.cdiv(m, block),), in_specs=[left_spec] + [p...  127 us
    ppermute x80, starting transfers between devices, move(): came = lax.ppermute(array, AXES, pairs)  87.8 us
    pallas_call x4, Pallas kernels, product_parts(): pl.pallas_call(body, grid_spec=pltpu.PrefetchScalarGridSpec(num_scalar_pr...  63.3 us
    pallas_call x1, Pallas kernels, attention_back(): pl.pallas_call(backward_kernel, grid=(OWN_HEADS,), in_specs=[whole_spec((...  28.9 us
    pallas_call x1, Pallas kernels, attention(): pl.pallas_call(forward_kernel, grid=(OWN_HEADS,), in_specs=[whole_spec((1...  26.6 us
    unnamed x166, local copies, waits for them, and re-layouts  16 us
  transfers between devices with their start and end apart: 80, of which 25 were waited for; matrix products, arithmetic and copies ran while one was open for 13% of the time, Pallas kernels for 38%

profile of v7, /device:TPU:1, one launch (start us, length us, event | category | flops | bytes accessed | tf_op | source)
XLA Modules:
  0.0 780.0 jit_solution(5321600118619363208)
XLA Ops:
  25.1 59.8 %collective-permute-done.2 = bf16[1600,256]{1,0:T(8,128)(2,1)} collective-permute-done((bf16[1600,256]{1,0:T(8,128)(2,1)S(1)}, bf16[1600,256]{1,0:T(8,128)(2,1)}, u32[]{:S(2)}, u32[]{:S(2)}) %collective-permute-start.2) | collective-permute-done | bytes 819232 | tf_op jit(solution)/shard_map/ppermute | solution.py:987
  104.1 18.7 %collective-permute-done.7.refs_4_ = bf16[400,1600]{1,0:T(8,128)(2,1)} collective-permute-done((bf16[400,1600]{1,0:T(8,128)(2,1)S(1)}, bf16[400,1600]{1,0:T(8,128)(2,1)}, u32[]{:S(2)}, u32[]{:S(2)}) %collective-permute-start.7) | collective-permute-done | bytes 1280032 | tf_op jit(solution)/shard_map/ppermute | solution.py:987
  134.7 9.7 %collective-permute-done.13 = bf16[1600,256]{1,0:T(8,128)(2,1)} collective-permute-done((bf16[1600,256]{1,0:T(8,128)(2,1)S(1)}, bf16[1600,256]{1,0:T(8,128)(2,1)}, u32[]{:S(2)}, u32[]{:S(2)}) %collective-permute-start.13) | collective-permute-done | bytes 819232 | tf_op jit(solution)/shard_map/ppermute | solution.py:987
  155.3 14.7 %lay_heads.1 = (bf16[2496,1600]{1,0:T(8,128)(2,1)}, bf16[1600,832]{1,0:T(8,128)(2,1)}) custom-call(s32[1]{0:T(128)} %bitcast.5.core_ref, s32[4]{0:T(128)} %pad_add_fusion.1.places_ref, bf16[816,1600]{1,0:T(8,128)(2,1)} %pad_maximum_fusion.3.refs_0_, bf16[816,1600]{1,0:T(8,128)(2,1)} %collective-permute-done.refs_1_, ...), custom_call_target="tpu_custom_call" | custom-call | bytes 368640000 | tf_op jit(solution)/shard_map/lay_heads/pallas_call | solution.py:583
  173.9 14.0 %project_qkv.1.q_ref.k_ref.v_ref = bf16[2496,1024]{1,0:T(8,128)(2,1)} custom-call(bf16[2496,1600]{1,0:T(8,128)(2,1)} %get-tuple-element.157.left_ref, bf16[1600,1024]{1,0:T(8,128)(2,1)} %pad_maximum_fusion.refs_12_.refs_0_.refs_1_, f32[2496,1]{1,0:T(8,128)} %broadcast_in_dim.74.refs_1_, f32[2496,1]{1,0:T(8,128)} %fusion.refs_2_), custom_call_target="tpu_custom_call" | custom-call | flops 98146713600 | bytes 196509696 | tf_op jit(solution)/shard_map/project_qkv/pallas_call | solution.py:205
  190.4 26.6 %attention_forward.1 = (bf16[832,1024]{1,0:T(8,128)(2,1)S(1)}, f32[13,1,1024]{2,1,0:T(1,128)S(1)}) custom-call(s32[1,1024]{1,0:T(1,128)S(1)} %bitcast.38, s32[1024,1]{1,0:T(8,128)S(1)} %get-tuple-element.288.seg_col, bf16[2496,1024]{1,0:T(8,128)(2,1)S(1)} %copy-done.9, bf16[2496,1024]{1,0:T(8,128)(2,1)S(1)} %copy-done.9, bf16[2496,1024]{1,0:T(8,128)(2,1)S(1)} %copy-done.9), custom_call_target="tpu_custom_call" | custom-call | flops 167503724544 | bytes 81788928 | tf_op jit(solution)/shard_map/attention_forward/pallas_call | solution.py:128
  255.0 16.3 %collective-permute-done.24.refs_0_ = bf16[400,1600]{1,0:T(8,128)(2,1)S(1)} collective-permute-done((bf16[400,1600]{1,0:T(8,128)(2,1)}, bf16[400,1600]{1,0:T(8,128)(2,1)S(1)}, u32[]{:S(2)}, u32[]{:S(2)}) %collective-permute-start.24) | collective-permute-done | bytes 1280032 | tf_op jit(solution)/shard_map/ppermute | solution.py:987
  284.1 23.9 %project_up.1 = (bf16[1600,2048]{1,0:T(8,128)(2,1)}, bf16[1600,2048]{1,0:T(8,128)(2,1)}) custom-call(bf16[1600,1600]{1,0:T(8,128)(2,1)} %lay_far.2.left_ref, bf16[1600,512]{1,0:T(8,128)(2,1)} %get-tuple-element.180.refs_0_.refs_2_, bf16[1600,512]{1,0:T(8,128)(2,1)} %copy-done.77, bf16[1600,512]{1,0:T(8,128)(2,1)} %collective-permute-done.26.refs_2_.refs_4_, ...), custom_call_target="tpu_custom_call" | custom-call | flops 125829120000 | bytes 218726400 | tf_op jit(solution)/shard_map/project_up/pallas_call | solution.py:205
  308.0 19.5 %product_parts.4 = (bf16[800,896]{1,0:T(8,128)(2,1)}, bf16[800,768]{1,0:T(8,128)(2,1)}, bf16[800,896]{1,0:T(8,128)(2,1)}, bf16[800,768]{1,0:T(8,128)(2,1)}) custom-call(s32[4]{0:T(128)} %pad_add_fusion.order_ref, bf16[1600,512]{1,0:T(8,128)(2,1)} %pad_maximum_fusion.4.refs_5_.refs_0_.refs_4_, bf16[1600,512]{1,0:T(8,128)(2,1)} %collective-permute-done.17.refs_6_.refs_1_, ...), custom_call_target="tpu_custom_call" | custom-call | flops 125829120000 | bytes 140083200 | tf_op jit(solution)/shard_map/product_parts/pallas_call | solution.py:695
  330.5 19.6 %back_down.1 = (bf16[1600,1024]{1,0:T(8,128)(2,1)}, bf16[1600,1024]{1,0:T(8,128)(2,1)}, f32[1600,512]{1,0:T(8,128)}) custom-call(bf16[1600,1600]{1,0:T(8,128)(2,1)} %lay_far.3.left_ref, bf16[1600,512]{1,0:T(8,128)(2,1)} %pad_maximum_fusion.4.refs_5_.refs_0_.refs_4_, bf16[1600,512]{1,0:T(8,128)(2,1)} %collective-permute-done.17.refs_6_.refs_1_, ...), custom_call_target="tpu_custom_call" | custom-call | flops 125829120000 | bytes 218726400 | tf_op jit(solution)/shard_map/back_down/pallas_call | solution.py:205
  350.1 11.4 %back_up.2.refs_1_ = bf16[1600,1024]{1,0:T(8,128)(2,1)} custom-call(bf16[1600,1600]{1,0:T(8,128)(2,1)} %lay_far.2.left_ref, bf16[1600,1024]{1,0:T(8,128)(2,1)} %get-tuple-element.185.refs_0_.refs_1_), custom_call_target="tpu_custom_call" | custom-call | flops 62914560000 | bytes 140083200 | tf_op jit(solution)/shard_map/back_up/pallas_call | solution.py:205
  362.5 11.6 %back_up.3.refs_2_.refs_0_ = bf16[1600,1024]{1,0:T(8,128)(2,1)} custom-call(bf16[1600,1600]{1,0:T(8,128)(2,1)} %lay_far.2.left_ref, bf16[1600,1024]{1,0:T(8,128)(2,1)} %get-tuple-element.186.refs_0_, bf16[1600,1024]{1,0:T(8,128)(2,1)} %back_up.2.refs_1_, bf16[800,896]{1,0:T(8,128)(2,1)} %collective-permute-done.29.refs_2_.refs_1_, ...), custom_call_target="tpu_custom_call" | custom-call | flops 62914560000 | bytes 140083200 | tf_op jit(solution)/shard_map/back_up/pallas_call | solution.py:205
  382.3 17.2 %project_down.1 = (bf16[1600,1024]{1,0:T(8,128)(2,1)}, bf16[1600,1024]{1,0:T(8,128)(2,1)}) custom-call(bf16[1600,1600]{1,0:T(8,128)(2,1)} %lay_far.3.left_ref, bf16[1600,2048]{1,0:T(8,128)(2,1)} %get-tuple-element.183.refs_4_.refs_0_, bf16[1600,1024]{1,0:T(8,128)(2,1)} %copy-done.13, bf16[1600,1024]{1,0:T(8,128)(2,1)} %back_up.3.refs_2_.refs_0_), custom_call_target="tpu_custom_call" | custom-call | flops 125829120000 | bytes 218726400 | tf_op jit(solution)/shard_map/project_down/pallas_call | solution.py:205
  399.5 19.2 %product_parts.5 = (bf16[800,896]{1,0:T(8,128)(2,1)}, bf16[800,768]{1,0:T(8,128)(2,1)}, bf16[800,896]{1,0:T(8,128)(2,1)}, bf16[800,768]{1,0:T(8,128)(2,1)}) custom-call(s32[4]{0:T(128)} %pad_add_fusion.order_ref, bf16[1600,1024]{1,0:T(8,128)(2,1)} %get-tuple-element.186.refs_0_, bf16[1600,1024]{1,0:T(8,128)(2,1)} %get-tuple-element.185.refs_0_.refs_1_, ...), custom_call_target="tpu_custom_call" | custom-call | flops 125829120000 | bytes 140083200 | tf_op jit(solution)/shard_map/product_parts/pallas_call | solution.py:695
  418.7 10.9 %norm_mid_back.1 = (f32[1600,512]{1,0:T(8,128)}, bf16[1600,512]{1,0:T(8,128)(2,1)}, f32[4,1600,128]{2,1,0:T(8,128)}) custom-call(bf16[1600,1024]{1,0:T(8,128)(2,1)} %back_up.3.refs_2_.refs_0_, bf16[1600,1024]{1,0:T(8,128)(2,1)} %copy-done.13, bf16[1600,512]{1,0:T(8,128)(2,1)} %collective-permute-done.31.refs_2_.refs_6_, ...), custom_call_target="tpu_custom_call" | custom-call | bytes 589824000 | tf_op jit(solution)/shard_map/norm_mid_back/pallas_call | solution.py:335
  453.2 28.9 %attention_backward.1 = bf16[3,832,1024]{2,1,0:T(8,128)(2,1)} custom-call(s32[1,1024]{1,0:T(1,128)S(1)} %bitcast.39, s32[1024,1]{1,0:T(8,128)S(1)} %copy-done.4, bf16[2496,1024]{1,0:T(8,128)(2,1)} %project_qkv.1.q_ref.k_ref.v_ref, bf16[2496,1024]{1,0:T(8,128)(2,1)} %project_qkv.1.q_ref.k_ref.v_ref, bf16[2496,1024]{1,0:T(8,128)(2,1)} %project_qkv.1.q_ref.k_ref.v_ref, ...), custom_call_target="tpu_custom_call" | custom-call | flops 418759311360 | bytes 163577856 | tf_op jit(solution)/shard_map/attention_backward/pallas_call | solution.py:150
  494.1 8.4 %product_parts.6 = (bf16[800,512]{1,0:T(8,128)(2,1)}, bf16[800,384]{1,0:T(8,128)(2,1)}, bf16[800,512]{1,0:T(8,128)(2,1)}, bf16[800,384]{1,0:T(8,128)(2,1)}) custom-call(s32[4]{0:T(128)} %pad_add_fusion.order_ref, bf16[1600,1024]{1,0:T(8,128)(2,1)} %pad_maximum_fusion.1.refs_0_, bf16[832,1024]{1,0:T(8,128)(2,1)} %copy-done.7, ...), custom_call_target="tpu_custom_call" | custom-call | flops 32715571200 | bytes 71270400 | tf_op jit(solution)/shard_map/product_parts/pallas_call | solution.py:695
  502.6 14.8 %back_qkv.1 = (bf16[1600,512]{1,0:T(8,128)(2,1)}, bf16[1600,512]{1,0:T(8,128)(2,1)}) custom-call(bf16[2496,1600]{1,0:T(8,128)(2,1)} %get-tuple-element.157.left_ref, bf16[2496,1024]{1,0:T(8,128)(2,1)} %bitcast.41, f32[1600,1]{1,0:T(8,128)} %broadcast_in_dim.65.refs_1_, bf16[800,512]{1,0:T(8,128)(2,1)} %get-tuple-element.224.refs_2_), custom_call_target="tpu_custom_call" | custom-call | flops 98146713600 | bytes 196509696 | tf_op jit(solution)/shard_map/back_qkv/pallas_call | solution.py:205
  531.9 16.2 %product_parts.7 = (bf16[1216,896]{1,0:T(8,128)(2,1)}, bf16[1216,768]{1,0:T(8,128)(2,1)}, bf16[1216,896]{1,0:T(8,128)(2,1)}, bf16[1216,768]{1,0:T(8,128)(2,1)}) custom-call(s32[4]{0:T(128)} %pad_add_fusion.order_ref, bf16[2432,1024]{1,0:T(8,128)(2,1)} %join_heads.1.refs_0_, bf16[1600,1024]{1,0:T(8,128)(2,1)} %pad_maximum_fusion.refs_12_.refs_0_.refs_1_, ...), custom_call_target="tpu_custom_call" | custom-call | flops 95630131200 | bytes 153157632 | tf_op jit(solution)/shard_map/product_parts/pallas_call | solution.py:695
  572.2 8.7 %norm_in_back.1 = (bf16[1600,512]{1,0:T(8,128)(2,1)}, f32[2,1600,128]{2,1,0:T(8,128)}) custom-call(bf16[1600,512]{1,0:T(8,128)(2,1)} %get-tuple-element.230.refs_0_, bf16[1600,512]{1,0:T(8,128)(2,1)} %copy-done.40, bf16[1600,512]{1,0:T(8,128)(2,1)} %get-tuple-element.163.tokens_ref.refs_2_, f32[1600,512]{1,0:T(8,128)} %get-tuple-element.232.refs_3_, ...), custom_call_target="tpu_custom_call" | custom-call | bytes 589824000 | tf_op jit(solution)/shard_map/norm_in_back/pallas_call | solution.py:375
  644.7 8.5 %collective-permute-done.63 = f32[150,128]{1,0:T(8,128)S(1)} collective-permute-done((f32[150,128]{1,0:T(8,128)S(1)}, f32[150,128]{1,0:T(8,128)S(1)}, u32[]{:S(2)}, u32[]{:S(2)}) %collective-permute-start.63) | collective-permute-done | bytes 76832 | tf_op jit(solution)/shard_map/ppermute | solution.py:987
  683.3 20.3 %collective-permute-done.65 = bf16[200,896]{1,0:T(8,128)(2,1)S(1)} collective-permute-done((bf16[200,896]{1,0:T(8,128)(2,1)S(1)}, bf16[200,896]{1,0:T(8,128)(2,1)S(1)}, u32[]{:S(2)}, u32[]{:S(2)}) %collective-permute-start.65) | collective-permute-done | bytes 358432 | tf_op jit(solution)/shard_map/ppermute | solution.py:987
  703.7 15.0 %collective-permute-done.64 = bf16[304,1600]{1,0:T(8,128)(2,1)S(1)} collective-permute-done((bf16[304,1600]{1,0:T(8,128)(2,1)S(1)}, bf16[304,1600]{1,0:T(8,128)(2,1)S(1)}, u32[]{:S(2)}, u32[]{:S(2)}) %collective-permute-start.64) | collective-permute-done | bytes 972832 | tf_op jit(solution)/shard_map/ppermute | solution.py:987
  735.9 17.8 %collective-permute-done.73 = bf16[200,896]{1,0:T(8,128)(2,1)S(1)} collective-permute-done((bf16[200,896]{1,0:T(8,128)(2,1)S(1)}, bf16[200,896]{1,0:T(8,128)(2,1)S(1)}, u32[]{:S(2)}, u32[]{:S(2)}) %collective-permute-start.73) | collective-permute-done | bytes 358432 | tf_op jit(solution)/shard_map/ppermute | solution.py:987
  (429 shorter events, 346.4 us)
Async XLA Ops:
  4.4 83.3 %collective-permute-start = (bf16[816,1600]{1,0:T(8,128)(2,1)}, bf16[816,1600]{1,0:T(8,128)(2,1)}, u32[]{:S(2)}, u32[]{:S(2)}) collective-permute-start(bf16[816,1600]{1,0:T(8,128)(2,1)} %pad_maximum_fusion.3.refs_0_), channel_id=1, source_target_pairs={{0,8},{1,9},{2,10},{3,11},{4,12},{5,13},{6,14},{7,15},{8,0},{9,1},... | collective-permute-start | bytes 7833608 | tf_op jit(solution)/shard_map/ppermute | solution.py:987
  6.4 81.3 %collective-permute-start.1 = (bf16[816,1600]{1,0:T(8,128)(2,1)}, bf16[816,1600]{1,0:T(8,128)(2,1)}, u32[]{:S(2)}, u32[]{:S(2)}) collective-permute-start(bf16[816,1600]{1,0:T(8,128)(2,1)} %pad_maximum_fusion.3.refs_0_), channel_id=1, source_target_pairs={{0,16},{1,17},{2,18},{3,19},{4,20},{5,21},{6,22},{7,23},{8,24},{9,... | collective-permute-start | bytes 7833608 | tf_op jit(solution)/shard_map/ppermute | solution.py:987
  7.7 80.0 %collective-permute-start.4 = (bf16[816,1600]{1,0:T(8,128)(2,1)}, bf16[816,1600]{1,0:T(8,128)(2,1)}, u32[]{:S(2)}, u32[]{:S(2)}) collective-permute-start(bf16[816,1600]{1,0:T(8,128)(2,1)} %pad_maximum_fusion.3.refs_0_), channel_id=1, source_target_pairs={{0,1},{1,0},{2,3},{3,2},{4,5},{5,4},{6,7},{7,6},{8,9},{9,8},{10,11... | collective-permute-start | bytes 7833608 | tf_op jit(solution)/shard_map/ppermute | solution.py:987
  11.3 73.6 %collective-permute-start.2 = (bf16[1600,256]{1,0:T(8,128)(2,1)S(1)}, bf16[1600,256]{1,0:T(8,128)(2,1)}, u32[]{:S(2)}, u32[]{:S(2)}) collective-permute-start(bf16[1600,256]{1,0:T(8,128)(2,1)S(1)} %get-tuple-element.308), channel_id=1, source_target_pairs={{1,16},{3,18},{5,20},{7,22},{9,24},{11,26},{13,28},{15,30},{16,1},... | collective-permute-start | bytes 2457608 | tf_op jit(solution)/shard_map/ppermute | solution.py:987
  13.3 74.4 %collective-permute-start.3 = (bf16[1600,256]{1,0:T(8,128)(2,1)}, bf16[1600,256]{1,0:T(8,128)(2,1)S(1)}, u32[]{:S(2)}, u32[]{:S(2)}) collective-permute-start(bf16[1600,256]{1,0:T(8,128)(2,1)} %get-tuple-element.307), channel_id=1, source_target_pairs={{0,8},{1,24},{2,10},{3,26},{4,12},{5,28},{6,14},{7,30},{8,0},{9,16... | collective-permute-start | bytes 2457608 | tf_op jit(solution)/shard_map/ppermute | solution.py:987
  87.7 35.8 %collective-permute-start.8 = (bf16[816,1600]{1,0:T(8,128)(2,1)}, bf16[816,1600]{1,0:T(8,128)(2,1)}, u32[]{:S(2)}, u32[]{:S(2)}) collective-permute-start(bf16[816,1600]{1,0:T(8,128)(2,1)} %collective-permute-done.refs_1_), channel_id=1, source_target_pairs={{0,1},{1,0},{2,3},{3,2},{4,5},{5,4},{6,7},{7,6},{8,9},{9,8},{10,11... | collective-permute-start | bytes 7833608 | tf_op jit(solution)/shard_map/ppermute | solution.py:987
  152.3 74.3 %collective-permute-start.15 = (bf16[400,1600]{1,0:T(8,128)(2,1)}, bf16[400,1600]{1,0:T(8,128)(2,1)}, u32[]{:S(2)}, u32[]{:S(2)}) collective-permute-start(bf16[400,1600]{1,0:T(8,128)(2,1)} %constant_dynamic-slice_fusion.7.refs_0_), channel_id=1, source_target_pairs={{0,16},{1,17},{2,18},{3,19},{4,20},{5,21},{6,22},{7,23},{8,24},{9,... | collective-permute-start | bytes 3840008 | tf_op jit(solution)/shard_map/ppermute | solution.py:987
  152.4 74.3 %collective-permute-start.18 = (bf16[400,1600]{1,0:T(8,128)(2,1)}, bf16[400,1600]{1,0:T(8,128)(2,1)}, u32[]{:S(2)}, u32[]{:S(2)}) collective-permute-start(bf16[400,1600]{1,0:T(8,128)(2,1)} %constant_dynamic-slice_fusion.7.refs_0_), channel_id=1, source_target_pairs={{0,8},{1,9},{2,10},{3,11},{4,12},{5,13},{6,14},{7,15},{8,0},{9,1},... | collective-permute-start | bytes 3840008 | tf_op jit(solution)/shard_map/ppermute | solution.py:987
  153.7 73.0 %collective-permute-start.16 = (bf16[400,1600]{1,0:T(8,128)(2,1)}, bf16[400,1600]{1,0:T(8,128)(2,1)}, u32[]{:S(2)}, u32[]{:S(2)}) collective-permute-start(bf16[400,1600]{1,0:T(8,128)(2,1)} %concatenate.34.refs_0_), channel_id=1, source_target_pairs={{0,16},{1,17},{2,18},{3,19},{4,20},{5,21},{6,22},{7,23},{8,24},{9,... | collective-permute-start | bytes 3840008 | tf_op jit(solution)/shard_map/ppermute | solution.py:987
  155.1 71.6 %collective-permute-start.19 = (bf16[400,1600]{1,0:T(8,128)(2,1)}, bf16[400,1600]{1,0:T(8,128)(2,1)}, u32[]{:S(2)}, u32[]{:S(2)}) collective-permute-start(bf16[400,1600]{1,0:T(8,128)(2,1)} %concatenate.34.refs_0_), channel_id=1, source_target_pairs={{0,8},{1,9},{2,10},{3,11},{4,12},{5,13},{6,14},{7,15},{8,0},{9,1},... | collective-permute-start | bytes 3840008 | tf_op jit(solution)/shard_map/ppermute | solution.py:987
  172.6 54.1 %collective-permute-start.17 = (bf16[1600,512]{1,0:T(8,128)(2,1)}, bf16[1600,512]{1,0:T(8,128)(2,1)}, u32[]{:S(2)}, u32[]{:S(2)}) collective-permute-start(bf16[1600,512]{1,0:T(8,128)(2,1)} %pad_maximum_fusion.4.refs_5_.refs_0_.refs_4_), channel_id=1, source_target_pairs={{0,2},{1,3},{2,0},{3,1},{4,6},{5,7},{6,4},{7,5},{8,10},{9,11},{10,... | collective-permute-start | bytes 4915208 | tf_op jit(solution)/shard_map/ppermute | solution.py:987
  240.2 39.6 %collective-permute-start.25 = (bf16[1600,512]{1,0:T(8,128)(2,1)}, bf16[1600,512]{1,0:T(8,128)(2,1)S(1)}, u32[]{:S(2)}, u32[]{:S(2)}) collective-permute-start(bf16[1600,512]{1,0:T(8,128)(2,1)} %get-tuple-element.180.refs_0_.refs_2_), channel_id=1, source_target_pairs={{0,2},{1,3},{2,0},{3,1},{4,6},{5,7},{6,4},{7,5},{8,10},{9,11},{10,... | collective-permute-start | bytes 4915208 | tf_op jit(solution)/shard_map/ppermute | solution.py:987
  243.5 39.3 %collective-permute-start.26 = (bf16[1600,512]{1,0:T(8,128)(2,1)}, bf16[1600,512]{1,0:T(8,128)(2,1)}, u32[]{:S(2)}, u32[]{:S(2)}) collective-permute-start(bf16[1600,512]{1,0:T(8,128)(2,1)} %get-tuple-element.180.refs_0_.refs_2_), channel_id=1, source_target_pairs={{0,1},{1,0},{2,3},{3,2},{4,5},{5,4},{6,7},{7,6},{8,9},{9,8},{10,11... | collective-permute-start | bytes 4915208 | tf_op jit(solution)/shard_map/ppermute | solution.py:987
  376.7 42.0 %collective-permute-start.33 = (bf16[400,768]{1,0:T(8,128)(2,1)}, bf16[400,768]{1,0:T(8,128)(2,1)}, u32[]{:S(2)}, u32[]{:S(2)}) collective-permute-start(bf16[400,768]{1,0:T(8,128)(2,1)} %slice_add_fusion.7), channel_id=1, source_target_pairs={{0,8},{1,9},{2,10},{3,11},{4,12},{5,13},{6,14},{7,15},{8,0},{9,1},... | collective-permute-start | bytes 1843208 | tf_op jit(solution)/shard_map/ppermute | solution.py:987
  378.8 39.9 %collective-permute-start.32 = (bf16[400,896]{1,0:T(8,128)(2,1)}, bf16[400,896]{1,0:T(8,128)(2,1)}, u32[]{:S(2)}, u32[]{:S(2)}) collective-permute-start(bf16[400,896]{1,0:T(8,128)(2,1)} %slice_add_fusion.5), channel_id=1, source_target_pairs={{0,16},{1,17},{2,18},{3,19},{4,20},{5,21},{6,22},{7,23},{8,24},{9,... | collective-permute-start | bytes 2150408 | tf_op jit(solution)/shard_map/ppermute | solution.py:987
  381.1 37.6 %collective-permute-start.31 = (bf16[1600,512]{1,0:T(8,128)(2,1)}, bf16[1600,512]{1,0:T(8,128)(2,1)}, u32[]{:S(2)}, u32[]{:S(2)}) collective-permute-start(bf16[1600,512]{1,0:T(8,128)(2,1)} %slice_add_fusion.1), channel_id=1, source_target_pairs={{0,2},{1,3},{2,0},{3,1},{4,6},{5,7},{6,4},{7,5},{8,10},{9,11},{10,... | collective-permute-start | bytes 4915208 | tf_op jit(solution)/shard_map/ppermute | solution.py:987
  448.6 37.9 %collective-permute-start.38 = (bf16[208,1600]{1,0:T(8,128)(2,1)}, bf16[208,1600]{1,0:T(8,128)(2,1)}, u32[]{:S(2)}, u32[]{:S(2)}) collective-permute-start(bf16[208,1600]{1,0:T(8,128)(2,1)} %slice.114.refs_1_), channel_id=1, source_target_pairs={{0,4},{1,5},{2,6},{3,7},{4,0},{5,1},{6,2},{7,3},{8,12},{9,13},{10,... | collective-permute-start | bytes 1996808 | tf_op jit(solution)/shard_map/ppermute | solution.py:987
  551.0 46.3 %collective-permute-start.48 = (bf16[1216,896]{1,0:T(8,128)(2,1)}, bf16[1216,896]{1,0:T(8,128)(2,1)}, u32[]{:S(2)}, u32[]{:S(2)}) collective-permute-start(bf16[1216,896]{1,0:T(8,128)(2,1)} %get-tuple-element.226), channel_id=1, source_target_pairs={{0,8},{1,9},{2,10},{3,11},{4,12},{5,13},{6,14},{7,15},{8,0},{9,1},... | collective-permute-start | bytes 6537224 | tf_op jit(solution)/shard_map/ppermute | solution.py:987
  551.2 44.9 %collective-permute-start.49 = (bf16[1216,768]{1,0:T(8,128)(2,1)}, bf16[1216,768]{1,0:T(8,128)(2,1)}, u32[]{:S(2)}, u32[]{:S(2)}) collective-permute-start(bf16[1216,768]{1,0:T(8,128)(2,1)} %get-tuple-element.227), channel_id=1, source_target_pairs={{0,16},{1,17},{2,18},{3,19},{4,20},{5,21},{6,22},{7,23},{8,24},{9,... | collective-permute-start | bytes 5603336 | tf_op jit(solution)/shard_map/ppermute | solution.py:987
  630.0 36.3 %collective-permute-start.58 = (bf16[400,1600]{1,0:T(8,128)(2,1)}, bf16[400,1600]{1,0:T(8,128)(2,1)}, u32[]{:S(2)}, u32[]{:S(2)}) collective-permute-start(bf16[400,1600]{1,0:T(8,128)(2,1)} %collective-permute-done.45.refs_2_), channel_id=1, source_target_pairs={{0,1},{1,0},{2,3},{3,2},{4,5},{5,4},{6,7},{7,6},{8,9},{9,8},{10,11... | collective-permute-start | bytes 3840008 | tf_op jit(solution)/shard_map/ppermute | solution.py:987
  666.4 52.5 %collective-permute-start.66 = (bf16[3200,256]{1,0:T(8,128)(2,1)S(1)}, bf16[3200,256]{1,0:T(8,128)(2,1)S(1)}, u32[]{:S(2)}, u32[]{:S(2)}) collective-permute-start(bf16[3200,256]{1,0:T(8,128)(2,1)S(1)} %copy-done.38), channel_id=1, source_target_pairs={{1,16},{3,18},{5,20},{7,22},{9,24},{11,26},{13,28},{15,30},{16,1},... | collective-permute-start | bytes 4915208 | tf_op jit(solution)/shard_map/ppermute | solution.py:987
  671.9 47.1 %collective-permute-start.67 = (bf16[3200,256]{1,0:T(8,128)(2,1)}, bf16[3200,256]{1,0:T(8,128)(2,1)}, u32[]{:S(2)}, u32[]{:S(2)}) collective-permute-start(bf16[3200,256]{1,0:T(8,128)(2,1)} %get-tuple-element.262), channel_id=1, source_target_pairs={{0,8},{1,24},{2,10},{3,26},{4,12},{5,28},{6,14},{7,30},{8,0},{9,16... | collective-permute-start | bytes 4915208 | tf_op jit(solution)/shard_map/ppermute | solution.py:987
  672.5 46.2 %collective-permute-start.64 = (bf16[304,1600]{1,0:T(8,128)(2,1)S(1)}, bf16[304,1600]{1,0:T(8,128)(2,1)S(1)}, u32[]{:S(2)}, u32[]{:S(2)}) collective-permute-start(bf16[304,1600]{1,0:T(8,128)(2,1)S(1)} %add.189), channel_id=1, source_target_pairs={{0,4},{1,5},{2,6},{3,7},{4,0},{5,1},{6,2},{7,3},{8,12},{9,13},{10,... | collective-permute-start | bytes 2918408 | tf_op jit(solution)/shard_map/ppermute | solution.py:987
  674.1 47.7 %collective-permute-start.68 = (bf16[192,1600]{1,0:T(8,128)(2,1)S(1)}, bf16[192,1600]{1,0:T(8,128)(2,1)}, u32[]{:S(2)}, u32[]{:S(2)}) collective-permute-start(bf16[192,1600]{1,0:T(8,128)(2,1)S(1)} %add.191), channel_id=1, source_target_pairs={{0,2},{1,3},{2,0},{3,1},{4,6},{5,7},{6,4},{7,5},{8,10},{9,11},{10,... | collective-permute-start | bytes 1843208 | tf_op jit(solution)/shard_map/ppermute | solution.py:987
  (138 other events, 1905.7 us)
